TPU v7x, 512 devices: a whole 4x8x8 slice. The times are simulated.
512 devices in a mesh: side: 2 (over core), row: 8 (over z), vocab: 32 (over y, x).
Axes of the slice: x: 4, y: 8, z: 8, core: 2. Of those that a mesh axis runs over, the one named last changes fastest.
Arguments:
- hidden: bfloat16 [1536, 4096], P('row'), may hold values from -6 to 6
- head: bfloat16 [4096, 81920], P('row', ('side', 'vocab')), may hold values from -8 to 8
- teacher_logits: bfloat16 [1536, 81920], P('row', ('side', 'vocab')), may hold values from -20 to 400
- lengths: int32 [96], replicated, may hold values from 1 to 16, 864 in all
- slot_rollout: int32 [96], replicated, may hold values from 0 to 95, each once
- token_mask: int32 [1536], P('row'), may hold values 0 or 1
Outputs:
- slot_loss: float32 [96], P('row')
- hidden_grad: bfloat16 [1536, 4096], P('row', ('side', 'vocab'))
Inputs may be any that keep to these rules, and one draw needn't show every extreme that they name: `lengths`: the longest rollout has exactly 16 scored positions. `slot_rollout`: each rollout stands in exactly one slot.
All inputs are finite; a program needn't handle non-finite values. No bound on the sum of `token_mask` on one device may be relied on, other than what follows from the above.
Results may differ from a plain program's by a relative error of at most 0.0052.
Values may be sent and summed in bfloat16 or wider, within the bound.
No kernel may reach another device: no remote copies, remote signals or barrier semaphores. Data moves between devices by JAX's collectives and lax.ppermute only.
A program may use at most 64 MiB of HBM per device.

v0:
```python
import jax
import jax.numpy as jnp
from jax import lax
from jax.sharding import PartitionSpec as P

WIN = 16


loss_scale = 256.0


def joined(value, axis, join):
    pieces = jax.tree.map(lambda part: lax.all_gather(part, axis), value)
    head = jax.tree.map(lambda part: part[0], pieces)
    tail = jax.tree.map(lambda part: part[1:], pieces)
    subtotal, _ = lax.scan(lambda subtotal, section: (join(subtotal, section), None), head, tail)
    return subtotal


def rescale(peak_one, total_one, peak_two, total_two):
    peak_val = jnp.maximum(peak_one, peak_two)
    return (
        peak_val,
        total_one * jnp.exp(peak_one - peak_val) + total_two * jnp.exp(peak_two - peak_val),
    )


def split_combine(former, latter):
    student_peak, student_total = rescale(former[0], former[1], latter[0], latter[1])
    teacher_peak, teacher_total = rescale(former[2], former[3], latter[2], latter[3])
    return (student_peak, student_total, teacher_peak, teacher_total)


def body(hidden, head, teacher_logits, lengths, slot_rollout, token_mask):
    tok_rows = hidden.shape[0]
    slot_count = tok_rows // WIN
    row_place = lax.axis_index("row")
    own_slots = lax.dynamic_slice_in_dim(slot_rollout, row_place * slot_count, slot_count)
    chosen = own_slots[:, None] == jnp.arange(lengths.shape[0], dtype=jnp.int32)[None, :]
    slot_length = jnp.sum(jnp.where(chosen, lengths[None, :], 0), axis=1)
    length_tok = jnp.repeat(slot_length, WIN)
    position = jnp.arange(tok_rows, dtype=jnp.int32) % WIN
    usable = (token_mask > 0) & (position < length_tok)
    weight = jnp.where(usable, 1.0 / length_tok.astype(jnp.float32), 0.0)
    columns = lax.all_gather(head, "row", axis=0, tiled=True)
    logits = jnp.dot(hidden, columns, preferred_element_type=jnp.float32)
    teacher = teacher_logits.astype(jnp.float32)
    student_peak = jnp.max(logits, axis=1)
    teacher_peak = jnp.max(teacher, axis=1)
    student_exp = jnp.exp(logits - student_peak[:, None])
    student_total = jnp.sum(student_exp, axis=1)
    teacher_total = jnp.sum(jnp.exp(teacher - teacher_peak[:, None]), axis=1)
    student_peak, student_total, teacher_peak, teacher_total = joined(
        (student_peak, student_total, teacher_peak, teacher_total), ("side", "vocab"), split_combine
    )
    student_lse = student_peak + jnp.log(student_total)
    teacher_lse = teacher_peak + jnp.log(teacher_total)
    student = logits - student_lse[:, None]
    teacher_logp = teacher - teacher_lse[:, None]
    student_prob = jnp.exp(student)
    local_terms = jnp.sum(student_prob * (student - teacher_logp), axis=1)
    diverge = lax.psum(local_terms, ("side", "vocab"))
    logit_grad = (
        loss_scale * weight[:, None] * student_prob * (student - teacher_logp - diverge[:, None])
    ).astype(jnp.bfloat16)
    partial_grad = lax.dot_general(
        logit_grad, columns, (((1,), (1,)), ((), ())), preferred_element_type=jnp.float32
    )
    hidden_grad = lax.psum_scatter(
        partial_grad, ("side", "vocab"), scatter_dimension=1, tiled=True
    ).astype(jnp.bfloat16)
    slot_loss = jnp.sum((weight * diverge).reshape(slot_count, WIN), axis=1)
    return (slot_loss, hidden_grad)


def solution(mesh):
    in_specs = (
        P("row", None),
        P("row", ("side", "vocab")),
        P("row", ("side", "vocab")),
        P(),
        P(),
        P("row"),
    )
    out_specs = (P("row"), P("row", ("side", "vocab")))
    return jax.shard_map(body, mesh=mesh, in_specs=in_specs, out_specs=out_specs, check_vma=False)
```

profile of v0, /device:TPU:1, one launch (start us, length us, event | category | flops | bytes accessed | tf_op | source)
XLA Modules:
  0.0 643.5 jit_solution(3421258838068378842)
XLA Ops:
  7.2 0.0 copy-start
  7.2 0.0 all-gather.6.cloned.1.call-start
  7.2 0.7 all-gather.6.cloned.1.call-update
  7.9 0.0 all-reduce.7.cloned.1.call-start
  8.0 0.7 dynamic_slice.16
  8.7 0.8 select_reduce_fusion
  9.5 0.1 broadcast_in_dim.30
  9.6 0.1 reshape.30
  9.7 1.2 reduce_max.28
  10.9 1.3 dynamic-slice
  12.8 1.3 fusion.1
  14.2 0.3 dynamic-update-slice.3
  14.4 0.0 copy-start.3
  14.4 0.1 convert_dynamic-update-slice_fusion
  14.6 0.0 copy-start.4
  14.6 0.0 copy-start.6
  14.6 0.0 copy-start.1
  14.6 118.3 %all-gather.6.cloned.1.call-done = bf16[4096,1280]{1,0:T(8,128)(2,1)} async-done(((bf16[512,1280]{1,0:T(8,128)(2,1)}), bf16[4096,1280]{1,0:T(8,128)(2,1)}) %all-gather.6.cloned.1.call-update) | async-done | bytes 10485776 | tf_op jit(solution)/shard_map/all_gather | solution.py:45
  132.9 0.0 copy-done
  132.9 6.3 fusion.8
  139.1 0.0 copy-done.3
  139.2 0.0 copy-done.4
  139.2 0.3 dynamic-update-slice
  139.5 0.0 copy-start.5
  139.5 0.3 exponential_reduce_fusion
  139.8 0.3 dynamic-update-slice.1
  140.0 0.0 copy-start.2
  140.0 0.0 copy-done.5
  140.1 0.6 copy-done.2
  140.7 0.0 all-reduce.7.cloned.1.call-update
  140.7 0.0 reduce-scatter.2.cloned.1.call-start
  140.7 0.0 copy-done.6
  140.8 186.8 %all-reduce.7.cloned.1.call-done = (f32[12288]{0:T(1024)}, f32[12288]{0:T(1024)}, f32[12288]{0:T(1024)}, f32[12288]{0:T(1024)}) async-done(((f32[12288]{0:T(1024)}, f32[12288]{0:T(1024)}, f32[12288]{0:T(1024)}, f32[12288]{0:T(1024)}), (f32[12288]{0:T(1024)}, f32[12288]{0:T(1024)}, f32[12288]{0:T(1024)}, f32[12288]{0:T(1024)})) %all-reduce.7.cloned.1.call-update) | async-done | bytes 196624
  327.6 0.7 slice.40
  328.3 0.9 slice.44
  329.2 0.7 slice.41
  329.8 0.9 slice.45
  330.7 0.7 slice.42
  331.4 0.9 slice.46
  332.3 0.7 slice.43
  332.9 0.9 slice.47
  333.8 0.1 reshape.45
  333.9 0.1 reshape.46
  334.0 0.1 reshape.47
  334.1 0.1 reshape.48
  334.1 5.8 while.16
  340.0 0.0 copy-done.1
  340.0 0.4 multiply_reduce_fusion
  340.4 127.2 %psum.7 = f32[192]{0:T(256)S(1)} all-reduce(f32[192]{0:T(256)S(1)} %multiply_reduce_fusion), channel_id=1, replica_groups=mesh['side'=2,'row'=8,'vocab'=32] {'side','vocab'}, use_global_device_ids=true, to_apply=%region_8.9 | all-reduce | flops 192 | bytes 1536 | tf_op jit(solution)/shard_map/psum | solution.py:62
  467.6 9.1 %fusion.3 = f32[192,4096]{0,1:T(8,128)} fusion(bf16[4096,1280]{1,0:T(8,128)(2,1)} %all-gather.6.cloned.1.call-done, f32[192,1280]{1,0:T(8,128)S(1)} %get-tuple-element.89, bf16[192,1280]{1,0:T(8,128)(2,1)S(1)} %copy-done.1, f32[192]{0:T(256)S(1)} %psum.7, f32[192]{0:T(256)S(1)} %get-tuple-element.82, f32[192]{0:T(256)S(1)} %get-tuple-element.90, ...), kind=kOutput, calls=%fused_computation.14 | convolution fusion | flops 2015232000 | bytes 15109120 | tf_op jit(solution)/shard_map/dot_general | solution.py:66
  476.8 0.0 reduce-scatter.2.cloned.1.call-update
  476.8 0.1 reshape.31
  476.9 0.6 reduce_sum.49
  477.5 158.0 %reduce-scatter.2.cloned.1.call-done = f32[192,64]{0,1:T(8,128)} async-done(((f32[192,4096]{0,1:T(8,128)}), f32[192,64]{0,1:T(8,128)}) %reduce-scatter.2.cloned.1.call-update) | async-done | bytes 49168 | tf_op jit(solution)/shard_map/reduce_scatter | solution.py:69
  635.5 1.5 convert_element_type.15
  (260 shorter events, 4.0 us)
Async XLA Ops:
  7.2 125.7 %copy-start = (bf16[192,4096]{1,0:T(8,128)(2,1)S(1)}, bf16[192,4096]{1,0:T(8,128)(2,1)}, u32[]{:S(2)}) copy-start(bf16[192,4096]{1,0:T(8,128)(2,1)} %param.8) | copy-start | bytes 4718596
  7.2 125.7 %all-gather.6.cloned.1.call-start = ((), (), s32[]{:S(2)}) async-start(), calls=%async_computation.1 | async-start | bytes 11796480 | tf_op jit(solution)/shard_map/all_gather | solution.py:45
  7.9 319.7 %all-reduce.7.cloned.1.call-start = ((), (), s32[]{:S(2)}) async-start(), calls=%async_computation.3 | async-start | bytes 393216
  14.4 124.7 %copy-start.3 = (f32[12288]{0:T(1024)}, f32[12288]{0:T(1024)S(1)}, u32[]{:S(2)}) copy-start(f32[12288]{0:T(1024)S(1)} %dynamic-update-slice.3) | copy-start | bytes 147460
  14.6 124.6 %copy-start.4 = (f32[12288]{0:T(1024)}, f32[12288]{0:T(1024)S(1)}, u32[]{:S(2)}) copy-start(f32[12288]{0:T(1024)S(1)} %convert_dynamic-update-slice_fusion) | copy-start | bytes 147460
  14.6 126.2 %copy-start.6 = (s32[192]{0:T(256)S(1)}, s32[192]{0:T(256)}, u32[]{:S(2)}) copy-start(s32[192]{0:T(256)} %param.13) | copy-start | bytes 2308
  14.6 325.4 %copy-start.1 = (bf16[192,1280]{1,0:T(8,128)(2,1)S(1)}, bf16[192,1280]{1,0:T(8,128)(2,1)}, u32[]{:S(2)}) copy-start(bf16[192,1280]{1,0:T(8,128)(2,1)} %param.10) | copy-start | bytes 1474564
  139.5 0.6 copy-start.5
  140.0 0.6 copy-start.2
  140.7 494.8 %reduce-scatter.2.cloned.1.call-start = ((), (), s32[]{:S(2)}) async-start(), calls=%async_computation.2 | async-start | bytes 4259840 | tf_op jit(solution)/shard_map/reduce_scatter | solution.py:69
Sparse Core Ops, SparseCore 0:
  10.1 122.7 all-gather.5
  140.8 186.7 all-reduce.6
  476.9 158.5 reduce-scatter.1
where the time goes:
time: 648 us; the launch traced here: 643 us
  waiting for transfers between devices  464 us (72%)
  blocking collectives  127 us (20%)
  matrix products  15.4 us (2%)
  between operations  14.5 us (2%)
  local copies, waits for them, and re-layouts  11.6 us (2%)
  other arithmetic  8.88 us (1%)
    unnamed x4, waiting for transfers between devices  188 us
    reduce_scatter x1, waiting for transfers between devices, body(): lax.psum_scatter(partial_grad, ('side', 'vocab'), scatter_dimension=1, ti...  158 us
    psum x1, blocking collectives, body(): diverge = lax.psum(local_terms, ('side', 'vocab'))  127 us
    all_gather x1, waiting for transfers between devices, body(): columns = lax.all_gather(head, 'row', axis=0, tiled=True)  118 us
  transfers between devices with their start and end apart: 3, of which 3 were waited for; matrix products, arithmetic and copies ran while one was open for 1% of the time, Pallas kernels for 0%

commit v1 on v0

v1 whole, which is shorter than its diff:
```python
import jax
import jax.numpy as jnp
from jax import lax
from jax.sharding import PartitionSpec as P

WIN = 16


loss_scale = 256.0


def swap_side(value):
    return lax.ppermute(value, "side", [(0, 1), (1, 0)])


def from_all(value, count):
    return lax.all_to_all(jnp.broadcast_to(value, (count,) + value.shape), "vocab", 0, 0)


def join(peak, total, term):
    top = jnp.max(peak, axis=0)
    shift = peak - top
    scale = jnp.exp(shift)
    total_all = jnp.sum(total * scale, axis=0)
    if term is None:
        return top, total_all
    return top, total_all, jnp.sum(scale * (term + total * shift), axis=0)


def global_stats(peak, total, term, count):
    rows = [peak, total] if term is None else [peak, total, term]
    own = jnp.stack(rows)
    pair = jnp.stack([own, swap_side(own)])
    own = jnp.stack(join(*[pair[:, i] for i in range(len(rows))], *([None] if term is None else [])))
    gathered = from_all(own, count)
    return join(*[gathered[:, i] for i in range(len(rows))], *([None] if term is None else []))


def body(hidden, head, teacher_logits, lengths, slot_rollout, token_mask):
    tok_rows = hidden.shape[0]
    width = hidden.shape[1]
    count = lax.axis_size("vocab")
    slot_count = tok_rows // WIN
    row_place = lax.axis_index("row")
    side_place = lax.axis_index("side")
    own_slots = lax.dynamic_slice_in_dim(slot_rollout, row_place * slot_count, slot_count)
    chosen = own_slots[:, None] == jnp.arange(lengths.shape[0], dtype=jnp.int32)[None, :]
    slot_length = jnp.sum(jnp.where(chosen, lengths[None, :], 0), axis=1)
    length_tok = jnp.repeat(slot_length, WIN)
    position = jnp.arange(tok_rows, dtype=jnp.int32) % WIN
    usable = (token_mask > 0) & (position < length_tok)
    weight = jnp.where(usable, 1.0 / length_tok.astype(jnp.float32), 0.0)

    columns = lax.all_gather(head, "row", axis=0, tiled=True)

    teacher = teacher_logits.astype(jnp.float32)
    teacher_peak = jnp.max(teacher, axis=1)
    teacher_total = jnp.sum(jnp.exp(teacher - teacher_peak[:, None]), axis=1)
    teacher_peak, teacher_total = global_stats(teacher_peak, teacher_total, None, count)
    teacher_lse = teacher_peak + jnp.log(teacher_total)

    logits = jnp.dot(hidden, columns, preferred_element_type=jnp.float32)
    local_peak = jnp.max(logits, axis=1)
    gap = (logits - local_peak[:, None]) - (teacher - teacher_lse[:, None])
    local_exp = jnp.exp(logits - local_peak[:, None])
    local_total = jnp.sum(local_exp, axis=1)
    local_term = jnp.sum(local_exp * gap, axis=1)
    peak, total, term = global_stats(local_peak, local_total, local_term, count)
    log_total = jnp.log(total)
    diverge = term / total - log_total
    scale = loss_scale * weight / total
    shift = teacher_lse - peak - term / total
    logit_grad = (
        scale[:, None]
        * jnp.exp(logits - peak[:, None])
        * (logits - teacher + shift[:, None])
    ).astype(jnp.bfloat16)
    partial_grad = lax.dot_general(
        logit_grad, columns, (((1,), (1,)), ((), ())), preferred_element_type=jnp.float32
    )
    half = width // 2
    mine = lax.dynamic_slice_in_dim(partial_grad, side_place * half, half, axis=1)
    other = lax.dynamic_slice_in_dim(partial_grad, (1 - side_place) * half, half, axis=1)
    both = mine + swap_side(other)
    lanes = half // count
    packed = both.reshape(2, tok_rows // 2, count, lanes).transpose(2, 1, 0, 3)
    packed = packed.reshape(count, tok_rows // 2, 2 * lanes).astype(jnp.bfloat16)
    pieces = lax.all_to_all(packed, "vocab", 0, 0)
    summed = jnp.sum(pieces.astype(jnp.float32), axis=0).astype(jnp.bfloat16)
    hidden_grad = summed.reshape(tok_rows // 2, 2, lanes).transpose(1, 0, 2).reshape(tok_rows, lanes)
    slot_loss = jnp.sum((weight * diverge).reshape(slot_count, WIN), axis=1)
    return (slot_loss, hidden_grad)


def solution(mesh):
    in_specs = (
        P("row", None),
        P("row", ("side", "vocab")),
        P("row", ("side", "vocab")),
        P(),
        P(),
        P("row"),
    )
    out_specs = (P("row"), P("row", ("side", "vocab")))
    return jax.shard_map(body, mesh=mesh, in_specs=in_specs, out_specs=out_specs, check_vma=False)
```

time: 648 us -> 220 us (0.34)
  waiting for transfers between devices: 464 us -> 135 us
  blocking collectives: 127 us -> 12.9 us
  starting transfers between devices: 0.12 us -> 28.6 us
    unnamed x4 -> x1, waiting for transfers between devices: 188 us -> 0.68 us
    reduce_scatter x1 -> x0, waiting for transfers between devices: 158 us -> none  [body(): lax.psum_scatter(partial_grad, ('side', 'vocab'), scatter_dimension=1, ti...]
    psum x1 -> x0, blocking collectives: 127 us -> none  [body(): diverge = lax.psum(local_terms, ('side', 'vocab'))]
    all_to_all x0 -> x2, waiting for transfers between devices: none -> 29.8 us  [the longest x1 20.8 us: body(): pieces = lax.all_to_all(packed, 'vocab', 0, 0)]
    all_gather x1, waiting for transfers between devices: 118 us -> 99.6 us  [body(): columns = lax.all_gather(head, 'row', axis=0, tiled=True)]
    ppermute x0 -> x3, starting transfers between devices: none -> 15.4 us  [swap_side(): return lax.ppermute(value, 'side', [(0, 1), (1, 0)])]
    all_to_all x0 -> x2, starting transfers between devices: none -> 13.2 us  [the longest x1 9.26 us: from_all(): lax.all_to_all(jnp.broadcast_to(value, (count,) + value.shape), 'vocab',...]
    all_to_all x0 -> x1, blocking collectives: none -> 12.9 us  [from_all(): lax.all_to_all(jnp.broadcast_to(value, (count,) + value.shape), 'vocab',...]
  transfers between devices with their start and end apart: 3 -> 6, of which waited for: 3 -> 6; matrix products, arithmetic and copies ran while one was open for 1% -> 2% of each run, Pallas kernels for 0% -> 0%
where the time goes in v1:
time: 220 us; the launch traced here: 219 us
  waiting for transfers between devices  135 us (61%)
  starting transfers between devices  28.6 us (13%)
  between operations  14.3 us (6%)
  matrix products  13.9 us (6%)
  blocking collectives  12.9 us (6%)
  local copies, waits for them, and re-layouts  8.34 us (4%)
  other arithmetic  6.41 us (3%)
    all_gather x1, waiting for transfers between devices, body(): columns = lax.all_gather(head, 'row', axis=0, tiled=True)  99.6 us
    all_to_all x1, waiting for transfers between devices, body(): pieces = lax.all_to_all(packed, 'vocab', 0, 0)  20.8 us
    ppermute x3, starting transfers between devices, swap_side(): return lax.ppermute(value, 'side', [(0, 1), (1, 0)])  15.4 us
    all_to_all x1, blocking collectives, from_all(): lax.all_to_all(jnp.broadcast_to(value, (count,) + value.shape), 'vocab',...  12.9 us
    all_to_all x1, starting transfers between devices, from_all(): lax.all_to_all(jnp.broadcast_to(value, (count,) + value.shape), 'vocab',...  9.26 us
    all_to_all x1, waiting for transfers between devices, from_all(): lax.all_to_all(jnp.broadcast_to(value, (count,) + value.shape), 'vocab',...  8.91 us
    dot_general x1, matrix products, body(): lax.dot_general(logit_grad, columns, (((1,), (1,)), ((), ())), preferred_...  7.59 us
    dot_general x1, matrix products, body(): logits = jnp.dot(hidden, columns, preferred_element_type=jnp.float32)  6.27 us
  transfers between devices with their start and end apart: 6, of which 6 were waited for; matrix products, arithmetic and copies ran while one was open for 2% of the time, Pallas kernels for 0%

profile of v1, /device:TPU:1, one launch (start us, length us, event | category | flops | bytes accessed | tf_op | source)
XLA Modules:
  0.0 219.2 jit_solution(7124769730906994199)
XLA Ops:
  7.2 0.0 copy-start
  7.2 0.0 all-gather.2.cloned.1.call-start
  7.2 0.7 all-gather.2.cloned.1.call-update
  7.9 1.2 reduce_max.64
  9.1 1.3 fusion.1
  10.5 8.8 %collective-permute-start = (f32[2,192]{1,0:T(2,128)S(1)}, f32[2,192]{1,0:T(2,128)S(1)}, u32[]{:S(2)}, u32[]{:S(2)}) collective-permute-start(f32[2,192]{1,0:T(2,128)S(1)} %get-tuple-element.26), channel_id=1, source_target_pairs={{0,256},{256,0},{1,257},{257,1},{2,258},{258,2},{3,259},{259,3},{4... | collective-permute-start | bytes 4616 | tf_op jit(solution)/shard_map/ppermute | solution.py:13
  19.3 0.8 collective-permute-done
  20.1 12.9 %all_to_all.15 = f32[32,2,192]{2,1,0:T(2,128)S(1)} all-to-all(f32[32,2,192]{2,1,0:T(2,128)S(1)} %broadcast_in_dim.26), channel_id=1, replica_groups=mesh['side'=2,'row'=8,'vocab'=32] {'vocab'}, dimensions={0} | all-to-all | bytes 98304 | tf_op jit(solution)/shard_map/all_to_all | solution.py:17
  33.1 0.1 fusion.42
  33.2 0.0 copy-start.2
  33.2 0.0 copy-start.4
  33.2 0.0 copy-start.5
  33.2 0.0 copy-start.3
  33.2 99.6 %all-gather.2.cloned.1.call-done = bf16[4096,1280]{1,0:T(8,128)(2,1)} async-done(((bf16[512,1280]{1,0:T(8,128)(2,1)}), bf16[4096,1280]{1,0:T(8,128)(2,1)}) %all-gather.2.cloned.1.call-update) | async-done | bytes 10485776 | tf_op jit(solution)/shard_map/all_gather | solution.py:54
  132.9 0.0 copy-done
  132.9 6.3 %fusion.43 = (f32[192]{0:T(256)S(1)}, f32[192,1280]{1,0:T(8,128)S(1)}) fusion(bf16[192,4096]{1,0:T(8,128)(2,1)S(1)} %copy-done, bf16[4096,1280]{1,0:T(8,128)(2,1)} %all-gather.2.cloned.1.call-done), kind=kOutput, calls=%fused_computation.77 | convolution fusion | flops 2013511424 | bytes 13042432 | tf_op jit(solution)/shard_map/dot_general | solution.py:62
  139.1 0.0 copy-done.2
  139.1 0.5 exponential_reduce_fusion
  139.6 2.6 %collective-permute-start.1 = (f32[3,192]{1,0:T(4,128)S(1)}, f32[3,192]{1,0:T(4,128)S(1)}, u32[]{:S(2)}, u32[]{:S(2)}) collective-permute-start(f32[3,192]{1,0:T(4,128)S(1)} %get-tuple-element.24), channel_id=1, source_target_pairs={{0,256},{256,0},{1,257},{257,1},{2,258},{258,2},{3,259},{259,3},{4... | collective-permute-start | bytes 6920 | tf_op jit(solution)/shard_map/ppermute | solution.py:13
  142.2 0.8 collective-permute-done.1
  143.1 0.7 broadcast_in_dim.44
  143.8 9.3 %all-to-all-start.1 = ((f32[32,3,192]{2,1,0:T(4,128)}), f32[32,3,192]{2,1,0:T(4,128)S(1)}, u32[]{:S(2)}, u32[]{:S(2)}) async-start(f32[32,3,192]{2,1,0:T(4,128)} %broadcast_in_dim.44), calls=%async_computation.1 | async-start | bytes 262144 | tf_op jit(solution)/shard_map/all_to_all | solution.py:17
  153.0 0.0 copy-done.4
  153.0 0.1 dynamic_slice.9
  153.1 0.0 copy-done.5
  153.1 0.2 select_reduce_fusion
  153.3 0.1 broadcast_in_dim.24
  153.4 0.1 reshape.60
  153.5 8.9 %all-to-all-done.1 = f32[32,3,192]{2,1,0:T(4,128)S(1)} async-done(((f32[32,3,192]{2,1,0:T(4,128)}), f32[32,3,192]{2,1,0:T(4,128)S(1)}, u32[]{:S(2)}, u32[]{:S(2)}) %all-to-all-start.1) | async-done | bytes 73760 | tf_op jit(solution)/shard_map/all_to_all | solution.py:17
  162.4 0.1 fusion.41
  162.5 0.0 copy-done.3
  162.5 7.6 %fusion.8 = f32[192,4096]{1,0:T(8,128)S(1)} fusion(bf16[4096,1280]{1,0:T(8,128)(2,1)} %all-gather.2.cloned.1.call-done, f32[192,1280]{1,0:T(8,128)S(1)} %get-tuple-element.30, bf16[192,1280]{1,0:T(8,128)(2,1)S(1)} %copy-done.2, f32[192]{0:T(256)S(1)} %get-tuple-element.10, f32[192]{0:T(256)S(1)} %get-tuple-element.17, f32[192]{0:T(256)S(1)} %get-tuple-element.27), kind=kOutput, calls=%fused_computation.13 | convolution fusion | flops 2014986240 | bytes 15108352 | tf_op jit(solution)/shard_map/dot_general | solution.py:78
  170.1 0.0 copy-start.1
  170.1 1.7 copy-done.1
  171.8 0.1 constant_dynamic-slice_fusion
  171.9 4.0 %collective-permute-start.2 = (f32[192,2048]{1,0:T(8,128)S(1)}, f32[192,2048]{1,0:T(8,128)}, u32[]{:S(2)}, u32[]{:S(2)}) collective-permute-start(f32[192,2048]{1,0:T(8,128)S(1)} %constant_dynamic-slice_fusion), channel_id=1, source_target_pairs={{0,256},{256,0},{1,257},{257,1},{2,258},{258,2},{3,259},{259,3},{4... | collective-permute-start | bytes 4718600 | tf_op jit(solution)/shard_map/ppermute | solution.py:13
  175.9 3.1 %collective-permute-done.2 = f32[192,2048]{1,0:T(8,128)} collective-permute-done((f32[192,2048]{1,0:T(8,128)S(1)}, f32[192,2048]{1,0:T(8,128)}, u32[]{:S(2)}, u32[]{:S(2)}) %collective-permute-start.2) | collective-permute-done | bytes 1572896 | tf_op jit(solution)/shard_map/ppermute | solution.py:13
  179.1 2.1 add_convert_fusion
  181.1 0.5 copy.64
  181.7 1.4 convert_element_type.27
  183.1 1.5 copy.65
  184.6 1.2 copy.66
  185.8 3.9 %all-to-all-start.2 = ((bf16[32,96,128]{2,1,0:T(8,128)(2,1)}), bf16[32,96,128]{2,1,0:T(8,128)(2,1)S(1)}, u32[]{:S(2)}, u32[]{:S(2)}) async-start(bf16[32,96,128]{2,1,0:T(8,128)(2,1)} %copy.66), calls=%async_computation.2 | async-start | bytes 1572864 | tf_op jit(solution)/shard_map/all_to_all | solution.py:88
  189.8 0.1 reshape.61
  189.8 0.6 reduce_sum.121
  190.5 20.8 %all-to-all-done.2 = bf16[32,96,128]{2,1,0:T(8,128)(2,1)S(1)} async-done(((bf16[32,96,128]{2,1,0:T(8,128)(2,1)}), bf16[32,96,128]{2,1,0:T(8,128)(2,1)S(1)}, u32[]{:S(2)}, u32[]{:S(2)}) %all-to-all-start.2) | async-done | bytes 786464 | tf_op jit(solution)/shard_map/all_to_all | solution.py:88
  211.3 0.1 reduce_sum.122
  211.4 0.1 copy.67
  211.6 0.7 reshape.63
  (20 shorter events, 0.3 us)
Async XLA Ops:
  7.2 125.7 %copy-start = (bf16[192,4096]{1,0:T(8,128)(2,1)S(1)}, bf16[192,4096]{1,0:T(8,128)(2,1)}, u32[]{:S(2)}) copy-start(bf16[192,4096]{1,0:T(8,128)(2,1)} %param.6) | copy-start | bytes 4718596
  7.2 125.7 %all-gather.2.cloned.1.call-start = ((), (), s32[]{:S(2)}) async-start(), calls=%async_computation.3 | async-start | bytes 11796480 | tf_op jit(solution)/shard_map/all_gather | solution.py:54
  10.5 9.6 %collective-permute-start = (f32[2,192]{1,0:T(2,128)S(1)}, f32[2,192]{1,0:T(2,128)S(1)}, u32[]{:S(2)}, u32[]{:S(2)}) collective-permute-start(f32[2,192]{1,0:T(2,128)S(1)} %get-tuple-element.26), channel_id=1, source_target_pairs={{0,256},{256,0},{1,257},{257,1},{2,258},{258,2},{3,259},{259,3},{4... | collective-permute-start | bytes 4616 | tf_op jit(solution)/shard_map/ppermute | solution.py:13
  33.2 105.9 %copy-start.2 = (bf16[192,1280]{1,0:T(8,128)(2,1)S(1)}, bf16[192,1280]{1,0:T(8,128)(2,1)}, u32[]{:S(2)}) copy-start(bf16[192,1280]{1,0:T(8,128)(2,1)} %param.8) | copy-start | bytes 1474564
  33.2 119.8 %copy-start.4 = (s32[96]{0:T(128)S(1)}, s32[96]{0:T(128)}, u32[]{:S(2)}) copy-start(s32[96]{0:T(128)} %param.10) | copy-start | bytes 1156
  33.2 119.9 %copy-start.5 = (s32[96]{0:T(128)S(1)}, s32[96]{0:T(128)}, u32[]{:S(2)}) copy-start(s32[96]{0:T(128)} %param.9) | copy-start | bytes 1156
  33.2 129.3 %copy-start.3 = (s32[192]{0:T(256)S(1)}, s32[192]{0:T(256)}, u32[]{:S(2)}) copy-start(s32[192]{0:T(256)} %param.11) | copy-start | bytes 2308
  139.6 3.4 %collective-permute-start.1 = (f32[3,192]{1,0:T(4,128)S(1)}, f32[3,192]{1,0:T(4,128)S(1)}, u32[]{:S(2)}, u32[]{:S(2)}) collective-permute-start(f32[3,192]{1,0:T(4,128)S(1)} %get-tuple-element.24), channel_id=1, source_target_pairs={{0,256},{256,0},{1,257},{257,1},{2,258},{258,2},{3,259},{259,3},{4... | collective-permute-start | bytes 6920 | tf_op jit(solution)/shard_map/ppermute | solution.py:13
  143.8 18.6 %all-to-all-start.1 = ((f32[32,3,192]{2,1,0:T(4,128)}), f32[32,3,192]{2,1,0:T(4,128)S(1)}, u32[]{:S(2)}, u32[]{:S(2)}) async-start(f32[32,3,192]{2,1,0:T(4,128)} %broadcast_in_dim.44), calls=%async_computation.1 | async-start | bytes 262144 | tf_op jit(solution)/shard_map/all_to_all | solution.py:17
  170.1 1.7 copy-start.1
  171.9 7.2 %collective-permute-start.2 = (f32[192,2048]{1,0:T(8,128)S(1)}, f32[192,2048]{1,0:T(8,128)}, u32[]{:S(2)}, u32[]{:S(2)}) collective-permute-start(f32[192,2048]{1,0:T(8,128)S(1)} %constant_dynamic-slice_fusion), channel_id=1, source_target_pairs={{0,256},{256,0},{1,257},{257,1},{2,258},{258,2},{3,259},{259,3},{4... | collective-permute-start | bytes 4718600 | tf_op jit(solution)/shard_map/ppermute | solution.py:13
  185.8 25.5 %all-to-all-start.2 = ((bf16[32,96,128]{2,1,0:T(8,128)(2,1)}), bf16[32,96,128]{2,1,0:T(8,128)(2,1)S(1)}, u32[]{:S(2)}, u32[]{:S(2)}) async-start(bf16[32,96,128]{2,1,0:T(8,128)(2,1)} %copy.66), calls=%async_computation.2 | async-start | bytes 1572864 | tf_op jit(solution)/shard_map/all_to_all | solution.py:88
Sparse Core Ops, SparseCore 0:
  10.1 122.7 all-gather.1

commit v2 on v1

v2 whole, which is shorter than its diff:
```python
import functools

import jax
import jax.numpy as jnp
from jax import lax
from jax.experimental import pallas as pl
from jax.experimental.pallas import tpu as pltpu
from jax.sharding import PartitionSpec as P

WIN = 16
HALVES = 2


loss_scale = 256.0


def swap_side(value):
    return lax.ppermute(value, "side", [(0, 1), (1, 0)])


def from_all(value, count):
    return lax.all_to_all(jnp.broadcast_to(value, (count,) + value.shape), "vocab", 0, 0)


def join(peak, total, term):
    top = jnp.max(peak, axis=0)
    shift = peak - top
    scale = jnp.exp(shift)
    total_all = jnp.sum(total * scale, axis=0)
    return top, total_all, jnp.sum(scale * (term + total * shift), axis=0)


def join_pair(own):
    other = swap_side(own)
    return join(*[jnp.stack([own[i], other[i]]) for i in range(own.shape[0])])


def join_vocab(own, count):
    gathered = from_all(own, count)
    return join(*[gathered[:, i] for i in range(own.shape[0])])


def grad_kernel(blocks, place_ref, rows_ref, own_ref, *refs):
    chunk_refs = refs[:-4]
    keep_x, keep_y, send_x, send_y = refs[-4:]
    side = place_ref[0]
    row = place_ref[1]
    step = 1 - 2 * side
    toks = rows_ref.shape[0] // 2
    half_toks = toks // 2
    depth = own_ref.shape[0] // HALVES
    low = lax.broadcasted_iota(jnp.int32, (half_toks, 128), 1) < 64

    def one(chunk, distance, part):
        owner = lax.rem(row - distance * step + blocks, blocks)
        product = lax.dot_general(
            rows_ref[...], chunk, (((1,), (1,)), ((), ())), preferred_element_type=jnp.float32
        )
        pieces = []
        for kind in range(2):
            found = []
            for pair in range(depth // 128):
                lanes = slice(128 * pair, 128 * pair + 128)
                upper = product[kind * toks : kind * toks + half_toks, lanes]
                lower = product[kind * toks + half_toks : (kind + 1) * toks, lanes]
                found.append(jnp.where(low, upper, pltpu.roll(lower, 64, 1)))
                found.append(jnp.where(low, pltpu.roll(upper, 64, 1), lower))
            pieces.append(found)
        first = lax.rem(owner, blocks // 2) * (HALVES * depth // 64) + part * (depth // 64)
        mine = lax.div(owner, blocks // 2) == side

        @pl.when(mine)
        def _():
            for i in range(depth // 64):
                keep_x[first + i] = pieces[0][i]
                keep_y[first + i] = pieces[1][i]

        @pl.when(jnp.logical_not(mine))
        def _():
            for i in range(depth // 64):
                send_x[first + i] = pieces[0][i].astype(send_x.dtype)
                send_y[first + i] = pieces[1][i].astype(send_y.dtype)

    for part in range(HALVES):
        one(own_ref[part * depth : (part + 1) * depth, :], 0, part)
    for index, ref in enumerate(chunk_refs):
        one(ref[...], 1 + index // HALVES, index % HALVES)


def grad_products(place, rows, own, chunks, blocks, count):
    toks, cols = rows.shape[0] // 2, rows.shape[1]
    width = own.shape[0] * blocks
    vmem = pl.BlockSpec(memory_space=pltpu.VMEM)
    shape = (count, toks // 2, 128)
    return pl.pallas_call(
        functools.partial(grad_kernel, blocks),
        out_shape=[jax.ShapeDtypeStruct(shape, jnp.float32)] * 2 + [jax.ShapeDtypeStruct(shape, jnp.bfloat16)] * 2,
        in_specs=[pl.BlockSpec(memory_space=pltpu.SMEM)] + [vmem] * (2 + len(chunks)),
        out_specs=[vmem] * 4,
        compiler_params=pltpu.CompilerParams(vmem_limit_bytes=40 * 1024 * 1024),
        cost_estimate=pl.CostEstimate(
            flops=4 * toks * cols * width, bytes_accessed=2 * cols * width, transcendentals=0
        ),
    )(place, rows, own, *chunks)


def spread(value, lanes):
    split = value.reshape(2, -1)
    return jnp.concatenate([jnp.broadcast_to(split[i][:, None], (split.shape[1], lanes)) for i in range(2)], axis=1)


def body(hidden, head, teacher_logits, lengths, slot_rollout, token_mask):
    tok_rows = hidden.shape[0]
    count = lax.axis_size("vocab")
    blocks = lax.axis_size("row")
    slot_count = tok_rows // WIN
    row_place = lax.axis_index("row")
    side_place = lax.axis_index("side")
    own_slots = lax.dynamic_slice_in_dim(slot_rollout, row_place * slot_count, slot_count)
    chosen = own_slots[:, None] == jnp.arange(lengths.shape[0], dtype=jnp.int32)[None, :]
    slot_length = jnp.sum(jnp.where(chosen, lengths[None, :], 0), axis=1)
    length_tok = jnp.repeat(slot_length, WIN)
    position = jnp.arange(tok_rows, dtype=jnp.int32) % WIN
    usable = (token_mask > 0) & (position < length_tok)
    weight = jnp.where(usable, 1.0 / length_tok.astype(jnp.float32), 0.0)

    full = head.shape[0]
    depth = full // HALVES
    ring = [(i, (i + 1) % blocks) for i in range(blocks)]
    ring += [(blocks + i, blocks + (i - 1) % blocks) for i in range(blocks)]
    step = 1 - 2 * side_place
    held = [head[part * depth : (part + 1) * depth] for part in range(HALVES)]
    logits = jnp.dot(
        lax.dynamic_slice_in_dim(hidden, row_place * full, full, axis=1), head, preferred_element_type=jnp.float32
    )
    chunks = []
    for distance in range(1, blocks):
        held = [lax.ppermute(part, ("side", "row"), ring) for part in held]
        owner = (row_place - distance * step + blocks) % blocks
        for part in range(HALVES):
            piece = lax.dynamic_slice_in_dim(hidden, owner * full + part * depth, depth, axis=1)
            logits = logits + jnp.dot(piece, held[part], preferred_element_type=jnp.float32)
        chunks += held

    teacher = teacher_logits.astype(jnp.float32)
    teacher_peak = jnp.max(teacher, axis=1)
    teacher_total = jnp.sum(jnp.exp(teacher - teacher_peak[:, None]), axis=1)
    teacher_own = jnp.stack([teacher_peak, teacher_total, jnp.zeros_like(teacher_peak)])
    teacher_peak, teacher_total, _ = join_vocab(jnp.stack(join_pair(teacher_own)), count)
    teacher_lse = teacher_peak + jnp.log(teacher_total)

    local_peak = jnp.max(logits, axis=1)
    shifted = logits - local_peak[:, None]
    local_exp = jnp.exp(shifted)
    local_total = jnp.sum(local_exp, axis=1)
    local_term = jnp.sum(local_exp * (shifted - (teacher - teacher_lse[:, None])), axis=1)
    pair_peak, pair_total, pair_term = join_pair(jnp.stack([local_peak, local_total, local_term]))
    pair_mean = pair_term / pair_total
    shifted = logits - pair_peak[:, None]
    pair_exp = jnp.exp(shifted)
    centred = pair_exp * (shifted - (teacher - teacher_lse[:, None]) - pair_mean[:, None])
    rows = jnp.concatenate([centred, pair_exp]).astype(jnp.bfloat16)

    peak, total, term = join_vocab(jnp.stack([pair_peak, pair_total, pair_term]), count)
    mean = term / total
    diverge = mean - jnp.log(total)
    fall = pair_peak - peak
    scale = loss_scale * weight / total * jnp.exp(fall)
    offset = fall + pair_mean - mean

    place = jnp.stack([side_place, row_place]).astype(jnp.int32)
    keep_x, keep_y, send_x, send_y = grad_products(place, rows, head, chunks, blocks, count)
    sum_x = keep_x + swap_side(send_x).astype(jnp.float32)
    sum_y = keep_y + swap_side(send_y).astype(jnp.float32)
    packed = (spread(scale, 64) * (sum_x + spread(offset, 64) * sum_y)).astype(jnp.bfloat16)
    pieces = lax.all_to_all(packed, "vocab", 0, 0)
    summed = jnp.sum(pieces.astype(jnp.float32), axis=0).astype(jnp.bfloat16)
    hidden_grad = jnp.concatenate([summed[:, :64], summed[:, 64:]], axis=0)
    slot_loss = jnp.sum((weight * diverge).reshape(slot_count, WIN), axis=1)
    return (slot_loss, hidden_grad)


def solution(mesh):
    in_specs = (
        P("row", None),
        P("row", ("side", "vocab")),
        P("row", ("side", "vocab")),
        P(),
        P(),
        P("row"),
    )
    out_specs = (P("row"), P("row", ("side", "vocab")))
    return jax.shard_map(body, mesh=mesh, in_specs=in_specs, out_specs=out_specs, check_vma=False)
```

time: 220 us -> 212 us (0.964)
  waiting for transfers between devices: 135 us -> 72.6 us
  starting transfers between devices: 28.6 us -> 83.8 us
  Pallas kernels: 0 us -> 16.1 us
  between operations: 14.3 us -> 1.22 us
  blocking collectives: 12.9 us -> 0 us
  other arithmetic: 6.41 us -> 13.3 us
  local copies, waits for them, and re-layouts: 8.34 us -> 11.9 us
  matrix products: 13.9 us -> 11.5 us
    all_gather x1 -> x0, waiting for transfers between devices: 99.6 us -> none  [body(): columns = lax.all_gather(head, 'row', axis=0, tiled=True)]
    ppermute x0 -> x14, starting transfers between devices: none -> 50.1 us  [body(): held = [lax.ppermute(part, ('side', 'row'), ring) for part in held]]
    ppermute x0 -> x14, waiting for transfers between devices: none -> 35.9 us  [body(): held = [lax.ppermute(part, ('side', 'row'), ring) for part in held]]
    pallas_call x0 -> x1, Pallas kernels: none -> 16.1 us  [grad_products(): pl.pallas_call(functools.partial(grad_kernel, blocks), out_shape=[jax.Sha...]
    all_to_all x1 -> x0, blocking collectives: 12.9 us -> none  [from_all(): lax.all_to_all(jnp.broadcast_to(value, (count,) + value.shape), 'vocab',...]
    all_to_all x1 -> x2, starting transfers between devices: 9.26 us -> 19.3 us  [from_all(): lax.all_to_all(jnp.broadcast_to(value, (count,) + value.shape), 'vocab',...]
    ppermute x3 -> x4, starting transfers between devices: 15.4 us -> 10.3 us  [swap_side(): return lax.ppermute(value, 'side', [(0, 1), (1, 0)])]
    convert_element_type x4 -> x0, local copies, waits for them, and re-layouts: 4.67 us -> none  [body(): packed.reshape(count, tok_rows // 2, 2 * lanes).astype(jnp.bfloat16)]
  transfers between devices with their start and end apart: 6 -> 21, of which waited for: 6 -> 15; matrix products, arithmetic and copies ran while one was open for 2% -> 8% of each run, Pallas kernels for 0% -> 0%
where the time goes in v2:
time: 212 us; the launch traced here: 210 us
  starting transfers between devices  83.8 us (40%)
  waiting for transfers between devices  72.6 us (34%)
  Pallas kernels  16.1 us (8%)
  other arithmetic  13.3 us (6%)
  local copies, waits for them, and re-layouts  11.9 us (6%)
  matrix products  11.5 us (5%)
    ppermute x14, starting transfers between devices, body(): held = [lax.ppermute(part, ('side', 'row'), ring) for part in held]  50.1 us
    ppermute x14, waiting for transfers between devices, body(): held = [lax.ppermute(part, ('side', 'row'), ring) for part in held]  35.9 us
    all_to_all x1, waiting for transfers between devices, body(): pieces = lax.all_to_all(packed, 'vocab', 0, 0)  21.7 us
    all_to_all x2, starting transfers between devices, from_all(): lax.all_to_all(jnp.broadcast_to(value, (count,) + value.shape), 'vocab',...  19.3 us
    pallas_call x1, Pallas kernels, grad_products(): pl.pallas_call(functools.partial(grad_kernel, blocks), out_shape=[jax.Sha...  16.1 us
    all_to_all x2, waiting for transfers between devices, from_all(): lax.all_to_all(jnp.broadcast_to(value, (count,) + value.shape), 'vocab',...  13.4 us
    ppermute x4, starting transfers between devices, swap_side(): return lax.ppermute(value, 'side', [(0, 1), (1, 0)])  10.3 us
    dot_general x14, matrix products, body(): jnp.dot(piece, held[part], preferred_element_type=jnp.float32)  10.1 us
  transfers between devices with their start and end apart: 21, of which 15 were waited for; matrix products, arithmetic and copies ran while one was open for 8% of the time, Pallas kernels for 0%

profile of v2, /device:TPU:1, one launch (start us, length us, event | category | flops | bytes accessed | tf_op | source)
XLA Modules:
  0.0 210.3 jit_solution(12251306375037360474)
XLA Ops:
  0.7 2.6 %fusion.63 = (bf16[256,1280]{1,0:T(8,128)(2,1)}, bf16[256,1280]{1,0:T(8,128)(2,1)}) fusion(bf16[512,1280]{1,0:T(8,128)(2,1)} %own_ref.1), kind=kLoop, calls=%fused_computation.110 | loop fusion | bytes 2621440 | tf_op jit(solution)/shard_map/slice | solution.py:132
  3.3 11.5 %collective-permute-start.1 = (bf16[256,1280]{1,0:T(8,128)(2,1)}, bf16[256,1280]{1,0:T(8,128)(2,1)}, u32[]{:S(2)}, u32[]{:S(2)}) collective-permute-start(bf16[256,1280]{1,0:T(8,128)(2,1)} %get-tuple-element.31), channel_id=1, source_target_pairs={{0,32},{32,64},{64,96},{96,128},{128,160},{160,192},{192,224},{224... | collective-permute-start | bytes 1966088 | tf_op jit(solution)/shard_map/ppermute | solution.py:138
  14.8 2.2 %collective-permute-start = (bf16[256,1280]{1,0:T(8,128)(2,1)}, bf16[256,1280]{1,0:T(8,128)(2,1)}, u32[]{:S(2)}, u32[]{:S(2)}) collective-permute-start(bf16[256,1280]{1,0:T(8,128)(2,1)} %get-tuple-element.30), channel_id=1, source_target_pairs={{0,32},{32,64},{64,96},{96,128},{128,160},{160,192},{192,224},{224... | collective-permute-start | bytes 1966088 | tf_op jit(solution)/shard_map/ppermute | solution.py:138
  17.5 5.1 %collective-permute-done.1.refs_1_ = bf16[256,1280]{1,0:T(8,128)(2,1)} collective-permute-done((bf16[256,1280]{1,0:T(8,128)(2,1)}, bf16[256,1280]{1,0:T(8,128)(2,1)}, u32[]{:S(2)}, u32[]{:S(2)}) %collective-permute-start.1) | collective-permute-done | bytes 655392 | tf_op jit(solution)/shard_map/ppermute | solution.py:138
  22.6 5.0 %collective-permute-start.3 = (bf16[256,1280]{1,0:T(8,128)(2,1)}, bf16[256,1280]{1,0:T(8,128)(2,1)S(1)}, u32[]{:S(2)}, u32[]{:S(2)}) collective-permute-start(bf16[256,1280]{1,0:T(8,128)(2,1)} %collective-permute-done.1.refs_1_), channel_id=1, source_target_pairs={{0,32},{32,64},{64,96},{96,128},{128,160},{160,192},{192,224},{224... | collective-permute-start | bytes 1966088 | tf_op jit(solution)/shard_map/ppermute | solution.py:138
  27.7 1.9 collective-permute-start.14
  29.6 5.0 %collective-permute-start.2 = (bf16[256,1280]{1,0:T(8,128)(2,1)}, bf16[256,1280]{1,0:T(8,128)(2,1)}, u32[]{:S(2)}, u32[]{:S(2)}) collective-permute-start(bf16[256,1280]{1,0:T(8,128)(2,1)} %collective-permute-done.refs_0_), channel_id=1, source_target_pairs={{0,32},{32,64},{64,96},{96,128},{128,160},{160,192},{192,224},{224... | collective-permute-start | bytes 1966088 | tf_op jit(solution)/shard_map/ppermute | solution.py:138
  34.7 0.7 broadcast_in_dim.34
  35.4 9.8 %all-to-all-start = ((f32[32,3,192]{2,1,0:T(4,128)}), f32[32,3,192]{2,1,0:T(4,128)}, u32[]{:S(2)}, u32[]{:S(2)}) async-start(f32[32,3,192]{2,1,0:T(4,128)} %broadcast_in_dim.34), calls=%async_computation | async-start | bytes 262144 | tf_op jit(solution)/shard_map/all_to_all | solution.py:22
  45.2 1.9 collective-permute-start.5
  47.2 1.4 fusion.15
  48.5 1.9 collective-permute-start.4
  50.5 5.1 %all-to-all-done = f32[32,3,192]{2,1,0:T(4,128)} async-done(((f32[32,3,192]{2,1,0:T(4,128)}), f32[32,3,192]{2,1,0:T(4,128)}, u32[]{:S(2)}, u32[]{:S(2)}) %all-to-all-start) | async-done | bytes 73760 | tf_op jit(solution)/shard_map/all_to_all | solution.py:22
  55.6 1.1 fusion.65
  56.9 2.8 %collective-permute-start.7 = (bf16[256,1280]{1,0:T(8,128)(2,1)}, bf16[256,1280]{1,0:T(8,128)(2,1)S(1)}, u32[]{:S(2)}, u32[]{:S(2)}) collective-permute-start(bf16[256,1280]{1,0:T(8,128)(2,1)} %collective-permute-done.5.refs_5_), channel_id=1, source_target_pairs={{0,32},{32,64},{64,96},{96,128},{128,160},{160,192},{192,224},{224... | collective-permute-start | bytes 1966088 | tf_op jit(solution)/shard_map/ppermute | solution.py:138
  59.8 1.7 convolution_add_fusion.7
  61.5 2.5 %collective-permute-done.4.refs_4_ = bf16[256,1280]{1,0:T(8,128)(2,1)} collective-permute-done((bf16[256,1280]{1,0:T(8,128)(2,1)}, bf16[256,1280]{1,0:T(8,128)(2,1)}, u32[]{:S(2)}, u32[]{:S(2)}) %collective-permute-start.4) | collective-permute-done | bytes 655392 | tf_op jit(solution)/shard_map/ppermute | solution.py:138
  64.0 2.8 %collective-permute-start.6 = (bf16[256,1280]{1,0:T(8,128)(2,1)}, bf16[256,1280]{1,0:T(8,128)(2,1)S(1)}, u32[]{:S(2)}, u32[]{:S(2)}) collective-permute-start(bf16[256,1280]{1,0:T(8,128)(2,1)} %collective-permute-done.4.refs_4_), channel_id=1, source_target_pairs={{0,32},{32,64},{64,96},{96,128},{128,160},{160,192},{192,224},{224... | collective-permute-start | bytes 1966088 | tf_op jit(solution)/shard_map/ppermute | solution.py:138
  66.8 1.4 convolution_add_fusion.6
  68.5 2.4 %collective-permute-done.7.refs_7_ = bf16[256,1280]{1,0:T(8,128)(2,1)S(1)} collective-permute-done((bf16[256,1280]{1,0:T(8,128)(2,1)}, bf16[256,1280]{1,0:T(8,128)(2,1)S(1)}, u32[]{:S(2)}, u32[]{:S(2)}) %collective-permute-start.7) | collective-permute-done | bytes 655392 | tf_op jit(solution)/shard_map/ppermute | solution.py:138
  70.9 2.8 %collective-permute-start.9 = (bf16[256,1280]{1,0:T(8,128)(2,1)S(1)}, bf16[256,1280]{1,0:T(8,128)(2,1)S(1)}, u32[]{:S(2)}, u32[]{:S(2)}) collective-permute-start(bf16[256,1280]{1,0:T(8,128)(2,1)S(1)} %collective-permute-done.7.refs_7_), channel_id=1, source_target_pairs={{0,32},{32,64},{64,96},{96,128},{128,160},{160,192},{192,224},{224... | collective-permute-start | bytes 1966088 | tf_op jit(solution)/shard_map/ppermute | solution.py:138
  73.7 1.4 fusion
  75.1 2.8 %collective-permute-done.6.refs_6_ = bf16[256,1280]{1,0:T(8,128)(2,1)S(1)} collective-permute-done((bf16[256,1280]{1,0:T(8,128)(2,1)}, bf16[256,1280]{1,0:T(8,128)(2,1)S(1)}, u32[]{:S(2)}, u32[]{:S(2)}) %collective-permute-start.6) | collective-permute-done | bytes 655392 | tf_op jit(solution)/shard_map/ppermute | solution.py:138
  77.9 2.8 %collective-permute-start.8 = (bf16[256,1280]{1,0:T(8,128)(2,1)S(1)}, bf16[256,1280]{1,0:T(8,128)(2,1)S(1)}, u32[]{:S(2)}, u32[]{:S(2)}) collective-permute-start(bf16[256,1280]{1,0:T(8,128)(2,1)S(1)} %collective-permute-done.6.refs_6_), channel_id=1, source_target_pairs={{0,32},{32,64},{64,96},{96,128},{128,160},{160,192},{192,224},{224... | collective-permute-start | bytes 1966088 | tf_op jit(solution)/shard_map/ppermute | solution.py:138
  80.7 1.4 fusion.29
  82.1 1.4 fusion.1
  83.5 1.4 collective-permute-done.9.refs_9_
  84.9 2.8 %collective-permute-start.11 = (bf16[256,1280]{1,0:T(8,128)(2,1)S(1)}, bf16[256,1280]{1,0:T(8,128)(2,1)S(1)}, u32[]{:S(2)}, u32[]{:S(2)}) collective-permute-start(bf16[256,1280]{1,0:T(8,128)(2,1)S(1)} %collective-permute-done.9.refs_9_), channel_id=1, source_target_pairs={{0,32},{32,64},{64,96},{96,128},{128,160},{160,192},{192,224},{224... | collective-permute-start | bytes 1966088 | tf_op jit(solution)/shard_map/ppermute | solution.py:138
  88.1 3.9 %collective-permute-done.8.refs_8_ = bf16[256,1280]{1,0:T(8,128)(2,1)S(1)} collective-permute-done((bf16[256,1280]{1,0:T(8,128)(2,1)S(1)}, bf16[256,1280]{1,0:T(8,128)(2,1)S(1)}, u32[]{:S(2)}, u32[]{:S(2)}) %collective-permute-start.8) | collective-permute-done | bytes 655392 | tf_op jit(solution)/shard_map/ppermute | solution.py:138
  91.9 2.8 %collective-permute-start.10 = (bf16[256,1280]{1,0:T(8,128)(2,1)S(1)}, bf16[256,1280]{1,0:T(8,128)(2,1)S(1)}, u32[]{:S(2)}, u32[]{:S(2)}) collective-permute-start(bf16[256,1280]{1,0:T(8,128)(2,1)S(1)} %collective-permute-done.8.refs_8_), channel_id=1, source_target_pairs={{0,32},{32,64},{64,96},{96,128},{128,160},{160,192},{192,224},{224... | collective-permute-start | bytes 1966088 | tf_op jit(solution)/shard_map/ppermute | solution.py:138
  95.4 3.6 %collective-permute-done.11.refs_11_ = bf16[256,1280]{1,0:T(8,128)(2,1)S(1)} collective-permute-done((bf16[256,1280]{1,0:T(8,128)(2,1)S(1)}, bf16[256,1280]{1,0:T(8,128)(2,1)S(1)}, u32[]{:S(2)}, u32[]{:S(2)}) %collective-permute-start.11) | collective-permute-done | bytes 655392 | tf_op jit(solution)/shard_map/ppermute | solution.py:138
  99.0 2.8 %collective-permute-start.13 = (bf16[256,1280]{1,0:T(8,128)(2,1)S(1)}, bf16[256,1280]{1,0:T(8,128)(2,1)S(1)}, u32[]{:S(2)}, u32[]{:S(2)}) collective-permute-start(bf16[256,1280]{1,0:T(8,128)(2,1)S(1)} %collective-permute-done.11.refs_11_), channel_id=1, source_target_pairs={{0,32},{32,64},{64,96},{96,128},{128,160},{160,192},{192,224},{224... | collective-permute-start | bytes 1966088 | tf_op jit(solution)/shard_map/ppermute | solution.py:138
  102.1 3.9 %collective-permute-done.10.refs_10_ = bf16[256,1280]{1,0:T(8,128)(2,1)S(1)} collective-permute-done((bf16[256,1280]{1,0:T(8,128)(2,1)S(1)}, bf16[256,1280]{1,0:T(8,128)(2,1)S(1)}, u32[]{:S(2)}, u32[]{:S(2)}) %collective-permute-start.10) | collective-permute-done | bytes 655392 | tf_op jit(solution)/shard_map/ppermute | solution.py:138
  106.0 2.8 %collective-permute-start.12 = (bf16[256,1280]{1,0:T(8,128)(2,1)S(1)}, bf16[256,1280]{1,0:T(8,128)(2,1)S(1)}, u32[]{:S(2)}, u32[]{:S(2)}) collective-permute-start(bf16[256,1280]{1,0:T(8,128)(2,1)S(1)} %collective-permute-done.10.refs_10_), channel_id=1, source_target_pairs={{0,32},{32,64},{64,96},{96,128},{128,160},{160,192},{192,224},{224... | collective-permute-start | bytes 1966088 | tf_op jit(solution)/shard_map/ppermute | solution.py:138
  109.5 3.6 %collective-permute-done.13.refs_13_ = bf16[256,1280]{1,0:T(8,128)(2,1)S(1)} collective-permute-done((bf16[256,1280]{1,0:T(8,128)(2,1)S(1)}, bf16[256,1280]{1,0:T(8,128)(2,1)S(1)}, u32[]{:S(2)}, u32[]{:S(2)}) %collective-permute-start.13) | collective-permute-done | bytes 655392 | tf_op jit(solution)/shard_map/ppermute | solution.py:138
  113.3 6.7 %collective-permute-done.12.refs_12_ = bf16[256,1280]{1,0:T(8,128)(2,1)S(1)} collective-permute-done((bf16[256,1280]{1,0:T(8,128)(2,1)S(1)}, bf16[256,1280]{1,0:T(8,128)(2,1)S(1)}, u32[]{:S(2)}, u32[]{:S(2)}) %collective-permute-start.12) | collective-permute-done | bytes 655392 | tf_op jit(solution)/shard_map/ppermute | solution.py:138
  120.0 0.4 fusion.71
  120.4 0.5 copy-done.10
  120.9 0.9 copy-done.18
  121.9 0.5 exponential_reduce_fusion
  122.4 3.1 %collective-permute-start.15 = (f32[3,192]{1,0:T(4,128)S(1)}, f32[3,192]{1,0:T(4,128)}, u32[]{:S(2)}, u32[]{:S(2)}) collective-permute-start(f32[3,192]{1,0:T(4,128)S(1)} %pad_maximum_fusion.5), channel_id=1, source_target_pairs={{0,256},{256,0},{1,257},{257,1},{2,258},{258,2},{3,259},{259,3},{4... | collective-permute-start | bytes 6920 | tf_op jit(solution)/shard_map/ppermute | solution.py:18
  125.5 1.3 dynamic_slice.48
  126.9 0.8 fusion.67
  127.7 0.5 copy-done.23
  128.3 0.7 broadcast_in_dim.35
  128.9 9.6 %all-to-all-start.1 = ((f32[32,3,192]{2,1,0:T(4,128)}), f32[32,3,192]{2,1,0:T(4,128)}, u32[]{:S(2)}, u32[]{:S(2)}) async-start(f32[32,3,192]{2,1,0:T(4,128)} %broadcast_in_dim.35), calls=%async_computation.1 | async-start | bytes 262144 | tf_op jit(solution)/shard_map/all_to_all | solution.py:22
  138.5 0.9 select_reduce_fusion
  139.4 0.7 reshape.72
  140.2 8.2 %all-to-all-done.1 = f32[32,3,192]{2,1,0:T(4,128)} async-done(((f32[32,3,192]{2,1,0:T(4,128)}), f32[32,3,192]{2,1,0:T(4,128)}, u32[]{:S(2)}, u32[]{:S(2)}) %all-to-all-start.1) | async-done | bytes 73760 | tf_op jit(solution)/shard_map/all_to_all | solution.py:22
  148.4 1.2 fusion.64
  149.7 0.8 exponential_multiply_fusion
  150.4 1.2 add_subtract_fusion
  151.7 1.9 fusion.12
  153.7 1.0 copy-done.3
  155.0 1.1 copy-done.17
  156.1 16.1 %shard_map.77 = (f32[32,96,128]{2,1,0:T(8,128)}, f32[32,96,128]{2,1,0:T(8,128)}, bf16[32,96,128]{2,1,0:T(8,128)(2,1)S(1)}, bf16[32,96,128]{2,1,0:T(8,128)(2,1)S(1)}) custom-call(s32[2]{0:T(128)S(1)} %pad_add_fusion.place_ref, bf16[384,1280]{1,0:T(8,128)(2,1)S(1)} %pad_maximum_fusion.rows_ref, bf16[512,1280]{1,0:T(8,128)(2,1)S(1)} %copy-done.1, ...), custom_call_target="tpu_custom_call" | custom-call | flops 4026531840 | bytes 10485760 | tf_op jit(solution)/shard_map/pallas_call | solution.py:95
  172.2 3.3 %collective-permute-start.17 = (bf16[32,96,128]{2,1,0:T(8,128)(2,1)S(1)}, bf16[32,96,128]{2,1,0:T(8,128)(2,1)S(1)}, u32[]{:S(2)}, u32[]{:S(2)}) collective-permute-start(bf16[32,96,128]{2,1,0:T(8,128)(2,1)S(1)} %get-tuple-element.9), channel_id=1, source_target_pairs={{0,256},{256,0},{1,257},{257,1},{2,258},{258,2},{3,259},{259,3},{4... | collective-permute-start | bytes 2359304 | tf_op jit(solution)/shard_map/ppermute | solution.py:18
  175.5 1.9 collective-permute-start.16
  178.0 1.7 collective-permute-done.16
  179.7 3.3 %multiply_convert_fusion = bf16[32,96,128]{2,1,0:T(8,128)(2,1)} fusion(f32[32,96,128]{2,1,0:T(8,128)} %get-tuple-element.8, bf16[32,96,128]{2,1,0:T(8,128)(2,1)S(1)} %collective-permute-done.17, f32[32,96,128]{2,1,0:T(8,128)} %get-tuple-element.6, bf16[32,96,128]{2,1,0:T(8,128)(2,1)S(1)} %collective-permute-done.16, f32[96,128]{1,0:T(8,128)S(1)} %get-tuple-element.58, ...), kind=kLoop, calls=%fused_computation.14 | loop fusion | flops 3145728 | bytes 5603328 | tf_op jit(solution)/shard_map/convert_element_type | solution.py:175
  182.9 4.0 %all-to-all-start.2 = ((bf16[32,96,128]{2,1,0:T(8,128)(2,1)}), bf16[32,96,128]{2,1,0:T(8,128)(2,1)S(1)}, u32[]{:S(2)}, u32[]{:S(2)}) async-start(bf16[32,96,128]{2,1,0:T(8,128)(2,1)} %multiply_convert_fusion), calls=%async_computation.2 | async-start | bytes 1572864 | tf_op jit(solution)/shard_map/all_to_all | solution.py:176
  187.1 0.6 reduce_sum.131
  187.7 21.7 %all-to-all-done.2 = bf16[32,96,128]{2,1,0:T(8,128)(2,1)S(1)} async-done(((bf16[32,96,128]{2,1,0:T(8,128)(2,1)}), bf16[32,96,128]{2,1,0:T(8,128)(2,1)S(1)}, u32[]{:S(2)}, u32[]{:S(2)}) %all-to-all-start.2) | async-done | bytes 786464 | tf_op jit(solution)/shard_map/all_to_all | solution.py:176
  209.6 0.7 copy.19
  (91 shorter events, 5.0 us)
Async XLA Ops:
  0.6 46.5 %copy-start = (bf16[192,4096]{1,0:T(8,128)(2,1)S(1)}, bf16[192,4096]{1,0:T(8,128)(2,1)}, u32[]{:S(2)}) copy-start(bf16[192,4096]{1,0:T(8,128)(2,1)} %param.6) | copy-start | bytes 4718596
  0.6 46.5 %copy-start.1 = (bf16[512,1280]{1,0:T(8,128)(2,1)S(1)}, bf16[512,1280]{1,0:T(8,128)(2,1)}, u32[]{:S(2)}) copy-start(bf16[512,1280]{1,0:T(8,128)(2,1)} %own_ref.1) | copy-start | bytes 3932164
  0.7 16.3 %copy-start.19 = (bf16[192,1280]{1,0:T(8,128)(2,1)S(1)}, bf16[192,1280]{1,0:T(8,128)(2,1)}, u32[]{:S(2)}) copy-start(bf16[192,1280]{1,0:T(8,128)(2,1)} %param.8) | copy-start | bytes 1474564
  3.3 19.3 %collective-permute-start.1 = (bf16[256,1280]{1,0:T(8,128)(2,1)}, bf16[256,1280]{1,0:T(8,128)(2,1)}, u32[]{:S(2)}, u32[]{:S(2)}) collective-permute-start(bf16[256,1280]{1,0:T(8,128)(2,1)} %get-tuple-element.31), channel_id=1, source_target_pairs={{0,32},{32,64},{64,96},{96,128},{128,160},{160,192},{192,224},{224... | collective-permute-start | bytes 1966088 | tf_op jit(solution)/shard_map/ppermute | solution.py:138
  14.8 14.8 %collective-permute-start = (bf16[256,1280]{1,0:T(8,128)(2,1)}, bf16[256,1280]{1,0:T(8,128)(2,1)}, u32[]{:S(2)}, u32[]{:S(2)}) collective-permute-start(bf16[256,1280]{1,0:T(8,128)(2,1)} %get-tuple-element.30), channel_id=1, source_target_pairs={{0,32},{32,64},{64,96},{96,128},{128,160},{160,192},{192,224},{224... | collective-permute-start | bytes 1966088 | tf_op jit(solution)/shard_map/ppermute | solution.py:138
  22.6 22.6 %collective-permute-start.3 = (bf16[256,1280]{1,0:T(8,128)(2,1)}, bf16[256,1280]{1,0:T(8,128)(2,1)S(1)}, u32[]{:S(2)}, u32[]{:S(2)}) collective-permute-start(bf16[256,1280]{1,0:T(8,128)(2,1)} %collective-permute-done.1.refs_1_), channel_id=1, source_target_pairs={{0,32},{32,64},{64,96},{96,128},{128,160},{160,192},{192,224},{224... | collective-permute-start | bytes 1966088 | tf_op jit(solution)/shard_map/ppermute | solution.py:138
  27.7 7.0 %collective-permute-start.14 = (f32[3,192]{1,0:T(4,128)S(1)}, f32[3,192]{1,0:T(4,128)S(1)}, u32[]{:S(2)}, u32[]{:S(2)}) collective-permute-start(f32[3,192]{1,0:T(4,128)S(1)} %maximum_maximum_fusion), channel_id=1, source_target_pairs={{0,256},{256,0},{1,257},{257,1},{2,258},{258,2},{3,259},{259,3},{4... | collective-permute-start | bytes 6920 | tf_op jit(solution)/shard_map/ppermute | solution.py:18
  29.6 18.9 %collective-permute-start.2 = (bf16[256,1280]{1,0:T(8,128)(2,1)}, bf16[256,1280]{1,0:T(8,128)(2,1)}, u32[]{:S(2)}, u32[]{:S(2)}) collective-permute-start(bf16[256,1280]{1,0:T(8,128)(2,1)} %collective-permute-done.refs_0_), channel_id=1, source_target_pairs={{0,32},{32,64},{64,96},{96,128},{128,160},{160,192},{192,224},{224... | collective-permute-start | bytes 1966088 | tf_op jit(solution)/shard_map/ppermute | solution.py:138
  35.4 20.2 %all-to-all-start = ((f32[32,3,192]{2,1,0:T(4,128)}), f32[32,3,192]{2,1,0:T(4,128)}, u32[]{:S(2)}, u32[]{:S(2)}) async-start(f32[32,3,192]{2,1,0:T(4,128)} %broadcast_in_dim.34), calls=%async_computation | async-start | bytes 262144 | tf_op jit(solution)/shard_map/all_to_all | solution.py:22
  45.2 11.7 %collective-permute-start.5 = (bf16[256,1280]{1,0:T(8,128)(2,1)S(1)}, bf16[256,1280]{1,0:T(8,128)(2,1)}, u32[]{:S(2)}, u32[]{:S(2)}) collective-permute-start(bf16[256,1280]{1,0:T(8,128)(2,1)S(1)} %collective-permute-done.3.refs_3_), channel_id=1, source_target_pairs={{0,32},{32,64},{64,96},{96,128},{128,160},{160,192},{192,224},{224... | collective-permute-start | bytes 1966088 | tf_op jit(solution)/shard_map/ppermute | solution.py:138
  48.5 15.4 %collective-permute-start.4 = (bf16[256,1280]{1,0:T(8,128)(2,1)}, bf16[256,1280]{1,0:T(8,128)(2,1)}, u32[]{:S(2)}, u32[]{:S(2)}) collective-permute-start(bf16[256,1280]{1,0:T(8,128)(2,1)} %collective-permute-done.2.refs_2_), channel_id=1, source_target_pairs={{0,32},{32,64},{64,96},{96,128},{128,160},{160,192},{192,224},{224... | collective-permute-start | bytes 1966088 | tf_op jit(solution)/shard_map/ppermute | solution.py:138
  56.7 64.2 %copy-start.24 = (f32[192]{0:T(256)}, f32[192]{0:T(256)S(1)}, u32[]{:S(2)}) copy-start(f32[192]{0:T(256)S(1)} %log_add_fusion) | copy-start | bytes 2308
  56.9 13.9 %collective-permute-start.7 = (bf16[256,1280]{1,0:T(8,128)(2,1)}, bf16[256,1280]{1,0:T(8,128)(2,1)S(1)}, u32[]{:S(2)}, u32[]{:S(2)}) collective-permute-start(bf16[256,1280]{1,0:T(8,128)(2,1)} %collective-permute-done.5.refs_5_), channel_id=1, source_target_pairs={{0,32},{32,64},{64,96},{96,128},{128,160},{160,192},{192,224},{224... | collective-permute-start | bytes 1966088 | tf_op jit(solution)/shard_map/ppermute | solution.py:138
  64.0 13.9 %collective-permute-start.6 = (bf16[256,1280]{1,0:T(8,128)(2,1)}, bf16[256,1280]{1,0:T(8,128)(2,1)S(1)}, u32[]{:S(2)}, u32[]{:S(2)}) collective-permute-start(bf16[256,1280]{1,0:T(8,128)(2,1)} %collective-permute-done.4.refs_4_), channel_id=1, source_target_pairs={{0,32},{32,64},{64,96},{96,128},{128,160},{160,192},{192,224},{224... | collective-permute-start | bytes 1966088 | tf_op jit(solution)/shard_map/ppermute | solution.py:138
  70.9 16.9 %copy-start.2 = (bf16[256,1280]{1,0:T(8,128)(2,1)}, bf16[256,1280]{1,0:T(8,128)(2,1)S(1)}, u32[]{:S(2)}) copy-start(bf16[256,1280]{1,0:T(8,128)(2,1)S(1)} %collective-permute-done.7.refs_7_) | copy-start | bytes 1966084
  70.9 14.0 %collective-permute-start.9 = (bf16[256,1280]{1,0:T(8,128)(2,1)S(1)}, bf16[256,1280]{1,0:T(8,128)(2,1)S(1)}, u32[]{:S(2)}, u32[]{:S(2)}) collective-permute-start(bf16[256,1280]{1,0:T(8,128)(2,1)S(1)} %collective-permute-done.7.refs_7_), channel_id=1, source_target_pairs={{0,32},{32,64},{64,96},{96,128},{128,160},{160,192},{192,224},{224... | collective-permute-start | bytes 1966088 | tf_op jit(solution)/shard_map/ppermute | solution.py:138
  77.9 16.9 %copy-start.12 = (bf16[256,1280]{1,0:T(8,128)(2,1)}, bf16[256,1280]{1,0:T(8,128)(2,1)S(1)}, u32[]{:S(2)}) copy-start(bf16[256,1280]{1,0:T(8,128)(2,1)S(1)} %collective-permute-done.6.refs_6_) | copy-start | bytes 1966084
  77.9 14.0 %collective-permute-start.8 = (bf16[256,1280]{1,0:T(8,128)(2,1)S(1)}, bf16[256,1280]{1,0:T(8,128)(2,1)S(1)}, u32[]{:S(2)}, u32[]{:S(2)}) collective-permute-start(bf16[256,1280]{1,0:T(8,128)(2,1)S(1)} %collective-permute-done.6.refs_6_), channel_id=1, source_target_pairs={{0,32},{32,64},{64,96},{96,128},{128,160},{160,192},{192,224},{224... | collective-permute-start | bytes 1966088 | tf_op jit(solution)/shard_map/ppermute | solution.py:138
  84.9 10.2 %copy-start.4 = (bf16[256,1280]{1,0:T(8,128)(2,1)}, bf16[256,1280]{1,0:T(8,128)(2,1)S(1)}, u32[]{:S(2)}) copy-start(bf16[256,1280]{1,0:T(8,128)(2,1)S(1)} %collective-permute-done.9.refs_9_) | copy-start | bytes 1966084
  84.9 14.0 %collective-permute-start.11 = (bf16[256,1280]{1,0:T(8,128)(2,1)S(1)}, bf16[256,1280]{1,0:T(8,128)(2,1)S(1)}, u32[]{:S(2)}, u32[]{:S(2)}) collective-permute-start(bf16[256,1280]{1,0:T(8,128)(2,1)S(1)} %collective-permute-done.9.refs_9_), channel_id=1, source_target_pairs={{0,32},{32,64},{64,96},{96,128},{128,160},{160,192},{192,224},{224... | collective-permute-start | bytes 1966088 | tf_op jit(solution)/shard_map/ppermute | solution.py:138
  91.9 9.9 %copy-start.14 = (bf16[256,1280]{1,0:T(8,128)(2,1)}, bf16[256,1280]{1,0:T(8,128)(2,1)S(1)}, u32[]{:S(2)}) copy-start(bf16[256,1280]{1,0:T(8,128)(2,1)S(1)} %collective-permute-done.8.refs_8_) | copy-start | bytes 1966084
  91.9 14.0 %collective-permute-start.10 = (bf16[256,1280]{1,0:T(8,128)(2,1)S(1)}, bf16[256,1280]{1,0:T(8,128)(2,1)S(1)}, u32[]{:S(2)}, u32[]{:S(2)}) collective-permute-start(bf16[256,1280]{1,0:T(8,128)(2,1)S(1)} %collective-permute-done.8.refs_8_), channel_id=1, source_target_pairs={{0,32},{32,64},{64,96},{96,128},{128,160},{160,192},{192,224},{224... | collective-permute-start | bytes 1966088 | tf_op jit(solution)/shard_map/ppermute | solution.py:138
  99.0 9.9 %copy-start.6 = (bf16[256,1280]{1,0:T(8,128)(2,1)}, bf16[256,1280]{1,0:T(8,128)(2,1)S(1)}, u32[]{:S(2)}) copy-start(bf16[256,1280]{1,0:T(8,128)(2,1)S(1)} %collective-permute-done.11.refs_11_) | copy-start | bytes 1966084
  99.0 14.0 %collective-permute-start.13 = (bf16[256,1280]{1,0:T(8,128)(2,1)S(1)}, bf16[256,1280]{1,0:T(8,128)(2,1)S(1)}, u32[]{:S(2)}, u32[]{:S(2)}) collective-permute-start(bf16[256,1280]{1,0:T(8,128)(2,1)S(1)} %collective-permute-done.11.refs_11_), channel_id=1, source_target_pairs={{0,32},{32,64},{64,96},{96,128},{128,160},{160,192},{192,224},{224... | collective-permute-start | bytes 1966088 | tf_op jit(solution)/shard_map/ppermute | solution.py:138
  106.0 3.5 %copy-start.16 = (bf16[256,1280]{1,0:T(8,128)(2,1)}, bf16[256,1280]{1,0:T(8,128)(2,1)S(1)}, u32[]{:S(2)}) copy-start(bf16[256,1280]{1,0:T(8,128)(2,1)S(1)} %collective-permute-done.10.refs_10_) | copy-start | bytes 1966084
  106.0 14.0 %collective-permute-start.12 = (bf16[256,1280]{1,0:T(8,128)(2,1)S(1)}, bf16[256,1280]{1,0:T(8,128)(2,1)S(1)}, u32[]{:S(2)}, u32[]{:S(2)}) collective-permute-start(bf16[256,1280]{1,0:T(8,128)(2,1)S(1)} %collective-permute-done.10.refs_10_), channel_id=1, source_target_pairs={{0,32},{32,64},{64,96},{96,128},{128,160},{160,192},{192,224},{224... | collective-permute-start | bytes 1966088 | tf_op jit(solution)/shard_map/ppermute | solution.py:138
  113.0 7.4 %copy-start.8 = (bf16[256,1280]{1,0:T(8,128)(2,1)}, bf16[256,1280]{1,0:T(8,128)(2,1)S(1)}, u32[]{:S(2)}) copy-start(bf16[256,1280]{1,0:T(8,128)(2,1)S(1)} %collective-permute-done.13.refs_13_) | copy-start | bytes 1966084
  113.3 8.6 %copy-start.20 = (bf16[192,1280]{1,0:T(8,128)(2,1)S(1)}, bf16[192,1280]{1,0:T(8,128)(2,1)}, u32[]{:S(2)}) copy-start(bf16[192,1280]{1,0:T(8,128)(2,1)} %param.8) | copy-start | bytes 1474564
  120.0 0.9 copy-start.10
  120.9 1.0 copy-start.18
  122.4 4.5 %collective-permute-start.15 = (f32[3,192]{1,0:T(4,128)S(1)}, f32[3,192]{1,0:T(4,128)}, u32[]{:S(2)}, u32[]{:S(2)}) collective-permute-start(f32[3,192]{1,0:T(4,128)S(1)} %pad_maximum_fusion.5), channel_id=1, source_target_pairs={{0,256},{256,0},{1,257},{257,1},{2,258},{258,2},{3,259},{259,3},{4... | collective-permute-start | bytes 6920 | tf_op jit(solution)/shard_map/ppermute | solution.py:18
  127.7 0.6 copy-start.23
  127.7 0.5 copy-start.21
  127.7 0.6 copy-start.22
  128.9 19.5 %all-to-all-start.1 = ((f32[32,3,192]{2,1,0:T(4,128)}), f32[32,3,192]{2,1,0:T(4,128)}, u32[]{:S(2)}, u32[]{:S(2)}) async-start(f32[32,3,192]{2,1,0:T(4,128)} %broadcast_in_dim.35), calls=%async_computation.1 | async-start | bytes 262144 | tf_op jit(solution)/shard_map/all_to_all | solution.py:22
  148.4 5.2 %copy-start.15 = (bf16[256,1280]{1,0:T(8,128)(2,1)S(1)}, bf16[256,1280]{1,0:T(8,128)(2,1)}, u32[]{:S(2)}) copy-start(bf16[256,1280]{1,0:T(8,128)(2,1)} %copy-done.14) | copy-start | bytes 1966084
  151.7 2.0 copy-start.9
  151.7 2.0 copy-start.11
  151.7 2.0 copy-start.13
  153.5 1.1 copy-start.3
  153.5 1.3 copy-start.5
  153.6 1.5 copy-start.7
  155.0 1.1 copy-start.17
  172.2 5.8 %collective-permute-start.17 = (bf16[32,96,128]{2,1,0:T(8,128)(2,1)S(1)}, bf16[32,96,128]{2,1,0:T(8,128)(2,1)S(1)}, u32[]{:S(2)}, u32[]{:S(2)}) collective-permute-start(bf16[32,96,128]{2,1,0:T(8,128)(2,1)S(1)} %get-tuple-element.9), channel_id=1, source_target_pairs={{0,256},{256,0},{1,257},{257,1},{2,258},{258,2},{3,259},{259,3},{4... | collective-permute-start | bytes 2359304 | tf_op jit(solution)/shard_map/ppermute | solution.py:18
  175.5 4.2 %collective-permute-start.16 = (bf16[32,96,128]{2,1,0:T(8,128)(2,1)S(1)}, bf16[32,96,128]{2,1,0:T(8,128)(2,1)S(1)}, u32[]{:S(2)}, u32[]{:S(2)}) collective-permute-start(bf16[32,96,128]{2,1,0:T(8,128)(2,1)S(1)} %get-tuple-element.7), channel_id=1, source_target_pairs={{0,256},{256,0},{1,257},{257,1},{2,258},{258,2},{3,259},{259,3},{4... | collective-permute-start | bytes 2359304 | tf_op jit(solution)/shard_map/ppermute | solution.py:18
  182.9 4.1 %copy-start.25 = (f32[192]{0:T(256)S(1)}, f32[192]{0:T(256)}, u32[]{:S(2)}) copy-start(f32[192]{0:T(256)} %get-tuple-element.29) | copy-start | bytes 2308
  182.9 26.5 %all-to-all-start.2 = ((bf16[32,96,128]{2,1,0:T(8,128)(2,1)}), bf16[32,96,128]{2,1,0:T(8,128)(2,1)S(1)}, u32[]{:S(2)}, u32[]{:S(2)}) async-start(bf16[32,96,128]{2,1,0:T(8,128)(2,1)} %multiply_convert_fusion), calls=%async_computation.2 | async-start | bytes 1572864 | tf_op jit(solution)/shard_map/all_to_all | solution.py:176

commit v3 on v2

v3 whole, which is shorter than its diff:
```python
import functools

import jax
import jax.numpy as jnp
from jax import lax
from jax.experimental import pallas as pl
from jax.experimental.pallas import tpu as pltpu
from jax.sharding import PartitionSpec as P

WIN = 16
HALVES = 2
LANES = 128


loss_scale = 256.0


def swap_side(value):
    return lax.ppermute(value, "side", [(0, 1), (1, 0)])


def join(peak, total, teacher_peak, teacher_total, term):
    top = jnp.max(peak, axis=0, keepdims=True)
    teacher_top = jnp.max(teacher_peak, axis=0, keepdims=True)
    shift = peak - top
    teacher_shift = teacher_peak - teacher_top
    scale = jnp.exp(shift)
    return (
        top,
        jnp.sum(total * scale, axis=0, keepdims=True),
        teacher_top,
        jnp.sum(teacher_total * jnp.exp(teacher_shift), axis=0, keepdims=True),
        jnp.sum(scale * (term + total * (shift - teacher_shift)), axis=0, keepdims=True),
    )


def grad_kernel(blocks, place_ref, stats_ref, weight_ref, logits_ref, teacher_ref, own_ref, *refs):
    chunk_refs = refs[:-4]
    keep_ref, send_ref, diverge_ref, grad_ref = refs[-4:]
    side = place_ref[0]
    row = place_ref[1]
    step = 1 - 2 * side
    toks = logits_ref.shape[0]
    rest = toks - LANES
    depth = own_ref.shape[0] // HALVES

    peak, total, teacher_peak, teacher_total, term = join(*[stats_ref[:, i, :] for i in range(5)])
    mean = term / total
    diverge_ref[...] = mean - jnp.log(total) + jnp.log(teacher_total)
    scale = loss_scale * weight_ref[...] / total
    offset = teacher_peak - mean
    table = jnp.concatenate([peak, scale, offset, jnp.zeros((LANES - 3, toks), jnp.float32)], axis=0)
    table = jnp.concatenate([table, jnp.zeros((LANES, 2 * LANES - toks), jnp.float32)], axis=1)
    columns = jnp.transpose(table)[:toks]
    shifted = logits_ref[...] - columns[:, 0:1]
    slope = shifted - teacher_ref[...].astype(jnp.float32) + columns[:, 2:3]
    grad = columns[:, 1:2] * jnp.exp(shifted) * slope
    grad_ref[...] = jnp.transpose(grad).astype(jnp.bfloat16)
    low = lax.broadcasted_iota(jnp.int32, (32, LANES), 1) < rest

    def one(chunk, distance, part):
        owner = lax.rem(row - distance * step + blocks, blocks)
        product = jnp.dot(chunk, grad_ref[...], preferred_element_type=jnp.float32)
        first = lax.rem(owner, blocks // 2) * (HALVES * depth // 64) + part * (depth // 64)
        mine = lax.div(owner, blocks // 2) == side
        wide = jnp.concatenate([product[:, LANES:], jnp.zeros((depth, LANES - rest), jnp.float32)], axis=1)
        pieces = []
        for i in range(depth // 64):
            left = wide[64 * i : 64 * i + 32]
            right = wide[64 * i + 32 : 64 * i + 64]
            pieces.append((product[64 * i : 64 * i + 64, :LANES], jnp.where(low, left, pltpu.roll(right, rest, 1))))

        @pl.when(mine)
        def _():
            for i, (upper, lower) in enumerate(pieces):
                keep_ref[first + i, :64] = upper
                keep_ref[first + i, 64:] = lower

        @pl.when(jnp.logical_not(mine))
        def _():
            for i, (upper, lower) in enumerate(pieces):
                send_ref[first + i, :64] = upper.astype(send_ref.dtype)
                send_ref[first + i, 64:] = lower.astype(send_ref.dtype)

    for part in range(HALVES):
        one(own_ref[part * depth : (part + 1) * depth, :], 0, part)
    for index, ref in enumerate(chunk_refs):
        one(ref[...], 1 + index // HALVES, index % HALVES)


def grad_products(place, stats, weight, logits, teacher, own, chunks, blocks, count):
    toks, cols = logits.shape
    width = own.shape[0] * blocks
    vmem = pl.BlockSpec(memory_space=pltpu.VMEM)
    shape = (count, toks // 2, LANES)
    return pl.pallas_call(
        functools.partial(grad_kernel, blocks),
        out_shape=[
            jax.ShapeDtypeStruct(shape, jnp.float32),
            jax.ShapeDtypeStruct(shape, jnp.bfloat16),
            jax.ShapeDtypeStruct((1, toks), jnp.float32),
        ],
        in_specs=[pl.BlockSpec(memory_space=pltpu.SMEM)] + [vmem] * (5 + len(chunks)),
        out_specs=[vmem] * 3,
        scratch_shapes=[pltpu.VMEM((cols, toks), jnp.bfloat16)],
        compiler_params=pltpu.CompilerParams(vmem_limit_bytes=24 * 1024 * 1024),
        cost_estimate=pl.CostEstimate(
            flops=2 * toks * cols * width, bytes_accessed=2 * cols * width, transcendentals=toks * cols
        ),
    )(place, stats, weight, logits, teacher, own, *chunks)


def body(hidden, head, teacher_logits, lengths, slot_rollout, token_mask):
    tok_rows = hidden.shape[0]
    count = lax.axis_size("vocab")
    blocks = lax.axis_size("row")
    slot_count = tok_rows // WIN
    row_place = lax.axis_index("row")
    side_place = lax.axis_index("side")
    own_slots = lax.dynamic_slice_in_dim(slot_rollout, row_place * slot_count, slot_count)
    chosen = own_slots[:, None] == jnp.arange(lengths.shape[0], dtype=jnp.int32)[None, :]
    slot_length = jnp.sum(jnp.where(chosen, lengths[None, :], 0), axis=1)
    length_tok = jnp.repeat(slot_length, WIN)
    position = jnp.arange(tok_rows, dtype=jnp.int32) % WIN
    usable = (token_mask > 0) & (position < length_tok)
    weight = jnp.where(usable, 1.0 / length_tok.astype(jnp.float32), 0.0)

    full = head.shape[0]
    depth = full // HALVES
    ring = [(i, (i + 1) % blocks) for i in range(blocks)]
    ring += [(blocks + i, blocks + (i - 1) % blocks) for i in range(blocks)]
    step = 1 - 2 * side_place
    held = [head[part * depth : (part + 1) * depth] for part in range(HALVES)]
    logits = jnp.dot(
        lax.dynamic_slice_in_dim(hidden, row_place * full, full, axis=1), head, preferred_element_type=jnp.float32
    )
    chunks = []
    for distance in range(1, blocks):
        held = [lax.ppermute(part, ("side", "row"), ring) for part in held]
        owner = (row_place - distance * step + blocks) % blocks
        for part in range(HALVES):
            piece = lax.dynamic_slice_in_dim(hidden, owner * full + part * depth, depth, axis=1)
            logits = logits + jnp.dot(piece, held[part], preferred_element_type=jnp.float32)
        chunks += held

    teacher = teacher_logits.astype(jnp.float32)
    teacher_peak = jnp.max(teacher, axis=1)
    teacher_gap = teacher - teacher_peak[:, None]
    teacher_total = jnp.sum(jnp.exp(teacher_gap), axis=1)
    peak = jnp.max(logits, axis=1)
    shifted = logits - peak[:, None]
    powers = jnp.exp(shifted)
    total = jnp.sum(powers, axis=1)
    term = jnp.sum(powers * (shifted - teacher_gap), axis=1)
    blank = jnp.zeros_like(peak)
    own = jnp.stack([peak, total, teacher_peak, teacher_total, term, blank, blank, blank])
    other = swap_side(own)
    pair = jnp.concatenate([*join(*[jnp.stack([own[i], other[i]]) for i in range(5)]), own[5:]])
    stats = lax.all_to_all(jnp.broadcast_to(pair, (count,) + pair.shape), "vocab", 0, 0)

    place = jnp.stack([side_place, row_place]).astype(jnp.int32)
    keep, send, diverge = grad_products(
        place, stats, weight[None], logits, teacher_logits, head, chunks, blocks, count
    )
    packed = (keep + swap_side(send).astype(jnp.float32)).astype(jnp.bfloat16)
    pieces = lax.all_to_all(packed, "vocab", 0, 0)
    summed = jnp.sum(pieces.astype(jnp.float32), axis=0).astype(jnp.bfloat16)
    rest = tok_rows - LANES
    lower = jnp.concatenate([summed[64:, :rest], summed[64:, rest:]], axis=0)
    hidden_grad = jnp.concatenate([summed[:64], lower], axis=1).T
    slot_loss = jnp.sum((weight * diverge[0]).reshape(slot_count, WIN), axis=1)
    return (slot_loss, hidden_grad)


def solution(mesh):
    in_specs = (
        P("row", None),
        P("row", ("side", "vocab")),
        P("row", ("side", "vocab")),
        P(),
        P(),
        P("row"),
    )
    out_specs = (P("row"), P("row", ("side", "vocab")))
    return jax.shard_map(body, mesh=mesh, in_specs=in_specs, out_specs=out_specs, check_vma=False)
```

time: 212 us -> 201 us (0.948)
  waiting for transfers between devices: 72.6 us -> 61 us
  starting transfers between devices: 83.8 us -> 95.3 us
  other arithmetic: 13.3 us -> 3.48 us
  local copies, waits for them, and re-layouts: 11.9 us -> 17.6 us
  Pallas kernels: 16.1 us -> 11.3 us
  matrix products: 11.5 us -> 9.13 us
    ppermute x14, starting transfers between devices: 50.1 us -> 73 us  [body(): held = [lax.ppermute(part, ('side', 'row'), ring) for part in held]]
    unnamed x53 -> x60, local copies, waits for them, and re-layouts: 5.22 us -> 14.9 us
    all_to_all x2 -> x1, starting transfers between devices: 19.3 us -> 9.8 us  [body(): lax.all_to_all(jnp.broadcast_to(pair, (count,) + pair.shape), 'vocab', 0, 0)]
    ppermute x14, waiting for transfers between devices: 35.9 us -> 26.4 us  [body(): held = [lax.ppermute(part, ('side', 'row'), ring) for part in held]]
    pallas_call x1, Pallas kernels: 16.1 us -> 11.3 us  [grad_products(): pl.pallas_call(functools.partial(grad_kernel, blocks), out_shape=[jax.Sha...]
    slice x4 -> x1, other arithmetic: 3.08 us -> 0.01 us  [body(): other[i]]
    all_to_all x2 -> x1, waiting for transfers between devices: 13.4 us -> 11.1 us  [body(): lax.all_to_all(jnp.broadcast_to(pair, (count,) + pair.shape), 'vocab', 0, 0)]
    convert_element_type x1, other arithmetic: 3.26 us -> 1.05 us  [body(): packed = (keep + swap_side(send).astype(jnp.float32)).astype(jnp.bfloat16)]
  transfers between devices with their start and end apart: 21 -> 18, of which waited for: 15 -> 17; matrix products, arithmetic and copies ran while one was open for 8% -> 5% of each run, Pallas kernels for 0% -> 0%
where the time goes in v3:
time: 201 us; the launch traced here: 199 us
  starting transfers between devices  95.3 us (47%)
  waiting for transfers between devices  61 us (30%)
  local copies, waits for them, and re-layouts  17.6 us (9%)
  Pallas kernels  11.3 us (6%)
  matrix products  9.13 us (5%)
  other arithmetic  3.48 us (2%)
    ppermute x14, starting transfers between devices, body(): held = [lax.ppermute(part, ('side', 'row'), ring) for part in held]  73 us
    ppermute x14, waiting for transfers between devices, body(): held = [lax.ppermute(part, ('side', 'row'), ring) for part in held]  26.4 us
    all_to_all x1, waiting for transfers between devices, body(): pieces = lax.all_to_all(packed, 'vocab', 0, 0)  20.8 us
    unnamed x60, local copies, waits for them, and re-layouts  14.9 us
    pallas_call x1, Pallas kernels, grad_products(): pl.pallas_call(functools.partial(grad_kernel, blocks), out_shape=[jax.Sha...  11.3 us
    all_to_all x1, waiting for transfers between devices, body(): lax.all_to_all(jnp.broadcast_to(pair, (count,) + pair.shape), 'vocab', 0, 0)  11.1 us
    all_to_all x1, starting transfers between devices, body(): lax.all_to_all(jnp.broadcast_to(pair, (count,) + pair.shape), 'vocab', 0, 0)  9.8 us
    dot_general x14, matrix products, body(): jnp.dot(piece, held[part], preferred_element_type=jnp.float32)  8.7 us
  transfers between devices with their start and end apart: 18, of which 17 were waited for; matrix products, arithmetic and copies ran while one was open for 5% of the time, Pallas kernels for 0%

profile of v3, /device:TPU:1, one launch (start us, length us, event | category | flops | bytes accessed | tf_op | source)
XLA Modules:
  0.0 199.2 jit_solution(2986157113901460453)
XLA Ops:
  0.7 1.5 fusion.46
  2.2 11.5 %collective-permute-start.1 = (bf16[256,1280]{1,0:T(8,128)(2,1)S(1)}, bf16[256,1280]{1,0:T(8,128)(2,1)S(1)}, u32[]{:S(2)}, u32[]{:S(2)}) collective-permute-start(bf16[256,1280]{1,0:T(8,128)(2,1)S(1)} %get-tuple-element.15), channel_id=1, source_target_pairs={{0,32},{32,64},{64,96},{96,128},{128,160},{160,192},{192,224},{224... | collective-permute-start | bytes 1966088 | tf_op jit(solution)/shard_map/ppermute | solution.py:139
  13.7 2.2 %collective-permute-start = (bf16[256,1280]{1,0:T(8,128)(2,1)S(1)}, bf16[256,1280]{1,0:T(8,128)(2,1)S(1)}, u32[]{:S(2)}, u32[]{:S(2)}) collective-permute-start(bf16[256,1280]{1,0:T(8,128)(2,1)S(1)} %get-tuple-element.14), channel_id=1, source_target_pairs={{0,32},{32,64},{64,96},{96,128},{128,160},{160,192},{192,224},{224... | collective-permute-start | bytes 1966088 | tf_op jit(solution)/shard_map/ppermute | solution.py:139
  15.9 5.3 %collective-permute-done.1.refs_1_ = bf16[256,1280]{1,0:T(8,128)(2,1)S(1)} collective-permute-done((bf16[256,1280]{1,0:T(8,128)(2,1)S(1)}, bf16[256,1280]{1,0:T(8,128)(2,1)S(1)}, u32[]{:S(2)}, u32[]{:S(2)}) %collective-permute-start.1) | collective-permute-done | bytes 655392 | tf_op jit(solution)/shard_map/ppermute | solution.py:139
  21.2 0.8 copy-done.13
  22.0 5.0 %collective-permute-start.3 = (bf16[256,1280]{1,0:T(8,128)(2,1)S(1)}, bf16[256,1280]{1,0:T(8,128)(2,1)}, u32[]{:S(2)}, u32[]{:S(2)}) collective-permute-start(bf16[256,1280]{1,0:T(8,128)(2,1)S(1)} %collective-permute-done.1.refs_1_), channel_id=1, source_target_pairs={{0,32},{32,64},{64,96},{96,128},{128,160},{160,192},{192,224},{224... | collective-permute-start | bytes 1966088 | tf_op jit(solution)/shard_map/ppermute | solution.py:139
  27.1 1.2 collective-permute-done.refs_0_
  28.2 5.0 %collective-permute-start.2 = (bf16[256,1280]{1,0:T(8,128)(2,1)S(1)}, bf16[256,1280]{1,0:T(8,128)(2,1)}, u32[]{:S(2)}, u32[]{:S(2)}) collective-permute-start(bf16[256,1280]{1,0:T(8,128)(2,1)S(1)} %collective-permute-done.refs_0_), channel_id=1, source_target_pairs={{0,32},{32,64},{64,96},{96,128},{128,160},{160,192},{192,224},{224... | collective-permute-start | bytes 1966088 | tf_op jit(solution)/shard_map/ppermute | solution.py:139
  33.3 2.0 %collective-permute-done.3.refs_3_ = bf16[256,1280]{1,0:T(8,128)(2,1)} collective-permute-done((bf16[256,1280]{1,0:T(8,128)(2,1)S(1)}, bf16[256,1280]{1,0:T(8,128)(2,1)}, u32[]{:S(2)}, u32[]{:S(2)}) %collective-permute-start.3) | collective-permute-done | bytes 655392 | tf_op jit(solution)/shard_map/ppermute | solution.py:139
  35.3 5.1 %collective-permute-start.5 = (bf16[256,1280]{1,0:T(8,128)(2,1)}, bf16[256,1280]{1,0:T(8,128)(2,1)}, u32[]{:S(2)}, u32[]{:S(2)}) collective-permute-start(bf16[256,1280]{1,0:T(8,128)(2,1)} %collective-permute-done.3.refs_3_), channel_id=1, source_target_pairs={{0,32},{32,64},{64,96},{96,128},{128,160},{160,192},{192,224},{224... | collective-permute-start | bytes 1966088 | tf_op jit(solution)/shard_map/ppermute | solution.py:139
  40.4 1.9 collective-permute-done.2.refs_2_
  42.3 5.1 %collective-permute-start.4 = (bf16[256,1280]{1,0:T(8,128)(2,1)}, bf16[256,1280]{1,0:T(8,128)(2,1)}, u32[]{:S(2)}, u32[]{:S(2)}) collective-permute-start(bf16[256,1280]{1,0:T(8,128)(2,1)} %collective-permute-done.2.refs_2_), channel_id=1, source_target_pairs={{0,32},{32,64},{64,96},{96,128},{128,160},{160,192},{192,224},{224... | collective-permute-start | bytes 1966088 | tf_op jit(solution)/shard_map/ppermute | solution.py:139
  47.8 0.4 fusion.6
  48.3 1.1 collective-permute-done.5.refs_5_
  49.4 5.0 %collective-permute-start.7 = (bf16[256,1280]{1,0:T(8,128)(2,1)}, bf16[256,1280]{1,0:T(8,128)(2,1)S(1)}, u32[]{:S(2)}, u32[]{:S(2)}) collective-permute-start(bf16[256,1280]{1,0:T(8,128)(2,1)} %collective-permute-done.5.refs_5_), channel_id=1, source_target_pairs={{0,32},{32,64},{64,96},{96,128},{128,160},{160,192},{192,224},{224... | collective-permute-start | bytes 1966088 | tf_op jit(solution)/shard_map/ppermute | solution.py:139
  54.7 1.7 collective-permute-done.4.refs_4_
  56.4 5.0 %collective-permute-start.6 = (bf16[256,1280]{1,0:T(8,128)(2,1)}, bf16[256,1280]{1,0:T(8,128)(2,1)S(1)}, u32[]{:S(2)}, u32[]{:S(2)}) collective-permute-start(bf16[256,1280]{1,0:T(8,128)(2,1)} %collective-permute-done.4.refs_4_), channel_id=1, source_target_pairs={{0,32},{32,64},{64,96},{96,128},{128,160},{160,192},{192,224},{224... | collective-permute-start | bytes 1966088 | tf_op jit(solution)/shard_map/ppermute | solution.py:139
  61.5 0.3 convolution_add_fusion.6
  61.8 1.4 fusion.23
  63.5 4.9 %collective-permute-start.9 = (bf16[256,1280]{1,0:T(8,128)(2,1)S(1)}, bf16[256,1280]{1,0:T(8,128)(2,1)S(1)}, u32[]{:S(2)}, u32[]{:S(2)}) collective-permute-start(bf16[256,1280]{1,0:T(8,128)(2,1)S(1)} %collective-permute-done.7.refs_7_), channel_id=1, source_target_pairs={{0,32},{32,64},{64,96},{96,128},{128,160},{160,192},{192,224},{224... | collective-permute-start | bytes 1966088 | tf_op jit(solution)/shard_map/ppermute | solution.py:139
  68.4 1.4 fusion
  69.8 0.7 collective-permute-done.6.refs_6_
  70.5 4.9 %collective-permute-start.8 = (bf16[256,1280]{1,0:T(8,128)(2,1)S(1)}, bf16[256,1280]{1,0:T(8,128)(2,1)S(1)}, u32[]{:S(2)}, u32[]{:S(2)}) collective-permute-start(bf16[256,1280]{1,0:T(8,128)(2,1)S(1)} %collective-permute-done.6.refs_6_), channel_id=1, source_target_pairs={{0,32},{32,64},{64,96},{96,128},{128,160},{160,192},{192,224},{224... | collective-permute-start | bytes 1966088 | tf_op jit(solution)/shard_map/ppermute | solution.py:139
  75.4 1.4 fusion.20
  76.8 1.4 fusion.1
  78.2 4.2 %collective-permute-start.11 = (bf16[256,1280]{1,0:T(8,128)(2,1)S(1)}, bf16[256,1280]{1,0:T(8,128)(2,1)S(1)}, u32[]{:S(2)}, u32[]{:S(2)}) collective-permute-start(bf16[256,1280]{1,0:T(8,128)(2,1)S(1)} %collective-permute-done.9.refs_9_), channel_id=1, source_target_pairs={{0,32},{32,64},{64,96},{96,128},{128,160},{160,192},{192,224},{224... | collective-permute-start | bytes 1966088 | tf_op jit(solution)/shard_map/ppermute | solution.py:139
  82.7 1.7 collective-permute-done.8.refs_8_
  84.4 5.0 %collective-permute-start.10 = (bf16[256,1280]{1,0:T(8,128)(2,1)S(1)}, bf16[256,1280]{1,0:T(8,128)(2,1)S(1)}, u32[]{:S(2)}, u32[]{:S(2)}) collective-permute-start(bf16[256,1280]{1,0:T(8,128)(2,1)S(1)} %collective-permute-done.8.refs_8_), channel_id=1, source_target_pairs={{0,32},{32,64},{64,96},{96,128},{128,160},{160,192},{192,224},{224... | collective-permute-start | bytes 1966088 | tf_op jit(solution)/shard_map/ppermute | solution.py:139
  90.1 1.4 collective-permute-done.11.refs_11_
  91.4 5.0 %collective-permute-start.13 = (bf16[256,1280]{1,0:T(8,128)(2,1)S(1)}, bf16[256,1280]{1,0:T(8,128)(2,1)S(1)}, u32[]{:S(2)}, u32[]{:S(2)}) collective-permute-start(bf16[256,1280]{1,0:T(8,128)(2,1)S(1)} %collective-permute-done.11.refs_11_), channel_id=1, source_target_pairs={{0,32},{32,64},{64,96},{96,128},{128,160},{160,192},{192,224},{224... | collective-permute-start | bytes 1966088 | tf_op jit(solution)/shard_map/ppermute | solution.py:139
  96.5 0.3 fusion.3
  96.8 1.7 collective-permute-done.10.refs_10_
  98.5 5.0 %collective-permute-start.12 = (bf16[256,1280]{1,0:T(8,128)(2,1)S(1)}, bf16[256,1280]{1,0:T(8,128)(2,1)S(1)}, u32[]{:S(2)}, u32[]{:S(2)}) collective-permute-start(bf16[256,1280]{1,0:T(8,128)(2,1)S(1)} %collective-permute-done.10.refs_10_), channel_id=1, source_target_pairs={{0,32},{32,64},{64,96},{96,128},{128,160},{160,192},{192,224},{224... | collective-permute-start | bytes 1966088 | tf_op jit(solution)/shard_map/ppermute | solution.py:139
  104.1 1.4 collective-permute-done.13.refs_13_
  105.8 0.5 copy-done.11
  106.3 6.2 %collective-permute-done.12.refs_12_ = bf16[256,1280]{1,0:T(8,128)(2,1)S(1)} collective-permute-done((bf16[256,1280]{1,0:T(8,128)(2,1)S(1)}, bf16[256,1280]{1,0:T(8,128)(2,1)S(1)}, u32[]{:S(2)}, u32[]{:S(2)}) %collective-permute-start.12) | collective-permute-done | bytes 655392 | tf_op jit(solution)/shard_map/ppermute | solution.py:139
  112.5 0.4 fusion.49
  112.9 0.5 copy-done.19
  113.4 0.6 multiply_reduce_fusion
  114.0 1.0 copy-done.2
  115.0 4.4 %collective-permute-start.14 = (f32[8,192]{1,0:T(8,128)S(1)}, f32[8,192]{1,0:T(8,128)S(1)}, u32[]{:S(2)}, u32[]{:S(2)}) collective-permute-start(f32[8,192]{1,0:T(8,128)S(1)} %stack.53), channel_id=1, source_target_pairs={{0,256},{256,0},{1,257},{257,1},{2,258},{258,2},{3,259},{259,3},{4... | collective-permute-start | bytes 18440 | tf_op jit(solution)/shard_map/ppermute | solution.py:19
  119.5 0.7 collective-permute-done.14
  120.2 0.7 broadcast_in_dim.48
  121.0 9.8 %all-to-all-start = ((f32[32,8,192]{2,1,0:T(8,128)}), f32[32,8,192]{2,1,0:T(8,128)}, u32[]{:S(2)}, u32[]{:S(2)}) async-start(f32[32,8,192]{2,1,0:T(8,128)} %broadcast_in_dim.48), calls=%async_computation | async-start | bytes 524288 | tf_op jit(solution)/shard_map/all_to_all | solution.py:159
  131.2 11.1 %all-to-all-done.stats_ref = f32[32,8,192]{2,1,0:T(8,128)} async-done(((f32[32,8,192]{2,1,0:T(8,128)}), f32[32,8,192]{2,1,0:T(8,128)}, u32[]{:S(2)}, u32[]{:S(2)}) %all-to-all-start) | async-done | bytes 196640 | tf_op jit(solution)/shard_map/all_to_all | solution.py:159
  142.4 1.2 copy-done.3
  143.6 1.1 copy-done.6
  144.6 1.1 copy-done.8
  145.7 1.1 copy-done.10
  146.8 1.1 copy-done.12
  147.9 1.1 copy-done.15
  149.0 1.1 copy-done.18
  150.1 1.1 copy-done.20
  151.2 1.1 copy-done.22
  152.3 1.1 copy-done.24
  153.3 1.1 copy-done.26
  154.4 11.3 %shard_map.77 = (f32[32,96,128]{2,1,0:T(8,128)S(1)}, bf16[32,96,128]{2,1,0:T(8,128)(2,1)S(1)}, f32[1,192]{1,0:T(1,128)S(1)}) custom-call(s32[2]{0:T(128)S(1)} %pad_add_fusion.place_ref, f32[32,8,192]{2,1,0:T(8,128)} %all-to-all-done.stats_ref, f32[1,192]{1,0:T(1,128)S(1)} %bitcast.31, f32[192,1280]{1,0:T(8,128)S(1)} %copy-done.3, ...), custom_call_target="tpu_custom_call" | custom-call | flops 2013265920 | bytes 10485760 | tf_op jit(solution)/shard_map/pallas_call | solution.py:96
  165.7 4.2 %collective-permute-start.15 = (bf16[32,96,128]{2,1,0:T(8,128)(2,1)S(1)}, bf16[32,96,128]{2,1,0:T(8,128)(2,1)S(1)}, u32[]{:S(2)}, u32[]{:S(2)}) collective-permute-start(bf16[32,96,128]{2,1,0:T(8,128)(2,1)S(1)} %get-tuple-element.7), channel_id=1, source_target_pairs={{0,256},{256,0},{1,257},{257,1},{2,258},{258,2},{3,259},{259,3},{4... | collective-permute-start | bytes 2359304 | tf_op jit(solution)/shard_map/ppermute | solution.py:19
  169.9 1.9 collective-permute-done.15
  171.8 1.1 add_convert_fusion
  172.9 3.9 %all-to-all-start.1 = ((bf16[32,96,128]{2,1,0:T(8,128)(2,1)}), bf16[32,96,128]{2,1,0:T(8,128)(2,1)S(1)}, u32[]{:S(2)}, u32[]{:S(2)}) async-start(bf16[32,96,128]{2,1,0:T(8,128)(2,1)} %add_convert_fusion), calls=%async_computation.1 | async-start | bytes 1572864 | tf_op jit(solution)/shard_map/all_to_all | solution.py:166
  176.9 0.6 reduce_sum.91
  177.5 20.8 %all-to-all-done.1 = bf16[32,96,128]{2,1,0:T(8,128)(2,1)S(1)} async-done(((bf16[32,96,128]{2,1,0:T(8,128)(2,1)}), bf16[32,96,128]{2,1,0:T(8,128)(2,1)S(1)}, u32[]{:S(2)}, u32[]{:S(2)}) %all-to-all-start.1) | async-done | bytes 786464 | tf_op jit(solution)/shard_map/all_to_all | solution.py:166
  198.6 0.6 maximum_bitcast_fusion
  (74 shorter events, 3.5 us)
Async XLA Ops:
  0.6 47.2 %copy-start = (bf16[192,4096]{1,0:T(8,128)(2,1)S(1)}, bf16[192,4096]{1,0:T(8,128)(2,1)}, u32[]{:S(2)}) copy-start(bf16[192,4096]{1,0:T(8,128)(2,1)} %param.6) | copy-start | bytes 4718596
  0.6 47.2 %copy-start.1 = (bf16[512,1280]{1,0:T(8,128)(2,1)S(1)}, bf16[512,1280]{1,0:T(8,128)(2,1)}, u32[]{:S(2)}) copy-start(bf16[512,1280]{1,0:T(8,128)(2,1)} %own_ref.1) | copy-start | bytes 3932164
  0.7 46.9 %copy-start.4 = (bf16[192,1280]{1,0:T(8,128)(2,1)S(1)}, bf16[192,1280]{1,0:T(8,128)(2,1)}, u32[]{:S(2)}) copy-start(bf16[192,1280]{1,0:T(8,128)(2,1)} %teacher_ref.1) | copy-start | bytes 1474564
  2.2 19.0 %collective-permute-start.1 = (bf16[256,1280]{1,0:T(8,128)(2,1)S(1)}, bf16[256,1280]{1,0:T(8,128)(2,1)S(1)}, u32[]{:S(2)}, u32[]{:S(2)}) collective-permute-start(bf16[256,1280]{1,0:T(8,128)(2,1)S(1)} %get-tuple-element.15), channel_id=1, source_target_pairs={{0,32},{32,64},{64,96},{96,128},{128,160},{160,192},{192,224},{224... | collective-permute-start | bytes 1966088 | tf_op jit(solution)/shard_map/ppermute | solution.py:139
  13.7 14.5 %collective-permute-start = (bf16[256,1280]{1,0:T(8,128)(2,1)S(1)}, bf16[256,1280]{1,0:T(8,128)(2,1)S(1)}, u32[]{:S(2)}, u32[]{:S(2)}) collective-permute-start(bf16[256,1280]{1,0:T(8,128)(2,1)S(1)} %get-tuple-element.14), channel_id=1, source_target_pairs={{0,32},{32,64},{64,96},{96,128},{128,160},{160,192},{192,224},{224... | collective-permute-start | bytes 1966088 | tf_op jit(solution)/shard_map/ppermute | solution.py:139
  21.2 0.8 copy-start.13
  22.0 13.2 %collective-permute-start.3 = (bf16[256,1280]{1,0:T(8,128)(2,1)S(1)}, bf16[256,1280]{1,0:T(8,128)(2,1)}, u32[]{:S(2)}, u32[]{:S(2)}) collective-permute-start(bf16[256,1280]{1,0:T(8,128)(2,1)S(1)} %collective-permute-done.1.refs_1_), channel_id=1, source_target_pairs={{0,32},{32,64},{64,96},{96,128},{128,160},{160,192},{192,224},{224... | collective-permute-start | bytes 1966088 | tf_op jit(solution)/shard_map/ppermute | solution.py:139
  28.2 7.0 %copy-start.16 = (bf16[256,1280]{1,0:T(8,128)(2,1)}, bf16[256,1280]{1,0:T(8,128)(2,1)S(1)}, u32[]{:S(2)}) copy-start(bf16[256,1280]{1,0:T(8,128)(2,1)S(1)} %collective-permute-done.refs_0_) | copy-start | bytes 1966084
  28.2 14.0 %collective-permute-start.2 = (bf16[256,1280]{1,0:T(8,128)(2,1)S(1)}, bf16[256,1280]{1,0:T(8,128)(2,1)}, u32[]{:S(2)}, u32[]{:S(2)}) collective-permute-start(bf16[256,1280]{1,0:T(8,128)(2,1)S(1)} %collective-permute-done.refs_0_), channel_id=1, source_target_pairs={{0,32},{32,64},{64,96},{96,128},{128,160},{160,192},{192,224},{224... | collective-permute-start | bytes 1966088 | tf_op jit(solution)/shard_map/ppermute | solution.py:139
  35.3 14.1 %collective-permute-start.5 = (bf16[256,1280]{1,0:T(8,128)(2,1)}, bf16[256,1280]{1,0:T(8,128)(2,1)}, u32[]{:S(2)}, u32[]{:S(2)}) collective-permute-start(bf16[256,1280]{1,0:T(8,128)(2,1)} %collective-permute-done.3.refs_3_), channel_id=1, source_target_pairs={{0,32},{32,64},{64,96},{96,128},{128,160},{160,192},{192,224},{224... | collective-permute-start | bytes 1966088 | tf_op jit(solution)/shard_map/ppermute | solution.py:139
  42.3 14.1 %collective-permute-start.4 = (bf16[256,1280]{1,0:T(8,128)(2,1)}, bf16[256,1280]{1,0:T(8,128)(2,1)}, u32[]{:S(2)}, u32[]{:S(2)}) collective-permute-start(bf16[256,1280]{1,0:T(8,128)(2,1)} %collective-permute-done.2.refs_2_), channel_id=1, source_target_pairs={{0,32},{32,64},{64,96},{96,128},{128,160},{160,192},{192,224},{224... | collective-permute-start | bytes 1966088 | tf_op jit(solution)/shard_map/ppermute | solution.py:139
  47.8 6.6 %copy-start.17 = (bf16[256,1280]{1,0:T(8,128)(2,1)S(1)}, bf16[256,1280]{1,0:T(8,128)(2,1)}, u32[]{:S(2)}) copy-start(bf16[256,1280]{1,0:T(8,128)(2,1)} %copy-done.16) | copy-start | bytes 1966084
  48.3 13.2 %copy-start.14 = (bf16[256,1280]{1,0:T(8,128)(2,1)S(1)}, bf16[256,1280]{1,0:T(8,128)(2,1)}, u32[]{:S(2)}) copy-start(bf16[256,1280]{1,0:T(8,128)(2,1)} %copy-done.13) | copy-start | bytes 1966084
  49.4 14.0 %collective-permute-start.7 = (bf16[256,1280]{1,0:T(8,128)(2,1)}, bf16[256,1280]{1,0:T(8,128)(2,1)S(1)}, u32[]{:S(2)}, u32[]{:S(2)}) collective-permute-start(bf16[256,1280]{1,0:T(8,128)(2,1)} %collective-permute-done.5.refs_5_), channel_id=1, source_target_pairs={{0,32},{32,64},{64,96},{96,128},{128,160},{160,192},{192,224},{224... | collective-permute-start | bytes 1966088 | tf_op jit(solution)/shard_map/ppermute | solution.py:139
  56.4 14.0 %collective-permute-start.6 = (bf16[256,1280]{1,0:T(8,128)(2,1)}, bf16[256,1280]{1,0:T(8,128)(2,1)S(1)}, u32[]{:S(2)}, u32[]{:S(2)}) collective-permute-start(bf16[256,1280]{1,0:T(8,128)(2,1)} %collective-permute-done.4.refs_4_), channel_id=1, source_target_pairs={{0,32},{32,64},{64,96},{96,128},{128,160},{160,192},{192,224},{224... | collective-permute-start | bytes 1966088 | tf_op jit(solution)/shard_map/ppermute | solution.py:139
  63.4 19.0 %copy-start.5 = (bf16[256,1280]{1,0:T(8,128)(2,1)}, bf16[256,1280]{1,0:T(8,128)(2,1)S(1)}, u32[]{:S(2)}) copy-start(bf16[256,1280]{1,0:T(8,128)(2,1)S(1)} %collective-permute-done.7.refs_7_) | copy-start | bytes 1966084
  63.5 14.7 %collective-permute-start.9 = (bf16[256,1280]{1,0:T(8,128)(2,1)S(1)}, bf16[256,1280]{1,0:T(8,128)(2,1)S(1)}, u32[]{:S(2)}, u32[]{:S(2)}) collective-permute-start(bf16[256,1280]{1,0:T(8,128)(2,1)S(1)} %collective-permute-done.7.refs_7_), channel_id=1, source_target_pairs={{0,32},{32,64},{64,96},{96,128},{128,160},{160,192},{192,224},{224... | collective-permute-start | bytes 1966088 | tf_op jit(solution)/shard_map/ppermute | solution.py:139
  70.5 19.0 %copy-start.21 = (bf16[256,1280]{1,0:T(8,128)(2,1)}, bf16[256,1280]{1,0:T(8,128)(2,1)S(1)}, u32[]{:S(2)}) copy-start(bf16[256,1280]{1,0:T(8,128)(2,1)S(1)} %collective-permute-done.6.refs_6_) | copy-start | bytes 1966084
  70.5 13.9 %collective-permute-start.8 = (bf16[256,1280]{1,0:T(8,128)(2,1)S(1)}, bf16[256,1280]{1,0:T(8,128)(2,1)S(1)}, u32[]{:S(2)}, u32[]{:S(2)}) collective-permute-start(bf16[256,1280]{1,0:T(8,128)(2,1)S(1)} %collective-permute-done.6.refs_6_), channel_id=1, source_target_pairs={{0,32},{32,64},{64,96},{96,128},{128,160},{160,192},{192,224},{224... | collective-permute-start | bytes 1966088 | tf_op jit(solution)/shard_map/ppermute | solution.py:139
  78.2 11.6 %copy-start.7 = (bf16[256,1280]{1,0:T(8,128)(2,1)}, bf16[256,1280]{1,0:T(8,128)(2,1)S(1)}, u32[]{:S(2)}) copy-start(bf16[256,1280]{1,0:T(8,128)(2,1)S(1)} %collective-permute-done.9.refs_9_) | copy-start | bytes 1966084
  78.2 13.2 %collective-permute-start.11 = (bf16[256,1280]{1,0:T(8,128)(2,1)S(1)}, bf16[256,1280]{1,0:T(8,128)(2,1)S(1)}, u32[]{:S(2)}, u32[]{:S(2)}) collective-permute-start(bf16[256,1280]{1,0:T(8,128)(2,1)S(1)} %collective-permute-done.9.refs_9_), channel_id=1, source_target_pairs={{0,32},{32,64},{64,96},{96,128},{128,160},{160,192},{192,224},{224... | collective-permute-start | bytes 1966088 | tf_op jit(solution)/shard_map/ppermute | solution.py:139
  84.4 12.0 %copy-start.23 = (bf16[256,1280]{1,0:T(8,128)(2,1)}, bf16[256,1280]{1,0:T(8,128)(2,1)S(1)}, u32[]{:S(2)}) copy-start(bf16[256,1280]{1,0:T(8,128)(2,1)S(1)} %collective-permute-done.8.refs_8_) | copy-start | bytes 1966084
  84.4 14.0 %collective-permute-start.10 = (bf16[256,1280]{1,0:T(8,128)(2,1)S(1)}, bf16[256,1280]{1,0:T(8,128)(2,1)S(1)}, u32[]{:S(2)}, u32[]{:S(2)}) collective-permute-start(bf16[256,1280]{1,0:T(8,128)(2,1)S(1)} %collective-permute-done.8.refs_8_), channel_id=1, source_target_pairs={{0,32},{32,64},{64,96},{96,128},{128,160},{160,192},{192,224},{224... | collective-permute-start | bytes 1966088 | tf_op jit(solution)/shard_map/ppermute | solution.py:139
  91.4 12.0 %copy-start.9 = (bf16[256,1280]{1,0:T(8,128)(2,1)}, bf16[256,1280]{1,0:T(8,128)(2,1)S(1)}, u32[]{:S(2)}) copy-start(bf16[256,1280]{1,0:T(8,128)(2,1)S(1)} %collective-permute-done.11.refs_11_) | copy-start | bytes 1966084
  91.4 14.0 %collective-permute-start.13 = (bf16[256,1280]{1,0:T(8,128)(2,1)S(1)}, bf16[256,1280]{1,0:T(8,128)(2,1)S(1)}, u32[]{:S(2)}, u32[]{:S(2)}) collective-permute-start(bf16[256,1280]{1,0:T(8,128)(2,1)S(1)} %collective-permute-done.11.refs_11_), channel_id=1, source_target_pairs={{0,32},{32,64},{64,96},{96,128},{128,160},{160,192},{192,224},{224... | collective-permute-start | bytes 1966088 | tf_op jit(solution)/shard_map/ppermute | solution.py:139
  98.5 5.7 %copy-start.25 = (bf16[256,1280]{1,0:T(8,128)(2,1)}, bf16[256,1280]{1,0:T(8,128)(2,1)S(1)}, u32[]{:S(2)}) copy-start(bf16[256,1280]{1,0:T(8,128)(2,1)S(1)} %collective-permute-done.10.refs_10_) | copy-start | bytes 1966084
  98.5 14.0 %collective-permute-start.12 = (bf16[256,1280]{1,0:T(8,128)(2,1)S(1)}, bf16[256,1280]{1,0:T(8,128)(2,1)S(1)}, u32[]{:S(2)}, u32[]{:S(2)}) collective-permute-start(bf16[256,1280]{1,0:T(8,128)(2,1)S(1)} %collective-permute-done.10.refs_10_), channel_id=1, source_target_pairs={{0,32},{32,64},{64,96},{96,128},{128,160},{160,192},{192,224},{224... | collective-permute-start | bytes 1966088 | tf_op jit(solution)/shard_map/ppermute | solution.py:139
  105.5 0.8 copy-start.11
  106.3 13.1 %copy-start.28 = (s32[96]{0:T(128)S(1)}, s32[96]{0:T(128)}, u32[]{:S(2)}) copy-start(s32[96]{0:T(128)} %param.10) | copy-start | bytes 1156
  112.5 0.9 copy-start.19
  113.4 17.4 %copy-start.29 = (s32[96]{0:T(128)S(1)}, s32[96]{0:T(128)}, u32[]{:S(2)}) copy-start(s32[96]{0:T(128)} %param.9) | copy-start | bytes 1156
  113.4 17.8 %copy-start.27 = (s32[192]{0:T(256)S(1)}, s32[192]{0:T(256)}, u32[]{:S(2)}) copy-start(s32[192]{0:T(256)} %param.11) | copy-start | bytes 2308
  114.0 1.0 copy-start.2
  115.0 5.2 %collective-permute-start.14 = (f32[8,192]{1,0:T(8,128)S(1)}, f32[8,192]{1,0:T(8,128)S(1)}, u32[]{:S(2)}, u32[]{:S(2)}) collective-permute-start(f32[8,192]{1,0:T(8,128)S(1)} %stack.53), channel_id=1, source_target_pairs={{0,256},{256,0},{1,257},{257,1},{2,258},{258,2},{3,259},{259,3},{4... | collective-permute-start | bytes 18440 | tf_op jit(solution)/shard_map/ppermute | solution.py:19
  121.0 21.4 %all-to-all-start = ((f32[32,8,192]{2,1,0:T(8,128)}), f32[32,8,192]{2,1,0:T(8,128)}, u32[]{:S(2)}, u32[]{:S(2)}) async-start(f32[32,8,192]{2,1,0:T(8,128)} %broadcast_in_dim.48), calls=%async_computation | async-start | bytes 524288 | tf_op jit(solution)/shard_map/all_to_all | solution.py:159
  142.3 1.2 copy-start.3
  143.6 1.1 copy-start.6
  144.6 1.1 copy-start.8
  145.7 1.1 copy-start.10
  146.8 1.1 copy-start.12
  147.9 1.1 copy-start.15
  149.0 1.1 copy-start.18
  150.1 1.1 copy-start.20
  151.2 1.1 copy-start.22
  152.3 1.1 copy-start.24
  153.3 1.1 copy-start.26
  165.7 6.1 %collective-permute-start.15 = (bf16[32,96,128]{2,1,0:T(8,128)(2,1)S(1)}, bf16[32,96,128]{2,1,0:T(8,128)(2,1)S(1)}, u32[]{:S(2)}, u32[]{:S(2)}) collective-permute-start(bf16[32,96,128]{2,1,0:T(8,128)(2,1)S(1)} %get-tuple-element.7), channel_id=1, source_target_pairs={{0,256},{256,0},{1,257},{257,1},{2,258},{258,2},{3,259},{259,3},{4... | collective-permute-start | bytes 2359304 | tf_op jit(solution)/shard_map/ppermute | solution.py:19
  172.9 25.5 %all-to-all-start.1 = ((bf16[32,96,128]{2,1,0:T(8,128)(2,1)}), bf16[32,96,128]{2,1,0:T(8,128)(2,1)S(1)}, u32[]{:S(2)}, u32[]{:S(2)}) async-start(bf16[32,96,128]{2,1,0:T(8,128)(2,1)} %add_convert_fusion), calls=%async_computation.1 | async-start | bytes 1572864 | tf_op jit(solution)/shard_map/all_to_all | solution.py:166

commit v4 on v3

--- a/solution.py
+++ b/solution.py
@@ -35,14 +35,23 @@
 
 
 def grad_kernel(blocks, place_ref, stats_ref, weight_ref, logits_ref, teacher_ref, own_ref, *refs):
-    chunk_refs = refs[:-4]
-    keep_ref, send_ref, diverge_ref, grad_ref = refs[-4:]
+    chunk_refs = refs[:-8]
+    keep_ref, send_ref, diverge_ref, grad_ref, logits_buf, teacher_buf, head_buf, sems = refs[-8:]
     side = place_ref[0]
     row = place_ref[1]
     step = 1 - 2 * side
     toks = logits_ref.shape[0]
     rest = toks - LANES
     depth = own_ref.shape[0] // HALVES
+    copies = [
+        pltpu.make_async_copy(logits_ref, logits_buf, sems.at[0]),
+        pltpu.make_async_copy(teacher_ref, teacher_buf, sems.at[1]),
+    ]
+    sources = [own_ref.at[part * depth : (part + 1) * depth] for part in range(HALVES)] + list(chunk_refs)
+    for index, source in enumerate(sources):
+        copies.append(pltpu.make_async_copy(source, head_buf.at[index], sems.at[2 + index]))
+    for copy in copies:
+        copy.start()
 
     peak, total, teacher_peak, teacher_total, term = join(*[stats_ref[:, i, :] for i in range(5)])
     mean = term / total
@@ -52,15 +61,16 @@
     table = jnp.concatenate([peak, scale, offset, jnp.zeros((LANES - 3, toks), jnp.float32)], axis=0)
     table = jnp.concatenate([table, jnp.zeros((LANES, 2 * LANES - toks), jnp.float32)], axis=1)
     columns = jnp.transpose(table)[:toks]
-    shifted = logits_ref[...] - columns[:, 0:1]
-    slope = shifted - teacher_ref[...].astype(jnp.float32) + columns[:, 2:3]
+    copies[0].wait()
+    copies[1].wait()
+    shifted = logits_buf[...] - columns[:, 0:1]
+    slope = shifted - teacher_buf[...].astype(jnp.float32) + columns[:, 2:3]
     grad = columns[:, 1:2] * jnp.exp(shifted) * slope
     grad_ref[...] = jnp.transpose(grad).astype(jnp.bfloat16)
     low = lax.broadcasted_iota(jnp.int32, (32, LANES), 1) < rest
 
-    def one(chunk, distance, part):
+    def one(product, distance, part):
         owner = lax.rem(row - distance * step + blocks, blocks)
-        product = jnp.dot(chunk, grad_ref[...], preferred_element_type=jnp.float32)
         first = lax.rem(owner, blocks // 2) * (HALVES * depth // 64) + part * (depth // 64)
         mine = lax.div(owner, blocks // 2) == side
         wide = jnp.concatenate([product[:, LANES:], jnp.zeros((depth, LANES - rest), jnp.float32)], axis=1)
@@ -82,16 +92,20 @@
                 send_ref[first + i, :64] = upper.astype(send_ref.dtype)
                 send_ref[first + i, 64:] = lower.astype(send_ref.dtype)
 
-    for part in range(HALVES):
-        one(own_ref[part * depth : (part + 1) * depth, :], 0, part)
-    for index, ref in enumerate(chunk_refs):
-        one(ref[...], 1 + index // HALVES, index % HALVES)
+    for base in range(0, len(sources), HALVES):
+        for index in range(base, base + HALVES):
+            copies[2 + index].wait()
+        block = head_buf[base : base + HALVES].reshape(HALVES * depth, head_buf.shape[2])
+        product = jnp.dot(block, grad_ref[...], preferred_element_type=jnp.float32)
+        for part in range(HALVES):
+            one(product[part * depth : (part + 1) * depth], base // HALVES, part)
 
 
 def grad_products(place, stats, weight, logits, teacher, own, chunks, blocks, count):
     toks, cols = logits.shape
     width = own.shape[0] * blocks
     vmem = pl.BlockSpec(memory_space=pltpu.VMEM)
+    hbm = pl.BlockSpec(memory_space=pltpu.HBM)
     shape = (count, toks // 2, LANES)
     return pl.pallas_call(
         functools.partial(grad_kernel, blocks),
@@ -100,10 +114,16 @@
             jax.ShapeDtypeStruct(shape, jnp.bfloat16),
             jax.ShapeDtypeStruct((1, toks), jnp.float32),
         ],
-        in_specs=[pl.BlockSpec(memory_space=pltpu.SMEM)] + [vmem] * (5 + len(chunks)),
+        in_specs=[pl.BlockSpec(memory_space=pltpu.SMEM)] + [vmem] * 2 + [hbm] * (3 + len(chunks)),
         out_specs=[vmem] * 3,
-        scratch_shapes=[pltpu.VMEM((cols, toks), jnp.bfloat16)],
-        compiler_params=pltpu.CompilerParams(vmem_limit_bytes=24 * 1024 * 1024),
+        scratch_shapes=[
+            pltpu.VMEM((cols, toks), jnp.bfloat16),
+            pltpu.VMEM((toks, cols), jnp.float32),
+            pltpu.VMEM((toks, cols), jnp.bfloat16),
+            pltpu.VMEM((len(chunks) + HALVES, own.shape[0] // HALVES, cols), jnp.bfloat16),
+            pltpu.SemaphoreType.DMA((len(chunks) + HALVES + 2,)),
+        ],
+        compiler_params=pltpu.CompilerParams(vmem_limit_bytes=60 * 1024 * 1024),
         cost_estimate=pl.CostEstimate(
             flops=2 * toks * cols * width, bytes_accessed=2 * cols * width, transcendentals=toks * cols
         ),

time: 201 us -> 190 us (0.945)
  local copies, waits for them, and re-layouts: 17.6 us -> 4.8 us
  other arithmetic: 3.48 us -> 5.98 us
    unnamed x60 -> x44, local copies, waits for them, and re-layouts: 14.9 us -> 2.08 us
  transfers between devices with their start and end apart: 18 -> 18, of which waited for: 17 -> 17; matrix products, arithmetic and copies ran while one was open for 5% -> 6% of each run, Pallas kernels for 0% -> 0%
where the time goes in v4:
time: 190 us; the launch traced here: 189 us
  starting transfers between devices  95.3 us (50%)
  waiting for transfers between devices  60.6 us (32%)
  Pallas kernels  11.7 us (6%)
  matrix products  9.13 us (5%)
  other arithmetic  5.98 us (3%)
  local copies, waits for them, and re-layouts  4.8 us (3%)
    ppermute x14, starting transfers between devices, body(): held = [lax.ppermute(part, ('side', 'row'), ring) for part in held]  73 us
    ppermute x14, waiting for transfers between devices, body(): held = [lax.ppermute(part, ('side', 'row'), ring) for part in held]  26.9 us
    all_to_all x1, waiting for transfers between devices, body(): pieces = lax.all_to_all(packed, 'vocab', 0, 0)  20.8 us
    pallas_call x1, Pallas kernels, grad_products(): pl.pallas_call(functools.partial(grad_kernel, blocks), out_shape=[jax.Sha...  11.7 us
    all_to_all x1, waiting for transfers between devices, body(): lax.all_to_all(jnp.broadcast_to(pair, (count,) + pair.shape), 'vocab', 0, 0)  10.1 us
    all_to_all x1, starting transfers between devices, body(): lax.all_to_all(jnp.broadcast_to(pair, (count,) + pair.shape), 'vocab', 0, 0)  9.67 us
    dot_general x14, matrix products, body(): jnp.dot(piece, held[part], preferred_element_type=jnp.float32)  8.7 us
    ppermute x2, starting transfers between devices, swap_side(): return lax.ppermute(value, 'side', [(0, 1), (1, 0)])  8.6 us
  transfers between devices with their start and end apart: 18, of which 17 were waited for; matrix products, arithmetic and copies ran while one was open for 6% of the time, Pallas kernels for 0%

profile of v4, /device:TPU:1, one launch (start us, length us, event | category | flops | bytes accessed | tf_op | source)
XLA Modules:
  0.0 188.9 jit_solution(6240444065053074025)
XLA Ops:
  0.7 1.5 fusion.46
  2.2 11.5 %collective-permute-start.1 = (bf16[256,1280]{1,0:T(8,128)(2,1)S(1)}, bf16[256,1280]{1,0:T(8,128)(2,1)S(1)}, u32[]{:S(2)}, u32[]{:S(2)}) collective-permute-start(bf16[256,1280]{1,0:T(8,128)(2,1)S(1)} %get-tuple-element.15), channel_id=1, source_target_pairs={{0,32},{32,64},{64,96},{96,128},{128,160},{160,192},{192,224},{224... | collective-permute-start | bytes 1966088 | tf_op jit(solution)/shard_map/ppermute | solution.py:159
  13.7 2.2 %collective-permute-start = (bf16[256,1280]{1,0:T(8,128)(2,1)S(1)}, bf16[256,1280]{1,0:T(8,128)(2,1)S(1)}, u32[]{:S(2)}, u32[]{:S(2)}) collective-permute-start(bf16[256,1280]{1,0:T(8,128)(2,1)S(1)} %get-tuple-element.14), channel_id=1, source_target_pairs={{0,32},{32,64},{64,96},{96,128},{128,160},{160,192},{192,224},{224... | collective-permute-start | bytes 1966088 | tf_op jit(solution)/shard_map/ppermute | solution.py:159
  15.9 5.3 %collective-permute-done.1.refs_1_ = bf16[256,1280]{1,0:T(8,128)(2,1)S(1)} collective-permute-done((bf16[256,1280]{1,0:T(8,128)(2,1)S(1)}, bf16[256,1280]{1,0:T(8,128)(2,1)S(1)}, u32[]{:S(2)}, u32[]{:S(2)}) %collective-permute-start.1) | collective-permute-done | bytes 655392 | tf_op jit(solution)/shard_map/ppermute | solution.py:159
  21.2 0.9 copy-done.8
  22.1 5.0 %collective-permute-start.3 = (bf16[256,1280]{1,0:T(8,128)(2,1)S(1)}, bf16[256,1280]{1,0:T(8,128)(2,1)}, u32[]{:S(2)}, u32[]{:S(2)}) collective-permute-start(bf16[256,1280]{1,0:T(8,128)(2,1)S(1)} %collective-permute-done.1.refs_1_), channel_id=1, source_target_pairs={{0,32},{32,64},{64,96},{96,128},{128,160},{160,192},{192,224},{224... | collective-permute-start | bytes 1966088 | tf_op jit(solution)/shard_map/ppermute | solution.py:159
  27.1 1.1 collective-permute-done.refs_0_
  28.2 5.0 %collective-permute-start.2 = (bf16[256,1280]{1,0:T(8,128)(2,1)S(1)}, bf16[256,1280]{1,0:T(8,128)(2,1)}, u32[]{:S(2)}, u32[]{:S(2)}) collective-permute-start(bf16[256,1280]{1,0:T(8,128)(2,1)S(1)} %collective-permute-done.refs_0_), channel_id=1, source_target_pairs={{0,32},{32,64},{64,96},{96,128},{128,160},{160,192},{192,224},{224... | collective-permute-start | bytes 1966088 | tf_op jit(solution)/shard_map/ppermute | solution.py:159
  33.3 2.0 %collective-permute-done.3.refs_3_ = bf16[256,1280]{1,0:T(8,128)(2,1)} collective-permute-done((bf16[256,1280]{1,0:T(8,128)(2,1)S(1)}, bf16[256,1280]{1,0:T(8,128)(2,1)}, u32[]{:S(2)}, u32[]{:S(2)}) %collective-permute-start.3) | collective-permute-done | bytes 655392 | tf_op jit(solution)/shard_map/ppermute | solution.py:159
  35.3 5.1 %collective-permute-start.5 = (bf16[256,1280]{1,0:T(8,128)(2,1)}, bf16[256,1280]{1,0:T(8,128)(2,1)}, u32[]{:S(2)}, u32[]{:S(2)}) collective-permute-start(bf16[256,1280]{1,0:T(8,128)(2,1)} %collective-permute-done.3.refs_3_), channel_id=1, source_target_pairs={{0,32},{32,64},{64,96},{96,128},{128,160},{160,192},{192,224},{224... | collective-permute-start | bytes 1966088 | tf_op jit(solution)/shard_map/ppermute | solution.py:159
  40.4 1.9 %collective-permute-done.2.refs_2_ = bf16[256,1280]{1,0:T(8,128)(2,1)} collective-permute-done((bf16[256,1280]{1,0:T(8,128)(2,1)S(1)}, bf16[256,1280]{1,0:T(8,128)(2,1)}, u32[]{:S(2)}, u32[]{:S(2)}) %collective-permute-start.2) | collective-permute-done | bytes 655392 | tf_op jit(solution)/shard_map/ppermute | solution.py:159
  42.3 5.1 %collective-permute-start.4 = (bf16[256,1280]{1,0:T(8,128)(2,1)}, bf16[256,1280]{1,0:T(8,128)(2,1)}, u32[]{:S(2)}, u32[]{:S(2)}) collective-permute-start(bf16[256,1280]{1,0:T(8,128)(2,1)} %collective-permute-done.2.refs_2_), channel_id=1, source_target_pairs={{0,32},{32,64},{64,96},{96,128},{128,160},{160,192},{192,224},{224... | collective-permute-start | bytes 1966088 | tf_op jit(solution)/shard_map/ppermute | solution.py:159
  47.6 0.1 reduce_max.45
  47.9 0.4 fusion.6
  48.3 1.1 collective-permute-done.5.refs_5_
  49.4 5.0 %collective-permute-start.7 = (bf16[256,1280]{1,0:T(8,128)(2,1)}, bf16[256,1280]{1,0:T(8,128)(2,1)S(1)}, u32[]{:S(2)}, u32[]{:S(2)}) collective-permute-start(bf16[256,1280]{1,0:T(8,128)(2,1)} %collective-permute-done.5.refs_5_), channel_id=1, source_target_pairs={{0,32},{32,64},{64,96},{96,128},{128,160},{160,192},{192,224},{224... | collective-permute-start | bytes 1966088 | tf_op jit(solution)/shard_map/ppermute | solution.py:159
  54.4 0.3 convolution_add_fusion.7
  54.8 1.7 collective-permute-done.4.refs_4_
  56.4 5.0 %collective-permute-start.6 = (bf16[256,1280]{1,0:T(8,128)(2,1)}, bf16[256,1280]{1,0:T(8,128)(2,1)S(1)}, u32[]{:S(2)}, u32[]{:S(2)}) collective-permute-start(bf16[256,1280]{1,0:T(8,128)(2,1)} %collective-permute-done.4.refs_4_), channel_id=1, source_target_pairs={{0,32},{32,64},{64,96},{96,128},{128,160},{160,192},{192,224},{224... | collective-permute-start | bytes 1966088 | tf_op jit(solution)/shard_map/ppermute | solution.py:159
  61.5 0.3 convolution_add_fusion.6
  61.8 1.4 fusion.23
  63.2 0.3 collective-permute-done.7.refs_7_
  63.5 4.9 %collective-permute-start.9 = (bf16[256,1280]{1,0:T(8,128)(2,1)S(1)}, bf16[256,1280]{1,0:T(8,128)(2,1)S(1)}, u32[]{:S(2)}, u32[]{:S(2)}) collective-permute-start(bf16[256,1280]{1,0:T(8,128)(2,1)S(1)} %collective-permute-done.7.refs_7_), channel_id=1, source_target_pairs={{0,32},{32,64},{64,96},{96,128},{128,160},{160,192},{192,224},{224... | collective-permute-start | bytes 1966088 | tf_op jit(solution)/shard_map/ppermute | solution.py:159
  68.4 1.4 fusion
  69.8 0.7 collective-permute-done.6.refs_6_
  70.5 4.9 %collective-permute-start.8 = (bf16[256,1280]{1,0:T(8,128)(2,1)S(1)}, bf16[256,1280]{1,0:T(8,128)(2,1)S(1)}, u32[]{:S(2)}, u32[]{:S(2)}) collective-permute-start(bf16[256,1280]{1,0:T(8,128)(2,1)S(1)} %collective-permute-done.6.refs_6_), channel_id=1, source_target_pairs={{0,32},{32,64},{64,96},{96,128},{128,160},{160,192},{192,224},{224... | collective-permute-start | bytes 1966088 | tf_op jit(solution)/shard_map/ppermute | solution.py:159
  75.4 1.4 fusion.20
  76.8 1.4 fusion.1
  78.2 4.2 %collective-permute-start.11 = (bf16[256,1280]{1,0:T(8,128)(2,1)S(1)}, bf16[256,1280]{1,0:T(8,128)(2,1)S(1)}, u32[]{:S(2)}, u32[]{:S(2)}) collective-permute-start(bf16[256,1280]{1,0:T(8,128)(2,1)S(1)} %collective-permute-done.9.refs_9_), channel_id=1, source_target_pairs={{0,32},{32,64},{64,96},{96,128},{128,160},{160,192},{192,224},{224... | collective-permute-start | bytes 1966088 | tf_op jit(solution)/shard_map/ppermute | solution.py:159
  82.4 0.3 fusion.17
  82.7 1.7 collective-permute-done.8.refs_8_
  84.4 5.0 %collective-permute-start.10 = (bf16[256,1280]{1,0:T(8,128)(2,1)S(1)}, bf16[256,1280]{1,0:T(8,128)(2,1)S(1)}, u32[]{:S(2)}, u32[]{:S(2)}) collective-permute-start(bf16[256,1280]{1,0:T(8,128)(2,1)S(1)} %collective-permute-done.8.refs_8_), channel_id=1, source_target_pairs={{0,32},{32,64},{64,96},{96,128},{128,160},{160,192},{192,224},{224... | collective-permute-start | bytes 1966088 | tf_op jit(solution)/shard_map/ppermute | solution.py:159
  89.5 0.3 fusion.2
  89.8 0.3 fusion.14
  90.1 1.4 collective-permute-done.11.refs_11_
  91.4 5.0 %collective-permute-start.13 = (bf16[256,1280]{1,0:T(8,128)(2,1)S(1)}, bf16[256,1280]{1,0:T(8,128)(2,1)S(1)}, u32[]{:S(2)}, u32[]{:S(2)}) collective-permute-start(bf16[256,1280]{1,0:T(8,128)(2,1)S(1)} %collective-permute-done.11.refs_11_), channel_id=1, source_target_pairs={{0,32},{32,64},{64,96},{96,128},{128,160},{160,192},{192,224},{224... | collective-permute-start | bytes 1966088 | tf_op jit(solution)/shard_map/ppermute | solution.py:159
  96.5 0.3 fusion.3
  96.8 1.7 collective-permute-done.10.refs_10_
  98.5 5.0 %collective-permute-start.12 = (bf16[256,1280]{1,0:T(8,128)(2,1)S(1)}, bf16[256,1280]{1,0:T(8,128)(2,1)S(1)}, u32[]{:S(2)}, u32[]{:S(2)}) collective-permute-start(bf16[256,1280]{1,0:T(8,128)(2,1)S(1)} %collective-permute-done.10.refs_10_), channel_id=1, source_target_pairs={{0,32},{32,64},{64,96},{96,128},{128,160},{160,192},{192,224},{224... | collective-permute-start | bytes 1966088 | tf_op jit(solution)/shard_map/ppermute | solution.py:159
  103.5 0.3 fusion.11
  103.8 0.3 fusion.4
  104.1 1.4 collective-permute-done.13.refs_13_
  105.5 0.3 fusion.8
  105.8 6.7 %collective-permute-done.12.refs_12_ = bf16[256,1280]{1,0:T(8,128)(2,1)S(1)} collective-permute-done((bf16[256,1280]{1,0:T(8,128)(2,1)S(1)}, bf16[256,1280]{1,0:T(8,128)(2,1)S(1)}, u32[]{:S(2)}, u32[]{:S(2)}) %collective-permute-start.12) | collective-permute-done | bytes 655392 | tf_op jit(solution)/shard_map/ppermute | solution.py:159
  112.5 0.4 fusion.49
  112.9 0.4 copy-done.12
  113.3 0.6 multiply_reduce_fusion
  114.0 4.4 %collective-permute-start.14 = (f32[8,192]{1,0:T(8,128)S(1)}, f32[8,192]{1,0:T(8,128)S(1)}, u32[]{:S(2)}, u32[]{:S(2)}) collective-permute-start(f32[8,192]{1,0:T(8,128)S(1)} %stack.53), channel_id=1, source_target_pairs={{0,256},{256,0},{1,257},{257,1},{2,258},{258,2},{3,259},{259,3},{4... | collective-permute-start | bytes 18440 | tf_op jit(solution)/shard_map/ppermute | solution.py:19
  118.5 0.7 collective-permute-done.14
  119.3 0.7 broadcast_in_dim.48
  120.0 9.7 %all-to-all-start = ((f32[32,8,192]{2,1,0:T(8,128)}), f32[32,8,192]{2,1,0:T(8,128)S(1)}, u32[]{:S(2)}, u32[]{:S(2)}) async-start(f32[32,8,192]{2,1,0:T(8,128)} %broadcast_in_dim.48), calls=%async_computation | async-start | bytes 524288 | tf_op jit(solution)/shard_map/all_to_all | solution.py:179
  129.7 0.2 select_reduce_fusion
  130.0 0.6 pad_add_fusion.place_ref
  130.6 0.6 and_select_fusion
  131.2 10.1 %all-to-all-done.stats_ref = f32[32,8,192]{2,1,0:T(8,128)S(1)} async-done(((f32[32,8,192]{2,1,0:T(8,128)}), f32[32,8,192]{2,1,0:T(8,128)S(1)}, u32[]{:S(2)}, u32[]{:S(2)}) %all-to-all-start) | async-done | bytes 196640 | tf_op jit(solution)/shard_map/all_to_all | solution.py:179
  141.3 0.7 copy-done.16
  142.0 11.7 %shard_map.77 = (f32[32,96,128]{2,1,0:T(8,128)}, bf16[32,96,128]{2,1,0:T(8,128)(2,1)}, f32[1,192]{1,0:T(1,128)}) custom-call(s32[2]{0:T(128)} %pad_add_fusion.place_ref, f32[32,8,192]{2,1,0:T(8,128)} %copy-done.16, f32[1,192]{1,0:T(1,128)} %bitcast.37, f32[192,1280]{1,0:T(8,128)} %copy-done.2, bf16[192,1280]{1,0:T(8,128)(2,1)} %teacher_ref.1, ...), custom_call_target="tpu_custom_call" | custom-call | flops 2013265920 | bytes 10485760 | tf_op jit(solution)/shard_map/pallas_call | solution.py:110
  153.7 4.2 %collective-permute-start.15 = (bf16[32,96,128]{2,1,0:T(8,128)(2,1)}, bf16[32,96,128]{2,1,0:T(8,128)(2,1)S(1)}, u32[]{:S(2)}, u32[]{:S(2)}) collective-permute-start(bf16[32,96,128]{2,1,0:T(8,128)(2,1)} %get-tuple-element.7), channel_id=1, source_target_pairs={{0,256},{256,0},{1,257},{257,1},{2,258},{258,2},{3,259},{259,3},{4... | collective-permute-start | bytes 2359304 | tf_op jit(solution)/shard_map/ppermute | solution.py:19
  157.9 2.1 %collective-permute-done.15 = bf16[32,96,128]{2,1,0:T(8,128)(2,1)S(1)} collective-permute-done((bf16[32,96,128]{2,1,0:T(8,128)(2,1)}, bf16[32,96,128]{2,1,0:T(8,128)(2,1)S(1)}, u32[]{:S(2)}, u32[]{:S(2)}) %collective-permute-start.15) | collective-permute-done | bytes 786464 | tf_op jit(solution)/shard_map/ppermute | solution.py:19
  160.0 2.5 %add_convert_fusion = bf16[32,96,128]{2,1,0:T(8,128)(2,1)} fusion(f32[32,96,128]{2,1,0:T(8,128)} %get-tuple-element.6, bf16[32,96,128]{2,1,0:T(8,128)(2,1)S(1)} %collective-permute-done.15), kind=kLoop, calls=%fused_computation.14 | loop fusion | flops 1179648 | bytes 3145728 | tf_op jit(solution)/shard_map/convert_element_type | solution.py:185
  162.5 4.0 %all-to-all-start.1 = ((bf16[32,96,128]{2,1,0:T(8,128)(2,1)}), bf16[32,96,128]{2,1,0:T(8,128)(2,1)S(1)}, u32[]{:S(2)}, u32[]{:S(2)}) async-start(bf16[32,96,128]{2,1,0:T(8,128)(2,1)} %add_convert_fusion), calls=%async_computation.1 | async-start | bytes 1572864 | tf_op jit(solution)/shard_map/all_to_all | solution.py:186
  166.6 0.6 reduce_sum.91
  167.3 20.8 %all-to-all-done.1 = bf16[32,96,128]{2,1,0:T(8,128)(2,1)S(1)} async-done(((bf16[32,96,128]{2,1,0:T(8,128)(2,1)}), bf16[32,96,128]{2,1,0:T(8,128)(2,1)S(1)}, u32[]{:S(2)}, u32[]{:S(2)}) %all-to-all-start.1) | async-done | bytes 786464 | tf_op jit(solution)/shard_map/all_to_all | solution.py:186
  188.3 0.6 maximum_bitcast_fusion
  (58 shorter events, 0.7 us)
Async XLA Ops:
  0.6 47.2 %copy-start = (bf16[192,4096]{1,0:T(8,128)(2,1)S(1)}, bf16[192,4096]{1,0:T(8,128)(2,1)}, u32[]{:S(2)}) copy-start(bf16[192,4096]{1,0:T(8,128)(2,1)} %param.6) | copy-start | bytes 4718596
  0.6 47.2 %copy-start.1 = (bf16[512,1280]{1,0:T(8,128)(2,1)S(1)}, bf16[512,1280]{1,0:T(8,128)(2,1)}, u32[]{:S(2)}) copy-start(bf16[512,1280]{1,0:T(8,128)(2,1)} %own_ref.1) | copy-start | bytes 3932164
  0.7 46.9 %copy-start.3 = (bf16[192,1280]{1,0:T(8,128)(2,1)S(1)}, bf16[192,1280]{1,0:T(8,128)(2,1)}, u32[]{:S(2)}) copy-start(bf16[192,1280]{1,0:T(8,128)(2,1)} %teacher_ref.1) | copy-start | bytes 1474564
  2.2 19.0 %collective-permute-start.1 = (bf16[256,1280]{1,0:T(8,128)(2,1)S(1)}, bf16[256,1280]{1,0:T(8,128)(2,1)S(1)}, u32[]{:S(2)}, u32[]{:S(2)}) collective-permute-start(bf16[256,1280]{1,0:T(8,128)(2,1)S(1)} %get-tuple-element.15), channel_id=1, source_target_pairs={{0,32},{32,64},{64,96},{96,128},{128,160},{160,192},{192,224},{224... | collective-permute-start | bytes 1966088 | tf_op jit(solution)/shard_map/ppermute | solution.py:159
  13.7 14.5 %collective-permute-start = (bf16[256,1280]{1,0:T(8,128)(2,1)S(1)}, bf16[256,1280]{1,0:T(8,128)(2,1)S(1)}, u32[]{:S(2)}, u32[]{:S(2)}) collective-permute-start(bf16[256,1280]{1,0:T(8,128)(2,1)S(1)} %get-tuple-element.14), channel_id=1, source_target_pairs={{0,32},{32,64},{64,96},{96,128},{128,160},{160,192},{192,224},{224... | collective-permute-start | bytes 1966088 | tf_op jit(solution)/shard_map/ppermute | solution.py:159
  21.2 0.9 copy-start.8
  22.1 13.2 %collective-permute-start.3 = (bf16[256,1280]{1,0:T(8,128)(2,1)S(1)}, bf16[256,1280]{1,0:T(8,128)(2,1)}, u32[]{:S(2)}, u32[]{:S(2)}) collective-permute-start(bf16[256,1280]{1,0:T(8,128)(2,1)S(1)} %collective-permute-done.1.refs_1_), channel_id=1, source_target_pairs={{0,32},{32,64},{64,96},{96,128},{128,160},{160,192},{192,224},{224... | collective-permute-start | bytes 1966088 | tf_op jit(solution)/shard_map/ppermute | solution.py:159
  28.2 7.0 %copy-start.10 = (bf16[256,1280]{1,0:T(8,128)(2,1)}, bf16[256,1280]{1,0:T(8,128)(2,1)S(1)}, u32[]{:S(2)}) copy-start(bf16[256,1280]{1,0:T(8,128)(2,1)S(1)} %collective-permute-done.refs_0_) | copy-start | bytes 1966084
  28.2 14.0 %collective-permute-start.2 = (bf16[256,1280]{1,0:T(8,128)(2,1)S(1)}, bf16[256,1280]{1,0:T(8,128)(2,1)}, u32[]{:S(2)}, u32[]{:S(2)}) collective-permute-start(bf16[256,1280]{1,0:T(8,128)(2,1)S(1)} %collective-permute-done.refs_0_), channel_id=1, source_target_pairs={{0,32},{32,64},{64,96},{96,128},{128,160},{160,192},{192,224},{224... | collective-permute-start | bytes 1966088 | tf_op jit(solution)/shard_map/ppermute | solution.py:159
  35.3 14.1 %collective-permute-start.5 = (bf16[256,1280]{1,0:T(8,128)(2,1)}, bf16[256,1280]{1,0:T(8,128)(2,1)}, u32[]{:S(2)}, u32[]{:S(2)}) collective-permute-start(bf16[256,1280]{1,0:T(8,128)(2,1)} %collective-permute-done.3.refs_3_), channel_id=1, source_target_pairs={{0,32},{32,64},{64,96},{96,128},{128,160},{160,192},{192,224},{224... | collective-permute-start | bytes 1966088 | tf_op jit(solution)/shard_map/ppermute | solution.py:159
  42.3 14.1 %collective-permute-start.4 = (bf16[256,1280]{1,0:T(8,128)(2,1)}, bf16[256,1280]{1,0:T(8,128)(2,1)}, u32[]{:S(2)}, u32[]{:S(2)}) collective-permute-start(bf16[256,1280]{1,0:T(8,128)(2,1)} %collective-permute-done.2.refs_2_), channel_id=1, source_target_pairs={{0,32},{32,64},{64,96},{96,128},{128,160},{160,192},{192,224},{224... | collective-permute-start | bytes 1966088 | tf_op jit(solution)/shard_map/ppermute | solution.py:159
  47.8 6.6 %copy-start.11 = (bf16[256,1280]{1,0:T(8,128)(2,1)S(1)}, bf16[256,1280]{1,0:T(8,128)(2,1)}, u32[]{:S(2)}) copy-start(bf16[256,1280]{1,0:T(8,128)(2,1)} %copy-done.10) | copy-start | bytes 1966084
  48.3 13.2 %copy-start.9 = (bf16[256,1280]{1,0:T(8,128)(2,1)S(1)}, bf16[256,1280]{1,0:T(8,128)(2,1)}, u32[]{:S(2)}) copy-start(bf16[256,1280]{1,0:T(8,128)(2,1)} %copy-done.8) | copy-start | bytes 1966084
  49.4 14.0 %collective-permute-start.7 = (bf16[256,1280]{1,0:T(8,128)(2,1)}, bf16[256,1280]{1,0:T(8,128)(2,1)S(1)}, u32[]{:S(2)}, u32[]{:S(2)}) collective-permute-start(bf16[256,1280]{1,0:T(8,128)(2,1)} %collective-permute-done.5.refs_5_), channel_id=1, source_target_pairs={{0,32},{32,64},{64,96},{96,128},{128,160},{160,192},{192,224},{224... | collective-permute-start | bytes 1966088 | tf_op jit(solution)/shard_map/ppermute | solution.py:159
  56.4 14.0 %collective-permute-start.6 = (bf16[256,1280]{1,0:T(8,128)(2,1)}, bf16[256,1280]{1,0:T(8,128)(2,1)S(1)}, u32[]{:S(2)}, u32[]{:S(2)}) collective-permute-start(bf16[256,1280]{1,0:T(8,128)(2,1)} %collective-permute-done.4.refs_4_), channel_id=1, source_target_pairs={{0,32},{32,64},{64,96},{96,128},{128,160},{160,192},{192,224},{224... | collective-permute-start | bytes 1966088 | tf_op jit(solution)/shard_map/ppermute | solution.py:159
  63.5 19.0 %copy-start.4 = (bf16[256,1280]{1,0:T(8,128)(2,1)}, bf16[256,1280]{1,0:T(8,128)(2,1)S(1)}, u32[]{:S(2)}) copy-start(bf16[256,1280]{1,0:T(8,128)(2,1)S(1)} %collective-permute-done.7.refs_7_) | copy-start | bytes 1966084
  63.5 14.7 %collective-permute-start.9 = (bf16[256,1280]{1,0:T(8,128)(2,1)S(1)}, bf16[256,1280]{1,0:T(8,128)(2,1)S(1)}, u32[]{:S(2)}, u32[]{:S(2)}) collective-permute-start(bf16[256,1280]{1,0:T(8,128)(2,1)S(1)} %collective-permute-done.7.refs_7_), channel_id=1, source_target_pairs={{0,32},{32,64},{64,96},{96,128},{128,160},{160,192},{192,224},{224... | collective-permute-start | bytes 1966088 | tf_op jit(solution)/shard_map/ppermute | solution.py:159
  70.5 19.0 %copy-start.13 = (bf16[256,1280]{1,0:T(8,128)(2,1)}, bf16[256,1280]{1,0:T(8,128)(2,1)S(1)}, u32[]{:S(2)}) copy-start(bf16[256,1280]{1,0:T(8,128)(2,1)S(1)} %collective-permute-done.6.refs_6_) | copy-start | bytes 1966084
  70.5 13.9 %collective-permute-start.8 = (bf16[256,1280]{1,0:T(8,128)(2,1)S(1)}, bf16[256,1280]{1,0:T(8,128)(2,1)S(1)}, u32[]{:S(2)}, u32[]{:S(2)}) collective-permute-start(bf16[256,1280]{1,0:T(8,128)(2,1)S(1)} %collective-permute-done.6.refs_6_), channel_id=1, source_target_pairs={{0,32},{32,64},{64,96},{96,128},{128,160},{160,192},{192,224},{224... | collective-permute-start | bytes 1966088 | tf_op jit(solution)/shard_map/ppermute | solution.py:159
  78.2 11.6 %copy-start.5 = (bf16[256,1280]{1,0:T(8,128)(2,1)}, bf16[256,1280]{1,0:T(8,128)(2,1)S(1)}, u32[]{:S(2)}) copy-start(bf16[256,1280]{1,0:T(8,128)(2,1)S(1)} %collective-permute-done.9.refs_9_) | copy-start | bytes 1966084
  78.2 13.2 %collective-permute-start.11 = (bf16[256,1280]{1,0:T(8,128)(2,1)S(1)}, bf16[256,1280]{1,0:T(8,128)(2,1)S(1)}, u32[]{:S(2)}, u32[]{:S(2)}) collective-permute-start(bf16[256,1280]{1,0:T(8,128)(2,1)S(1)} %collective-permute-done.9.refs_9_), channel_id=1, source_target_pairs={{0,32},{32,64},{64,96},{96,128},{128,160},{160,192},{192,224},{224... | collective-permute-start | bytes 1966088 | tf_op jit(solution)/shard_map/ppermute | solution.py:159
  84.4 12.0 %copy-start.14 = (bf16[256,1280]{1,0:T(8,128)(2,1)}, bf16[256,1280]{1,0:T(8,128)(2,1)S(1)}, u32[]{:S(2)}) copy-start(bf16[256,1280]{1,0:T(8,128)(2,1)S(1)} %collective-permute-done.8.refs_8_) | copy-start | bytes 1966084
  84.4 14.0 %collective-permute-start.10 = (bf16[256,1280]{1,0:T(8,128)(2,1)S(1)}, bf16[256,1280]{1,0:T(8,128)(2,1)S(1)}, u32[]{:S(2)}, u32[]{:S(2)}) collective-permute-start(bf16[256,1280]{1,0:T(8,128)(2,1)S(1)} %collective-permute-done.8.refs_8_), channel_id=1, source_target_pairs={{0,32},{32,64},{64,96},{96,128},{128,160},{160,192},{192,224},{224... | collective-permute-start | bytes 1966088 | tf_op jit(solution)/shard_map/ppermute | solution.py:159
  91.4 12.0 %copy-start.6 = (bf16[256,1280]{1,0:T(8,128)(2,1)}, bf16[256,1280]{1,0:T(8,128)(2,1)S(1)}, u32[]{:S(2)}) copy-start(bf16[256,1280]{1,0:T(8,128)(2,1)S(1)} %collective-permute-done.11.refs_11_) | copy-start | bytes 1966084
  91.4 14.0 %collective-permute-start.13 = (bf16[256,1280]{1,0:T(8,128)(2,1)S(1)}, bf16[256,1280]{1,0:T(8,128)(2,1)S(1)}, u32[]{:S(2)}, u32[]{:S(2)}) collective-permute-start(bf16[256,1280]{1,0:T(8,128)(2,1)S(1)} %collective-permute-done.11.refs_11_), channel_id=1, source_target_pairs={{0,32},{32,64},{64,96},{96,128},{128,160},{160,192},{192,224},{224... | collective-permute-start | bytes 1966088 | tf_op jit(solution)/shard_map/ppermute | solution.py:159
  98.5 5.7 %copy-start.15 = (bf16[256,1280]{1,0:T(8,128)(2,1)}, bf16[256,1280]{1,0:T(8,128)(2,1)S(1)}, u32[]{:S(2)}) copy-start(bf16[256,1280]{1,0:T(8,128)(2,1)S(1)} %collective-permute-done.10.refs_10_) | copy-start | bytes 1966084
  98.5 14.0 %collective-permute-start.12 = (bf16[256,1280]{1,0:T(8,128)(2,1)S(1)}, bf16[256,1280]{1,0:T(8,128)(2,1)S(1)}, u32[]{:S(2)}, u32[]{:S(2)}) collective-permute-start(bf16[256,1280]{1,0:T(8,128)(2,1)S(1)} %collective-permute-done.10.refs_10_), channel_id=1, source_target_pairs={{0,32},{32,64},{64,96},{96,128},{128,160},{160,192},{192,224},{224... | collective-permute-start | bytes 1966088 | tf_op jit(solution)/shard_map/ppermute | solution.py:159
  105.5 7.4 %copy-start.7 = (bf16[256,1280]{1,0:T(8,128)(2,1)}, bf16[256,1280]{1,0:T(8,128)(2,1)S(1)}, u32[]{:S(2)}) copy-start(bf16[256,1280]{1,0:T(8,128)(2,1)S(1)} %collective-permute-done.13.refs_13_) | copy-start | bytes 1966084
  105.8 12.6 %copy-start.20 = (s32[96]{0:T(128)S(1)}, s32[96]{0:T(128)}, u32[]{:S(2)}) copy-start(s32[96]{0:T(128)} %param.10) | copy-start | bytes 1156
  112.5 0.8 copy-start.12
  113.3 28.0 %copy-start.2 = (f32[192,1280]{1,0:T(8,128)}, f32[192,1280]{1,0:T(8,128)S(1)}, u32[]{:S(2)}) copy-start(f32[192,1280]{1,0:T(8,128)S(1)} %get-tuple-element.26.logits_ref) | copy-start | bytes 2949124
  113.3 16.3 %copy-start.21 = (s32[96]{0:T(128)S(1)}, s32[96]{0:T(128)}, u32[]{:S(2)}) copy-start(s32[96]{0:T(128)} %param.9) | copy-start | bytes 1156
  113.3 17.3 %copy-start.18 = (s32[192]{0:T(256)S(1)}, s32[192]{0:T(256)}, u32[]{:S(2)}) copy-start(s32[192]{0:T(256)} %param.11) | copy-start | bytes 2308
  114.0 5.2 %collective-permute-start.14 = (f32[8,192]{1,0:T(8,128)S(1)}, f32[8,192]{1,0:T(8,128)S(1)}, u32[]{:S(2)}, u32[]{:S(2)}) collective-permute-start(f32[8,192]{1,0:T(8,128)S(1)} %stack.53), channel_id=1, source_target_pairs={{0,256},{256,0},{1,257},{257,1},{2,258},{258,2},{3,259},{259,3},{4... | collective-permute-start | bytes 18440 | tf_op jit(solution)/shard_map/ppermute | solution.py:19
  120.0 21.3 %all-to-all-start = ((f32[32,8,192]{2,1,0:T(8,128)}), f32[32,8,192]{2,1,0:T(8,128)S(1)}, u32[]{:S(2)}, u32[]{:S(2)}) async-start(f32[32,8,192]{2,1,0:T(8,128)} %broadcast_in_dim.48), calls=%async_computation | async-start | bytes 524288 | tf_op jit(solution)/shard_map/all_to_all | solution.py:179
  141.3 0.7 copy-start.16
  153.7 6.3 %collective-permute-start.15 = (bf16[32,96,128]{2,1,0:T(8,128)(2,1)}, bf16[32,96,128]{2,1,0:T(8,128)(2,1)S(1)}, u32[]{:S(2)}, u32[]{:S(2)}) collective-permute-start(bf16[32,96,128]{2,1,0:T(8,128)(2,1)} %get-tuple-element.7), channel_id=1, source_target_pairs={{0,256},{256,0},{1,257},{257,1},{2,258},{258,2},{3,259},{259,3},{4... | collective-permute-start | bytes 2359304 | tf_op jit(solution)/shard_map/ppermute | solution.py:19
  162.5 4.1 %copy-start.17 = (f32[192]{0:T(256)S(1)}, f32[192]{0:T(256)}, u32[]{:S(2)}) copy-start(f32[192]{0:T(256)} %and_select_fusion) | copy-start | bytes 2308
  162.5 4.1 %copy-start.19 = (f32[1,192]{1,0:T(1,128)S(1)}, f32[1,192]{1,0:T(1,128)}, u32[]{:S(2)}) copy-start(f32[1,192]{1,0:T(1,128)} %get-tuple-element.5) | copy-start | bytes 2308
  162.5 25.6 %all-to-all-start.1 = ((bf16[32,96,128]{2,1,0:T(8,128)(2,1)}), bf16[32,96,128]{2,1,0:T(8,128)(2,1)S(1)}, u32[]{:S(2)}, u32[]{:S(2)}) async-start(bf16[32,96,128]{2,1,0:T(8,128)(2,1)} %add_convert_fusion), calls=%async_computation.1 | async-start | bytes 1572864 | tf_op jit(solution)/shard_map/all_to_all | solution.py:186

commit v5 on v4

--- a/solution.py
+++ b/solution.py
@@ -107,6 +107,7 @@
     vmem = pl.BlockSpec(memory_space=pltpu.VMEM)
     hbm = pl.BlockSpec(memory_space=pltpu.HBM)
     shape = (count, toks // 2, LANES)
+    large = [pltpu.with_memory_space_constraint(value, pltpu.HBM) for value in (logits, teacher, own, *chunks)]
     return pl.pallas_call(
         functools.partial(grad_kernel, blocks),
         out_shape=[
@@ -123,11 +124,11 @@
             pltpu.VMEM((len(chunks) + HALVES, own.shape[0] // HALVES, cols), jnp.bfloat16),
             pltpu.SemaphoreType.DMA((len(chunks) + HALVES + 2,)),
         ],
-        compiler_params=pltpu.CompilerParams(vmem_limit_bytes=60 * 1024 * 1024),
+        compiler_params=pltpu.CompilerParams(vmem_limit_bytes=24 * 1024 * 1024),
         cost_estimate=pl.CostEstimate(
             flops=2 * toks * cols * width, bytes_accessed=2 * cols * width, transcendentals=toks * cols
         ),
-    )(place, stats, weight, logits, teacher, own, *chunks)
+    )(place, stats, weight, *large)
 
 
 def body(hidden, head, teacher_logits, lengths, slot_rollout, token_mask):

time: 190 us -> 186 us (0.979)
  other arithmetic: 5.98 us -> 3.5 us
  transfers between devices with their start and end apart: 18 -> 18, of which waited for: 17 -> 17; matrix products, arithmetic and copies ran while one was open for 6% -> 5% of each run, Pallas kernels for 0% -> 0%
where the time goes in v5:
time: 186 us; the launch traced here: 185 us
  starting transfers between devices  95.2 us (51%)
  waiting for transfers between devices  61.5 us (33%)
  Pallas kernels  10 us (5%)
  matrix products  9.12 us (5%)
  local copies, waits for them, and re-layouts  4.09 us (2%)
  other arithmetic  3.5 us (2%)
    ppermute x14, starting transfers between devices, body(): held = [lax.ppermute(part, ('side', 'row'), ring) for part in held]  73 us
    ppermute x14, waiting for transfers between devices, body(): held = [lax.ppermute(part, ('side', 'row'), ring) for part in held]  26.9 us
    all_to_all x1, waiting for transfers between devices, body(): pieces = lax.all_to_all(packed, 'vocab', 0, 0)  20.8 us
    all_to_all x1, waiting for transfers between devices, body(): lax.all_to_all(jnp.broadcast_to(pair, (count,) + pair.shape), 'vocab', 0, 0)  11.2 us
    pallas_call x1, Pallas kernels, grad_products(): pl.pallas_call(functools.partial(grad_kernel, blocks), out_shape=[jax.Sha...  10 us
    all_to_all x1, starting transfers between devices, body(): lax.all_to_all(jnp.broadcast_to(pair, (count,) + pair.shape), 'vocab', 0, 0)  9.67 us
    dot_general x14, matrix products, body(): jnp.dot(piece, held[part], preferred_element_type=jnp.float32)  8.7 us
    ppermute x2, starting transfers between devices, swap_side(): return lax.ppermute(value, 'side', [(0, 1), (1, 0)])  8.56 us
  transfers between devices with their start and end apart: 18, of which 17 were waited for; matrix products, arithmetic and copies ran while one was open for 5% of the time, Pallas kernels for 0%

profile of v5, /device:TPU:1, one launch (start us, length us, event | category | flops | bytes accessed | tf_op | source)
XLA Modules:
  0.0 184.8 jit_solution(7974339614325437317)
XLA Ops:
  0.7 1.5 fusion.46
  2.2 11.5 %collective-permute-start.1 = (bf16[256,1280]{1,0:T(8,128)(2,1)S(1)}, bf16[256,1280]{1,0:T(8,128)(2,1)S(1)}, u32[]{:S(2)}, u32[]{:S(2)}) collective-permute-start(bf16[256,1280]{1,0:T(8,128)(2,1)S(1)} %get-tuple-element.15), channel_id=1, source_target_pairs={{0,32},{32,64},{64,96},{96,128},{128,160},{160,192},{192,224},{224... | collective-permute-start | bytes 1966088 | tf_op jit(solution)/shard_map/ppermute | solution.py:160
  13.7 2.2 %collective-permute-start = (bf16[256,1280]{1,0:T(8,128)(2,1)S(1)}, bf16[256,1280]{1,0:T(8,128)(2,1)S(1)}, u32[]{:S(2)}, u32[]{:S(2)}) collective-permute-start(bf16[256,1280]{1,0:T(8,128)(2,1)S(1)} %get-tuple-element.14), channel_id=1, source_target_pairs={{0,32},{32,64},{64,96},{96,128},{128,160},{160,192},{192,224},{224... | collective-permute-start | bytes 1966088 | tf_op jit(solution)/shard_map/ppermute | solution.py:160
  15.9 5.3 %collective-permute-done.1.refs_1_ = bf16[256,1280]{1,0:T(8,128)(2,1)S(1)} collective-permute-done((bf16[256,1280]{1,0:T(8,128)(2,1)S(1)}, bf16[256,1280]{1,0:T(8,128)(2,1)S(1)}, u32[]{:S(2)}, u32[]{:S(2)}) %collective-permute-start.1) | collective-permute-done | bytes 655392 | tf_op jit(solution)/shard_map/ppermute | solution.py:160
  21.2 0.8 copy-done.8
  22.1 5.0 %collective-permute-start.3 = (bf16[256,1280]{1,0:T(8,128)(2,1)S(1)}, bf16[256,1280]{1,0:T(8,128)(2,1)}, u32[]{:S(2)}, u32[]{:S(2)}) collective-permute-start(bf16[256,1280]{1,0:T(8,128)(2,1)S(1)} %collective-permute-done.1.refs_1_), channel_id=1, source_target_pairs={{0,32},{32,64},{64,96},{96,128},{128,160},{160,192},{192,224},{224... | collective-permute-start | bytes 1966088 | tf_op jit(solution)/shard_map/ppermute | solution.py:160
  27.1 1.2 collective-permute-done.refs_0_
  28.2 5.0 %collective-permute-start.2 = (bf16[256,1280]{1,0:T(8,128)(2,1)S(1)}, bf16[256,1280]{1,0:T(8,128)(2,1)}, u32[]{:S(2)}, u32[]{:S(2)}) collective-permute-start(bf16[256,1280]{1,0:T(8,128)(2,1)S(1)} %collective-permute-done.refs_0_), channel_id=1, source_target_pairs={{0,32},{32,64},{64,96},{96,128},{128,160},{160,192},{192,224},{224... | collective-permute-start | bytes 1966088 | tf_op jit(solution)/shard_map/ppermute | solution.py:160
  33.3 2.0 %collective-permute-done.3.refs_3_ = bf16[256,1280]{1,0:T(8,128)(2,1)} collective-permute-done((bf16[256,1280]{1,0:T(8,128)(2,1)S(1)}, bf16[256,1280]{1,0:T(8,128)(2,1)}, u32[]{:S(2)}, u32[]{:S(2)}) %collective-permute-start.3) | collective-permute-done | bytes 655392 | tf_op jit(solution)/shard_map/ppermute | solution.py:160
  35.3 5.1 %collective-permute-start.5 = (bf16[256,1280]{1,0:T(8,128)(2,1)}, bf16[256,1280]{1,0:T(8,128)(2,1)}, u32[]{:S(2)}, u32[]{:S(2)}) collective-permute-start(bf16[256,1280]{1,0:T(8,128)(2,1)} %collective-permute-done.3.refs_3_), channel_id=1, source_target_pairs={{0,32},{32,64},{64,96},{96,128},{128,160},{160,192},{192,224},{224... | collective-permute-start | bytes 1966088 | tf_op jit(solution)/shard_map/ppermute | solution.py:160
  40.4 1.9 %collective-permute-done.2.refs_2_ = bf16[256,1280]{1,0:T(8,128)(2,1)} collective-permute-done((bf16[256,1280]{1,0:T(8,128)(2,1)S(1)}, bf16[256,1280]{1,0:T(8,128)(2,1)}, u32[]{:S(2)}, u32[]{:S(2)}) %collective-permute-start.2) | collective-permute-done | bytes 655392 | tf_op jit(solution)/shard_map/ppermute | solution.py:160
  42.3 5.1 %collective-permute-start.4 = (bf16[256,1280]{1,0:T(8,128)(2,1)}, bf16[256,1280]{1,0:T(8,128)(2,1)}, u32[]{:S(2)}, u32[]{:S(2)}) collective-permute-start(bf16[256,1280]{1,0:T(8,128)(2,1)} %collective-permute-done.2.refs_2_), channel_id=1, source_target_pairs={{0,32},{32,64},{64,96},{96,128},{128,160},{160,192},{192,224},{224... | collective-permute-start | bytes 1966088 | tf_op jit(solution)/shard_map/ppermute | solution.py:160
  47.6 0.1 reduce_max.45
  47.9 0.4 fusion.6
  48.3 1.1 collective-permute-done.5.refs_5_
  49.4 5.0 %collective-permute-start.7 = (bf16[256,1280]{1,0:T(8,128)(2,1)}, bf16[256,1280]{1,0:T(8,128)(2,1)S(1)}, u32[]{:S(2)}, u32[]{:S(2)}) collective-permute-start(bf16[256,1280]{1,0:T(8,128)(2,1)} %collective-permute-done.5.refs_5_), channel_id=1, source_target_pairs={{0,32},{32,64},{64,96},{96,128},{128,160},{160,192},{192,224},{224... | collective-permute-start | bytes 1966088 | tf_op jit(solution)/shard_map/ppermute | solution.py:160
  54.4 0.3 convolution_add_fusion.7
  54.8 1.7 collective-permute-done.4.refs_4_
  56.4 5.0 %collective-permute-start.6 = (bf16[256,1280]{1,0:T(8,128)(2,1)}, bf16[256,1280]{1,0:T(8,128)(2,1)S(1)}, u32[]{:S(2)}, u32[]{:S(2)}) collective-permute-start(bf16[256,1280]{1,0:T(8,128)(2,1)} %collective-permute-done.4.refs_4_), channel_id=1, source_target_pairs={{0,32},{32,64},{64,96},{96,128},{128,160},{160,192},{192,224},{224... | collective-permute-start | bytes 1966088 | tf_op jit(solution)/shard_map/ppermute | solution.py:160
  61.5 0.3 convolution_add_fusion.6
  61.8 1.4 fusion.23
  63.2 0.3 collective-permute-done.7.refs_7_
  63.5 4.9 %collective-permute-start.9 = (bf16[256,1280]{1,0:T(8,128)(2,1)S(1)}, bf16[256,1280]{1,0:T(8,128)(2,1)S(1)}, u32[]{:S(2)}, u32[]{:S(2)}) collective-permute-start(bf16[256,1280]{1,0:T(8,128)(2,1)S(1)} %collective-permute-done.7.refs_7_), channel_id=1, source_target_pairs={{0,32},{32,64},{64,96},{96,128},{128,160},{160,192},{192,224},{224... | collective-permute-start | bytes 1966088 | tf_op jit(solution)/shard_map/ppermute | solution.py:160
  68.4 1.4 fusion
  69.8 0.7 collective-permute-done.6.refs_6_
  70.5 4.9 %collective-permute-start.8 = (bf16[256,1280]{1,0:T(8,128)(2,1)S(1)}, bf16[256,1280]{1,0:T(8,128)(2,1)S(1)}, u32[]{:S(2)}, u32[]{:S(2)}) collective-permute-start(bf16[256,1280]{1,0:T(8,128)(2,1)S(1)} %collective-permute-done.6.refs_6_), channel_id=1, source_target_pairs={{0,32},{32,64},{64,96},{96,128},{128,160},{160,192},{192,224},{224... | collective-permute-start | bytes 1966088 | tf_op jit(solution)/shard_map/ppermute | solution.py:160
  75.4 1.4 fusion.20
  76.8 1.4 fusion.1
  78.2 4.2 %collective-permute-start.11 = (bf16[256,1280]{1,0:T(8,128)(2,1)S(1)}, bf16[256,1280]{1,0:T(8,128)(2,1)S(1)}, u32[]{:S(2)}, u32[]{:S(2)}) collective-permute-start(bf16[256,1280]{1,0:T(8,128)(2,1)S(1)} %collective-permute-done.9.refs_9_), channel_id=1, source_target_pairs={{0,32},{32,64},{64,96},{96,128},{128,160},{160,192},{192,224},{224... | collective-permute-start | bytes 1966088 | tf_op jit(solution)/shard_map/ppermute | solution.py:160
  82.4 0.3 fusion.17
  82.7 1.7 collective-permute-done.8.refs_8_
  84.4 5.0 %collective-permute-start.10 = (bf16[256,1280]{1,0:T(8,128)(2,1)S(1)}, bf16[256,1280]{1,0:T(8,128)(2,1)S(1)}, u32[]{:S(2)}, u32[]{:S(2)}) collective-permute-start(bf16[256,1280]{1,0:T(8,128)(2,1)S(1)} %collective-permute-done.8.refs_8_), channel_id=1, source_target_pairs={{0,32},{32,64},{64,96},{96,128},{128,160},{160,192},{192,224},{224... | collective-permute-start | bytes 1966088 | tf_op jit(solution)/shard_map/ppermute | solution.py:160
  89.5 0.3 fusion.2
  89.8 0.3 fusion.14
  90.1 1.4 collective-permute-done.11.refs_11_
  91.4 5.0 %collective-permute-start.13 = (bf16[256,1280]{1,0:T(8,128)(2,1)S(1)}, bf16[256,1280]{1,0:T(8,128)(2,1)S(1)}, u32[]{:S(2)}, u32[]{:S(2)}) collective-permute-start(bf16[256,1280]{1,0:T(8,128)(2,1)S(1)} %collective-permute-done.11.refs_11_), channel_id=1, source_target_pairs={{0,32},{32,64},{64,96},{96,128},{128,160},{160,192},{192,224},{224... | collective-permute-start | bytes 1966088 | tf_op jit(solution)/shard_map/ppermute | solution.py:160
  96.5 0.3 fusion.3
  96.8 1.7 collective-permute-done.10.refs_10_
  98.5 5.0 %collective-permute-start.12 = (bf16[256,1280]{1,0:T(8,128)(2,1)S(1)}, bf16[256,1280]{1,0:T(8,128)(2,1)S(1)}, u32[]{:S(2)}, u32[]{:S(2)}) collective-permute-start(bf16[256,1280]{1,0:T(8,128)(2,1)S(1)} %collective-permute-done.10.refs_10_), channel_id=1, source_target_pairs={{0,32},{32,64},{64,96},{96,128},{128,160},{160,192},{192,224},{224... | collective-permute-start | bytes 1966088 | tf_op jit(solution)/shard_map/ppermute | solution.py:160
  103.5 0.3 fusion.11
  103.8 0.3 fusion.4
  104.1 1.4 collective-permute-done.13.refs_13_
  105.5 0.3 fusion.8
  105.8 6.7 %collective-permute-done.12.refs_12_ = bf16[256,1280]{1,0:T(8,128)(2,1)S(1)} collective-permute-done((bf16[256,1280]{1,0:T(8,128)(2,1)S(1)}, bf16[256,1280]{1,0:T(8,128)(2,1)S(1)}, u32[]{:S(2)}, u32[]{:S(2)}) %collective-permute-start.12) | collective-permute-done | bytes 655392 | tf_op jit(solution)/shard_map/ppermute | solution.py:160
  112.5 0.4 fusion.49
  112.9 0.5 copy-done.12
  113.4 0.6 multiply_reduce_fusion
  114.0 4.4 %collective-permute-start.14 = (f32[8,192]{1,0:T(8,128)S(1)}, f32[8,192]{1,0:T(8,128)S(1)}, u32[]{:S(2)}, u32[]{:S(2)}) collective-permute-start(f32[8,192]{1,0:T(8,128)S(1)} %stack.53), channel_id=1, source_target_pairs={{0,256},{256,0},{1,257},{257,1},{2,258},{258,2},{3,259},{259,3},{4... | collective-permute-start | bytes 18440 | tf_op jit(solution)/shard_map/ppermute | solution.py:19
  118.5 0.7 collective-permute-done.14
  119.3 0.7 broadcast_in_dim.48
  120.0 9.7 %all-to-all-start = ((f32[32,8,192]{2,1,0:T(8,128)}), f32[32,8,192]{2,1,0:T(8,128)S(1)}, u32[]{:S(2)}, u32[]{:S(2)}) async-start(f32[32,8,192]{2,1,0:T(8,128)} %broadcast_in_dim.48), calls=%async_computation | async-start | bytes 524288 | tf_op jit(solution)/shard_map/all_to_all | solution.py:180
  129.7 0.2 select_reduce_fusion
  129.9 0.1 reshape.38
  130.1 11.2 %all-to-all-done.stats_ref = f32[32,8,192]{2,1,0:T(8,128)S(1)} async-done(((f32[32,8,192]{2,1,0:T(8,128)}), f32[32,8,192]{2,1,0:T(8,128)S(1)}, u32[]{:S(2)}, u32[]{:S(2)}) %all-to-all-start) | async-done | bytes 196640 | tf_op jit(solution)/shard_map/all_to_all | solution.py:180
  141.3 10.0 %shard_map.77 = (f32[32,96,128]{2,1,0:T(8,128)S(1)}, bf16[32,96,128]{2,1,0:T(8,128)(2,1)S(1)}, f32[1,192]{1,0:T(1,128)S(1)}) custom-call(s32[2]{0:T(128)S(1)} %pad_add_fusion.place_ref, f32[32,8,192]{2,1,0:T(8,128)S(1)} %all-to-all-done.stats_ref, f32[1,192]{1,0:T(1,128)S(1)} %bitcast.31, f32[192,1280]{1,0:T(8,128)} %copy-done.2, ...), custom_call_target="tpu_custom_call" | custom-call | flops 2013265920 | bytes 10485760 | tf_op jit(solution)/shard_map/pallas_call | solution.py:111
  151.3 4.2 %collective-permute-start.15 = (bf16[32,96,128]{2,1,0:T(8,128)(2,1)S(1)}, bf16[32,96,128]{2,1,0:T(8,128)(2,1)S(1)}, u32[]{:S(2)}, u32[]{:S(2)}) collective-permute-start(bf16[32,96,128]{2,1,0:T(8,128)(2,1)S(1)} %get-tuple-element.7), channel_id=1, source_target_pairs={{0,256},{256,0},{1,257},{257,1},{2,258},{258,2},{3,259},{259,3},{4... | collective-permute-start | bytes 2359304 | tf_op jit(solution)/shard_map/ppermute | solution.py:19
  155.5 1.9 %collective-permute-done.15 = bf16[32,96,128]{2,1,0:T(8,128)(2,1)S(1)} collective-permute-done((bf16[32,96,128]{2,1,0:T(8,128)(2,1)S(1)}, bf16[32,96,128]{2,1,0:T(8,128)(2,1)S(1)}, u32[]{:S(2)}, u32[]{:S(2)}) %collective-permute-start.15) | collective-permute-done | bytes 786464 | tf_op jit(solution)/shard_map/ppermute | solution.py:19
  157.4 1.1 add_convert_fusion
  158.5 3.9 %all-to-all-start.1 = ((bf16[32,96,128]{2,1,0:T(8,128)(2,1)}), bf16[32,96,128]{2,1,0:T(8,128)(2,1)S(1)}, u32[]{:S(2)}, u32[]{:S(2)}) async-start(bf16[32,96,128]{2,1,0:T(8,128)(2,1)} %add_convert_fusion), calls=%async_computation.1 | async-start | bytes 1572864 | tf_op jit(solution)/shard_map/all_to_all | solution.py:187
  162.5 0.6 reduce_sum.91
  163.1 20.8 %all-to-all-done.1 = bf16[32,96,128]{2,1,0:T(8,128)(2,1)S(1)} async-done(((bf16[32,96,128]{2,1,0:T(8,128)(2,1)}), bf16[32,96,128]{2,1,0:T(8,128)(2,1)S(1)}, u32[]{:S(2)}, u32[]{:S(2)}) %all-to-all-start.1) | async-done | bytes 786464 | tf_op jit(solution)/shard_map/all_to_all | solution.py:187
  184.0 0.1 reduce_sum.92
  184.1 0.1 fusion.47
  184.2 0.6 maximum_bitcast_fusion
  (52 shorter events, 0.5 us)
Async XLA Ops:
  0.6 47.2 %copy-start = (bf16[192,4096]{1,0:T(8,128)(2,1)S(1)}, bf16[192,4096]{1,0:T(8,128)(2,1)}, u32[]{:S(2)}) copy-start(bf16[192,4096]{1,0:T(8,128)(2,1)} %param.6) | copy-start | bytes 4718596
  0.6 47.2 %copy-start.1 = (bf16[512,1280]{1,0:T(8,128)(2,1)S(1)}, bf16[512,1280]{1,0:T(8,128)(2,1)}, u32[]{:S(2)}) copy-start(bf16[512,1280]{1,0:T(8,128)(2,1)} %own_ref.1) | copy-start | bytes 3932164
  0.7 46.9 %copy-start.3 = (bf16[192,1280]{1,0:T(8,128)(2,1)S(1)}, bf16[192,1280]{1,0:T(8,128)(2,1)}, u32[]{:S(2)}) copy-start(bf16[192,1280]{1,0:T(8,128)(2,1)} %teacher_ref.1) | copy-start | bytes 1474564
  2.2 19.0 %collective-permute-start.1 = (bf16[256,1280]{1,0:T(8,128)(2,1)S(1)}, bf16[256,1280]{1,0:T(8,128)(2,1)S(1)}, u32[]{:S(2)}, u32[]{:S(2)}) collective-permute-start(bf16[256,1280]{1,0:T(8,128)(2,1)S(1)} %get-tuple-element.15), channel_id=1, source_target_pairs={{0,32},{32,64},{64,96},{96,128},{128,160},{160,192},{192,224},{224... | collective-permute-start | bytes 1966088 | tf_op jit(solution)/shard_map/ppermute | solution.py:160
  13.7 14.5 %collective-permute-start = (bf16[256,1280]{1,0:T(8,128)(2,1)S(1)}, bf16[256,1280]{1,0:T(8,128)(2,1)S(1)}, u32[]{:S(2)}, u32[]{:S(2)}) collective-permute-start(bf16[256,1280]{1,0:T(8,128)(2,1)S(1)} %get-tuple-element.14), channel_id=1, source_target_pairs={{0,32},{32,64},{64,96},{96,128},{128,160},{160,192},{192,224},{224... | collective-permute-start | bytes 1966088 | tf_op jit(solution)/shard_map/ppermute | solution.py:160
  21.2 0.8 copy-start.8
  22.1 13.2 %collective-permute-start.3 = (bf16[256,1280]{1,0:T(8,128)(2,1)S(1)}, bf16[256,1280]{1,0:T(8,128)(2,1)}, u32[]{:S(2)}, u32[]{:S(2)}) collective-permute-start(bf16[256,1280]{1,0:T(8,128)(2,1)S(1)} %collective-permute-done.1.refs_1_), channel_id=1, source_target_pairs={{0,32},{32,64},{64,96},{96,128},{128,160},{160,192},{192,224},{224... | collective-permute-start | bytes 1966088 | tf_op jit(solution)/shard_map/ppermute | solution.py:160
  28.2 7.0 %copy-start.10 = (bf16[256,1280]{1,0:T(8,128)(2,1)}, bf16[256,1280]{1,0:T(8,128)(2,1)S(1)}, u32[]{:S(2)}) copy-start(bf16[256,1280]{1,0:T(8,128)(2,1)S(1)} %collective-permute-done.refs_0_) | copy-start | bytes 1966084
  28.2 14.0 %collective-permute-start.2 = (bf16[256,1280]{1,0:T(8,128)(2,1)S(1)}, bf16[256,1280]{1,0:T(8,128)(2,1)}, u32[]{:S(2)}, u32[]{:S(2)}) collective-permute-start(bf16[256,1280]{1,0:T(8,128)(2,1)S(1)} %collective-permute-done.refs_0_), channel_id=1, source_target_pairs={{0,32},{32,64},{64,96},{96,128},{128,160},{160,192},{192,224},{224... | collective-permute-start | bytes 1966088 | tf_op jit(solution)/shard_map/ppermute | solution.py:160
  35.3 14.1 %collective-permute-start.5 = (bf16[256,1280]{1,0:T(8,128)(2,1)}, bf16[256,1280]{1,0:T(8,128)(2,1)}, u32[]{:S(2)}, u32[]{:S(2)}) collective-permute-start(bf16[256,1280]{1,0:T(8,128)(2,1)} %collective-permute-done.3.refs_3_), channel_id=1, source_target_pairs={{0,32},{32,64},{64,96},{96,128},{128,160},{160,192},{192,224},{224... | collective-permute-start | bytes 1966088 | tf_op jit(solution)/shard_map/ppermute | solution.py:160
  42.3 14.1 %collective-permute-start.4 = (bf16[256,1280]{1,0:T(8,128)(2,1)}, bf16[256,1280]{1,0:T(8,128)(2,1)}, u32[]{:S(2)}, u32[]{:S(2)}) collective-permute-start(bf16[256,1280]{1,0:T(8,128)(2,1)} %collective-permute-done.2.refs_2_), channel_id=1, source_target_pairs={{0,32},{32,64},{64,96},{96,128},{128,160},{160,192},{192,224},{224... | collective-permute-start | bytes 1966088 | tf_op jit(solution)/shard_map/ppermute | solution.py:160
  47.8 6.6 %copy-start.11 = (bf16[256,1280]{1,0:T(8,128)(2,1)S(1)}, bf16[256,1280]{1,0:T(8,128)(2,1)}, u32[]{:S(2)}) copy-start(bf16[256,1280]{1,0:T(8,128)(2,1)} %copy-done.10) | copy-start | bytes 1966084
  48.3 13.2 %copy-start.9 = (bf16[256,1280]{1,0:T(8,128)(2,1)S(1)}, bf16[256,1280]{1,0:T(8,128)(2,1)}, u32[]{:S(2)}) copy-start(bf16[256,1280]{1,0:T(8,128)(2,1)} %copy-done.8) | copy-start | bytes 1966084
  49.4 14.0 %collective-permute-start.7 = (bf16[256,1280]{1,0:T(8,128)(2,1)}, bf16[256,1280]{1,0:T(8,128)(2,1)S(1)}, u32[]{:S(2)}, u32[]{:S(2)}) collective-permute-start(bf16[256,1280]{1,0:T(8,128)(2,1)} %collective-permute-done.5.refs_5_), channel_id=1, source_target_pairs={{0,32},{32,64},{64,96},{96,128},{128,160},{160,192},{192,224},{224... | collective-permute-start | bytes 1966088 | tf_op jit(solution)/shard_map/ppermute | solution.py:160
  56.4 14.0 %collective-permute-start.6 = (bf16[256,1280]{1,0:T(8,128)(2,1)}, bf16[256,1280]{1,0:T(8,128)(2,1)S(1)}, u32[]{:S(2)}, u32[]{:S(2)}) collective-permute-start(bf16[256,1280]{1,0:T(8,128)(2,1)} %collective-permute-done.4.refs_4_), channel_id=1, source_target_pairs={{0,32},{32,64},{64,96},{96,128},{128,160},{160,192},{192,224},{224... | collective-permute-start | bytes 1966088 | tf_op jit(solution)/shard_map/ppermute | solution.py:160
  63.5 19.0 %copy-start.4 = (bf16[256,1280]{1,0:T(8,128)(2,1)}, bf16[256,1280]{1,0:T(8,128)(2,1)S(1)}, u32[]{:S(2)}) copy-start(bf16[256,1280]{1,0:T(8,128)(2,1)S(1)} %collective-permute-done.7.refs_7_) | copy-start | bytes 1966084
  63.5 14.7 %collective-permute-start.9 = (bf16[256,1280]{1,0:T(8,128)(2,1)S(1)}, bf16[256,1280]{1,0:T(8,128)(2,1)S(1)}, u32[]{:S(2)}, u32[]{:S(2)}) collective-permute-start(bf16[256,1280]{1,0:T(8,128)(2,1)S(1)} %collective-permute-done.7.refs_7_), channel_id=1, source_target_pairs={{0,32},{32,64},{64,96},{96,128},{128,160},{160,192},{192,224},{224... | collective-permute-start | bytes 1966088 | tf_op jit(solution)/shard_map/ppermute | solution.py:160
  70.5 19.0 %copy-start.13 = (bf16[256,1280]{1,0:T(8,128)(2,1)}, bf16[256,1280]{1,0:T(8,128)(2,1)S(1)}, u32[]{:S(2)}) copy-start(bf16[256,1280]{1,0:T(8,128)(2,1)S(1)} %collective-permute-done.6.refs_6_) | copy-start | bytes 1966084
  70.5 13.9 %collective-permute-start.8 = (bf16[256,1280]{1,0:T(8,128)(2,1)S(1)}, bf16[256,1280]{1,0:T(8,128)(2,1)S(1)}, u32[]{:S(2)}, u32[]{:S(2)}) collective-permute-start(bf16[256,1280]{1,0:T(8,128)(2,1)S(1)} %collective-permute-done.6.refs_6_), channel_id=1, source_target_pairs={{0,32},{32,64},{64,96},{96,128},{128,160},{160,192},{192,224},{224... | collective-permute-start | bytes 1966088 | tf_op jit(solution)/shard_map/ppermute | solution.py:160
  78.2 11.6 %copy-start.5 = (bf16[256,1280]{1,0:T(8,128)(2,1)}, bf16[256,1280]{1,0:T(8,128)(2,1)S(1)}, u32[]{:S(2)}) copy-start(bf16[256,1280]{1,0:T(8,128)(2,1)S(1)} %collective-permute-done.9.refs_9_) | copy-start | bytes 1966084
  78.2 13.2 %collective-permute-start.11 = (bf16[256,1280]{1,0:T(8,128)(2,1)S(1)}, bf16[256,1280]{1,0:T(8,128)(2,1)S(1)}, u32[]{:S(2)}, u32[]{:S(2)}) collective-permute-start(bf16[256,1280]{1,0:T(8,128)(2,1)S(1)} %collective-permute-done.9.refs_9_), channel_id=1, source_target_pairs={{0,32},{32,64},{64,96},{96,128},{128,160},{160,192},{192,224},{224... | collective-permute-start | bytes 1966088 | tf_op jit(solution)/shard_map/ppermute | solution.py:160
  84.4 12.0 %copy-start.14 = (bf16[256,1280]{1,0:T(8,128)(2,1)}, bf16[256,1280]{1,0:T(8,128)(2,1)S(1)}, u32[]{:S(2)}) copy-start(bf16[256,1280]{1,0:T(8,128)(2,1)S(1)} %collective-permute-done.8.refs_8_) | copy-start | bytes 1966084
  84.4 14.0 %collective-permute-start.10 = (bf16[256,1280]{1,0:T(8,128)(2,1)S(1)}, bf16[256,1280]{1,0:T(8,128)(2,1)S(1)}, u32[]{:S(2)}, u32[]{:S(2)}) collective-permute-start(bf16[256,1280]{1,0:T(8,128)(2,1)S(1)} %collective-permute-done.8.refs_8_), channel_id=1, source_target_pairs={{0,32},{32,64},{64,96},{96,128},{128,160},{160,192},{192,224},{224... | collective-permute-start | bytes 1966088 | tf_op jit(solution)/shard_map/ppermute | solution.py:160
  91.4 12.0 %copy-start.6 = (bf16[256,1280]{1,0:T(8,128)(2,1)}, bf16[256,1280]{1,0:T(8,128)(2,1)S(1)}, u32[]{:S(2)}) copy-start(bf16[256,1280]{1,0:T(8,128)(2,1)S(1)} %collective-permute-done.11.refs_11_) | copy-start | bytes 1966084
  91.4 14.0 %collective-permute-start.13 = (bf16[256,1280]{1,0:T(8,128)(2,1)S(1)}, bf16[256,1280]{1,0:T(8,128)(2,1)S(1)}, u32[]{:S(2)}, u32[]{:S(2)}) collective-permute-start(bf16[256,1280]{1,0:T(8,128)(2,1)S(1)} %collective-permute-done.11.refs_11_), channel_id=1, source_target_pairs={{0,32},{32,64},{64,96},{96,128},{128,160},{160,192},{192,224},{224... | collective-permute-start | bytes 1966088 | tf_op jit(solution)/shard_map/ppermute | solution.py:160
  98.5 5.7 %copy-start.15 = (bf16[256,1280]{1,0:T(8,128)(2,1)}, bf16[256,1280]{1,0:T(8,128)(2,1)S(1)}, u32[]{:S(2)}) copy-start(bf16[256,1280]{1,0:T(8,128)(2,1)S(1)} %collective-permute-done.10.refs_10_) | copy-start | bytes 1966084
  98.5 14.0 %collective-permute-start.12 = (bf16[256,1280]{1,0:T(8,128)(2,1)S(1)}, bf16[256,1280]{1,0:T(8,128)(2,1)S(1)}, u32[]{:S(2)}, u32[]{:S(2)}) collective-permute-start(bf16[256,1280]{1,0:T(8,128)(2,1)S(1)} %collective-permute-done.10.refs_10_), channel_id=1, source_target_pairs={{0,32},{32,64},{64,96},{96,128},{128,160},{160,192},{192,224},{224... | collective-permute-start | bytes 1966088 | tf_op jit(solution)/shard_map/ppermute | solution.py:160
  105.5 7.4 %copy-start.7 = (bf16[256,1280]{1,0:T(8,128)(2,1)}, bf16[256,1280]{1,0:T(8,128)(2,1)S(1)}, u32[]{:S(2)}) copy-start(bf16[256,1280]{1,0:T(8,128)(2,1)S(1)} %collective-permute-done.13.refs_13_) | copy-start | bytes 1966084
  105.8 12.6 %copy-start.17 = (s32[96]{0:T(128)S(1)}, s32[96]{0:T(128)}, u32[]{:S(2)}) copy-start(s32[96]{0:T(128)} %param.10) | copy-start | bytes 1156
  112.5 0.9 copy-start.12
  113.4 27.9 %copy-start.2 = (f32[192,1280]{1,0:T(8,128)}, f32[192,1280]{1,0:T(8,128)S(1)}, u32[]{:S(2)}) copy-start(f32[192,1280]{1,0:T(8,128)S(1)} %get-tuple-element.26.logits_ref) | copy-start | bytes 2949124
  113.4 16.3 %copy-start.18 = (s32[96]{0:T(128)S(1)}, s32[96]{0:T(128)}, u32[]{:S(2)}) copy-start(s32[96]{0:T(128)} %param.9) | copy-start | bytes 1156
  113.4 16.7 %copy-start.16 = (s32[192]{0:T(256)S(1)}, s32[192]{0:T(256)}, u32[]{:S(2)}) copy-start(s32[192]{0:T(256)} %param.11) | copy-start | bytes 2308
  114.0 5.2 %collective-permute-start.14 = (f32[8,192]{1,0:T(8,128)S(1)}, f32[8,192]{1,0:T(8,128)S(1)}, u32[]{:S(2)}, u32[]{:S(2)}) collective-permute-start(f32[8,192]{1,0:T(8,128)S(1)} %stack.53), channel_id=1, source_target_pairs={{0,256},{256,0},{1,257},{257,1},{2,258},{258,2},{3,259},{259,3},{4... | collective-permute-start | bytes 18440 | tf_op jit(solution)/shard_map/ppermute | solution.py:19
  120.0 21.3 %all-to-all-start = ((f32[32,8,192]{2,1,0:T(8,128)}), f32[32,8,192]{2,1,0:T(8,128)S(1)}, u32[]{:S(2)}, u32[]{:S(2)}) async-start(f32[32,8,192]{2,1,0:T(8,128)} %broadcast_in_dim.48), calls=%async_computation | async-start | bytes 524288 | tf_op jit(solution)/shard_map/all_to_all | solution.py:180
  151.3 6.1 %collective-permute-start.15 = (bf16[32,96,128]{2,1,0:T(8,128)(2,1)S(1)}, bf16[32,96,128]{2,1,0:T(8,128)(2,1)S(1)}, u32[]{:S(2)}, u32[]{:S(2)}) collective-permute-start(bf16[32,96,128]{2,1,0:T(8,128)(2,1)S(1)} %get-tuple-element.7), channel_id=1, source_target_pairs={{0,256},{256,0},{1,257},{257,1},{2,258},{258,2},{3,259},{259,3},{4... | collective-permute-start | bytes 2359304 | tf_op jit(solution)/shard_map/ppermute | solution.py:19
  158.5 25.5 %all-to-all-start.1 = ((bf16[32,96,128]{2,1,0:T(8,128)(2,1)}), bf16[32,96,128]{2,1,0:T(8,128)(2,1)S(1)}, u32[]{:S(2)}, u32[]{:S(2)}) async-start(bf16[32,96,128]{2,1,0:T(8,128)(2,1)} %add_convert_fusion), calls=%async_computation.1 | async-start | bytes 1572864 | tf_op jit(solution)/shard_map/all_to_all | solution.py:187

commit v6 on v5

--- a/solution.py
+++ b/solution.py
@@ -175,9 +175,7 @@
     term = jnp.sum(powers * (shifted - teacher_gap), axis=1)
     blank = jnp.zeros_like(peak)
     own = jnp.stack([peak, total, teacher_peak, teacher_total, term, blank, blank, blank])
-    other = swap_side(own)
-    pair = jnp.concatenate([*join(*[jnp.stack([own[i], other[i]]) for i in range(5)]), own[5:]])
-    stats = lax.all_to_all(jnp.broadcast_to(pair, (count,) + pair.shape), "vocab", 0, 0)
+    stats = lax.all_to_all(jnp.broadcast_to(own, (2 * count,) + own.shape), ("side", "vocab"), 0, 0)
 
     place = jnp.stack([side_place, row_place]).astype(jnp.int32)
     keep, send, diverge = grad_products(

time: 186 us -> 189 us (1.016)
  waiting for transfers between devices: 61.5 us -> 66.6 us
  starting transfers between devices: 95.2 us -> 92.7 us
    ppermute x2 -> x1, starting transfers between devices: 8.56 us -> 1.92 us  [swap_side(): return lax.ppermute(value, 'side', [(0, 1), (1, 0)])]
    all_to_all x1, waiting for transfers between devices: 11.2 us -> 16.9 us  [body(): lax.all_to_all(jnp.broadcast_to(own, (2 * count,) + own.shape), ('side',...]
    all_to_all x1, starting transfers between devices: 9.67 us -> 12.7 us  [body(): lax.all_to_all(jnp.broadcast_to(own, (2 * count,) + own.shape), ('side',...]
  transfers between devices with their start and end apart: 18 -> 17, of which waited for: 17 -> 16; matrix products, arithmetic and copies ran while one was open for 5% -> 5% of each run, Pallas kernels for 0% -> 0%
where the time goes in v6:
time: 189 us; the launch traced here: 187 us
  starting transfers between devices  92.7 us (49%)
  waiting for transfers between devices  66.6 us (35%)
  Pallas kernels  9.85 us (5%)
  matrix products  9.12 us (5%)
  local copies, waits for them, and re-layouts  4.18 us (2%)
  other arithmetic  3.49 us (2%)
    ppermute x14, starting transfers between devices, body(): held = [lax.ppermute(part, ('side', 'row'), ring) for part in held]  73 us
    ppermute x14, waiting for transfers between devices, body(): held = [lax.ppermute(part, ('side', 'row'), ring) for part in held]  27 us
    all_to_all x1, waiting for transfers between devices, body(): pieces = lax.all_to_all(packed, 'vocab', 0, 0)  20.5 us
    all_to_all x1, waiting for transfers between devices, body(): lax.all_to_all(jnp.broadcast_to(own, (2 * count,) + own.shape), ('side',...  16.9 us
    all_to_all x1, starting transfers between devices, body(): lax.all_to_all(jnp.broadcast_to(own, (2 * count,) + own.shape), ('side',...  12.7 us
    pallas_call x1, Pallas kernels, grad_products(): pl.pallas_call(functools.partial(grad_kernel, blocks), out_shape=[jax.Sha...  9.85 us
    dot_general x14, matrix products, body(): jnp.dot(piece, held[part], preferred_element_type=jnp.float32)  8.7 us
    all_to_all x1, starting transfers between devices, body(): pieces = lax.all_to_all(packed, 'vocab', 0, 0)  5.06 us
  transfers between devices with their start and end apart: 17, of which 16 were waited for; matrix products, arithmetic and copies ran while one was open for 5% of the time, Pallas kernels for 0%

profile of v6, /device:TPU:1, one launch (start us, length us, event | category | flops | bytes accessed | tf_op | source)
XLA Modules:
  0.0 187.3 jit_solution(5732191731058893055)
XLA Ops:
  0.7 1.5 fusion.43
  2.2 11.5 %collective-permute-start.1 = (bf16[256,1280]{1,0:T(8,128)(2,1)S(1)}, bf16[256,1280]{1,0:T(8,128)(2,1)S(1)}, u32[]{:S(2)}, u32[]{:S(2)}) collective-permute-start(bf16[256,1280]{1,0:T(8,128)(2,1)S(1)} %get-tuple-element.12), channel_id=1, source_target_pairs={{0,32},{32,64},{64,96},{96,128},{128,160},{160,192},{192,224},{224... | collective-permute-start | bytes 1966088 | tf_op jit(solution)/shard_map/ppermute | solution.py:160
  13.7 2.2 %collective-permute-start = (bf16[256,1280]{1,0:T(8,128)(2,1)S(1)}, bf16[256,1280]{1,0:T(8,128)(2,1)S(1)}, u32[]{:S(2)}, u32[]{:S(2)}) collective-permute-start(bf16[256,1280]{1,0:T(8,128)(2,1)S(1)} %get-tuple-element.11), channel_id=1, source_target_pairs={{0,32},{32,64},{64,96},{96,128},{128,160},{160,192},{192,224},{224... | collective-permute-start | bytes 1966088 | tf_op jit(solution)/shard_map/ppermute | solution.py:160
  15.9 5.3 %collective-permute-done.1.refs_1_ = bf16[256,1280]{1,0:T(8,128)(2,1)S(1)} collective-permute-done((bf16[256,1280]{1,0:T(8,128)(2,1)S(1)}, bf16[256,1280]{1,0:T(8,128)(2,1)S(1)}, u32[]{:S(2)}, u32[]{:S(2)}) %collective-permute-start.1) | collective-permute-done | bytes 655392 | tf_op jit(solution)/shard_map/ppermute | solution.py:160
  21.2 0.8 copy-done.8
  22.1 5.0 %collective-permute-start.3 = (bf16[256,1280]{1,0:T(8,128)(2,1)S(1)}, bf16[256,1280]{1,0:T(8,128)(2,1)}, u32[]{:S(2)}, u32[]{:S(2)}) collective-permute-start(bf16[256,1280]{1,0:T(8,128)(2,1)S(1)} %collective-permute-done.1.refs_1_), channel_id=1, source_target_pairs={{0,32},{32,64},{64,96},{96,128},{128,160},{160,192},{192,224},{224... | collective-permute-start | bytes 1966088 | tf_op jit(solution)/shard_map/ppermute | solution.py:160
  27.1 1.2 collective-permute-done.refs_0_
  28.2 5.0 %collective-permute-start.2 = (bf16[256,1280]{1,0:T(8,128)(2,1)S(1)}, bf16[256,1280]{1,0:T(8,128)(2,1)}, u32[]{:S(2)}, u32[]{:S(2)}) collective-permute-start(bf16[256,1280]{1,0:T(8,128)(2,1)S(1)} %collective-permute-done.refs_0_), channel_id=1, source_target_pairs={{0,32},{32,64},{64,96},{96,128},{128,160},{160,192},{192,224},{224... | collective-permute-start | bytes 1966088 | tf_op jit(solution)/shard_map/ppermute | solution.py:160
  33.3 2.0 %collective-permute-done.3.refs_3_ = bf16[256,1280]{1,0:T(8,128)(2,1)} collective-permute-done((bf16[256,1280]{1,0:T(8,128)(2,1)S(1)}, bf16[256,1280]{1,0:T(8,128)(2,1)}, u32[]{:S(2)}, u32[]{:S(2)}) %collective-permute-start.3) | collective-permute-done | bytes 655392 | tf_op jit(solution)/shard_map/ppermute | solution.py:160
  35.3 5.1 %collective-permute-start.5 = (bf16[256,1280]{1,0:T(8,128)(2,1)}, bf16[256,1280]{1,0:T(8,128)(2,1)}, u32[]{:S(2)}, u32[]{:S(2)}) collective-permute-start(bf16[256,1280]{1,0:T(8,128)(2,1)} %collective-permute-done.3.refs_3_), channel_id=1, source_target_pairs={{0,32},{32,64},{64,96},{96,128},{128,160},{160,192},{192,224},{224... | collective-permute-start | bytes 1966088 | tf_op jit(solution)/shard_map/ppermute | solution.py:160
  40.4 1.9 %collective-permute-done.2.refs_2_ = bf16[256,1280]{1,0:T(8,128)(2,1)} collective-permute-done((bf16[256,1280]{1,0:T(8,128)(2,1)S(1)}, bf16[256,1280]{1,0:T(8,128)(2,1)}, u32[]{:S(2)}, u32[]{:S(2)}) %collective-permute-start.2) | collective-permute-done | bytes 655392 | tf_op jit(solution)/shard_map/ppermute | solution.py:160
  42.3 5.1 %collective-permute-start.4 = (bf16[256,1280]{1,0:T(8,128)(2,1)}, bf16[256,1280]{1,0:T(8,128)(2,1)}, u32[]{:S(2)}, u32[]{:S(2)}) collective-permute-start(bf16[256,1280]{1,0:T(8,128)(2,1)} %collective-permute-done.2.refs_2_), channel_id=1, source_target_pairs={{0,32},{32,64},{64,96},{96,128},{128,160},{160,192},{192,224},{224... | collective-permute-start | bytes 1966088 | tf_op jit(solution)/shard_map/ppermute | solution.py:160
  47.6 0.1 reduce_max.28
  47.9 0.4 fusion.6
  48.3 1.1 collective-permute-done.5.refs_5_
  49.4 5.0 %collective-permute-start.7 = (bf16[256,1280]{1,0:T(8,128)(2,1)}, bf16[256,1280]{1,0:T(8,128)(2,1)S(1)}, u32[]{:S(2)}, u32[]{:S(2)}) collective-permute-start(bf16[256,1280]{1,0:T(8,128)(2,1)} %collective-permute-done.5.refs_5_), channel_id=1, source_target_pairs={{0,32},{32,64},{64,96},{96,128},{128,160},{160,192},{192,224},{224... | collective-permute-start | bytes 1966088 | tf_op jit(solution)/shard_map/ppermute | solution.py:160
  54.4 0.3 convolution_add_fusion.7
  54.8 1.7 collective-permute-done.4.refs_4_
  56.4 5.0 %collective-permute-start.6 = (bf16[256,1280]{1,0:T(8,128)(2,1)}, bf16[256,1280]{1,0:T(8,128)(2,1)S(1)}, u32[]{:S(2)}, u32[]{:S(2)}) collective-permute-start(bf16[256,1280]{1,0:T(8,128)(2,1)} %collective-permute-done.4.refs_4_), channel_id=1, source_target_pairs={{0,32},{32,64},{64,96},{96,128},{128,160},{160,192},{192,224},{224... | collective-permute-start | bytes 1966088 | tf_op jit(solution)/shard_map/ppermute | solution.py:160
  61.5 0.3 convolution_add_fusion.6
  61.8 1.4 fusion.23
  63.2 0.3 collective-permute-done.7.refs_7_
  63.5 4.9 %collective-permute-start.9 = (bf16[256,1280]{1,0:T(8,128)(2,1)S(1)}, bf16[256,1280]{1,0:T(8,128)(2,1)S(1)}, u32[]{:S(2)}, u32[]{:S(2)}) collective-permute-start(bf16[256,1280]{1,0:T(8,128)(2,1)S(1)} %collective-permute-done.7.refs_7_), channel_id=1, source_target_pairs={{0,32},{32,64},{64,96},{96,128},{128,160},{160,192},{192,224},{224... | collective-permute-start | bytes 1966088 | tf_op jit(solution)/shard_map/ppermute | solution.py:160
  68.4 1.4 fusion
  69.8 0.7 collective-permute-done.6.refs_6_
  70.5 4.9 %collective-permute-start.8 = (bf16[256,1280]{1,0:T(8,128)(2,1)S(1)}, bf16[256,1280]{1,0:T(8,128)(2,1)S(1)}, u32[]{:S(2)}, u32[]{:S(2)}) collective-permute-start(bf16[256,1280]{1,0:T(8,128)(2,1)S(1)} %collective-permute-done.6.refs_6_), channel_id=1, source_target_pairs={{0,32},{32,64},{64,96},{96,128},{128,160},{160,192},{192,224},{224... | collective-permute-start | bytes 1966088 | tf_op jit(solution)/shard_map/ppermute | solution.py:160
  75.4 1.4 fusion.20
  76.8 1.4 fusion.1
  78.2 4.2 %collective-permute-start.11 = (bf16[256,1280]{1,0:T(8,128)(2,1)S(1)}, bf16[256,1280]{1,0:T(8,128)(2,1)S(1)}, u32[]{:S(2)}, u32[]{:S(2)}) collective-permute-start(bf16[256,1280]{1,0:T(8,128)(2,1)S(1)} %collective-permute-done.9.refs_9_), channel_id=1, source_target_pairs={{0,32},{32,64},{64,96},{96,128},{128,160},{160,192},{192,224},{224... | collective-permute-start | bytes 1966088 | tf_op jit(solution)/shard_map/ppermute | solution.py:160
  82.4 0.3 fusion.17
  82.7 1.7 collective-permute-done.8.refs_8_
  84.4 5.0 %collective-permute-start.10 = (bf16[256,1280]{1,0:T(8,128)(2,1)S(1)}, bf16[256,1280]{1,0:T(8,128)(2,1)S(1)}, u32[]{:S(2)}, u32[]{:S(2)}) collective-permute-start(bf16[256,1280]{1,0:T(8,128)(2,1)S(1)} %collective-permute-done.8.refs_8_), channel_id=1, source_target_pairs={{0,32},{32,64},{64,96},{96,128},{128,160},{160,192},{192,224},{224... | collective-permute-start | bytes 1966088 | tf_op jit(solution)/shard_map/ppermute | solution.py:160
  89.5 0.3 fusion.2
  89.8 0.3 fusion.14
  90.1 1.4 collective-permute-done.11.refs_11_
  91.4 5.0 %collective-permute-start.13 = (bf16[256,1280]{1,0:T(8,128)(2,1)S(1)}, bf16[256,1280]{1,0:T(8,128)(2,1)S(1)}, u32[]{:S(2)}, u32[]{:S(2)}) collective-permute-start(bf16[256,1280]{1,0:T(8,128)(2,1)S(1)} %collective-permute-done.11.refs_11_), channel_id=1, source_target_pairs={{0,32},{32,64},{64,96},{96,128},{128,160},{160,192},{192,224},{224... | collective-permute-start | bytes 1966088 | tf_op jit(solution)/shard_map/ppermute | solution.py:160
  96.5 0.3 fusion.3
  96.8 1.7 collective-permute-done.10.refs_10_
  98.5 5.0 %collective-permute-start.12 = (bf16[256,1280]{1,0:T(8,128)(2,1)S(1)}, bf16[256,1280]{1,0:T(8,128)(2,1)S(1)}, u32[]{:S(2)}, u32[]{:S(2)}) collective-permute-start(bf16[256,1280]{1,0:T(8,128)(2,1)S(1)} %collective-permute-done.10.refs_10_), channel_id=1, source_target_pairs={{0,32},{32,64},{64,96},{96,128},{128,160},{160,192},{192,224},{224... | collective-permute-start | bytes 1966088 | tf_op jit(solution)/shard_map/ppermute | solution.py:160
  103.5 0.3 fusion.11
  103.8 0.3 fusion.4
  104.1 1.4 collective-permute-done.13.refs_13_
  105.5 0.3 fusion.8
  105.8 6.7 %collective-permute-done.12.refs_12_ = bf16[256,1280]{1,0:T(8,128)(2,1)S(1)} collective-permute-done((bf16[256,1280]{1,0:T(8,128)(2,1)S(1)}, bf16[256,1280]{1,0:T(8,128)(2,1)S(1)}, u32[]{:S(2)}, u32[]{:S(2)}) %collective-permute-start.12) | collective-permute-done | bytes 655392 | tf_op jit(solution)/shard_map/ppermute | solution.py:160
  112.5 0.4 fusion.45
  112.9 0.4 copy-done.12
  113.4 0.6 multiply_reduce_fusion
  114.0 0.9 broadcast_in_dim.34
  114.9 12.7 %all-to-all-start = ((f32[64,8,192]{2,1,0:T(8,128)}), f32[64,8,192]{2,1,0:T(8,128)S(1)}, u32[]{:S(2)}, u32[]{:S(2)}) async-start(f32[64,8,192]{2,1,0:T(8,128)} %broadcast_in_dim.34), calls=%async_computation | async-start | bytes 1048576 | tf_op jit(solution)/shard_map/all_to_all | solution.py:178
  127.6 0.1 dynamic_slice.48
  127.7 0.2 select_reduce_fusion
  127.9 0.1 reshape.25
  128.1 16.9 %all-to-all-done.stats_ref = f32[64,8,192]{2,1,0:T(8,128)S(1)} async-done(((f32[64,8,192]{2,1,0:T(8,128)}), f32[64,8,192]{2,1,0:T(8,128)S(1)}, u32[]{:S(2)}, u32[]{:S(2)}) %all-to-all-start) | async-done | bytes 393248 | tf_op jit(solution)/shard_map/all_to_all | solution.py:178
  145.0 9.9 %shard_map.77 = (f32[32,96,128]{2,1,0:T(8,128)S(1)}, bf16[32,96,128]{2,1,0:T(8,128)(2,1)S(1)}, f32[1,192]{1,0:T(1,128)S(1)}) custom-call(s32[2]{0:T(128)S(1)} %pad_add_fusion.place_ref, f32[64,8,192]{2,1,0:T(8,128)S(1)} %all-to-all-done.stats_ref, f32[1,192]{1,0:T(1,128)S(1)} %bitcast.26, f32[192,1280]{1,0:T(8,128)} %copy-done.2, ...), custom_call_target="tpu_custom_call" | custom-call | flops 2013265920 | bytes 10485760 | tf_op jit(solution)/shard_map/pallas_call | solution.py:111
  154.8 1.9 %collective-permute-start.14 = (bf16[32,96,128]{2,1,0:T(8,128)(2,1)S(1)}, bf16[32,96,128]{2,1,0:T(8,128)(2,1)S(1)}, u32[]{:S(2)}, u32[]{:S(2)}) collective-permute-start(bf16[32,96,128]{2,1,0:T(8,128)(2,1)S(1)} %get-tuple-element.7), channel_id=1, source_target_pairs={{0,256},{256,0},{1,257},{257,1},{2,258},{258,2},{3,259},{259,3},{4... | collective-permute-start | bytes 2359304 | tf_op jit(solution)/shard_map/ppermute | solution.py:19
  156.7 2.3 %collective-permute-done.14 = bf16[32,96,128]{2,1,0:T(8,128)(2,1)S(1)} collective-permute-done((bf16[32,96,128]{2,1,0:T(8,128)(2,1)S(1)}, bf16[32,96,128]{2,1,0:T(8,128)(2,1)S(1)}, u32[]{:S(2)}, u32[]{:S(2)}) %collective-permute-start.14) | collective-permute-done | bytes 786464 | tf_op jit(solution)/shard_map/ppermute | solution.py:19
  159.0 1.1 add_convert_fusion
  160.1 5.1 %all-to-all-start.1 = ((bf16[32,96,128]{2,1,0:T(8,128)(2,1)}), bf16[32,96,128]{2,1,0:T(8,128)(2,1)S(1)}, u32[]{:S(2)}, u32[]{:S(2)}) async-start(bf16[32,96,128]{2,1,0:T(8,128)(2,1)} %add_convert_fusion), calls=%async_computation.1 | async-start | bytes 1572864 | tf_op jit(solution)/shard_map/all_to_all | solution.py:185
  165.2 0.1 reshape.26
  165.3 0.6 reduce_sum.61
  165.9 20.5 %all-to-all-done.1 = bf16[32,96,128]{2,1,0:T(8,128)(2,1)S(1)} async-done(((bf16[32,96,128]{2,1,0:T(8,128)(2,1)}), bf16[32,96,128]{2,1,0:T(8,128)(2,1)S(1)}, u32[]{:S(2)}, u32[]{:S(2)}) %all-to-all-start.1) | async-done | bytes 786464 | tf_op jit(solution)/shard_map/all_to_all | solution.py:185
  186.4 0.1 reduce_sum.62
  186.5 0.1 fusion.44
  186.6 0.6 maximum_bitcast_fusion
  (46 shorter events, 0.3 us)
Async XLA Ops:
  0.6 47.2 %copy-start = (bf16[192,4096]{1,0:T(8,128)(2,1)S(1)}, bf16[192,4096]{1,0:T(8,128)(2,1)}, u32[]{:S(2)}) copy-start(bf16[192,4096]{1,0:T(8,128)(2,1)} %param.6) | copy-start | bytes 4718596
  0.6 47.2 %copy-start.1 = (bf16[512,1280]{1,0:T(8,128)(2,1)S(1)}, bf16[512,1280]{1,0:T(8,128)(2,1)}, u32[]{:S(2)}) copy-start(bf16[512,1280]{1,0:T(8,128)(2,1)} %own_ref.1) | copy-start | bytes 3932164
  0.7 46.9 %copy-start.3 = (bf16[192,1280]{1,0:T(8,128)(2,1)S(1)}, bf16[192,1280]{1,0:T(8,128)(2,1)}, u32[]{:S(2)}) copy-start(bf16[192,1280]{1,0:T(8,128)(2,1)} %teacher_ref.1) | copy-start | bytes 1474564
  2.2 19.0 %collective-permute-start.1 = (bf16[256,1280]{1,0:T(8,128)(2,1)S(1)}, bf16[256,1280]{1,0:T(8,128)(2,1)S(1)}, u32[]{:S(2)}, u32[]{:S(2)}) collective-permute-start(bf16[256,1280]{1,0:T(8,128)(2,1)S(1)} %get-tuple-element.12), channel_id=1, source_target_pairs={{0,32},{32,64},{64,96},{96,128},{128,160},{160,192},{192,224},{224... | collective-permute-start | bytes 1966088 | tf_op jit(solution)/shard_map/ppermute | solution.py:160
  13.7 14.5 %collective-permute-start = (bf16[256,1280]{1,0:T(8,128)(2,1)S(1)}, bf16[256,1280]{1,0:T(8,128)(2,1)S(1)}, u32[]{:S(2)}, u32[]{:S(2)}) collective-permute-start(bf16[256,1280]{1,0:T(8,128)(2,1)S(1)} %get-tuple-element.11), channel_id=1, source_target_pairs={{0,32},{32,64},{64,96},{96,128},{128,160},{160,192},{192,224},{224... | collective-permute-start | bytes 1966088 | tf_op jit(solution)/shard_map/ppermute | solution.py:160
  21.2 0.8 copy-start.8
  22.1 13.2 %collective-permute-start.3 = (bf16[256,1280]{1,0:T(8,128)(2,1)S(1)}, bf16[256,1280]{1,0:T(8,128)(2,1)}, u32[]{:S(2)}, u32[]{:S(2)}) collective-permute-start(bf16[256,1280]{1,0:T(8,128)(2,1)S(1)} %collective-permute-done.1.refs_1_), channel_id=1, source_target_pairs={{0,32},{32,64},{64,96},{96,128},{128,160},{160,192},{192,224},{224... | collective-permute-start | bytes 1966088 | tf_op jit(solution)/shard_map/ppermute | solution.py:160
  28.2 7.0 %copy-start.10 = (bf16[256,1280]{1,0:T(8,128)(2,1)}, bf16[256,1280]{1,0:T(8,128)(2,1)S(1)}, u32[]{:S(2)}) copy-start(bf16[256,1280]{1,0:T(8,128)(2,1)S(1)} %collective-permute-done.refs_0_) | copy-start | bytes 1966084
  28.2 14.0 %collective-permute-start.2 = (bf16[256,1280]{1,0:T(8,128)(2,1)S(1)}, bf16[256,1280]{1,0:T(8,128)(2,1)}, u32[]{:S(2)}, u32[]{:S(2)}) collective-permute-start(bf16[256,1280]{1,0:T(8,128)(2,1)S(1)} %collective-permute-done.refs_0_), channel_id=1, source_target_pairs={{0,32},{32,64},{64,96},{96,128},{128,160},{160,192},{192,224},{224... | collective-permute-start | bytes 1966088 | tf_op jit(solution)/shard_map/ppermute | solution.py:160
  35.3 14.1 %collective-permute-start.5 = (bf16[256,1280]{1,0:T(8,128)(2,1)}, bf16[256,1280]{1,0:T(8,128)(2,1)}, u32[]{:S(2)}, u32[]{:S(2)}) collective-permute-start(bf16[256,1280]{1,0:T(8,128)(2,1)} %collective-permute-done.3.refs_3_), channel_id=1, source_target_pairs={{0,32},{32,64},{64,96},{96,128},{128,160},{160,192},{192,224},{224... | collective-permute-start | bytes 1966088 | tf_op jit(solution)/shard_map/ppermute | solution.py:160
  42.3 14.1 %collective-permute-start.4 = (bf16[256,1280]{1,0:T(8,128)(2,1)}, bf16[256,1280]{1,0:T(8,128)(2,1)}, u32[]{:S(2)}, u32[]{:S(2)}) collective-permute-start(bf16[256,1280]{1,0:T(8,128)(2,1)} %collective-permute-done.2.refs_2_), channel_id=1, source_target_pairs={{0,32},{32,64},{64,96},{96,128},{128,160},{160,192},{192,224},{224... | collective-permute-start | bytes 1966088 | tf_op jit(solution)/shard_map/ppermute | solution.py:160
  47.8 6.6 %copy-start.11 = (bf16[256,1280]{1,0:T(8,128)(2,1)S(1)}, bf16[256,1280]{1,0:T(8,128)(2,1)}, u32[]{:S(2)}) copy-start(bf16[256,1280]{1,0:T(8,128)(2,1)} %copy-done.10) | copy-start | bytes 1966084
  48.3 13.2 %copy-start.9 = (bf16[256,1280]{1,0:T(8,128)(2,1)S(1)}, bf16[256,1280]{1,0:T(8,128)(2,1)}, u32[]{:S(2)}) copy-start(bf16[256,1280]{1,0:T(8,128)(2,1)} %copy-done.8) | copy-start | bytes 1966084
  49.4 14.0 %collective-permute-start.7 = (bf16[256,1280]{1,0:T(8,128)(2,1)}, bf16[256,1280]{1,0:T(8,128)(2,1)S(1)}, u32[]{:S(2)}, u32[]{:S(2)}) collective-permute-start(bf16[256,1280]{1,0:T(8,128)(2,1)} %collective-permute-done.5.refs_5_), channel_id=1, source_target_pairs={{0,32},{32,64},{64,96},{96,128},{128,160},{160,192},{192,224},{224... | collective-permute-start | bytes 1966088 | tf_op jit(solution)/shard_map/ppermute | solution.py:160
  56.4 14.0 %collective-permute-start.6 = (bf16[256,1280]{1,0:T(8,128)(2,1)}, bf16[256,1280]{1,0:T(8,128)(2,1)S(1)}, u32[]{:S(2)}, u32[]{:S(2)}) collective-permute-start(bf16[256,1280]{1,0:T(8,128)(2,1)} %collective-permute-done.4.refs_4_), channel_id=1, source_target_pairs={{0,32},{32,64},{64,96},{96,128},{128,160},{160,192},{192,224},{224... | collective-permute-start | bytes 1966088 | tf_op jit(solution)/shard_map/ppermute | solution.py:160
  63.5 19.0 %copy-start.4 = (bf16[256,1280]{1,0:T(8,128)(2,1)}, bf16[256,1280]{1,0:T(8,128)(2,1)S(1)}, u32[]{:S(2)}) copy-start(bf16[256,1280]{1,0:T(8,128)(2,1)S(1)} %collective-permute-done.7.refs_7_) | copy-start | bytes 1966084
  63.5 14.7 %collective-permute-start.9 = (bf16[256,1280]{1,0:T(8,128)(2,1)S(1)}, bf16[256,1280]{1,0:T(8,128)(2,1)S(1)}, u32[]{:S(2)}, u32[]{:S(2)}) collective-permute-start(bf16[256,1280]{1,0:T(8,128)(2,1)S(1)} %collective-permute-done.7.refs_7_), channel_id=1, source_target_pairs={{0,32},{32,64},{64,96},{96,128},{128,160},{160,192},{192,224},{224... | collective-permute-start | bytes 1966088 | tf_op jit(solution)/shard_map/ppermute | solution.py:160
  70.5 19.0 %copy-start.13 = (bf16[256,1280]{1,0:T(8,128)(2,1)}, bf16[256,1280]{1,0:T(8,128)(2,1)S(1)}, u32[]{:S(2)}) copy-start(bf16[256,1280]{1,0:T(8,128)(2,1)S(1)} %collective-permute-done.6.refs_6_) | copy-start | bytes 1966084
  70.5 13.9 %collective-permute-start.8 = (bf16[256,1280]{1,0:T(8,128)(2,1)S(1)}, bf16[256,1280]{1,0:T(8,128)(2,1)S(1)}, u32[]{:S(2)}, u32[]{:S(2)}) collective-permute-start(bf16[256,1280]{1,0:T(8,128)(2,1)S(1)} %collective-permute-done.6.refs_6_), channel_id=1, source_target_pairs={{0,32},{32,64},{64,96},{96,128},{128,160},{160,192},{192,224},{224... | collective-permute-start | bytes 1966088 | tf_op jit(solution)/shard_map/ppermute | solution.py:160
  78.2 11.6 %copy-start.5 = (bf16[256,1280]{1,0:T(8,128)(2,1)}, bf16[256,1280]{1,0:T(8,128)(2,1)S(1)}, u32[]{:S(2)}) copy-start(bf16[256,1280]{1,0:T(8,128)(2,1)S(1)} %collective-permute-done.9.refs_9_) | copy-start | bytes 1966084
  78.2 13.2 %collective-permute-start.11 = (bf16[256,1280]{1,0:T(8,128)(2,1)S(1)}, bf16[256,1280]{1,0:T(8,128)(2,1)S(1)}, u32[]{:S(2)}, u32[]{:S(2)}) collective-permute-start(bf16[256,1280]{1,0:T(8,128)(2,1)S(1)} %collective-permute-done.9.refs_9_), channel_id=1, source_target_pairs={{0,32},{32,64},{64,96},{96,128},{128,160},{160,192},{192,224},{224... | collective-permute-start | bytes 1966088 | tf_op jit(solution)/shard_map/ppermute | solution.py:160
  84.4 12.0 %copy-start.14 = (bf16[256,1280]{1,0:T(8,128)(2,1)}, bf16[256,1280]{1,0:T(8,128)(2,1)S(1)}, u32[]{:S(2)}) copy-start(bf16[256,1280]{1,0:T(8,128)(2,1)S(1)} %collective-permute-done.8.refs_8_) | copy-start | bytes 1966084
  84.4 14.0 %collective-permute-start.10 = (bf16[256,1280]{1,0:T(8,128)(2,1)S(1)}, bf16[256,1280]{1,0:T(8,128)(2,1)S(1)}, u32[]{:S(2)}, u32[]{:S(2)}) collective-permute-start(bf16[256,1280]{1,0:T(8,128)(2,1)S(1)} %collective-permute-done.8.refs_8_), channel_id=1, source_target_pairs={{0,32},{32,64},{64,96},{96,128},{128,160},{160,192},{192,224},{224... | collective-permute-start | bytes 1966088 | tf_op jit(solution)/shard_map/ppermute | solution.py:160
  91.4 12.0 %copy-start.6 = (bf16[256,1280]{1,0:T(8,128)(2,1)}, bf16[256,1280]{1,0:T(8,128)(2,1)S(1)}, u32[]{:S(2)}) copy-start(bf16[256,1280]{1,0:T(8,128)(2,1)S(1)} %collective-permute-done.11.refs_11_) | copy-start | bytes 1966084
  91.4 14.0 %collective-permute-start.13 = (bf16[256,1280]{1,0:T(8,128)(2,1)S(1)}, bf16[256,1280]{1,0:T(8,128)(2,1)S(1)}, u32[]{:S(2)}, u32[]{:S(2)}) collective-permute-start(bf16[256,1280]{1,0:T(8,128)(2,1)S(1)} %collective-permute-done.11.refs_11_), channel_id=1, source_target_pairs={{0,32},{32,64},{64,96},{96,128},{128,160},{160,192},{192,224},{224... | collective-permute-start | bytes 1966088 | tf_op jit(solution)/shard_map/ppermute | solution.py:160
  98.5 5.7 %copy-start.15 = (bf16[256,1280]{1,0:T(8,128)(2,1)}, bf16[256,1280]{1,0:T(8,128)(2,1)S(1)}, u32[]{:S(2)}) copy-start(bf16[256,1280]{1,0:T(8,128)(2,1)S(1)} %collective-permute-done.10.refs_10_) | copy-start | bytes 1966084
  98.5 14.0 %collective-permute-start.12 = (bf16[256,1280]{1,0:T(8,128)(2,1)S(1)}, bf16[256,1280]{1,0:T(8,128)(2,1)S(1)}, u32[]{:S(2)}, u32[]{:S(2)}) collective-permute-start(bf16[256,1280]{1,0:T(8,128)(2,1)S(1)} %collective-permute-done.10.refs_10_), channel_id=1, source_target_pairs={{0,32},{32,64},{64,96},{96,128},{128,160},{160,192},{192,224},{224... | collective-permute-start | bytes 1966088 | tf_op jit(solution)/shard_map/ppermute | solution.py:160
  105.5 7.4 %copy-start.7 = (bf16[256,1280]{1,0:T(8,128)(2,1)}, bf16[256,1280]{1,0:T(8,128)(2,1)S(1)}, u32[]{:S(2)}) copy-start(bf16[256,1280]{1,0:T(8,128)(2,1)S(1)} %collective-permute-done.13.refs_13_) | copy-start | bytes 1966084
  112.5 0.9 copy-start.12
  113.4 31.6 %copy-start.2 = (f32[192,1280]{1,0:T(8,128)}, f32[192,1280]{1,0:T(8,128)S(1)}, u32[]{:S(2)}) copy-start(f32[192,1280]{1,0:T(8,128)S(1)} %get-tuple-element.16.logits_ref) | copy-start | bytes 2949124
  113.4 14.2 %copy-start.17 = (s32[96]{0:T(128)S(1)}, s32[96]{0:T(128)}, u32[]{:S(2)}) copy-start(s32[96]{0:T(128)} %param.10) | copy-start | bytes 1156
  113.4 14.3 %copy-start.18 = (s32[96]{0:T(128)S(1)}, s32[96]{0:T(128)}, u32[]{:S(2)}) copy-start(s32[96]{0:T(128)} %param.9) | copy-start | bytes 1156
  113.4 14.7 %copy-start.16 = (s32[192]{0:T(256)S(1)}, s32[192]{0:T(256)}, u32[]{:S(2)}) copy-start(s32[192]{0:T(256)} %param.11) | copy-start | bytes 2308
  114.9 30.1 %all-to-all-start = ((f32[64,8,192]{2,1,0:T(8,128)}), f32[64,8,192]{2,1,0:T(8,128)S(1)}, u32[]{:S(2)}, u32[]{:S(2)}) async-start(f32[64,8,192]{2,1,0:T(8,128)} %broadcast_in_dim.34), calls=%async_computation | async-start | bytes 1048576 | tf_op jit(solution)/shard_map/all_to_all | solution.py:178
  154.8 4.2 %collective-permute-start.14 = (bf16[32,96,128]{2,1,0:T(8,128)(2,1)S(1)}, bf16[32,96,128]{2,1,0:T(8,128)(2,1)S(1)}, u32[]{:S(2)}, u32[]{:S(2)}) collective-permute-start(bf16[32,96,128]{2,1,0:T(8,128)(2,1)S(1)} %get-tuple-element.7), channel_id=1, source_target_pairs={{0,256},{256,0},{1,257},{257,1},{2,258},{258,2},{3,259},{259,3},{4... | collective-permute-start | bytes 2359304 | tf_op jit(solution)/shard_map/ppermute | solution.py:19
  160.1 26.3 %all-to-all-start.1 = ((bf16[32,96,128]{2,1,0:T(8,128)(2,1)}), bf16[32,96,128]{2,1,0:T(8,128)(2,1)S(1)}, u32[]{:S(2)}, u32[]{:S(2)}) async-start(bf16[32,96,128]{2,1,0:T(8,128)(2,1)} %add_convert_fusion), calls=%async_computation.1 | async-start | bytes 1572864 | tf_op jit(solution)/shard_map/all_to_all | solution.py:185

commit v7 on v5

--- a/solution.py
+++ b/solution.py
@@ -156,13 +156,21 @@
         lax.dynamic_slice_in_dim(hidden, row_place * full, full, axis=1), head, preferred_element_type=jnp.float32
     )
     chunks = []
+
+    def add(logits, distance, part):
+        owner = (row_place - distance * step + blocks) % blocks
+        piece = lax.dynamic_slice_in_dim(hidden, owner * full + part * depth, depth, axis=1)
+        return logits + jnp.dot(piece, held[part], preferred_element_type=jnp.float32)
+
     for distance in range(1, blocks):
-        held = [lax.ppermute(part, ("side", "row"), ring) for part in held]
-        owner = (row_place - distance * step + blocks) % blocks
         for part in range(HALVES):
-            piece = lax.dynamic_slice_in_dim(hidden, owner * full + part * depth, depth, axis=1)
-            logits = logits + jnp.dot(piece, held[part], preferred_element_type=jnp.float32)
+            arrived = lax.ppermute(held[part], ("side", "row"), ring)
+            if distance > 1:
+                logits = add(logits, distance - 1, part)
+            held[part], logits = lax.optimization_barrier((arrived, logits))
         chunks += held
+    for part in range(HALVES):
+        logits = add(logits, blocks - 1, part)
 
     teacher = teacher_logits.astype(jnp.float32)
     teacher_peak = jnp.max(teacher, axis=1)

time: 186 us -> 190 us (1.022)
  matrix products: 9.12 us -> 18.8 us
  waiting for transfers between devices: 61.5 us -> 56.3 us
  starting transfers between devices: 95.2 us -> 92.6 us
    dot_general x14, matrix products: 8.7 us -> 17.4 us  [add(): jnp.dot(piece, held[part], preferred_element_type=jnp.float32)]
    ppermute x14, waiting for transfers between devices: 26.9 us -> 21.7 us  [body(): arrived = lax.ppermute(held[part], ('side', 'row'), ring)]
    ppermute x14, starting transfers between devices: 73 us -> 71 us  [body(): arrived = lax.ppermute(held[part], ('side', 'row'), ring)]
  transfers between devices with their start and end apart: 18 -> 18, of which waited for: 17 -> 12; matrix products, arithmetic and copies ran while one was open for 5% -> 10% of each run, Pallas kernels for 0% -> 0%
where the time goes in v7:
time: 190 us; the launch traced here: 188 us
  starting transfers between devices  92.6 us (49%)
  waiting for transfers between devices  56.3 us (30%)
  matrix products  18.8 us (10%)
  Pallas kernels  10 us (5%)
  other arithmetic  4.82 us (3%)
  local copies, waits for them, and re-layouts  3.83 us (2%)
    ppermute x14, starting transfers between devices, body(): arrived = lax.ppermute(held[part], ('side', 'row'), ring)  71 us
    ppermute x14, waiting for transfers between devices, body(): arrived = lax.ppermute(held[part], ('side', 'row'), ring)  21.7 us
    all_to_all x1, waiting for transfers between devices, body(): pieces = lax.all_to_all(packed, 'vocab', 0, 0)  20.8 us
    dot_general x14, matrix products, add(): jnp.dot(piece, held[part], preferred_element_type=jnp.float32)  17.4 us
    all_to_all x1, waiting for transfers between devices, body(): lax.all_to_all(jnp.broadcast_to(pair, (count,) + pair.shape), 'vocab', 0, 0)  11.2 us
    pallas_call x1, Pallas kernels, grad_products(): pl.pallas_call(functools.partial(grad_kernel, blocks), out_shape=[jax.Sha...  10 us
    all_to_all x1, starting transfers between devices, body(): lax.all_to_all(jnp.broadcast_to(pair, (count,) + pair.shape), 'vocab', 0, 0)  9.67 us
    ppermute x2, starting transfers between devices, swap_side(): return lax.ppermute(value, 'side', [(0, 1), (1, 0)])  8.1 us
  transfers between devices with their start and end apart: 18, of which 12 were waited for; matrix products, arithmetic and copies ran while one was open for 10% of the time, Pallas kernels for 0%

profile of v7, /device:TPU:1, one launch (start us, length us, event | category | flops | bytes accessed | tf_op | source)
XLA Modules:
  0.0 187.8 jit_solution(7521044893613726316)
XLA Ops:
  0.7 2.6 %fusion.50 = (bf16[256,1280]{1,0:T(8,128)(2,1)}, bf16[256,1280]{1,0:T(8,128)(2,1)}) fusion(bf16[512,1280]{1,0:T(8,128)(2,1)} %own_ref.1), kind=kLoop, calls=%fused_computation.68 | loop fusion | bytes 2621440 | tf_op jit(solution)/shard_map/slice | solution.py:154
  3.2 11.5 %collective-permute-start.1 = (bf16[256,1280]{1,0:T(8,128)(2,1)}, bf16[256,1280]{1,0:T(8,128)(2,1)}, u32[]{:S(2)}, u32[]{:S(2)}) collective-permute-start(bf16[256,1280]{1,0:T(8,128)(2,1)} %get-tuple-element.70), channel_id=1, source_target_pairs={{0,32},{32,64},{64,96},{96,128},{128,160},{160,192},{192,224},{224... | collective-permute-start | bytes 1966088 | tf_op jit(solution)/shard_map/ppermute | solution.py:167
  14.7 2.2 %collective-permute-start = (bf16[256,1280]{1,0:T(8,128)(2,1)}, bf16[256,1280]{1,0:T(8,128)(2,1)}, u32[]{:S(2)}, u32[]{:S(2)}) collective-permute-start(bf16[256,1280]{1,0:T(8,128)(2,1)} %get-tuple-element.71), channel_id=1, source_target_pairs={{0,32},{32,64},{64,96},{96,128},{128,160},{160,192},{192,224},{224... | collective-permute-start | bytes 1966088 | tf_op jit(solution)/shard_map/ppermute | solution.py:167
  17.0 1.4 fusion
  18.4 4.2 %collective-permute-done.1.refs_0_ = bf16[256,1280]{1,0:T(8,128)(2,1)} collective-permute-done((bf16[256,1280]{1,0:T(8,128)(2,1)}, bf16[256,1280]{1,0:T(8,128)(2,1)}, u32[]{:S(2)}, u32[]{:S(2)}) %collective-permute-start.1) | collective-permute-done | bytes 655392 | tf_op jit(solution)/shard_map/ppermute | solution.py:167
  22.6 5.0 %collective-permute-start.3 = (bf16[256,1280]{1,0:T(8,128)(2,1)}, bf16[256,1280]{1,0:T(8,128)(2,1)S(1)}, u32[]{:S(2)}, u32[]{:S(2)}) collective-permute-start(bf16[256,1280]{1,0:T(8,128)(2,1)} %collective-permute-done.1.refs_0_), channel_id=1, source_target_pairs={{0,32},{32,64},{64,96},{96,128},{128,160},{160,192},{192,224},{224... | collective-permute-start | bytes 1966088 | tf_op jit(solution)/shard_map/ppermute | solution.py:167
  27.6 2.0 %collective-permute-done.refs_1_ = bf16[256,1280]{1,0:T(8,128)(2,1)} collective-permute-done((bf16[256,1280]{1,0:T(8,128)(2,1)}, bf16[256,1280]{1,0:T(8,128)(2,1)}, u32[]{:S(2)}, u32[]{:S(2)}) %collective-permute-start) | collective-permute-done | bytes 655392 | tf_op jit(solution)/shard_map/ppermute | solution.py:167
  29.6 5.0 %collective-permute-start.2 = (bf16[256,1280]{1,0:T(8,128)(2,1)}, bf16[256,1280]{1,0:T(8,128)(2,1)}, u32[]{:S(2)}, u32[]{:S(2)}) collective-permute-start(bf16[256,1280]{1,0:T(8,128)(2,1)} %collective-permute-done.refs_1_), channel_id=1, source_target_pairs={{0,32},{32,64},{64,96},{96,128},{128,160},{160,192},{192,224},{224... | collective-permute-start | bytes 1966088 | tf_op jit(solution)/shard_map/ppermute | solution.py:167
  34.6 1.4 fusion.30
  36.0 0.1 add.202
  36.2 1.4 fusion.28
  37.6 3.9 %collective-permute-start.5 = (bf16[256,1280]{1,0:T(8,128)(2,1)S(1)}, bf16[256,1280]{1,0:T(8,128)(2,1)}, u32[]{:S(2)}, u32[]{:S(2)}) collective-permute-start(bf16[256,1280]{1,0:T(8,128)(2,1)S(1)} %collective-permute-done.3.refs_2_), channel_id=1, source_target_pairs={{0,32},{32,64},{64,96},{96,128},{128,160},{160,192},{192,224},{224... | collective-permute-start | bytes 1966088 | tf_op jit(solution)/shard_map/ppermute | solution.py:167
  41.5 0.1 add.205
  41.6 2.0 %collective-permute-done.2.refs_3_ = bf16[256,1280]{1,0:T(8,128)(2,1)} collective-permute-done((bf16[256,1280]{1,0:T(8,128)(2,1)}, bf16[256,1280]{1,0:T(8,128)(2,1)}, u32[]{:S(2)}, u32[]{:S(2)}) %collective-permute-start.2) | collective-permute-done | bytes 655392 | tf_op jit(solution)/shard_map/ppermute | solution.py:167
  43.6 5.0 %collective-permute-start.4 = (bf16[256,1280]{1,0:T(8,128)(2,1)}, bf16[256,1280]{1,0:T(8,128)(2,1)}, u32[]{:S(2)}, u32[]{:S(2)}) collective-permute-start(bf16[256,1280]{1,0:T(8,128)(2,1)} %collective-permute-done.2.refs_3_), channel_id=1, source_target_pairs={{0,32},{32,64},{64,96},{96,128},{128,160},{160,192},{192,224},{224... | collective-permute-start | bytes 1966088 | tf_op jit(solution)/shard_map/ppermute | solution.py:167
  48.7 0.3 fusion.26
  49.0 0.1 add.209
  49.1 1.4 fusion.24
  50.5 5.1 %collective-permute-start.7 = (bf16[256,1280]{1,0:T(8,128)(2,1)}, bf16[256,1280]{1,0:T(8,128)(2,1)S(1)}, u32[]{:S(2)}, u32[]{:S(2)}) collective-permute-start(bf16[256,1280]{1,0:T(8,128)(2,1)} %collective-permute-done.5.refs_4_), channel_id=1, source_target_pairs={{0,32},{32,64},{64,96},{96,128},{128,160},{160,192},{192,224},{224... | collective-permute-start | bytes 1966088 | tf_op jit(solution)/shard_map/ppermute | solution.py:167
  55.7 0.1 add.212
  55.8 1.9 %collective-permute-done.4.refs_5_ = bf16[256,1280]{1,0:T(8,128)(2,1)} collective-permute-done((bf16[256,1280]{1,0:T(8,128)(2,1)}, bf16[256,1280]{1,0:T(8,128)(2,1)}, u32[]{:S(2)}, u32[]{:S(2)}) %collective-permute-start.4) | collective-permute-done | bytes 655392 | tf_op jit(solution)/shard_map/ppermute | solution.py:167
  57.7 5.0 %collective-permute-start.6 = (bf16[256,1280]{1,0:T(8,128)(2,1)}, bf16[256,1280]{1,0:T(8,128)(2,1)}, u32[]{:S(2)}, u32[]{:S(2)}) collective-permute-start(bf16[256,1280]{1,0:T(8,128)(2,1)} %collective-permute-done.4.refs_5_), channel_id=1, source_target_pairs={{0,32},{32,64},{64,96},{96,128},{128,160},{160,192},{192,224},{224... | collective-permute-start | bytes 1966088 | tf_op jit(solution)/shard_map/ppermute | solution.py:167
  62.7 1.4 fusion.22
  64.1 0.1 add.216
  64.2 1.4 fusion.20
  65.6 4.0 %collective-permute-start.9 = (bf16[256,1280]{1,0:T(8,128)(2,1)S(1)}, bf16[256,1280]{1,0:T(8,128)(2,1)}, u32[]{:S(2)}, u32[]{:S(2)}) collective-permute-start(bf16[256,1280]{1,0:T(8,128)(2,1)S(1)} %collective-permute-done.7.refs_6_), channel_id=1, source_target_pairs={{0,32},{32,64},{64,96},{96,128},{128,160},{160,192},{192,224},{224... | collective-permute-start | bytes 1966088 | tf_op jit(solution)/shard_map/ppermute | solution.py:167
  69.6 0.1 add.219
  69.7 2.0 %collective-permute-done.6.refs_7_ = bf16[256,1280]{1,0:T(8,128)(2,1)} collective-permute-done((bf16[256,1280]{1,0:T(8,128)(2,1)}, bf16[256,1280]{1,0:T(8,128)(2,1)}, u32[]{:S(2)}, u32[]{:S(2)}) %collective-permute-start.6) | collective-permute-done | bytes 655392 | tf_op jit(solution)/shard_map/ppermute | solution.py:167
  71.7 5.0 %collective-permute-start.8 = (bf16[256,1280]{1,0:T(8,128)(2,1)}, bf16[256,1280]{1,0:T(8,128)(2,1)}, u32[]{:S(2)}, u32[]{:S(2)}) collective-permute-start(bf16[256,1280]{1,0:T(8,128)(2,1)} %collective-permute-done.6.refs_7_), channel_id=1, source_target_pairs={{0,32},{32,64},{64,96},{96,128},{128,160},{160,192},{192,224},{224... | collective-permute-start | bytes 1966088 | tf_op jit(solution)/shard_map/ppermute | solution.py:167
  76.8 0.3 fusion.18
  77.1 0.1 add.223
  77.2 1.4 fusion.16
  78.6 5.1 %collective-permute-start.11 = (bf16[256,1280]{1,0:T(8,128)(2,1)}, bf16[256,1280]{1,0:T(8,128)(2,1)}, u32[]{:S(2)}, u32[]{:S(2)}) collective-permute-start(bf16[256,1280]{1,0:T(8,128)(2,1)} %collective-permute-done.9.refs_8_), channel_id=1, source_target_pairs={{0,32},{32,64},{64,96},{96,128},{128,160},{160,192},{192,224},{224... | collective-permute-start | bytes 1966088 | tf_op jit(solution)/shard_map/ppermute | solution.py:167
  83.8 0.1 add.226
  83.9 1.9 %collective-permute-done.8.refs_9_ = bf16[256,1280]{1,0:T(8,128)(2,1)} collective-permute-done((bf16[256,1280]{1,0:T(8,128)(2,1)}, bf16[256,1280]{1,0:T(8,128)(2,1)}, u32[]{:S(2)}, u32[]{:S(2)}) %collective-permute-start.8) | collective-permute-done | bytes 655392 | tf_op jit(solution)/shard_map/ppermute | solution.py:167
  85.8 5.0 %collective-permute-start.10 = (bf16[256,1280]{1,0:T(8,128)(2,1)}, bf16[256,1280]{1,0:T(8,128)(2,1)}, u32[]{:S(2)}, u32[]{:S(2)}) collective-permute-start(bf16[256,1280]{1,0:T(8,128)(2,1)} %collective-permute-done.8.refs_9_), channel_id=1, source_target_pairs={{0,32},{32,64},{64,96},{96,128},{128,160},{160,192},{192,224},{224... | collective-permute-start | bytes 1966088 | tf_op jit(solution)/shard_map/ppermute | solution.py:167
  90.8 1.4 fusion.14
  92.2 0.1 add.230
  92.3 1.4 fusion.12
  93.7 4.1 %collective-permute-start.13 = (bf16[256,1280]{1,0:T(8,128)(2,1)}, bf16[256,1280]{1,0:T(8,128)(2,1)}, u32[]{:S(2)}, u32[]{:S(2)}) collective-permute-start(bf16[256,1280]{1,0:T(8,128)(2,1)} %collective-permute-done.11.refs_10_), channel_id=1, source_target_pairs={{0,32},{32,64},{64,96},{96,128},{128,160},{160,192},{192,224},{224... | collective-permute-start | bytes 1966088 | tf_op jit(solution)/shard_map/ppermute | solution.py:167
  97.9 1.9 %collective-permute-done.10.refs_11_ = bf16[256,1280]{1,0:T(8,128)(2,1)} collective-permute-done((bf16[256,1280]{1,0:T(8,128)(2,1)}, bf16[256,1280]{1,0:T(8,128)(2,1)}, u32[]{:S(2)}, u32[]{:S(2)}) %collective-permute-start.10) | collective-permute-done | bytes 655392 | tf_op jit(solution)/shard_map/ppermute | solution.py:167
  99.8 5.0 %collective-permute-start.12 = (bf16[256,1280]{1,0:T(8,128)(2,1)}, bf16[256,1280]{1,0:T(8,128)(2,1)}, u32[]{:S(2)}, u32[]{:S(2)}) collective-permute-start(bf16[256,1280]{1,0:T(8,128)(2,1)} %collective-permute-done.10.refs_11_), channel_id=1, source_target_pairs={{0,32},{32,64},{64,96},{96,128},{128,160},{160,192},{192,224},{224... | collective-permute-start | bytes 1966088 | tf_op jit(solution)/shard_map/ppermute | solution.py:167
  104.9 0.1 reduce_max.45
  105.1 1.4 fusion.10
  106.6 1.4 fusion.8
  108.1 5.8 %collective-permute-done.12.refs_13_ = bf16[256,1280]{1,0:T(8,128)(2,1)} collective-permute-done((bf16[256,1280]{1,0:T(8,128)(2,1)}, bf16[256,1280]{1,0:T(8,128)(2,1)}, u32[]{:S(2)}, u32[]{:S(2)}) %collective-permute-start.12) | collective-permute-done | bytes 655392 | tf_op jit(solution)/shard_map/ppermute | solution.py:167
  113.8 1.4 fusion.6
  115.3 1.5 fusion.53
  116.8 0.6 multiply_reduce_fusion
  117.4 3.9 %collective-permute-start.14 = (f32[8,192]{1,0:T(8,128)S(1)}, f32[8,192]{1,0:T(8,128)S(1)}, u32[]{:S(2)}, u32[]{:S(2)}) collective-permute-start(f32[8,192]{1,0:T(8,128)S(1)} %stack.53), channel_id=1, source_target_pairs={{0,256},{256,0},{1,257},{257,1},{2,258},{258,2},{3,259},{259,3},{4... | collective-permute-start | bytes 18440 | tf_op jit(solution)/shard_map/ppermute | solution.py:19
  121.4 0.7 collective-permute-done.14
  122.2 0.7 broadcast_in_dim.48
  122.9 9.7 %all-to-all-start = ((f32[32,8,192]{2,1,0:T(8,128)}), f32[32,8,192]{2,1,0:T(8,128)S(1)}, u32[]{:S(2)}, u32[]{:S(2)}) async-start(f32[32,8,192]{2,1,0:T(8,128)} %broadcast_in_dim.48), calls=%async_computation | async-start | bytes 524288 | tf_op jit(solution)/shard_map/all_to_all | solution.py:188
  132.6 0.2 select_reduce_fusion
  133.1 11.2 %all-to-all-done.stats_ref = f32[32,8,192]{2,1,0:T(8,128)S(1)} async-done(((f32[32,8,192]{2,1,0:T(8,128)}), f32[32,8,192]{2,1,0:T(8,128)S(1)}, u32[]{:S(2)}, u32[]{:S(2)}) %all-to-all-start) | async-done | bytes 196640 | tf_op jit(solution)/shard_map/all_to_all | solution.py:188
  144.2 10.0 %shard_map.77 = (f32[32,96,128]{2,1,0:T(8,128)S(1)}, bf16[32,96,128]{2,1,0:T(8,128)(2,1)S(1)}, f32[1,192]{1,0:T(1,128)S(1)}) custom-call(s32[2]{0:T(128)S(1)} %pad_add_fusion.place_ref, f32[32,8,192]{2,1,0:T(8,128)S(1)} %all-to-all-done.stats_ref, f32[1,192]{1,0:T(1,128)S(1)} %bitcast.31, f32[192,1280]{1,0:T(8,128)} %copy-done.2, ...), custom_call_target="tpu_custom_call" | custom-call | flops 2013265920 | bytes 10485760 | tf_op jit(solution)/shard_map/pallas_call | solution.py:111
  154.3 4.2 %collective-permute-start.15 = (bf16[32,96,128]{2,1,0:T(8,128)(2,1)S(1)}, bf16[32,96,128]{2,1,0:T(8,128)(2,1)S(1)}, u32[]{:S(2)}, u32[]{:S(2)}) collective-permute-start(bf16[32,96,128]{2,1,0:T(8,128)(2,1)S(1)} %get-tuple-element.63), channel_id=1, source_target_pairs={{0,256},{256,0},{1,257},{257,1},{2,258},{258,2},{3,259},{259,3},{4... | collective-permute-start | bytes 2359304 | tf_op jit(solution)/shard_map/ppermute | solution.py:19
  158.5 1.9 %collective-permute-done.15 = bf16[32,96,128]{2,1,0:T(8,128)(2,1)S(1)} collective-permute-done((bf16[32,96,128]{2,1,0:T(8,128)(2,1)S(1)}, bf16[32,96,128]{2,1,0:T(8,128)(2,1)S(1)}, u32[]{:S(2)}, u32[]{:S(2)}) %collective-permute-start.15) | collective-permute-done | bytes 786464 | tf_op jit(solution)/shard_map/ppermute | solution.py:19
  160.3 1.1 add_convert_fusion
  161.4 3.9 %all-to-all-start.1 = ((bf16[32,96,128]{2,1,0:T(8,128)(2,1)}), bf16[32,96,128]{2,1,0:T(8,128)(2,1)S(1)}, u32[]{:S(2)}, u32[]{:S(2)}) async-start(bf16[32,96,128]{2,1,0:T(8,128)(2,1)} %add_convert_fusion), calls=%async_computation.1 | async-start | bytes 1572864 | tf_op jit(solution)/shard_map/all_to_all | solution.py:195
  165.4 0.6 reduce_sum.91
  166.1 20.8 %all-to-all-done.1 = bf16[32,96,128]{2,1,0:T(8,128)(2,1)S(1)} async-done(((bf16[32,96,128]{2,1,0:T(8,128)(2,1)}), bf16[32,96,128]{2,1,0:T(8,128)(2,1)S(1)}, u32[]{:S(2)}, u32[]{:S(2)}) %all-to-all-start.1) | async-done | bytes 786464 | tf_op jit(solution)/shard_map/all_to_all | solution.py:195
  186.9 0.1 reduce_sum.92
  187.1 0.6 maximum_bitcast_fusion
  (46 shorter events, 1.1 us)
Async XLA Ops:
  0.6 16.3 %copy-start = (bf16[192,4096]{1,0:T(8,128)(2,1)S(1)}, bf16[192,4096]{1,0:T(8,128)(2,1)}, u32[]{:S(2)}) copy-start(bf16[192,4096]{1,0:T(8,128)(2,1)} %param.6) | copy-start | bytes 4718596
  0.6 16.3 %copy-start.1 = (bf16[512,1280]{1,0:T(8,128)(2,1)S(1)}, bf16[512,1280]{1,0:T(8,128)(2,1)}, u32[]{:S(2)}) copy-start(bf16[512,1280]{1,0:T(8,128)(2,1)} %own_ref.1) | copy-start | bytes 3932164
  3.2 19.3 %collective-permute-start.1 = (bf16[256,1280]{1,0:T(8,128)(2,1)}, bf16[256,1280]{1,0:T(8,128)(2,1)}, u32[]{:S(2)}, u32[]{:S(2)}) collective-permute-start(bf16[256,1280]{1,0:T(8,128)(2,1)} %get-tuple-element.70), channel_id=1, source_target_pairs={{0,32},{32,64},{64,96},{96,128},{128,160},{160,192},{192,224},{224... | collective-permute-start | bytes 1966088 | tf_op jit(solution)/shard_map/ppermute | solution.py:167
  14.7 14.8 %collective-permute-start = (bf16[256,1280]{1,0:T(8,128)(2,1)}, bf16[256,1280]{1,0:T(8,128)(2,1)}, u32[]{:S(2)}, u32[]{:S(2)}) collective-permute-start(bf16[256,1280]{1,0:T(8,128)(2,1)} %get-tuple-element.71), channel_id=1, source_target_pairs={{0,32},{32,64},{64,96},{96,128},{128,160},{160,192},{192,224},{224... | collective-permute-start | bytes 1966088 | tf_op jit(solution)/shard_map/ppermute | solution.py:167
  18.4 17.7 %copy-start.4 = (f32[192,1280]{1,0:T(8,128)S(1)}, f32[192,1280]{1,0:T(8,128)}, u32[]{:S(2)}) copy-start(f32[192,1280]{1,0:T(8,128)} %fusion) | copy-start | bytes 2949124
  22.6 15.0 %collective-permute-start.3 = (bf16[256,1280]{1,0:T(8,128)(2,1)}, bf16[256,1280]{1,0:T(8,128)(2,1)S(1)}, u32[]{:S(2)}, u32[]{:S(2)}) collective-permute-start(bf16[256,1280]{1,0:T(8,128)(2,1)} %collective-permute-done.1.refs_0_), channel_id=1, source_target_pairs={{0,32},{32,64},{64,96},{96,128},{128,160},{160,192},{192,224},{224... | collective-permute-start | bytes 1966088 | tf_op jit(solution)/shard_map/ppermute | solution.py:167
  29.6 14.0 %collective-permute-start.2 = (bf16[256,1280]{1,0:T(8,128)(2,1)}, bf16[256,1280]{1,0:T(8,128)(2,1)}, u32[]{:S(2)}, u32[]{:S(2)}) collective-permute-start(bf16[256,1280]{1,0:T(8,128)(2,1)} %collective-permute-done.refs_1_), channel_id=1, source_target_pairs={{0,32},{32,64},{64,96},{96,128},{128,160},{160,192},{192,224},{224... | collective-permute-start | bytes 1966088 | tf_op jit(solution)/shard_map/ppermute | solution.py:167
  37.6 11.4 %copy-start.5 = (bf16[256,1280]{1,0:T(8,128)(2,1)}, bf16[256,1280]{1,0:T(8,128)(2,1)S(1)}, u32[]{:S(2)}) copy-start(bf16[256,1280]{1,0:T(8,128)(2,1)S(1)} %collective-permute-done.3.refs_2_) | copy-start | bytes 1966084
  37.6 13.0 %collective-permute-start.5 = (bf16[256,1280]{1,0:T(8,128)(2,1)S(1)}, bf16[256,1280]{1,0:T(8,128)(2,1)}, u32[]{:S(2)}, u32[]{:S(2)}) collective-permute-start(bf16[256,1280]{1,0:T(8,128)(2,1)S(1)} %collective-permute-done.3.refs_2_), channel_id=1, source_target_pairs={{0,32},{32,64},{64,96},{96,128},{128,160},{160,192},{192,224},{224... | collective-permute-start | bytes 1966088 | tf_op jit(solution)/shard_map/ppermute | solution.py:167
  43.6 14.0 %collective-permute-start.4 = (bf16[256,1280]{1,0:T(8,128)(2,1)}, bf16[256,1280]{1,0:T(8,128)(2,1)}, u32[]{:S(2)}, u32[]{:S(2)}) collective-permute-start(bf16[256,1280]{1,0:T(8,128)(2,1)} %collective-permute-done.2.refs_3_), channel_id=1, source_target_pairs={{0,32},{32,64},{64,96},{96,128},{128,160},{160,192},{192,224},{224... | collective-permute-start | bytes 1966088 | tf_op jit(solution)/shard_map/ppermute | solution.py:167
  50.5 15.1 %collective-permute-start.7 = (bf16[256,1280]{1,0:T(8,128)(2,1)}, bf16[256,1280]{1,0:T(8,128)(2,1)S(1)}, u32[]{:S(2)}, u32[]{:S(2)}) collective-permute-start(bf16[256,1280]{1,0:T(8,128)(2,1)} %collective-permute-done.5.refs_4_), channel_id=1, source_target_pairs={{0,32},{32,64},{64,96},{96,128},{128,160},{160,192},{192,224},{224... | collective-permute-start | bytes 1966088 | tf_op jit(solution)/shard_map/ppermute | solution.py:167
  57.7 14.0 %collective-permute-start.6 = (bf16[256,1280]{1,0:T(8,128)(2,1)}, bf16[256,1280]{1,0:T(8,128)(2,1)}, u32[]{:S(2)}, u32[]{:S(2)}) collective-permute-start(bf16[256,1280]{1,0:T(8,128)(2,1)} %collective-permute-done.4.refs_5_), channel_id=1, source_target_pairs={{0,32},{32,64},{64,96},{96,128},{128,160},{160,192},{192,224},{224... | collective-permute-start | bytes 1966088 | tf_op jit(solution)/shard_map/ppermute | solution.py:167
  65.6 11.4 %copy-start.6 = (bf16[256,1280]{1,0:T(8,128)(2,1)}, bf16[256,1280]{1,0:T(8,128)(2,1)S(1)}, u32[]{:S(2)}) copy-start(bf16[256,1280]{1,0:T(8,128)(2,1)S(1)} %collective-permute-done.7.refs_6_) | copy-start | bytes 1966084
  65.6 13.0 %collective-permute-start.9 = (bf16[256,1280]{1,0:T(8,128)(2,1)S(1)}, bf16[256,1280]{1,0:T(8,128)(2,1)}, u32[]{:S(2)}, u32[]{:S(2)}) collective-permute-start(bf16[256,1280]{1,0:T(8,128)(2,1)S(1)} %collective-permute-done.7.refs_6_), channel_id=1, source_target_pairs={{0,32},{32,64},{64,96},{96,128},{128,160},{160,192},{192,224},{224... | collective-permute-start | bytes 1966088 | tf_op jit(solution)/shard_map/ppermute | solution.py:167
  71.7 14.0 %collective-permute-start.8 = (bf16[256,1280]{1,0:T(8,128)(2,1)}, bf16[256,1280]{1,0:T(8,128)(2,1)}, u32[]{:S(2)}, u32[]{:S(2)}) collective-permute-start(bf16[256,1280]{1,0:T(8,128)(2,1)} %collective-permute-done.6.refs_7_), channel_id=1, source_target_pairs={{0,32},{32,64},{64,96},{96,128},{128,160},{160,192},{192,224},{224... | collective-permute-start | bytes 1966088 | tf_op jit(solution)/shard_map/ppermute | solution.py:167
  78.6 15.1 %collective-permute-start.11 = (bf16[256,1280]{1,0:T(8,128)(2,1)}, bf16[256,1280]{1,0:T(8,128)(2,1)}, u32[]{:S(2)}, u32[]{:S(2)}) collective-permute-start(bf16[256,1280]{1,0:T(8,128)(2,1)} %collective-permute-done.9.refs_8_), channel_id=1, source_target_pairs={{0,32},{32,64},{64,96},{96,128},{128,160},{160,192},{192,224},{224... | collective-permute-start | bytes 1966088 | tf_op jit(solution)/shard_map/ppermute | solution.py:167
  85.8 14.0 %collective-permute-start.10 = (bf16[256,1280]{1,0:T(8,128)(2,1)}, bf16[256,1280]{1,0:T(8,128)(2,1)}, u32[]{:S(2)}, u32[]{:S(2)}) collective-permute-start(bf16[256,1280]{1,0:T(8,128)(2,1)} %collective-permute-done.8.refs_9_), channel_id=1, source_target_pairs={{0,32},{32,64},{64,96},{96,128},{128,160},{160,192},{192,224},{224... | collective-permute-start | bytes 1966088 | tf_op jit(solution)/shard_map/ppermute | solution.py:167
  93.7 11.2 %copy-start.3 = (bf16[192,1280]{1,0:T(8,128)(2,1)S(1)}, bf16[192,1280]{1,0:T(8,128)(2,1)}, u32[]{:S(2)}) copy-start(bf16[192,1280]{1,0:T(8,128)(2,1)} %teacher_ref.1) | copy-start | bytes 1474564
  93.7 14.2 %collective-permute-start.13 = (bf16[256,1280]{1,0:T(8,128)(2,1)}, bf16[256,1280]{1,0:T(8,128)(2,1)}, u32[]{:S(2)}, u32[]{:S(2)}) collective-permute-start(bf16[256,1280]{1,0:T(8,128)(2,1)} %collective-permute-done.11.refs_10_), channel_id=1, source_target_pairs={{0,32},{32,64},{64,96},{96,128},{128,160},{160,192},{192,224},{224... | collective-permute-start | bytes 1966088 | tf_op jit(solution)/shard_map/ppermute | solution.py:167
  99.8 14.0 %collective-permute-start.12 = (bf16[256,1280]{1,0:T(8,128)(2,1)}, bf16[256,1280]{1,0:T(8,128)(2,1)}, u32[]{:S(2)}, u32[]{:S(2)}) collective-permute-start(bf16[256,1280]{1,0:T(8,128)(2,1)} %collective-permute-done.10.refs_11_), channel_id=1, source_target_pairs={{0,32},{32,64},{64,96},{96,128},{128,160},{160,192},{192,224},{224... | collective-permute-start | bytes 1966088 | tf_op jit(solution)/shard_map/ppermute | solution.py:167
  115.2 6.1 %copy-start.8 = (s32[96]{0:T(128)S(1)}, s32[96]{0:T(128)}, u32[]{:S(2)}) copy-start(s32[96]{0:T(128)} %param.10) | copy-start | bytes 1156
  116.7 27.5 %copy-start.2 = (f32[192,1280]{1,0:T(8,128)}, f32[192,1280]{1,0:T(8,128)S(1)}, u32[]{:S(2)}) copy-start(f32[192,1280]{1,0:T(8,128)S(1)} %get-tuple-element.82.logits_ref) | copy-start | bytes 2949124
  116.8 15.9 %copy-start.9 = (s32[96]{0:T(128)S(1)}, s32[96]{0:T(128)}, u32[]{:S(2)}) copy-start(s32[96]{0:T(128)} %param.9) | copy-start | bytes 1156
  116.8 16.3 %copy-start.7 = (s32[192]{0:T(256)S(1)}, s32[192]{0:T(256)}, u32[]{:S(2)}) copy-start(s32[192]{0:T(256)} %param.11) | copy-start | bytes 2308
  117.4 4.7 %collective-permute-start.14 = (f32[8,192]{1,0:T(8,128)S(1)}, f32[8,192]{1,0:T(8,128)S(1)}, u32[]{:S(2)}, u32[]{:S(2)}) collective-permute-start(f32[8,192]{1,0:T(8,128)S(1)} %stack.53), channel_id=1, source_target_pairs={{0,256},{256,0},{1,257},{257,1},{2,258},{258,2},{3,259},{259,3},{4... | collective-permute-start | bytes 18440 | tf_op jit(solution)/shard_map/ppermute | solution.py:19
  122.9 21.3 %all-to-all-start = ((f32[32,8,192]{2,1,0:T(8,128)}), f32[32,8,192]{2,1,0:T(8,128)S(1)}, u32[]{:S(2)}, u32[]{:S(2)}) async-start(f32[32,8,192]{2,1,0:T(8,128)} %broadcast_in_dim.48), calls=%async_computation | async-start | bytes 524288 | tf_op jit(solution)/shard_map/all_to_all | solution.py:188
  154.3 6.1 %collective-permute-start.15 = (bf16[32,96,128]{2,1,0:T(8,128)(2,1)S(1)}, bf16[32,96,128]{2,1,0:T(8,128)(2,1)S(1)}, u32[]{:S(2)}, u32[]{:S(2)}) collective-permute-start(bf16[32,96,128]{2,1,0:T(8,128)(2,1)S(1)} %get-tuple-element.63), channel_id=1, source_target_pairs={{0,256},{256,0},{1,257},{257,1},{2,258},{258,2},{3,259},{259,3},{4... | collective-permute-start | bytes 2359304 | tf_op jit(solution)/shard_map/ppermute | solution.py:19
  161.4 25.5 %all-to-all-start.1 = ((bf16[32,96,128]{2,1,0:T(8,128)(2,1)}), bf16[32,96,128]{2,1,0:T(8,128)(2,1)S(1)}, u32[]{:S(2)}, u32[]{:S(2)}) async-start(bf16[32,96,128]{2,1,0:T(8,128)(2,1)} %add_convert_fusion), calls=%async_computation.1 | async-start | bytes 1572864 | tf_op jit(solution)/shard_map/all_to_all | solution.py:195

commit v8 on v5

--- a/solution.py
+++ b/solution.py
@@ -9,6 +9,7 @@
 
 WIN = 16
 HALVES = 2
+WAITED = 4
 LANES = 128
 
 
@@ -36,7 +37,7 @@
 
 def grad_kernel(blocks, place_ref, stats_ref, weight_ref, logits_ref, teacher_ref, own_ref, *refs):
     chunk_refs = refs[:-8]
-    keep_ref, send_ref, diverge_ref, grad_ref, logits_buf, teacher_buf, head_buf, sems = refs[-8:]
+    sums_ref, send_ref, diverge_ref, grad_ref, logits_buf, teacher_buf, head_buf, sems = refs[-8:]
     side = place_ref[0]
     row = place_ref[1]
     step = 1 - 2 * side
@@ -72,33 +73,21 @@
     def one(product, distance, part):
         owner = lax.rem(row - distance * step + blocks, blocks)
         first = lax.rem(owner, blocks // 2) * (HALVES * depth // 64) + part * (depth // 64)
-        mine = lax.div(owner, blocks // 2) == side
+        place = lax.rem(lax.div(owner, blocks // 2) + side, 2)
         wide = jnp.concatenate([product[:, LANES:], jnp.zeros((depth, LANES - rest), jnp.float32)], axis=1)
-        pieces = []
         for i in range(depth // 64):
             left = wide[64 * i : 64 * i + 32]
             right = wide[64 * i + 32 : 64 * i + 64]
-            pieces.append((product[64 * i : 64 * i + 64, :LANES], jnp.where(low, left, pltpu.roll(right, rest, 1))))
+            sums_ref[place, first + i, :64] = product[64 * i : 64 * i + 64, :LANES]
+            sums_ref[place, first + i, 64:] = jnp.where(low, left, pltpu.roll(right, rest, 1))
 
-        @pl.when(mine)
-        def _():
-            for i, (upper, lower) in enumerate(pieces):
-                keep_ref[first + i, :64] = upper
-                keep_ref[first + i, 64:] = lower
-
-        @pl.when(jnp.logical_not(mine))
-        def _():
-            for i, (upper, lower) in enumerate(pieces):
-                send_ref[first + i, :64] = upper.astype(send_ref.dtype)
-                send_ref[first + i, 64:] = lower.astype(send_ref.dtype)
-
-    for base in range(0, len(sources), HALVES):
-        for index in range(base, base + HALVES):
+    for base in range(0, len(sources), WAITED):
+        for index in range(base, base + WAITED):
             copies[2 + index].wait()
-        block = head_buf[base : base + HALVES].reshape(HALVES * depth, head_buf.shape[2])
-        product = jnp.dot(block, grad_ref[...], preferred_element_type=jnp.float32)
-        for part in range(HALVES):
-            one(product[part * depth : (part + 1) * depth], base // HALVES, part)
+        for index in range(base, base + WAITED):
+            product = jnp.dot(head_buf[index], grad_ref[...], preferred_element_type=jnp.float32)
+            one(product, index // HALVES, index % HALVES)
+    send_ref[...] = sums_ref[1].astype(send_ref.dtype)
 
 
 def grad_products(place, stats, weight, logits, teacher, own, chunks, blocks, count):
@@ -111,7 +100,7 @@
     return pl.pallas_call(
         functools.partial(grad_kernel, blocks),
         out_shape=[
-            jax.ShapeDtypeStruct(shape, jnp.float32),
+            jax.ShapeDtypeStruct((2,) + shape, jnp.float32),
             jax.ShapeDtypeStruct(shape, jnp.bfloat16),
             jax.ShapeDtypeStruct((1, toks), jnp.float32),
         ],
@@ -180,10 +169,10 @@
     stats = lax.all_to_all(jnp.broadcast_to(pair, (count,) + pair.shape), "vocab", 0, 0)
 
     place = jnp.stack([side_place, row_place]).astype(jnp.int32)
-    keep, send, diverge = grad_products(
+    sums, send, diverge = grad_products(
         place, stats, weight[None], logits, teacher_logits, head, chunks, blocks, count
     )
-    packed = (keep + swap_side(send).astype(jnp.float32)).astype(jnp.bfloat16)
+    packed = (sums[0] + swap_side(send).astype(jnp.float32)).astype(jnp.bfloat16)
     pieces = lax.all_to_all(packed, "vocab", 0, 0)
     summed = jnp.sum(pieces.astype(jnp.float32), axis=0).astype(jnp.bfloat16)
     rest = tok_rows - LANES

time: 186 us -> 183 us (0.984)
  Pallas kernels: 10 us -> 6.75 us
    pallas_call x1, Pallas kernels: 10 us -> 6.75 us  [grad_products(): pl.pallas_call(functools.partial(grad_kernel, blocks), out_shape=[jax.Sha...]
  transfers between devices with their start and end apart: 18 -> 18, of which waited for: 17 -> 17; matrix products, arithmetic and copies ran while one was open for 5% -> 6% of each run, Pallas kernels for 0% -> 0%
where the time goes in v8:
time: 183 us; the launch traced here: 182 us
  starting transfers between devices  95.2 us (52%)
  waiting for transfers between devices  61.5 us (34%)
  matrix products  9.12 us (5%)
  Pallas kernels  6.75 us (4%)
  local copies, waits for them, and re-layouts  4.09 us (2%)
  other arithmetic  3.5 us (2%)
    ppermute x14, starting transfers between devices, body(): held = [lax.ppermute(part, ('side', 'row'), ring) for part in held]  73 us
    ppermute x14, waiting for transfers between devices, body(): held = [lax.ppermute(part, ('side', 'row'), ring) for part in held]  26.9 us
    all_to_all x1, waiting for transfers between devices, body(): pieces = lax.all_to_all(packed, 'vocab', 0, 0)  20.8 us
    all_to_all x1, waiting for transfers between devices, body(): lax.all_to_all(jnp.broadcast_to(pair, (count,) + pair.shape), 'vocab', 0, 0)  11.2 us
    all_to_all x1, starting transfers between devices, body(): lax.all_to_all(jnp.broadcast_to(pair, (count,) + pair.shape), 'vocab', 0, 0)  9.67 us
    dot_general x14, matrix products, body(): jnp.dot(piece, held[part], preferred_element_type=jnp.float32)  8.7 us
    ppermute x2, starting transfers between devices, swap_side(): return lax.ppermute(value, 'side', [(0, 1), (1, 0)])  8.56 us
    pallas_call x1, Pallas kernels, grad_products(): pl.pallas_call(functools.partial(grad_kernel, blocks), out_shape=[jax.Sha...  6.75 us
  transfers between devices with their start and end apart: 18, of which 17 were waited for; matrix products, arithmetic and copies ran while one was open for 6% of the time, Pallas kernels for 0%

profile of v8, /device:TPU:1, one launch (start us, length us, event | category | flops | bytes accessed | tf_op | source)
XLA Modules:
  0.0 181.5 jit_solution(5705711443934554169)
XLA Ops:
  0.7 1.5 fusion.47
  2.2 11.5 %collective-permute-start.1 = (bf16[256,1280]{1,0:T(8,128)(2,1)S(1)}, bf16[256,1280]{1,0:T(8,128)(2,1)S(1)}, u32[]{:S(2)}, u32[]{:S(2)}) collective-permute-start(bf16[256,1280]{1,0:T(8,128)(2,1)S(1)} %get-tuple-element.15), channel_id=1, source_target_pairs={{0,32},{32,64},{64,96},{96,128},{128,160},{160,192},{192,224},{224... | collective-permute-start | bytes 1966088 | tf_op jit(solution)/shard_map/ppermute | solution.py:149
  13.7 2.2 %collective-permute-start = (bf16[256,1280]{1,0:T(8,128)(2,1)S(1)}, bf16[256,1280]{1,0:T(8,128)(2,1)S(1)}, u32[]{:S(2)}, u32[]{:S(2)}) collective-permute-start(bf16[256,1280]{1,0:T(8,128)(2,1)S(1)} %get-tuple-element.14), channel_id=1, source_target_pairs={{0,32},{32,64},{64,96},{96,128},{128,160},{160,192},{192,224},{224... | collective-permute-start | bytes 1966088 | tf_op jit(solution)/shard_map/ppermute | solution.py:149
  15.9 5.3 %collective-permute-done.1.refs_1_ = bf16[256,1280]{1,0:T(8,128)(2,1)S(1)} collective-permute-done((bf16[256,1280]{1,0:T(8,128)(2,1)S(1)}, bf16[256,1280]{1,0:T(8,128)(2,1)S(1)}, u32[]{:S(2)}, u32[]{:S(2)}) %collective-permute-start.1) | collective-permute-done | bytes 655392 | tf_op jit(solution)/shard_map/ppermute | solution.py:149
  21.2 0.8 copy-done.8
  22.1 5.0 %collective-permute-start.3 = (bf16[256,1280]{1,0:T(8,128)(2,1)S(1)}, bf16[256,1280]{1,0:T(8,128)(2,1)}, u32[]{:S(2)}, u32[]{:S(2)}) collective-permute-start(bf16[256,1280]{1,0:T(8,128)(2,1)S(1)} %collective-permute-done.1.refs_1_), channel_id=1, source_target_pairs={{0,32},{32,64},{64,96},{96,128},{128,160},{160,192},{192,224},{224... | collective-permute-start | bytes 1966088 | tf_op jit(solution)/shard_map/ppermute | solution.py:149
  27.1 1.2 collective-permute-done.refs_0_
  28.2 5.0 %collective-permute-start.2 = (bf16[256,1280]{1,0:T(8,128)(2,1)S(1)}, bf16[256,1280]{1,0:T(8,128)(2,1)}, u32[]{:S(2)}, u32[]{:S(2)}) collective-permute-start(bf16[256,1280]{1,0:T(8,128)(2,1)S(1)} %collective-permute-done.refs_0_), channel_id=1, source_target_pairs={{0,32},{32,64},{64,96},{96,128},{128,160},{160,192},{192,224},{224... | collective-permute-start | bytes 1966088 | tf_op jit(solution)/shard_map/ppermute | solution.py:149
  33.3 2.0 %collective-permute-done.3.refs_3_ = bf16[256,1280]{1,0:T(8,128)(2,1)} collective-permute-done((bf16[256,1280]{1,0:T(8,128)(2,1)S(1)}, bf16[256,1280]{1,0:T(8,128)(2,1)}, u32[]{:S(2)}, u32[]{:S(2)}) %collective-permute-start.3) | collective-permute-done | bytes 655392 | tf_op jit(solution)/shard_map/ppermute | solution.py:149
  35.3 5.1 %collective-permute-start.5 = (bf16[256,1280]{1,0:T(8,128)(2,1)}, bf16[256,1280]{1,0:T(8,128)(2,1)}, u32[]{:S(2)}, u32[]{:S(2)}) collective-permute-start(bf16[256,1280]{1,0:T(8,128)(2,1)} %collective-permute-done.3.refs_3_), channel_id=1, source_target_pairs={{0,32},{32,64},{64,96},{96,128},{128,160},{160,192},{192,224},{224... | collective-permute-start | bytes 1966088 | tf_op jit(solution)/shard_map/ppermute | solution.py:149
  40.4 1.9 %collective-permute-done.2.refs_2_ = bf16[256,1280]{1,0:T(8,128)(2,1)} collective-permute-done((bf16[256,1280]{1,0:T(8,128)(2,1)S(1)}, bf16[256,1280]{1,0:T(8,128)(2,1)}, u32[]{:S(2)}, u32[]{:S(2)}) %collective-permute-start.2) | collective-permute-done | bytes 655392 | tf_op jit(solution)/shard_map/ppermute | solution.py:149
  42.3 5.1 %collective-permute-start.4 = (bf16[256,1280]{1,0:T(8,128)(2,1)}, bf16[256,1280]{1,0:T(8,128)(2,1)}, u32[]{:S(2)}, u32[]{:S(2)}) collective-permute-start(bf16[256,1280]{1,0:T(8,128)(2,1)} %collective-permute-done.2.refs_2_), channel_id=1, source_target_pairs={{0,32},{32,64},{64,96},{96,128},{128,160},{160,192},{192,224},{224... | collective-permute-start | bytes 1966088 | tf_op jit(solution)/shard_map/ppermute | solution.py:149
  47.6 0.1 reduce_max.45
  47.9 0.4 fusion.7
  48.3 1.1 collective-permute-done.5.refs_5_
  49.4 5.0 %collective-permute-start.7 = (bf16[256,1280]{1,0:T(8,128)(2,1)}, bf16[256,1280]{1,0:T(8,128)(2,1)S(1)}, u32[]{:S(2)}, u32[]{:S(2)}) collective-permute-start(bf16[256,1280]{1,0:T(8,128)(2,1)} %collective-permute-done.5.refs_5_), channel_id=1, source_target_pairs={{0,32},{32,64},{64,96},{96,128},{128,160},{160,192},{192,224},{224... | collective-permute-start | bytes 1966088 | tf_op jit(solution)/shard_map/ppermute | solution.py:149
  54.4 0.3 convolution_add_fusion.7
  54.8 1.7 collective-permute-done.4.refs_4_
  56.4 5.0 %collective-permute-start.6 = (bf16[256,1280]{1,0:T(8,128)(2,1)}, bf16[256,1280]{1,0:T(8,128)(2,1)S(1)}, u32[]{:S(2)}, u32[]{:S(2)}) collective-permute-start(bf16[256,1280]{1,0:T(8,128)(2,1)} %collective-permute-done.4.refs_4_), channel_id=1, source_target_pairs={{0,32},{32,64},{64,96},{96,128},{128,160},{160,192},{192,224},{224... | collective-permute-start | bytes 1966088 | tf_op jit(solution)/shard_map/ppermute | solution.py:149
  61.5 0.3 convolution_add_fusion.6
  61.8 1.4 fusion.24
  63.2 0.3 collective-permute-done.7.refs_7_
  63.5 4.9 %collective-permute-start.9 = (bf16[256,1280]{1,0:T(8,128)(2,1)S(1)}, bf16[256,1280]{1,0:T(8,128)(2,1)S(1)}, u32[]{:S(2)}, u32[]{:S(2)}) collective-permute-start(bf16[256,1280]{1,0:T(8,128)(2,1)S(1)} %collective-permute-done.7.refs_7_), channel_id=1, source_target_pairs={{0,32},{32,64},{64,96},{96,128},{128,160},{160,192},{192,224},{224... | collective-permute-start | bytes 1966088 | tf_op jit(solution)/shard_map/ppermute | solution.py:149
  68.4 1.4 fusion
  69.8 0.7 collective-permute-done.6.refs_6_
  70.5 4.9 %collective-permute-start.8 = (bf16[256,1280]{1,0:T(8,128)(2,1)S(1)}, bf16[256,1280]{1,0:T(8,128)(2,1)S(1)}, u32[]{:S(2)}, u32[]{:S(2)}) collective-permute-start(bf16[256,1280]{1,0:T(8,128)(2,1)S(1)} %collective-permute-done.6.refs_6_), channel_id=1, source_target_pairs={{0,32},{32,64},{64,96},{96,128},{128,160},{160,192},{192,224},{224... | collective-permute-start | bytes 1966088 | tf_op jit(solution)/shard_map/ppermute | solution.py:149
  75.4 1.4 fusion.21
  76.8 1.4 fusion.1
  78.2 4.2 %collective-permute-start.11 = (bf16[256,1280]{1,0:T(8,128)(2,1)S(1)}, bf16[256,1280]{1,0:T(8,128)(2,1)S(1)}, u32[]{:S(2)}, u32[]{:S(2)}) collective-permute-start(bf16[256,1280]{1,0:T(8,128)(2,1)S(1)} %collective-permute-done.9.refs_9_), channel_id=1, source_target_pairs={{0,32},{32,64},{64,96},{96,128},{128,160},{160,192},{192,224},{224... | collective-permute-start | bytes 1966088 | tf_op jit(solution)/shard_map/ppermute | solution.py:149
  82.4 0.3 fusion.18
  82.7 1.7 collective-permute-done.8.refs_8_
  84.4 5.0 %collective-permute-start.10 = (bf16[256,1280]{1,0:T(8,128)(2,1)S(1)}, bf16[256,1280]{1,0:T(8,128)(2,1)S(1)}, u32[]{:S(2)}, u32[]{:S(2)}) collective-permute-start(bf16[256,1280]{1,0:T(8,128)(2,1)S(1)} %collective-permute-done.8.refs_8_), channel_id=1, source_target_pairs={{0,32},{32,64},{64,96},{96,128},{128,160},{160,192},{192,224},{224... | collective-permute-start | bytes 1966088 | tf_op jit(solution)/shard_map/ppermute | solution.py:149
  89.5 0.3 fusion.2
  89.8 0.3 fusion.15
  90.1 1.4 collective-permute-done.11.refs_11_
  91.4 5.0 %collective-permute-start.13 = (bf16[256,1280]{1,0:T(8,128)(2,1)S(1)}, bf16[256,1280]{1,0:T(8,128)(2,1)S(1)}, u32[]{:S(2)}, u32[]{:S(2)}) collective-permute-start(bf16[256,1280]{1,0:T(8,128)(2,1)S(1)} %collective-permute-done.11.refs_11_), channel_id=1, source_target_pairs={{0,32},{32,64},{64,96},{96,128},{128,160},{160,192},{192,224},{224... | collective-permute-start | bytes 1966088 | tf_op jit(solution)/shard_map/ppermute | solution.py:149
  96.5 0.3 fusion.3
  96.8 1.7 collective-permute-done.10.refs_10_
  98.5 5.0 %collective-permute-start.12 = (bf16[256,1280]{1,0:T(8,128)(2,1)S(1)}, bf16[256,1280]{1,0:T(8,128)(2,1)S(1)}, u32[]{:S(2)}, u32[]{:S(2)}) collective-permute-start(bf16[256,1280]{1,0:T(8,128)(2,1)S(1)} %collective-permute-done.10.refs_10_), channel_id=1, source_target_pairs={{0,32},{32,64},{64,96},{96,128},{128,160},{160,192},{192,224},{224... | collective-permute-start | bytes 1966088 | tf_op jit(solution)/shard_map/ppermute | solution.py:149
  103.5 0.3 fusion.12
  103.8 0.3 fusion.4
  104.1 1.4 collective-permute-done.13.refs_13_
  105.5 0.3 fusion.9
  105.8 6.7 %collective-permute-done.12.refs_12_ = bf16[256,1280]{1,0:T(8,128)(2,1)S(1)} collective-permute-done((bf16[256,1280]{1,0:T(8,128)(2,1)S(1)}, bf16[256,1280]{1,0:T(8,128)(2,1)S(1)}, u32[]{:S(2)}, u32[]{:S(2)}) %collective-permute-start.12) | collective-permute-done | bytes 655392 | tf_op jit(solution)/shard_map/ppermute | solution.py:149
  112.5 0.4 fusion.50
  112.9 0.5 copy-done.12
  113.4 0.6 multiply_reduce_fusion
  114.0 4.4 %collective-permute-start.14 = (f32[8,192]{1,0:T(8,128)S(1)}, f32[8,192]{1,0:T(8,128)S(1)}, u32[]{:S(2)}, u32[]{:S(2)}) collective-permute-start(f32[8,192]{1,0:T(8,128)S(1)} %stack.53), channel_id=1, source_target_pairs={{0,256},{256,0},{1,257},{257,1},{2,258},{258,2},{3,259},{259,3},{4... | collective-permute-start | bytes 18440 | tf_op jit(solution)/shard_map/ppermute | solution.py:20
  118.5 0.7 collective-permute-done.14
  119.3 0.7 broadcast_in_dim.48
  120.0 9.7 %all-to-all-start = ((f32[32,8,192]{2,1,0:T(8,128)}), f32[32,8,192]{2,1,0:T(8,128)S(1)}, u32[]{:S(2)}, u32[]{:S(2)}) async-start(f32[32,8,192]{2,1,0:T(8,128)} %broadcast_in_dim.48), calls=%async_computation | async-start | bytes 524288 | tf_op jit(solution)/shard_map/all_to_all | solution.py:169
  129.7 0.2 select_reduce_fusion
  129.9 0.1 reshape.38
  130.1 11.2 %all-to-all-done.stats_ref = f32[32,8,192]{2,1,0:T(8,128)S(1)} async-done(((f32[32,8,192]{2,1,0:T(8,128)}), f32[32,8,192]{2,1,0:T(8,128)S(1)}, u32[]{:S(2)}, u32[]{:S(2)}) %all-to-all-start) | async-done | bytes 196640 | tf_op jit(solution)/shard_map/all_to_all | solution.py:169
  141.3 6.7 %shard_map.77 = (f32[2,32,96,128]{3,2,1,0:T(8,128)S(1)}, bf16[32,96,128]{2,1,0:T(8,128)(2,1)S(1)}, f32[1,192]{1,0:T(1,128)S(1)}) custom-call(s32[2]{0:T(128)S(1)} %pad_add_fusion.place_ref, f32[32,8,192]{2,1,0:T(8,128)S(1)} %all-to-all-done.stats_ref, f32[1,192]{1,0:T(1,128)S(1)} %bitcast.35, f32[192,1280]{1,0:T(8,128)} %copy-done.2, ...), custom_call_target="tpu_custom_call" | custom-call | flops 2013265920 | bytes 10485760 | tf_op jit(solution)/shard_map/pallas_call | solution.py:100
  148.0 4.2 %collective-permute-start.15 = (bf16[32,96,128]{2,1,0:T(8,128)(2,1)S(1)}, bf16[32,96,128]{2,1,0:T(8,128)(2,1)S(1)}, u32[]{:S(2)}, u32[]{:S(2)}) collective-permute-start(bf16[32,96,128]{2,1,0:T(8,128)(2,1)S(1)} %get-tuple-element.7), channel_id=1, source_target_pairs={{0,256},{256,0},{1,257},{257,1},{2,258},{258,2},{3,259},{259,3},{4... | collective-permute-start | bytes 2359304 | tf_op jit(solution)/shard_map/ppermute | solution.py:20
  152.2 1.9 %collective-permute-done.15 = bf16[32,96,128]{2,1,0:T(8,128)(2,1)S(1)} collective-permute-done((bf16[32,96,128]{2,1,0:T(8,128)(2,1)S(1)}, bf16[32,96,128]{2,1,0:T(8,128)(2,1)S(1)}, u32[]{:S(2)}, u32[]{:S(2)}) %collective-permute-start.15) | collective-permute-done | bytes 786464 | tf_op jit(solution)/shard_map/ppermute | solution.py:20
  154.1 1.1 fusion.6
  155.2 3.9 %all-to-all-start.1 = ((bf16[32,96,128]{2,1,0:T(8,128)(2,1)}), bf16[32,96,128]{2,1,0:T(8,128)(2,1)S(1)}, u32[]{:S(2)}, u32[]{:S(2)}) async-start(bf16[32,96,128]{2,1,0:T(8,128)(2,1)} %fusion.6), calls=%async_computation.1 | async-start | bytes 1572864 | tf_op jit(solution)/shard_map/all_to_all | solution.py:176
  159.2 0.6 reduce_sum.91
  159.8 20.8 %all-to-all-done.1 = bf16[32,96,128]{2,1,0:T(8,128)(2,1)S(1)} async-done(((bf16[32,96,128]{2,1,0:T(8,128)(2,1)}), bf16[32,96,128]{2,1,0:T(8,128)(2,1)S(1)}, u32[]{:S(2)}, u32[]{:S(2)}) %all-to-all-start.1) | async-done | bytes 786464 | tf_op jit(solution)/shard_map/all_to_all | solution.py:176
  180.7 0.1 reduce_sum.92
  180.8 0.1 fusion.48
  180.9 0.6 maximum_bitcast_fusion
  (52 shorter events, 0.5 us)
Async XLA Ops:
  0.6 47.2 %copy-start = (bf16[192,4096]{1,0:T(8,128)(2,1)S(1)}, bf16[192,4096]{1,0:T(8,128)(2,1)}, u32[]{:S(2)}) copy-start(bf16[192,4096]{1,0:T(8,128)(2,1)} %param.6) | copy-start | bytes 4718596
  0.6 47.2 %copy-start.1 = (bf16[512,1280]{1,0:T(8,128)(2,1)S(1)}, bf16[512,1280]{1,0:T(8,128)(2,1)}, u32[]{:S(2)}) copy-start(bf16[512,1280]{1,0:T(8,128)(2,1)} %own_ref.1) | copy-start | bytes 3932164
  0.7 46.9 %copy-start.3 = (bf16[192,1280]{1,0:T(8,128)(2,1)S(1)}, bf16[192,1280]{1,0:T(8,128)(2,1)}, u32[]{:S(2)}) copy-start(bf16[192,1280]{1,0:T(8,128)(2,1)} %teacher_ref.1) | copy-start | bytes 1474564
  2.2 19.0 %collective-permute-start.1 = (bf16[256,1280]{1,0:T(8,128)(2,1)S(1)}, bf16[256,1280]{1,0:T(8,128)(2,1)S(1)}, u32[]{:S(2)}, u32[]{:S(2)}) collective-permute-start(bf16[256,1280]{1,0:T(8,128)(2,1)S(1)} %get-tuple-element.15), channel_id=1, source_target_pairs={{0,32},{32,64},{64,96},{96,128},{128,160},{160,192},{192,224},{224... | collective-permute-start | bytes 1966088 | tf_op jit(solution)/shard_map/ppermute | solution.py:149
  13.7 14.5 %collective-permute-start = (bf16[256,1280]{1,0:T(8,128)(2,1)S(1)}, bf16[256,1280]{1,0:T(8,128)(2,1)S(1)}, u32[]{:S(2)}, u32[]{:S(2)}) collective-permute-start(bf16[256,1280]{1,0:T(8,128)(2,1)S(1)} %get-tuple-element.14), channel_id=1, source_target_pairs={{0,32},{32,64},{64,96},{96,128},{128,160},{160,192},{192,224},{224... | collective-permute-start | bytes 1966088 | tf_op jit(solution)/shard_map/ppermute | solution.py:149
  21.2 0.8 copy-start.8
  22.1 13.2 %collective-permute-start.3 = (bf16[256,1280]{1,0:T(8,128)(2,1)S(1)}, bf16[256,1280]{1,0:T(8,128)(2,1)}, u32[]{:S(2)}, u32[]{:S(2)}) collective-permute-start(bf16[256,1280]{1,0:T(8,128)(2,1)S(1)} %collective-permute-done.1.refs_1_), channel_id=1, source_target_pairs={{0,32},{32,64},{64,96},{96,128},{128,160},{160,192},{192,224},{224... | collective-permute-start | bytes 1966088 | tf_op jit(solution)/shard_map/ppermute | solution.py:149
  28.2 7.0 %copy-start.10 = (bf16[256,1280]{1,0:T(8,128)(2,1)}, bf16[256,1280]{1,0:T(8,128)(2,1)S(1)}, u32[]{:S(2)}) copy-start(bf16[256,1280]{1,0:T(8,128)(2,1)S(1)} %collective-permute-done.refs_0_) | copy-start | bytes 1966084
  28.2 14.0 %collective-permute-start.2 = (bf16[256,1280]{1,0:T(8,128)(2,1)S(1)}, bf16[256,1280]{1,0:T(8,128)(2,1)}, u32[]{:S(2)}, u32[]{:S(2)}) collective-permute-start(bf16[256,1280]{1,0:T(8,128)(2,1)S(1)} %collective-permute-done.refs_0_), channel_id=1, source_target_pairs={{0,32},{32,64},{64,96},{96,128},{128,160},{160,192},{192,224},{224... | collective-permute-start | bytes 1966088 | tf_op jit(solution)/shard_map/ppermute | solution.py:149
  35.3 14.1 %collective-permute-start.5 = (bf16[256,1280]{1,0:T(8,128)(2,1)}, bf16[256,1280]{1,0:T(8,128)(2,1)}, u32[]{:S(2)}, u32[]{:S(2)}) collective-permute-start(bf16[256,1280]{1,0:T(8,128)(2,1)} %collective-permute-done.3.refs_3_), channel_id=1, source_target_pairs={{0,32},{32,64},{64,96},{96,128},{128,160},{160,192},{192,224},{224... | collective-permute-start | bytes 1966088 | tf_op jit(solution)/shard_map/ppermute | solution.py:149
  42.3 14.1 %collective-permute-start.4 = (bf16[256,1280]{1,0:T(8,128)(2,1)}, bf16[256,1280]{1,0:T(8,128)(2,1)}, u32[]{:S(2)}, u32[]{:S(2)}) collective-permute-start(bf16[256,1280]{1,0:T(8,128)(2,1)} %collective-permute-done.2.refs_2_), channel_id=1, source_target_pairs={{0,32},{32,64},{64,96},{96,128},{128,160},{160,192},{192,224},{224... | collective-permute-start | bytes 1966088 | tf_op jit(solution)/shard_map/ppermute | solution.py:149
  47.8 6.6 %copy-start.11 = (bf16[256,1280]{1,0:T(8,128)(2,1)S(1)}, bf16[256,1280]{1,0:T(8,128)(2,1)}, u32[]{:S(2)}) copy-start(bf16[256,1280]{1,0:T(8,128)(2,1)} %copy-done.10) | copy-start | bytes 1966084
  48.3 13.2 %copy-start.9 = (bf16[256,1280]{1,0:T(8,128)(2,1)S(1)}, bf16[256,1280]{1,0:T(8,128)(2,1)}, u32[]{:S(2)}) copy-start(bf16[256,1280]{1,0:T(8,128)(2,1)} %copy-done.8) | copy-start | bytes 1966084
  49.4 14.0 %collective-permute-start.7 = (bf16[256,1280]{1,0:T(8,128)(2,1)}, bf16[256,1280]{1,0:T(8,128)(2,1)S(1)}, u32[]{:S(2)}, u32[]{:S(2)}) collective-permute-start(bf16[256,1280]{1,0:T(8,128)(2,1)} %collective-permute-done.5.refs_5_), channel_id=1, source_target_pairs={{0,32},{32,64},{64,96},{96,128},{128,160},{160,192},{192,224},{224... | collective-permute-start | bytes 1966088 | tf_op jit(solution)/shard_map/ppermute | solution.py:149
  56.4 14.0 %collective-permute-start.6 = (bf16[256,1280]{1,0:T(8,128)(2,1)}, bf16[256,1280]{1,0:T(8,128)(2,1)S(1)}, u32[]{:S(2)}, u32[]{:S(2)}) collective-permute-start(bf16[256,1280]{1,0:T(8,128)(2,1)} %collective-permute-done.4.refs_4_), channel_id=1, source_target_pairs={{0,32},{32,64},{64,96},{96,128},{128,160},{160,192},{192,224},{224... | collective-permute-start | bytes 1966088 | tf_op jit(solution)/shard_map/ppermute | solution.py:149
  63.5 19.0 %copy-start.4 = (bf16[256,1280]{1,0:T(8,128)(2,1)}, bf16[256,1280]{1,0:T(8,128)(2,1)S(1)}, u32[]{:S(2)}) copy-start(bf16[256,1280]{1,0:T(8,128)(2,1)S(1)} %collective-permute-done.7.refs_7_) | copy-start | bytes 1966084
  63.5 14.7 %collective-permute-start.9 = (bf16[256,1280]{1,0:T(8,128)(2,1)S(1)}, bf16[256,1280]{1,0:T(8,128)(2,1)S(1)}, u32[]{:S(2)}, u32[]{:S(2)}) collective-permute-start(bf16[256,1280]{1,0:T(8,128)(2,1)S(1)} %collective-permute-done.7.refs_7_), channel_id=1, source_target_pairs={{0,32},{32,64},{64,96},{96,128},{128,160},{160,192},{192,224},{224... | collective-permute-start | bytes 1966088 | tf_op jit(solution)/shard_map/ppermute | solution.py:149
  70.5 19.0 %copy-start.13 = (bf16[256,1280]{1,0:T(8,128)(2,1)}, bf16[256,1280]{1,0:T(8,128)(2,1)S(1)}, u32[]{:S(2)}) copy-start(bf16[256,1280]{1,0:T(8,128)(2,1)S(1)} %collective-permute-done.6.refs_6_) | copy-start | bytes 1966084
  70.5 13.9 %collective-permute-start.8 = (bf16[256,1280]{1,0:T(8,128)(2,1)S(1)}, bf16[256,1280]{1,0:T(8,128)(2,1)S(1)}, u32[]{:S(2)}, u32[]{:S(2)}) collective-permute-start(bf16[256,1280]{1,0:T(8,128)(2,1)S(1)} %collective-permute-done.6.refs_6_), channel_id=1, source_target_pairs={{0,32},{32,64},{64,96},{96,128},{128,160},{160,192},{192,224},{224... | collective-permute-start | bytes 1966088 | tf_op jit(solution)/shard_map/ppermute | solution.py:149
  78.2 11.6 %copy-start.5 = (bf16[256,1280]{1,0:T(8,128)(2,1)}, bf16[256,1280]{1,0:T(8,128)(2,1)S(1)}, u32[]{:S(2)}) copy-start(bf16[256,1280]{1,0:T(8,128)(2,1)S(1)} %collective-permute-done.9.refs_9_) | copy-start | bytes 1966084
  78.2 13.2 %collective-permute-start.11 = (bf16[256,1280]{1,0:T(8,128)(2,1)S(1)}, bf16[256,1280]{1,0:T(8,128)(2,1)S(1)}, u32[]{:S(2)}, u32[]{:S(2)}) collective-permute-start(bf16[256,1280]{1,0:T(8,128)(2,1)S(1)} %collective-permute-done.9.refs_9_), channel_id=1, source_target_pairs={{0,32},{32,64},{64,96},{96,128},{128,160},{160,192},{192,224},{224... | collective-permute-start | bytes 1966088 | tf_op jit(solution)/shard_map/ppermute | solution.py:149
  84.4 12.0 %copy-start.14 = (bf16[256,1280]{1,0:T(8,128)(2,1)}, bf16[256,1280]{1,0:T(8,128)(2,1)S(1)}, u32[]{:S(2)}) copy-start(bf16[256,1280]{1,0:T(8,128)(2,1)S(1)} %collective-permute-done.8.refs_8_) | copy-start | bytes 1966084
  84.4 14.0 %collective-permute-start.10 = (bf16[256,1280]{1,0:T(8,128)(2,1)S(1)}, bf16[256,1280]{1,0:T(8,128)(2,1)S(1)}, u32[]{:S(2)}, u32[]{:S(2)}) collective-permute-start(bf16[256,1280]{1,0:T(8,128)(2,1)S(1)} %collective-permute-done.8.refs_8_), channel_id=1, source_target_pairs={{0,32},{32,64},{64,96},{96,128},{128,160},{160,192},{192,224},{224... | collective-permute-start | bytes 1966088 | tf_op jit(solution)/shard_map/ppermute | solution.py:149
  91.4 12.0 %copy-start.6 = (bf16[256,1280]{1,0:T(8,128)(2,1)}, bf16[256,1280]{1,0:T(8,128)(2,1)S(1)}, u32[]{:S(2)}) copy-start(bf16[256,1280]{1,0:T(8,128)(2,1)S(1)} %collective-permute-done.11.refs_11_) | copy-start | bytes 1966084
  91.4 14.0 %collective-permute-start.13 = (bf16[256,1280]{1,0:T(8,128)(2,1)S(1)}, bf16[256,1280]{1,0:T(8,128)(2,1)S(1)}, u32[]{:S(2)}, u32[]{:S(2)}) collective-permute-start(bf16[256,1280]{1,0:T(8,128)(2,1)S(1)} %collective-permute-done.11.refs_11_), channel_id=1, source_target_pairs={{0,32},{32,64},{64,96},{96,128},{128,160},{160,192},{192,224},{224... | collective-permute-start | bytes 1966088 | tf_op jit(solution)/shard_map/ppermute | solution.py:149
  98.5 5.7 %copy-start.15 = (bf16[256,1280]{1,0:T(8,128)(2,1)}, bf16[256,1280]{1,0:T(8,128)(2,1)S(1)}, u32[]{:S(2)}) copy-start(bf16[256,1280]{1,0:T(8,128)(2,1)S(1)} %collective-permute-done.10.refs_10_) | copy-start | bytes 1966084
  98.5 14.0 %collective-permute-start.12 = (bf16[256,1280]{1,0:T(8,128)(2,1)S(1)}, bf16[256,1280]{1,0:T(8,128)(2,1)S(1)}, u32[]{:S(2)}, u32[]{:S(2)}) collective-permute-start(bf16[256,1280]{1,0:T(8,128)(2,1)S(1)} %collective-permute-done.10.refs_10_), channel_id=1, source_target_pairs={{0,32},{32,64},{64,96},{96,128},{128,160},{160,192},{192,224},{224... | collective-permute-start | bytes 1966088 | tf_op jit(solution)/shard_map/ppermute | solution.py:149
  105.5 7.4 %copy-start.7 = (bf16[256,1280]{1,0:T(8,128)(2,1)}, bf16[256,1280]{1,0:T(8,128)(2,1)S(1)}, u32[]{:S(2)}) copy-start(bf16[256,1280]{1,0:T(8,128)(2,1)S(1)} %collective-permute-done.13.refs_13_) | copy-start | bytes 1966084
  105.8 12.6 %copy-start.17 = (s32[96]{0:T(128)S(1)}, s32[96]{0:T(128)}, u32[]{:S(2)}) copy-start(s32[96]{0:T(128)} %param.10) | copy-start | bytes 1156
  112.5 0.9 copy-start.12
  113.4 27.9 %copy-start.2 = (f32[192,1280]{1,0:T(8,128)}, f32[192,1280]{1,0:T(8,128)S(1)}, u32[]{:S(2)}) copy-start(f32[192,1280]{1,0:T(8,128)S(1)} %get-tuple-element.26.logits_ref) | copy-start | bytes 2949124
  113.4 16.3 %copy-start.18 = (s32[96]{0:T(128)S(1)}, s32[96]{0:T(128)}, u32[]{:S(2)}) copy-start(s32[96]{0:T(128)} %param.9) | copy-start | bytes 1156
  113.4 16.7 %copy-start.16 = (s32[192]{0:T(256)S(1)}, s32[192]{0:T(256)}, u32[]{:S(2)}) copy-start(s32[192]{0:T(256)} %param.11) | copy-start | bytes 2308
  114.0 5.2 %collective-permute-start.14 = (f32[8,192]{1,0:T(8,128)S(1)}, f32[8,192]{1,0:T(8,128)S(1)}, u32[]{:S(2)}, u32[]{:S(2)}) collective-permute-start(f32[8,192]{1,0:T(8,128)S(1)} %stack.53), channel_id=1, source_target_pairs={{0,256},{256,0},{1,257},{257,1},{2,258},{258,2},{3,259},{259,3},{4... | collective-permute-start | bytes 18440 | tf_op jit(solution)/shard_map/ppermute | solution.py:20
  120.0 21.3 %all-to-all-start = ((f32[32,8,192]{2,1,0:T(8,128)}), f32[32,8,192]{2,1,0:T(8,128)S(1)}, u32[]{:S(2)}, u32[]{:S(2)}) async-start(f32[32,8,192]{2,1,0:T(8,128)} %broadcast_in_dim.48), calls=%async_computation | async-start | bytes 524288 | tf_op jit(solution)/shard_map/all_to_all | solution.py:169
  148.0 6.1 %collective-permute-start.15 = (bf16[32,96,128]{2,1,0:T(8,128)(2,1)S(1)}, bf16[32,96,128]{2,1,0:T(8,128)(2,1)S(1)}, u32[]{:S(2)}, u32[]{:S(2)}) collective-permute-start(bf16[32,96,128]{2,1,0:T(8,128)(2,1)S(1)} %get-tuple-element.7), channel_id=1, source_target_pairs={{0,256},{256,0},{1,257},{257,1},{2,258},{258,2},{3,259},{259,3},{4... | collective-permute-start | bytes 2359304 | tf_op jit(solution)/shard_map/ppermute | solution.py:20
  155.2 25.5 %all-to-all-start.1 = ((bf16[32,96,128]{2,1,0:T(8,128)(2,1)}), bf16[32,96,128]{2,1,0:T(8,128)(2,1)S(1)}, u32[]{:S(2)}, u32[]{:S(2)}) async-start(bf16[32,96,128]{2,1,0:T(8,128)(2,1)} %fusion.6), calls=%async_computation.1 | async-start | bytes 1572864 | tf_op jit(solution)/shard_map/all_to_all | solution.py:176

commit v9 on v8

v9 whole, which is shorter than its diff:
```python
import functools

import jax
import jax.numpy as jnp
from jax import lax
from jax.experimental import pallas as pl
from jax.experimental.pallas import tpu as pltpu
from jax.sharding import PartitionSpec as P

WIN = 16
HALVES = 2
WAITED = 4
FEW = 144
LANES = 128


loss_scale = 256.0


def swap_side(value):
    return lax.ppermute(value, "side", [(0, 1), (1, 0)])


def join(peak, total, teacher_peak, teacher_total, term):
    top = jnp.max(peak, axis=0, keepdims=True)
    teacher_top = jnp.max(teacher_peak, axis=0, keepdims=True)
    shift = peak - top
    teacher_shift = teacher_peak - teacher_top
    scale = jnp.exp(shift)
    return (
        top,
        jnp.sum(total * scale, axis=0, keepdims=True),
        teacher_top,
        jnp.sum(teacher_total * jnp.exp(teacher_shift), axis=0, keepdims=True),
        jnp.sum(scale * (term + total * (shift - teacher_shift)), axis=0, keepdims=True),
    )


def grad_kernel(blocks, toks, place_ref, stats_ref, weight_ref, logits_ref, teacher_ref, own_ref, *refs):
    chunk_refs = refs[:-6]
    sums_ref, send_ref, diverge_ref, grad_ref, head_buf, sems = refs[-6:]
    side = place_ref[0]
    row = place_ref[1]
    step = 1 - 2 * side
    rest = toks - LANES
    groups = LANES // rest
    rows = 64 // groups
    depth = own_ref.shape[0] // HALVES
    sources = [own_ref.at[part * depth : (part + 1) * depth] for part in range(HALVES)] + list(chunk_refs)
    copies = [
        pltpu.make_async_copy(source, head_buf.at[index], sems.at[index]) for index, source in enumerate(sources)
    ]
    for copy in copies:
        copy.start()

    peak, total, teacher_peak, teacher_total, term = join(*[stats_ref[:, i, :toks] for i in range(5)])
    mean = term / total
    diverge_ref[...] = mean - jnp.log(total) + jnp.log(teacher_total)
    scale = loss_scale * weight_ref[:, :toks] / total
    offset = teacher_peak - mean
    table = jnp.concatenate([peak, scale, offset, jnp.zeros((LANES - 3, toks), jnp.float32)], axis=0)
    table = jnp.concatenate([table, jnp.zeros((LANES, 2 * LANES - toks), jnp.float32)], axis=1)
    columns = jnp.transpose(table)[:toks]
    shifted = logits_ref[:toks] - columns[:, 0:1]
    slope = shifted - teacher_ref[:toks].astype(jnp.float32) + columns[:, 2:3]
    grad = columns[:, 1:2] * jnp.exp(shifted) * slope
    grad_ref[...] = jnp.transpose(grad).astype(jnp.bfloat16)
    group = lax.broadcasted_iota(jnp.int32, (rows, LANES), 1) // rest

    def one(product, distance, part):
        owner = lax.rem(row - distance * step + blocks, blocks)
        first = lax.rem(owner, blocks // 2) * (HALVES * depth // 64) + part * (depth // 64)
        place = lax.rem(lax.div(owner, blocks // 2) + side, 2)
        wide = jnp.concatenate([product[:, LANES:], jnp.zeros((depth, LANES - rest), jnp.float32)], axis=1)
        for i in range(depth // 64):
            lower = wide[64 * i : 64 * i + rows]
            for near in range(1, groups):
                start = 64 * i + near * rows
                lower = jnp.where(group == near, pltpu.roll(wide[start : start + rows], near * rest, 1), lower)
            sums_ref[place, first + i, :64] = product[64 * i : 64 * i + 64, :LANES]
            sums_ref[place, first + i, 64:] = lower

    for base in range(0, len(sources), WAITED):
        for index in range(base, base + WAITED):
            copies[index].wait()
        for index in range(base, base + WAITED):
            product = jnp.dot(head_buf[index], grad_ref[...], preferred_element_type=jnp.float32)
            one(product, index // HALVES, index % HALVES)
    send_ref[...] = sums_ref[1].astype(send_ref.dtype)


def grad_products(place, stats, weight, logits, teacher, own, chunks, blocks, count, toks):
    cols = logits.shape[1]
    width = own.shape[0] * blocks
    vmem = pl.BlockSpec(memory_space=pltpu.VMEM)
    hbm = pl.BlockSpec(memory_space=pltpu.HBM)
    shape = (count, toks // 2, LANES)
    large = [pltpu.with_memory_space_constraint(value, pltpu.HBM) for value in (own, *chunks)]
    return pl.pallas_call(
        functools.partial(grad_kernel, blocks, toks),
        out_shape=[
            jax.ShapeDtypeStruct((2,) + shape, jnp.float32),
            jax.ShapeDtypeStruct(shape, jnp.bfloat16),
            jax.ShapeDtypeStruct((1, toks), jnp.float32),
        ],
        in_specs=[pl.BlockSpec(memory_space=pltpu.SMEM)] + [vmem] * 4 + [hbm] * (1 + len(chunks)),
        out_specs=[vmem] * 3,
        scratch_shapes=[
            pltpu.VMEM((cols, toks), jnp.bfloat16),
            pltpu.VMEM((len(chunks) + HALVES, own.shape[0] // HALVES, cols), jnp.bfloat16),
            pltpu.SemaphoreType.DMA((len(chunks) + HALVES,)),
        ],
        compiler_params=pltpu.CompilerParams(vmem_limit_bytes=24 * 1024 * 1024),
        cost_estimate=pl.CostEstimate(
            flops=2 * toks * cols * width, bytes_accessed=2 * cols * width, transcendentals=toks * cols
        ),
    )(place, stats, weight, logits, teacher, *large)


def body(hidden, head, teacher_logits, lengths, slot_rollout, token_mask):
    tok_rows = hidden.shape[0]
    count = lax.axis_size("vocab")
    blocks = lax.axis_size("row")
    slot_count = tok_rows // WIN
    row_place = lax.axis_index("row")
    side_place = lax.axis_index("side")
    chosen = slot_rollout[:, None] == jnp.arange(lengths.shape[0], dtype=jnp.int32)[None, :]
    all_lengths = jnp.sum(jnp.where(chosen, lengths[None, :], 0), axis=1)
    slot_length = lax.dynamic_slice_in_dim(all_lengths, row_place * slot_count, slot_count)
    length_tok = jnp.repeat(slot_length, WIN)
    token = jnp.arange(tok_rows, dtype=jnp.int32)
    inside = token % WIN < length_tok
    weight = jnp.where((token_mask > 0) & inside, 1.0 / length_tok.astype(jnp.float32), 0.0)

    earlier = token[None, :] < token[:, None]
    rank = jnp.sum((earlier & inside[None, :]).astype(jnp.int32), axis=1)
    spot = jnp.where(inside, rank, jnp.sum(inside.astype(jnp.int32)) + token - rank)
    pick = spot[None, :] == token[:, None]
    pick_low = pick.astype(jnp.bfloat16)
    hidden = jnp.dot(pick_low, hidden, preferred_element_type=jnp.float32).astype(jnp.bfloat16)
    teacher_logits = jnp.dot(pick_low, teacher_logits, preferred_element_type=jnp.float32).astype(jnp.bfloat16)
    weight = jnp.sum(jnp.where(pick, weight[None, :], 0.0), axis=1)
    fits = jnp.max(jnp.sum(all_lengths.reshape(blocks, slot_count), axis=1)) <= FEW

    full = head.shape[0]
    depth = full // HALVES
    ring = [(i, (i + 1) % blocks) for i in range(blocks)]
    ring += [(blocks + i, blocks + (i - 1) % blocks) for i in range(blocks)]
    step = 1 - 2 * side_place
    held = [head[part * depth : (part + 1) * depth] for part in range(HALVES)]
    logits = jnp.dot(
        lax.dynamic_slice_in_dim(hidden, row_place * full, full, axis=1), head, preferred_element_type=jnp.float32
    )
    chunks = []
    for distance in range(1, blocks):
        held = [lax.ppermute(part, ("side", "row"), ring) for part in held]
        owner = (row_place - distance * step + blocks) % blocks
        for part in range(HALVES):
            piece = lax.dynamic_slice_in_dim(hidden, owner * full + part * depth, depth, axis=1)
            logits = logits + jnp.dot(piece, held[part], preferred_element_type=jnp.float32)
        chunks += held

    teacher = teacher_logits.astype(jnp.float32)
    teacher_peak = jnp.max(teacher, axis=1)
    teacher_gap = teacher - teacher_peak[:, None]
    teacher_total = jnp.sum(jnp.exp(teacher_gap), axis=1)
    peak = jnp.max(logits, axis=1)
    shifted = logits - peak[:, None]
    powers = jnp.exp(shifted)
    total = jnp.sum(powers, axis=1)
    term = jnp.sum(powers * (shifted - teacher_gap), axis=1)
    blank = jnp.zeros_like(peak)
    own = jnp.stack([peak, total, teacher_peak, teacher_total, term, blank, blank, blank])
    other = swap_side(own)
    pair = jnp.concatenate([*join(*[jnp.stack([own[i], other[i]]) for i in range(5)]), own[5:]])
    stats = lax.all_to_all(jnp.broadcast_to(pair, (count,) + pair.shape), "vocab", 0, 0)

    place = jnp.stack([side_place, row_place]).astype(jnp.int32)

    def finish(toks, place, stats, weight, pick, logits, teacher_logits, head, *chunks):
        sums, send, diverge = grad_products(
            place, stats, weight[None], logits, teacher_logits, head, chunks, blocks, count, toks
        )
        packed = (sums[0] + swap_side(send).astype(jnp.float32)).astype(jnp.bfloat16)
        pieces = lax.all_to_all(packed, "vocab", 0, 0)
        summed = jnp.sum(pieces.astype(jnp.float32), axis=0).astype(jnp.bfloat16)
        rest = toks - LANES
        lower = jnp.concatenate([summed[64:, i : i + rest] for i in range(0, LANES, rest)], axis=0)
        block = jnp.concatenate([summed[:64], lower], axis=1)
        some = pick[:toks]
        block = jnp.dot(block, some.astype(jnp.bfloat16), preferred_element_type=jnp.float32).astype(jnp.bfloat16)
        loss = jnp.sum(jnp.where(some, (weight[:toks] * diverge[0])[:, None], 0.0), axis=0)
        return jnp.sum(loss.reshape(slot_count, WIN), axis=1), block.T

    stats, weight, pick = lax.optimization_barrier((stats, weight, pick))
    return lax.cond(
        fits,
        functools.partial(finish, FEW),
        functools.partial(finish, tok_rows),
        place, stats, weight, pick, logits, teacher_logits, head, *chunks,
    )


def solution(mesh):
    in_specs = (
        P("row", None),
        P("row", ("side", "vocab")),
        P("row", ("side", "vocab")),
        P(),
        P(),
        P("row"),
    )
    out_specs = (P("row"), P("row", ("side", "vocab")))
    return jax.shard_map(body, mesh=mesh, in_specs=in_specs, out_specs=out_specs, check_vma=False)
```

time: 183 us -> 179 us (0.978)
  waiting for transfers between devices: 61.5 us -> 52.6 us
  matrix products: 9.12 us -> 12.4 us
    all_to_all x1, waiting for transfers between devices: 20.8 us -> 16.9 us  [finish(): pieces = lax.all_to_all(packed, 'vocab', 0, 0)]
    ppermute x14, waiting for transfers between devices: 26.9 us -> 23.4 us  [body(): held = [lax.ppermute(part, ('side', 'row'), ring) for part in held]]
    dot_general x0 -> x3, matrix products: none -> 2.87 us  [the longest x1 1.73 us: body(): jnp.dot(pick_low, hidden, preferred_element_type=jnp.float32)]
  transfers between devices with their start and end apart: 18 -> 18, of which waited for: 17 -> 17; matrix products, arithmetic and copies ran while one was open for 6% -> 8% of each run, Pallas kernels for 0% -> 0%
where the time goes in v9:
time: 179 us; the launch traced here: 178 us
  starting transfers between devices  94.6 us (53%)
  waiting for transfers between devices  52.6 us (29%)
  matrix products  12.4 us (7%)
  Pallas kernels  6.16 us (3%)
  other arithmetic  5.08 us (3%)
  local copies, waits for them, and re-layouts  4.68 us (3%)
  between operations  2.05 us (1%)
    ppermute x14, starting transfers between devices, body(): held = [lax.ppermute(part, ('side', 'row'), ring) for part in held]  73 us
    ppermute x14, waiting for transfers between devices, body(): held = [lax.ppermute(part, ('side', 'row'), ring) for part in held]  23.4 us
    all_to_all x1, waiting for transfers between devices, finish(): pieces = lax.all_to_all(packed, 'vocab', 0, 0)  16.9 us
    all_to_all x1, waiting for transfers between devices, body(): lax.all_to_all(jnp.broadcast_to(pair, (count,) + pair.shape), 'vocab', 0, 0)  9.88 us
    all_to_all x1, starting transfers between devices, body(): lax.all_to_all(jnp.broadcast_to(pair, (count,) + pair.shape), 'vocab', 0, 0)  9.67 us
    ppermute x2, starting transfers between devices, swap_side(): return lax.ppermute(value, 'side', [(0, 1), (1, 0)])  8.09 us
    dot_general x14, matrix products, body(): jnp.dot(piece, held[part], preferred_element_type=jnp.float32)  7.6 us
    pallas_call x1, Pallas kernels, grad_products(): pl.pallas_call(functools.partial(grad_kernel, blocks, toks), out_shape=[j...  6.16 us
  transfers between devices with their start and end apart: 18, of which 17 were waited for; matrix products, arithmetic and copies ran while one was open for 8% of the time, Pallas kernels for 0%

profile of v9, /device:TPU:1, one launch (start us, length us, event | category | flops | bytes accessed | tf_op | source)
XLA Modules:
  0.0 177.7 jit_solution(178446739107592599)
XLA Ops:
  0.7 2.3 %fusion.68 = (bf16[256,1280]{1,0:T(8,128)(2,1)}, bf16[256,1280]{1,0:T(8,128)(2,1)S(1)}) fusion(bf16[512,1280]{1,0:T(8,128)(2,1)} %param.9), kind=kLoop, calls=%fused_computation.119 | loop fusion | bytes 2621440 | tf_op jit(solution)/shard_map/slice | solution.py:150
  3.0 11.5 %collective-permute-start.3 = (bf16[256,1280]{1,0:T(8,128)(2,1)S(1)}, bf16[256,1280]{1,0:T(8,128)(2,1)S(1)}, u32[]{:S(2)}, u32[]{:S(2)}) collective-permute-start(bf16[256,1280]{1,0:T(8,128)(2,1)S(1)} %get-tuple-element.159), channel_id=1, source_target_pairs={{0,32},{32,64},{64,96},{96,128},{128,160},{160,192},{192,224},{224... | collective-permute-start | bytes 1966088 | tf_op jit(solution)/shard_map/ppermute | solution.py:156
  14.5 2.2 %collective-permute-start.2 = (bf16[256,1280]{1,0:T(8,128)(2,1)}, bf16[256,1280]{1,0:T(8,128)(2,1)}, u32[]{:S(2)}, u32[]{:S(2)}) collective-permute-start(bf16[256,1280]{1,0:T(8,128)(2,1)} %get-tuple-element.158), channel_id=1, source_target_pairs={{0,32},{32,64},{64,96},{96,128},{128,160},{160,192},{192,224},{224... | collective-permute-start | bytes 1966088 | tf_op jit(solution)/shard_map/ppermute | solution.py:156
  17.1 4.9 %collective-permute-done.3 = bf16[256,1280]{1,0:T(8,128)(2,1)S(1)} collective-permute-done((bf16[256,1280]{1,0:T(8,128)(2,1)S(1)}, bf16[256,1280]{1,0:T(8,128)(2,1)S(1)}, u32[]{:S(2)}, u32[]{:S(2)}) %collective-permute-start.3) | collective-permute-done | bytes 655392 | tf_op jit(solution)/shard_map/ppermute | solution.py:156
  22.0 5.0 %collective-permute-start.5 = (bf16[256,1280]{1,0:T(8,128)(2,1)S(1)}, bf16[256,1280]{1,0:T(8,128)(2,1)S(1)}, u32[]{:S(2)}, u32[]{:S(2)}) collective-permute-start(bf16[256,1280]{1,0:T(8,128)(2,1)S(1)} %collective-permute-done.3), channel_id=1, source_target_pairs={{0,32},{32,64},{64,96},{96,128},{128,160},{160,192},{192,224},{224... | collective-permute-start | bytes 1966088 | tf_op jit(solution)/shard_map/ppermute | solution.py:156
  27.1 2.1 %collective-permute-done.2 = bf16[256,1280]{1,0:T(8,128)(2,1)} collective-permute-done((bf16[256,1280]{1,0:T(8,128)(2,1)}, bf16[256,1280]{1,0:T(8,128)(2,1)}, u32[]{:S(2)}, u32[]{:S(2)}) %collective-permute-start.2) | collective-permute-done | bytes 655392 | tf_op jit(solution)/shard_map/ppermute | solution.py:156
  29.1 5.0 %collective-permute-start.4 = (bf16[256,1280]{1,0:T(8,128)(2,1)}, bf16[256,1280]{1,0:T(8,128)(2,1)}, u32[]{:S(2)}, u32[]{:S(2)}) collective-permute-start(bf16[256,1280]{1,0:T(8,128)(2,1)} %collective-permute-done.2), channel_id=1, source_target_pairs={{0,32},{32,64},{64,96},{96,128},{128,160},{160,192},{192,224},{224... | collective-permute-start | bytes 1966088 | tf_op jit(solution)/shard_map/ppermute | solution.py:156
  34.2 0.7 convert_reduce_fusion.1
  35.0 0.7 subtract_select_fusion
  35.7 0.4 collective-permute-done.5
  36.1 5.0 %collective-permute-start.7 = (bf16[256,1280]{1,0:T(8,128)(2,1)S(1)}, bf16[256,1280]{1,0:T(8,128)(2,1)S(1)}, u32[]{:S(2)}, u32[]{:S(2)}) collective-permute-start(bf16[256,1280]{1,0:T(8,128)(2,1)S(1)} %collective-permute-done.5), channel_id=1, source_target_pairs={{0,32},{32,64},{64,96},{96,128},{128,160},{160,192},{192,224},{224... | collective-permute-start | bytes 1966088 | tf_op jit(solution)/shard_map/ppermute | solution.py:156
  41.1 1.7 convolution_convert_fusion.2
  42.8 0.4 collective-permute-done.4
  43.2 5.0 %collective-permute-start.6 = (bf16[256,1280]{1,0:T(8,128)(2,1)}, bf16[256,1280]{1,0:T(8,128)(2,1)}, u32[]{:S(2)}, u32[]{:S(2)}) collective-permute-start(bf16[256,1280]{1,0:T(8,128)(2,1)} %collective-permute-done.4), channel_id=1, source_target_pairs={{0,32},{32,64},{64,96},{96,128},{128,160},{160,192},{192,224},{224... | collective-permute-start | bytes 1966088 | tf_op jit(solution)/shard_map/ppermute | solution.py:156
  48.2 0.4 fusion.71
  48.9 2.0 %fusion.21 = f32[192,1280]{1,0:T(8,128)S(1)} fusion(bf16[512,1280]{1,0:T(8,128)(2,1)} %param.9, bf16[192,4096]{1,0:T(8,128)(2,1)} %convolution_convert_fusion.2, s32[]{:T(128)S(6)} %select_n.128), kind=kOutput, calls=%fused_computation.51 | convolution fusion | flops 251658240 | bytes 2490372 | tf_op jit(solution)/shard_map/dot_general | solution.py:151
  50.9 4.3 %collective-permute-start.9 = (bf16[256,1280]{1,0:T(8,128)(2,1)S(1)}, bf16[256,1280]{1,0:T(8,128)(2,1)S(1)}, u32[]{:S(2)}, u32[]{:S(2)}) collective-permute-start(bf16[256,1280]{1,0:T(8,128)(2,1)S(1)} %collective-permute-done.7), channel_id=1, source_target_pairs={{0,32},{32,64},{64,96},{96,128},{128,160},{160,192},{192,224},{224... | collective-permute-start | bytes 1966088 | tf_op jit(solution)/shard_map/ppermute | solution.py:156
  55.1 1.4 convolution_add_fusion.7
  56.5 0.7 collective-permute-done.6
  57.2 5.0 %collective-permute-start.8 = (bf16[256,1280]{1,0:T(8,128)(2,1)}, bf16[256,1280]{1,0:T(8,128)(2,1)S(1)}, u32[]{:S(2)}, u32[]{:S(2)}) collective-permute-start(bf16[256,1280]{1,0:T(8,128)(2,1)} %collective-permute-done.6), channel_id=1, source_target_pairs={{0,32},{32,64},{64,96},{96,128},{128,160},{160,192},{192,224},{224... | collective-permute-start | bytes 1966088 | tf_op jit(solution)/shard_map/ppermute | solution.py:156
  62.3 0.3 convolution_add_fusion.6
  62.6 0.3 fusion.39
  62.9 1.3 collective-permute-done.9
  64.2 5.0 %collective-permute-start.11 = (bf16[256,1280]{1,0:T(8,128)(2,1)S(1)}, bf16[256,1280]{1,0:T(8,128)(2,1)S(1)}, u32[]{:S(2)}, u32[]{:S(2)}) collective-permute-start(bf16[256,1280]{1,0:T(8,128)(2,1)S(1)} %collective-permute-done.9), channel_id=1, source_target_pairs={{0,32},{32,64},{64,96},{96,128},{128,160},{160,192},{192,224},{224... | collective-permute-start | bytes 1966088 | tf_op jit(solution)/shard_map/ppermute | solution.py:156
  69.2 1.4 fusion.15
  70.6 0.7 collective-permute-done.8
  71.3 4.9 %collective-permute-start.10 = (bf16[256,1280]{1,0:T(8,128)(2,1)S(1)}, bf16[256,1280]{1,0:T(8,128)(2,1)S(1)}, u32[]{:S(2)}, u32[]{:S(2)}) collective-permute-start(bf16[256,1280]{1,0:T(8,128)(2,1)S(1)} %collective-permute-done.8), channel_id=1, source_target_pairs={{0,32},{32,64},{64,96},{96,128},{128,160},{160,192},{192,224},{224... | collective-permute-start | bytes 1966088 | tf_op jit(solution)/shard_map/ppermute | solution.py:156
  76.2 0.3 fusion.36
  76.5 1.4 fusion.16
  77.9 0.3 collective-permute-done.11
  78.2 5.0 %collective-permute-start.13 = (bf16[256,1280]{1,0:T(8,128)(2,1)S(1)}, bf16[256,1280]{1,0:T(8,128)(2,1)S(1)}, u32[]{:S(2)}, u32[]{:S(2)}) collective-permute-start(bf16[256,1280]{1,0:T(8,128)(2,1)S(1)} %collective-permute-done.11), channel_id=1, source_target_pairs={{0,32},{32,64},{64,96},{96,128},{128,160},{160,192},{192,224},{224... | collective-permute-start | bytes 1966088 | tf_op jit(solution)/shard_map/ppermute | solution.py:156
  83.2 0.3 fusion.33
  83.5 1.7 collective-permute-done.10
  85.2 5.0 %collective-permute-start.12 = (bf16[256,1280]{1,0:T(8,128)(2,1)S(1)}, bf16[256,1280]{1,0:T(8,128)(2,1)S(1)}, u32[]{:S(2)}, u32[]{:S(2)}) collective-permute-start(bf16[256,1280]{1,0:T(8,128)(2,1)S(1)} %collective-permute-done.10), channel_id=1, source_target_pairs={{0,32},{32,64},{64,96},{96,128},{128,160},{160,192},{192,224},{224... | collective-permute-start | bytes 1966088 | tf_op jit(solution)/shard_map/ppermute | solution.py:156
  90.2 0.3 fusion.17
  90.6 0.3 fusion.30
  90.9 1.4 collective-permute-done.13
  92.2 5.0 %collective-permute-start.15 = (bf16[256,1280]{1,0:T(8,128)(2,1)S(1)}, bf16[256,1280]{1,0:T(8,128)(2,1)S(1)}, u32[]{:S(2)}, u32[]{:S(2)}) collective-permute-start(bf16[256,1280]{1,0:T(8,128)(2,1)S(1)} %collective-permute-done.13), channel_id=1, source_target_pairs={{0,32},{32,64},{64,96},{96,128},{128,160},{160,192},{192,224},{224... | collective-permute-start | bytes 1966088 | tf_op jit(solution)/shard_map/ppermute | solution.py:156
  97.3 0.3 fusion.18
  97.6 1.7 collective-permute-done.12
  99.3 5.0 %collective-permute-start.14 = (bf16[256,1280]{1,0:T(8,128)(2,1)S(1)}, bf16[256,1280]{1,0:T(8,128)(2,1)S(1)}, u32[]{:S(2)}, u32[]{:S(2)}) collective-permute-start(bf16[256,1280]{1,0:T(8,128)(2,1)S(1)} %collective-permute-done.12), channel_id=1, source_target_pairs={{0,32},{32,64},{64,96},{96,128},{128,160},{160,192},{192,224},{224... | collective-permute-start | bytes 1966088 | tf_op jit(solution)/shard_map/ppermute | solution.py:156
  104.3 0.3 fusion.27
  104.6 0.3 fusion.19
  104.9 1.4 collective-permute-done.15
  106.3 0.3 fusion.24
  106.6 6.7 %collective-permute-done.14 = bf16[256,1280]{1,0:T(8,128)(2,1)S(1)} collective-permute-done((bf16[256,1280]{1,0:T(8,128)(2,1)S(1)}, bf16[256,1280]{1,0:T(8,128)(2,1)S(1)}, u32[]{:S(2)}, u32[]{:S(2)}) %collective-permute-start.14) | collective-permute-done | bytes 655392 | tf_op jit(solution)/shard_map/ppermute | solution.py:156
  113.3 0.4 fusion.70
  113.7 0.5 copy-done.10
  114.2 0.6 multiply_reduce_fusion
  114.8 3.9 %collective-permute-start.16 = (f32[8,192]{1,0:T(8,128)S(1)}, f32[8,192]{1,0:T(8,128)S(1)}, u32[]{:S(2)}, u32[]{:S(2)}) collective-permute-start(f32[8,192]{1,0:T(8,128)S(1)} %stack.50), channel_id=1, source_target_pairs={{0,256},{256,0},{1,257},{257,1},{2,258},{258,2},{3,259},{259,3},{4... | collective-permute-start | bytes 18440 | tf_op jit(solution)/shard_map/ppermute | solution.py:21
  118.8 0.8 collective-permute-done.16
  119.6 0.7 broadcast_in_dim.94
  120.4 9.7 %all-to-all-start.2 = ((f32[32,8,192]{2,1,0:T(8,128)}), f32[32,8,192]{2,1,0:T(8,128)S(1)}, u32[]{:S(2)}, u32[]{:S(2)}) async-start(f32[32,8,192]{2,1,0:T(8,128)} %broadcast_in_dim.94), calls=%async_computation.2 | async-start | bytes 524288 | tf_op jit(solution)/shard_map/all_to_all | solution.py:176
  130.3 0.6 reduce_max.53
  131.8 9.9 %all-to-all-done.2 = f32[32,8,192]{2,1,0:T(8,128)S(1)} async-done(((f32[32,8,192]{2,1,0:T(8,128)}), f32[32,8,192]{2,1,0:T(8,128)S(1)}, u32[]{:S(2)}, u32[]{:S(2)}) %all-to-all-start.2) | async-done | bytes 196640 | tf_op jit(solution)/shard_map/all_to_all | solution.py:176
  141.6 36.1 %conditional.3 = (f32[12]{0:T(128)}, bf16[192,64]{0,1:T(8,128)(2,1)}) conditional(s32[]{:T(128)} %convert_element_type.61, (f32[192]{0:T(256)S(1)}, s32[2]{0:T(128)S(1)}, f32[32,8,192]{2,1,0:T(8,128)S(1)}, f32[192,1280]{1,0:T(8,128)S(1)}, bf16[192,1280]{1,0:T(8,128)(2,1)S(1)}, /*index=5*/bf16[512,1280]{1,0:T(8,128)(2,1)}, ...), branch_computations={%region_14.18_spmd, %region_18.22_spmd} | conditional | flops 2019704960 | bytes 20125838
  141.6 6.2 %branch_1_fun.1 = (f32[2,32,72,128]{3,2,1,0:T(8,128)S(1)}, bf16[32,72,128]{2,1,0:T(8,128)(2,1)S(1)}, f32[1,144]{1,0:T(1,128)S(1)}) custom-call(s32[2]{0:T(128)S(1)} %get-tuple-element.118.place_ref, f32[32,8,192]{2,1,0:T(8,128)S(1)} %get-tuple-element.119.stats_ref, f32[1,192]{1,0:T(1,128)S(1)} %bitcast.49, f32[192,1280]{1,0:T(8,128)S(1)} %get-tuple-element.120.logits_ref, ...), custom_call_target="tpu_custom_call" | custom-call | flops 1509949440 | bytes 10485760 | tf_op jit(solution)/shard_map/cond/branch_1_fun/pallas_call | solution.py:99
  147.8 4.2 %collective-permute-start = (bf16[32,72,128]{2,1,0:T(8,128)(2,1)S(1)}, bf16[32,72,128]{2,1,0:T(8,128)(2,1)S(1)}, u32[]{:S(2)}, u32[]{:S(2)}) collective-permute-start(bf16[32,72,128]{2,1,0:T(8,128)(2,1)S(1)} %get-tuple-element.139), channel_id=1, source_target_pairs={{0,256},{256,0},{1,257},{257,1},{2,258},{258,2},{3,259},{259,3},{4... | collective-permute-start | bytes 1769480 | tf_op jit(solution)/shard_map/cond/branch_1_fun/ppermute | solution.py:21
  152.0 1.6 collective-permute-done
  153.6 1.0 fusion.8
  154.6 3.9 %all-to-all-start = ((bf16[32,72,128]{2,1,0:T(8,128)(2,1)}), bf16[32,72,128]{2,1,0:T(8,128)(2,1)S(1)}, u32[]{:S(2)}, u32[]{:S(2)}) async-start(bf16[32,72,128]{2,1,0:T(8,128)(2,1)} %fusion.8), calls=%async_computation | async-start | bytes 1179648 | tf_op jit(solution)/shard_map/cond/branch_1_fun/all_to_all | solution.py:185
  158.7 0.6 reduce_sum.146
  159.3 16.9 %all-to-all-done = bf16[32,72,128]{2,1,0:T(8,128)(2,1)S(1)} async-done(((bf16[32,72,128]{2,1,0:T(8,128)(2,1)}), bf16[32,72,128]{2,1,0:T(8,128)(2,1)S(1)}, u32[]{:S(2)}, u32[]{:S(2)}) %all-to-all-start) | async-done | bytes 589856 | tf_op jit(solution)/shard_map/cond/branch_1_fun/all_to_all | solution.py:185
  177.0 0.8 fusion.9
  (70 shorter events, 2.0 us)
Async XLA Ops:
  0.6 40.5 %copy-start = (bf16[192,4096]{1,0:T(8,128)(2,1)S(1)}, bf16[192,4096]{1,0:T(8,128)(2,1)}, u32[]{:S(2)}) copy-start(bf16[192,4096]{1,0:T(8,128)(2,1)} %param.8) | copy-start | bytes 4718596
  0.6 16.1 %copy-start.16 = (s32[96]{0:T(128)S(1)}, s32[96]{0:T(128)}, u32[]{:S(2)}) copy-start(s32[96]{0:T(128)} %param.11) | copy-start | bytes 1156
  0.7 16.1 %copy-start.17 = (s32[96]{0:T(128)S(1)}, s32[96]{0:T(128)}, u32[]{:S(2)}) copy-start(s32[96]{0:T(128)} %param.12) | copy-start | bytes 1156
  3.0 19.0 %collective-permute-start.3 = (bf16[256,1280]{1,0:T(8,128)(2,1)S(1)}, bf16[256,1280]{1,0:T(8,128)(2,1)S(1)}, u32[]{:S(2)}, u32[]{:S(2)}) collective-permute-start(bf16[256,1280]{1,0:T(8,128)(2,1)S(1)} %get-tuple-element.159), channel_id=1, source_target_pairs={{0,32},{32,64},{64,96},{96,128},{128,160},{160,192},{192,224},{224... | collective-permute-start | bytes 1966088 | tf_op jit(solution)/shard_map/ppermute | solution.py:156
  14.5 14.6 %collective-permute-start.2 = (bf16[256,1280]{1,0:T(8,128)(2,1)}, bf16[256,1280]{1,0:T(8,128)(2,1)}, u32[]{:S(2)}, u32[]{:S(2)}) collective-permute-start(bf16[256,1280]{1,0:T(8,128)(2,1)} %get-tuple-element.158), channel_id=1, source_target_pairs={{0,32},{32,64},{64,96},{96,128},{128,160},{160,192},{192,224},{224... | collective-permute-start | bytes 1966088 | tf_op jit(solution)/shard_map/ppermute | solution.py:156
  22.0 13.6 %copy-start.8 = (bf16[256,1280]{1,0:T(8,128)(2,1)}, bf16[256,1280]{1,0:T(8,128)(2,1)S(1)}, u32[]{:S(2)}) copy-start(bf16[256,1280]{1,0:T(8,128)(2,1)S(1)} %collective-permute-done.3) | copy-start | bytes 1966084
  22.0 14.0 %collective-permute-start.5 = (bf16[256,1280]{1,0:T(8,128)(2,1)S(1)}, bf16[256,1280]{1,0:T(8,128)(2,1)S(1)}, u32[]{:S(2)}, u32[]{:S(2)}) collective-permute-start(bf16[256,1280]{1,0:T(8,128)(2,1)S(1)} %collective-permute-done.3), channel_id=1, source_target_pairs={{0,32},{32,64},{64,96},{96,128},{128,160},{160,192},{192,224},{224... | collective-permute-start | bytes 1966088 | tf_op jit(solution)/shard_map/ppermute | solution.py:156
  29.1 14.0 %collective-permute-start.4 = (bf16[256,1280]{1,0:T(8,128)(2,1)}, bf16[256,1280]{1,0:T(8,128)(2,1)}, u32[]{:S(2)}, u32[]{:S(2)}) collective-permute-start(bf16[256,1280]{1,0:T(8,128)(2,1)} %collective-permute-done.2), channel_id=1, source_target_pairs={{0,32},{32,64},{64,96},{96,128},{128,160},{160,192},{192,224},{224... | collective-permute-start | bytes 1966088 | tf_op jit(solution)/shard_map/ppermute | solution.py:156
  35.7 12.6 %copy-start.14 = (bf16[192,1280]{1,0:T(8,128)(2,1)S(1)}, bf16[192,1280]{1,0:T(8,128)(2,1)}, u32[]{:S(2)}) copy-start(bf16[192,1280]{1,0:T(8,128)(2,1)} %param.10) | copy-start | bytes 1474564
  36.1 26.5 %copy-start.2 = (bf16[256,1280]{1,0:T(8,128)(2,1)}, bf16[256,1280]{1,0:T(8,128)(2,1)S(1)}, u32[]{:S(2)}) copy-start(bf16[256,1280]{1,0:T(8,128)(2,1)S(1)} %collective-permute-done.5) | copy-start | bytes 1966084
  36.1 14.8 %collective-permute-start.7 = (bf16[256,1280]{1,0:T(8,128)(2,1)S(1)}, bf16[256,1280]{1,0:T(8,128)(2,1)S(1)}, u32[]{:S(2)}, u32[]{:S(2)}) collective-permute-start(bf16[256,1280]{1,0:T(8,128)(2,1)S(1)} %collective-permute-done.5), channel_id=1, source_target_pairs={{0,32},{32,64},{64,96},{96,128},{128,160},{160,192},{192,224},{224... | collective-permute-start | bytes 1966088 | tf_op jit(solution)/shard_map/ppermute | solution.py:156
  43.2 14.0 %collective-permute-start.6 = (bf16[256,1280]{1,0:T(8,128)(2,1)}, bf16[256,1280]{1,0:T(8,128)(2,1)}, u32[]{:S(2)}, u32[]{:S(2)}) collective-permute-start(bf16[256,1280]{1,0:T(8,128)(2,1)} %collective-permute-done.4), channel_id=1, source_target_pairs={{0,32},{32,64},{64,96},{96,128},{128,160},{160,192},{192,224},{224... | collective-permute-start | bytes 1966088 | tf_op jit(solution)/shard_map/ppermute | solution.py:156
  48.9 6.3 %copy-start.1 = (bf16[192,4096]{1,0:T(8,128)(2,1)S(1)}, bf16[192,4096]{1,0:T(8,128)(2,1)}, u32[]{:S(2)}) copy-start(bf16[192,4096]{1,0:T(8,128)(2,1)} %convolution_convert_fusion.2) | copy-start | bytes 4718596
  50.8 11.4 %copy-start.9 = (bf16[256,1280]{1,0:T(8,128)(2,1)S(1)}, bf16[256,1280]{1,0:T(8,128)(2,1)}, u32[]{:S(2)}) copy-start(bf16[256,1280]{1,0:T(8,128)(2,1)} %copy-done.8) | copy-start | bytes 1966084
  50.9 25.3 %copy-start.3 = (bf16[256,1280]{1,0:T(8,128)(2,1)}, bf16[256,1280]{1,0:T(8,128)(2,1)S(1)}, u32[]{:S(2)}) copy-start(bf16[256,1280]{1,0:T(8,128)(2,1)S(1)} %collective-permute-done.7) | copy-start | bytes 1966084
  50.9 13.3 %collective-permute-start.9 = (bf16[256,1280]{1,0:T(8,128)(2,1)S(1)}, bf16[256,1280]{1,0:T(8,128)(2,1)S(1)}, u32[]{:S(2)}, u32[]{:S(2)}) collective-permute-start(bf16[256,1280]{1,0:T(8,128)(2,1)S(1)} %collective-permute-done.7), channel_id=1, source_target_pairs={{0,32},{32,64},{64,96},{96,128},{128,160},{160,192},{192,224},{224... | collective-permute-start | bytes 1966088 | tf_op jit(solution)/shard_map/ppermute | solution.py:156
  57.2 14.0 %collective-permute-start.8 = (bf16[256,1280]{1,0:T(8,128)(2,1)}, bf16[256,1280]{1,0:T(8,128)(2,1)S(1)}, u32[]{:S(2)}, u32[]{:S(2)}) collective-permute-start(bf16[256,1280]{1,0:T(8,128)(2,1)} %collective-permute-done.6), channel_id=1, source_target_pairs={{0,32},{32,64},{64,96},{96,128},{128,160},{160,192},{192,224},{224... | collective-permute-start | bytes 1966088 | tf_op jit(solution)/shard_map/ppermute | solution.py:156
  64.1 19.1 %copy-start.4 = (bf16[256,1280]{1,0:T(8,128)(2,1)}, bf16[256,1280]{1,0:T(8,128)(2,1)S(1)}, u32[]{:S(2)}) copy-start(bf16[256,1280]{1,0:T(8,128)(2,1)S(1)} %collective-permute-done.9) | copy-start | bytes 1966084
  64.2 14.0 %collective-permute-start.11 = (bf16[256,1280]{1,0:T(8,128)(2,1)S(1)}, bf16[256,1280]{1,0:T(8,128)(2,1)S(1)}, u32[]{:S(2)}, u32[]{:S(2)}) collective-permute-start(bf16[256,1280]{1,0:T(8,128)(2,1)S(1)} %collective-permute-done.9), channel_id=1, source_target_pairs={{0,32},{32,64},{64,96},{96,128},{128,160},{160,192},{192,224},{224... | collective-permute-start | bytes 1966088 | tf_op jit(solution)/shard_map/ppermute | solution.py:156
  71.3 19.0 %copy-start.11 = (bf16[256,1280]{1,0:T(8,128)(2,1)}, bf16[256,1280]{1,0:T(8,128)(2,1)S(1)}, u32[]{:S(2)}) copy-start(bf16[256,1280]{1,0:T(8,128)(2,1)S(1)} %collective-permute-done.8) | copy-start | bytes 1966084
  71.3 13.9 %collective-permute-start.10 = (bf16[256,1280]{1,0:T(8,128)(2,1)S(1)}, bf16[256,1280]{1,0:T(8,128)(2,1)S(1)}, u32[]{:S(2)}, u32[]{:S(2)}) collective-permute-start(bf16[256,1280]{1,0:T(8,128)(2,1)S(1)} %collective-permute-done.8), channel_id=1, source_target_pairs={{0,32},{32,64},{64,96},{96,128},{128,160},{160,192},{192,224},{224... | collective-permute-start | bytes 1966088 | tf_op jit(solution)/shard_map/ppermute | solution.py:156
  78.2 12.4 %copy-start.5 = (bf16[256,1280]{1,0:T(8,128)(2,1)}, bf16[256,1280]{1,0:T(8,128)(2,1)S(1)}, u32[]{:S(2)}) copy-start(bf16[256,1280]{1,0:T(8,128)(2,1)S(1)} %collective-permute-done.11) | copy-start | bytes 1966084
  78.2 14.0 %collective-permute-start.13 = (bf16[256,1280]{1,0:T(8,128)(2,1)S(1)}, bf16[256,1280]{1,0:T(8,128)(2,1)S(1)}, u32[]{:S(2)}, u32[]{:S(2)}) collective-permute-start(bf16[256,1280]{1,0:T(8,128)(2,1)S(1)} %collective-permute-done.11), channel_id=1, source_target_pairs={{0,32},{32,64},{64,96},{96,128},{128,160},{160,192},{192,224},{224... | collective-permute-start | bytes 1966088 | tf_op jit(solution)/shard_map/ppermute | solution.py:156
  85.2 12.0 %copy-start.12 = (bf16[256,1280]{1,0:T(8,128)(2,1)}, bf16[256,1280]{1,0:T(8,128)(2,1)S(1)}, u32[]{:S(2)}) copy-start(bf16[256,1280]{1,0:T(8,128)(2,1)S(1)} %collective-permute-done.10) | copy-start | bytes 1966084
  85.2 14.0 %collective-permute-start.12 = (bf16[256,1280]{1,0:T(8,128)(2,1)S(1)}, bf16[256,1280]{1,0:T(8,128)(2,1)S(1)}, u32[]{:S(2)}, u32[]{:S(2)}) collective-permute-start(bf16[256,1280]{1,0:T(8,128)(2,1)S(1)} %collective-permute-done.10), channel_id=1, source_target_pairs={{0,32},{32,64},{64,96},{96,128},{128,160},{160,192},{192,224},{224... | collective-permute-start | bytes 1966088 | tf_op jit(solution)/shard_map/ppermute | solution.py:156
  92.2 12.0 %copy-start.6 = (bf16[256,1280]{1,0:T(8,128)(2,1)}, bf16[256,1280]{1,0:T(8,128)(2,1)S(1)}, u32[]{:S(2)}) copy-start(bf16[256,1280]{1,0:T(8,128)(2,1)S(1)} %collective-permute-done.13) | copy-start | bytes 1966084
  92.2 14.0 %collective-permute-start.15 = (bf16[256,1280]{1,0:T(8,128)(2,1)S(1)}, bf16[256,1280]{1,0:T(8,128)(2,1)S(1)}, u32[]{:S(2)}, u32[]{:S(2)}) collective-permute-start(bf16[256,1280]{1,0:T(8,128)(2,1)S(1)} %collective-permute-done.13), channel_id=1, source_target_pairs={{0,32},{32,64},{64,96},{96,128},{128,160},{160,192},{192,224},{224... | collective-permute-start | bytes 1966088 | tf_op jit(solution)/shard_map/ppermute | solution.py:156
  99.3 5.7 %copy-start.13 = (bf16[256,1280]{1,0:T(8,128)(2,1)}, bf16[256,1280]{1,0:T(8,128)(2,1)S(1)}, u32[]{:S(2)}) copy-start(bf16[256,1280]{1,0:T(8,128)(2,1)S(1)} %collective-permute-done.12) | copy-start | bytes 1966084
  99.3 14.0 %collective-permute-start.14 = (bf16[256,1280]{1,0:T(8,128)(2,1)S(1)}, bf16[256,1280]{1,0:T(8,128)(2,1)S(1)}, u32[]{:S(2)}, u32[]{:S(2)}) collective-permute-start(bf16[256,1280]{1,0:T(8,128)(2,1)S(1)} %collective-permute-done.12), channel_id=1, source_target_pairs={{0,32},{32,64},{64,96},{96,128},{128,160},{160,192},{192,224},{224... | collective-permute-start | bytes 1966088 | tf_op jit(solution)/shard_map/ppermute | solution.py:156
  106.3 7.4 %copy-start.7 = (bf16[256,1280]{1,0:T(8,128)(2,1)}, bf16[256,1280]{1,0:T(8,128)(2,1)S(1)}, u32[]{:S(2)}) copy-start(bf16[256,1280]{1,0:T(8,128)(2,1)S(1)} %collective-permute-done.15) | copy-start | bytes 1966084
  106.6 12.1 %copy-start.15 = (s32[192]{0:T(256)S(1)}, s32[192]{0:T(256)}, u32[]{:S(2)}) copy-start(s32[192]{0:T(256)} %param.13) | copy-start | bytes 2308
  113.3 0.9 copy-start.10
  114.8 4.7 %collective-permute-start.16 = (f32[8,192]{1,0:T(8,128)S(1)}, f32[8,192]{1,0:T(8,128)S(1)}, u32[]{:S(2)}, u32[]{:S(2)}) collective-permute-start(f32[8,192]{1,0:T(8,128)S(1)} %stack.50), channel_id=1, source_target_pairs={{0,256},{256,0},{1,257},{257,1},{2,258},{258,2},{3,259},{259,3},{4... | collective-permute-start | bytes 18440 | tf_op jit(solution)/shard_map/ppermute | solution.py:21
  120.4 21.3 %all-to-all-start.2 = ((f32[32,8,192]{2,1,0:T(8,128)}), f32[32,8,192]{2,1,0:T(8,128)S(1)}, u32[]{:S(2)}, u32[]{:S(2)}) async-start(f32[32,8,192]{2,1,0:T(8,128)} %broadcast_in_dim.94), calls=%async_computation.2 | async-start | bytes 524288 | tf_op jit(solution)/shard_map/all_to_all | solution.py:176
  147.8 5.8 %collective-permute-start = (bf16[32,72,128]{2,1,0:T(8,128)(2,1)S(1)}, bf16[32,72,128]{2,1,0:T(8,128)(2,1)S(1)}, u32[]{:S(2)}, u32[]{:S(2)}) collective-permute-start(bf16[32,72,128]{2,1,0:T(8,128)(2,1)S(1)} %get-tuple-element.139), channel_id=1, source_target_pairs={{0,256},{256,0},{1,257},{257,1},{2,258},{258,2},{3,259},{259,3},{4... | collective-permute-start | bytes 1769480 | tf_op jit(solution)/shard_map/cond/branch_1_fun/ppermute | solution.py:21
  154.6 21.7 %all-to-all-start = ((bf16[32,72,128]{2,1,0:T(8,128)(2,1)}), bf16[32,72,128]{2,1,0:T(8,128)(2,1)S(1)}, u32[]{:S(2)}, u32[]{:S(2)}) async-start(bf16[32,72,128]{2,1,0:T(8,128)(2,1)} %fusion.8), calls=%async_computation | async-start | bytes 1179648 | tf_op jit(solution)/shard_map/cond/branch_1_fun/all_to_all | solution.py:185

commit v10 on v9

--- a/solution.py
+++ b/solution.py
@@ -10,7 +10,7 @@
 WIN = 16
 HALVES = 2
 WAITED = 4
-FEW = 144
+FEW = 128
 LANES = 128
 
 
@@ -43,7 +43,7 @@
     row = place_ref[1]
     step = 1 - 2 * side
     rest = toks - LANES
-    groups = LANES // rest
+    groups = LANES // rest if rest else 1
     rows = 64 // groups
     depth = own_ref.shape[0] // HALVES
     sources = [own_ref.at[part * depth : (part + 1) * depth] for part in range(HALVES)] + list(chunk_refs)
@@ -65,19 +65,22 @@
     slope = shifted - teacher_ref[:toks].astype(jnp.float32) + columns[:, 2:3]
     grad = columns[:, 1:2] * jnp.exp(shifted) * slope
     grad_ref[...] = jnp.transpose(grad).astype(jnp.bfloat16)
-    group = lax.broadcasted_iota(jnp.int32, (rows, LANES), 1) // rest
+    group = lax.broadcasted_iota(jnp.int32, (rows, LANES), 1) // max(rest, 1)
 
     def one(product, distance, part):
         owner = lax.rem(row - distance * step + blocks, blocks)
         first = lax.rem(owner, blocks // 2) * (HALVES * depth // 64) + part * (depth // 64)
         place = lax.rem(lax.div(owner, blocks // 2) + side, 2)
+        for i in range(depth // 64):
+            sums_ref[place, first + i, :64] = product[64 * i : 64 * i + 64, :LANES]
+        if not rest:
+            return
         wide = jnp.concatenate([product[:, LANES:], jnp.zeros((depth, LANES - rest), jnp.float32)], axis=1)
         for i in range(depth // 64):
             lower = wide[64 * i : 64 * i + rows]
             for near in range(1, groups):
                 start = 64 * i + near * rows
                 lower = jnp.where(group == near, pltpu.roll(wide[start : start + rows], near * rest, 1), lower)
-            sums_ref[place, first + i, :64] = product[64 * i : 64 * i + 64, :LANES]
             sums_ref[place, first + i, 64:] = lower
 
     for base in range(0, len(sources), WAITED):
@@ -124,13 +127,13 @@
     slot_count = tok_rows // WIN
     row_place = lax.axis_index("row")
     side_place = lax.axis_index("side")
-    chosen = slot_rollout[:, None] == jnp.arange(lengths.shape[0], dtype=jnp.int32)[None, :]
-    all_lengths = jnp.sum(jnp.where(chosen, lengths[None, :], 0), axis=1)
-    slot_length = lax.dynamic_slice_in_dim(all_lengths, row_place * slot_count, slot_count)
+    own_slots = lax.dynamic_slice_in_dim(slot_rollout, row_place * slot_count, slot_count)
+    chosen = own_slots[:, None] == jnp.arange(lengths.shape[0], dtype=jnp.int32)[None, :]
+    slot_length = jnp.sum(jnp.where(chosen, lengths[None, :], 0), axis=1)
     length_tok = jnp.repeat(slot_length, WIN)
     token = jnp.arange(tok_rows, dtype=jnp.int32)
-    inside = token % WIN < length_tok
-    weight = jnp.where((token_mask > 0) & inside, 1.0 / length_tok.astype(jnp.float32), 0.0)
+    inside = (token_mask > 0) & (token % WIN < length_tok)
+    weight = jnp.where(inside, 1.0 / length_tok.astype(jnp.float32), 0.0)
 
     earlier = token[None, :] < token[:, None]
     rank = jnp.sum((earlier & inside[None, :]).astype(jnp.int32), axis=1)
@@ -140,7 +143,10 @@
     hidden = jnp.dot(pick_low, hidden, preferred_element_type=jnp.float32).astype(jnp.bfloat16)
     teacher_logits = jnp.dot(pick_low, teacher_logits, preferred_element_type=jnp.float32).astype(jnp.bfloat16)
     weight = jnp.sum(jnp.where(pick, weight[None, :], 0.0), axis=1)
-    fits = jnp.max(jnp.sum(all_lengths.reshape(blocks, slot_count), axis=1)) <= FEW
+    most = jnp.full((8, LANES), jnp.sum(inside.astype(jnp.float32)))
+    for apart in (1 << bit for bit in range((blocks - 1).bit_length())):
+        most = jnp.maximum(most, lax.ppermute(most, "row", [(i, i ^ apart) for i in range(blocks)]))
+    fits = most[0, 0] <= FEW
 
     full = head.shape[0]
     depth = full // HALVES
@@ -185,8 +191,10 @@
         pieces = lax.all_to_all(packed, "vocab", 0, 0)
         summed = jnp.sum(pieces.astype(jnp.float32), axis=0).astype(jnp.bfloat16)
         rest = toks - LANES
-        lower = jnp.concatenate([summed[64:, i : i + rest] for i in range(0, LANES, rest)], axis=0)
-        block = jnp.concatenate([summed[:64], lower], axis=1)
+        block = summed[:64]
+        if rest:
+            lower = jnp.concatenate([summed[64:, i : i + rest] for i in range(0, LANES, rest)], axis=0)
+            block = jnp.concatenate([block, lower], axis=1)
         some = pick[:toks]
         block = jnp.dot(block, some.astype(jnp.bfloat16), preferred_element_type=jnp.float32).astype(jnp.bfloat16)
         loss = jnp.sum(jnp.where(some, (weight[:toks] * diverge[0])[:, None], 0.0), axis=0)

time: 179 us -> 182 us (1.017)
  starting transfers between devices: 94.6 us -> 108 us
  waiting for transfers between devices: 52.6 us -> 40.8 us
    ppermute x0 -> x3, starting transfers between devices: none -> 10.7 us  [body(): lax.ppermute(most, 'row', [(i, i ^ apart) for i in range(blocks)])]
    all_to_all x1, waiting for transfers between devices: 9.88 us -> 1.49 us  [body(): lax.all_to_all(jnp.broadcast_to(pair, (count,) + pair.shape), 'vocab', 0, 0)]
    ppermute x14, waiting for transfers between devices: 23.4 us -> 19.3 us  [body(): held = [lax.ppermute(part, ('side', 'row'), ring) for part in held]]
    all_to_all x1, starting transfers between devices: 3.9 us -> 7.39 us  [finish(): pieces = lax.all_to_all(packed, 'vocab', 0, 0)]
    ppermute x0 -> x3, waiting for transfers between devices: none -> 2.77 us  [body(): lax.ppermute(most, 'row', [(i, i ^ apart) for i in range(blocks)])]
  transfers between devices with their start and end apart: 18 -> 21, of which waited for: 17 -> 16; matrix products, arithmetic and copies ran while one was open for 8% -> 11% of each run, Pallas kernels for 0% -> 0%
where the time goes in v10:
time: 182 us; the launch traced here: 181 us
  starting transfers between devices  108 us (59%)
  waiting for transfers between devices  40.8 us (22%)
  matrix products  12.4 us (7%)
  other arithmetic  6.17 us (3%)
  Pallas kernels  5.81 us (3%)
  local copies, waits for them, and re-layouts  5.18 us (3%)
  between operations  2.09 us (1%)
    ppermute x14, starting transfers between devices, body(): held = [lax.ppermute(part, ('side', 'row'), ring) for part in held]  72.8 us
    ppermute x14, waiting for transfers between devices, body(): held = [lax.ppermute(part, ('side', 'row'), ring) for part in held]  19.3 us
    all_to_all x1, waiting for transfers between devices, finish(): pieces = lax.all_to_all(packed, 'vocab', 0, 0)  15.7 us
    ppermute x3, starting transfers between devices, body(): lax.ppermute(most, 'row', [(i, i ^ apart) for i in range(blocks)])  10.7 us
    all_to_all x1, starting transfers between devices, body(): lax.all_to_all(jnp.broadcast_to(pair, (count,) + pair.shape), 'vocab', 0, 0)  9.67 us
    ppermute x2, starting transfers between devices, swap_side(): return lax.ppermute(value, 'side', [(0, 1), (1, 0)])  7.8 us
    dot_general x14, matrix products, body(): jnp.dot(piece, held[part], preferred_element_type=jnp.float32)  7.6 us
    all_to_all x1, starting transfers between devices, finish(): pieces = lax.all_to_all(packed, 'vocab', 0, 0)  7.39 us
  transfers between devices with their start and end apart: 21, of which 16 were waited for; matrix products, arithmetic and copies ran while one was open for 11% of the time, Pallas kernels for 0%

profile of v10, /device:TPU:1, one launch (start us, length us, event | category | flops | bytes accessed | tf_op | source)
XLA Modules:
  0.0 180.9 jit_solution(4990110367414078568)
XLA Ops:
  0.7 2.3 %fusion.61 = (bf16[256,1280]{1,0:T(8,128)(2,1)}, bf16[256,1280]{1,0:T(8,128)(2,1)S(1)}) fusion(bf16[512,1280]{1,0:T(8,128)(2,1)} %param.9), kind=kLoop, calls=%fused_computation.104 | loop fusion | bytes 2621440 | tf_op jit(solution)/shard_map/slice | solution.py:156
  3.0 11.5 %collective-permute-start.6 = (bf16[256,1280]{1,0:T(8,128)(2,1)S(1)}, bf16[256,1280]{1,0:T(8,128)(2,1)S(1)}, u32[]{:S(2)}, u32[]{:S(2)}) collective-permute-start(bf16[256,1280]{1,0:T(8,128)(2,1)S(1)} %get-tuple-element.161), channel_id=1, source_target_pairs={{0,32},{32,64},{64,96},{96,128},{128,160},{160,192},{192,224},{224... | collective-permute-start | bytes 1966088 | tf_op jit(solution)/shard_map/ppermute | solution.py:162
  14.5 2.2 %collective-permute-start.5 = (bf16[256,1280]{1,0:T(8,128)(2,1)}, bf16[256,1280]{1,0:T(8,128)(2,1)}, u32[]{:S(2)}, u32[]{:S(2)}) collective-permute-start(bf16[256,1280]{1,0:T(8,128)(2,1)} %get-tuple-element.160), channel_id=1, source_target_pairs={{0,32},{32,64},{64,96},{96,128},{128,160},{160,192},{192,224},{224... | collective-permute-start | bytes 1966088 | tf_op jit(solution)/shard_map/ppermute | solution.py:162
  17.2 0.6 convert_reduce_fusion.2
  17.8 0.6 broadcast_in_dim.94
  18.4 3.1 %collective-permute-start.2 = (f32[8,128]{1,0:T(8,128)S(1)}, f32[8,128]{1,0:T(8,128)S(1)}, u32[]{:S(2)}, u32[]{:S(2)}) collective-permute-start(f32[8,128]{1,0:T(8,128)S(1)} %broadcast_in_dim.94), channel_id=1, source_target_pairs={{0,32},{32,0},{64,96},{96,64},{128,160},{160,128},{192,224},{224,1... | collective-permute-start | bytes 12296 | tf_op jit(solution)/shard_map/ppermute | solution.py:148
  21.5 0.5 collective-permute-done.6
  22.0 5.0 %collective-permute-start.8 = (bf16[256,1280]{1,0:T(8,128)(2,1)S(1)}, bf16[256,1280]{1,0:T(8,128)(2,1)S(1)}, u32[]{:S(2)}, u32[]{:S(2)}) collective-permute-start(bf16[256,1280]{1,0:T(8,128)(2,1)S(1)} %collective-permute-done.6), channel_id=1, source_target_pairs={{0,32},{32,64},{64,96},{96,128},{128,160},{160,192},{192,224},{224... | collective-permute-start | bytes 1966088 | tf_op jit(solution)/shard_map/ppermute | solution.py:162
  27.0 0.7 convert_reduce_fusion.1
  27.8 1.3 collective-permute-done.5
  29.2 5.0 %collective-permute-start.7 = (bf16[256,1280]{1,0:T(8,128)(2,1)}, bf16[256,1280]{1,0:T(8,128)(2,1)}, u32[]{:S(2)}, u32[]{:S(2)}) collective-permute-start(bf16[256,1280]{1,0:T(8,128)(2,1)} %collective-permute-done.5), channel_id=1, source_target_pairs={{0,32},{32,64},{64,96},{96,128},{128,160},{160,192},{192,224},{224... | collective-permute-start | bytes 1966088 | tf_op jit(solution)/shard_map/ppermute | solution.py:162
  34.2 0.6 subtract_select_fusion
  34.8 1.7 convolution_convert_fusion.2
  36.6 4.5 %collective-permute-start.10 = (bf16[256,1280]{1,0:T(8,128)(2,1)S(1)}, bf16[256,1280]{1,0:T(8,128)(2,1)S(1)}, u32[]{:S(2)}, u32[]{:S(2)}) collective-permute-start(bf16[256,1280]{1,0:T(8,128)(2,1)S(1)} %collective-permute-done.8), channel_id=1, source_target_pairs={{0,32},{32,64},{64,96},{96,128},{128,160},{160,192},{192,224},{224... | collective-permute-start | bytes 1966088 | tf_op jit(solution)/shard_map/ppermute | solution.py:162
  41.1 0.4 fusion.64
  41.5 1.7 collective-permute-done.7
  43.2 5.0 %collective-permute-start.9 = (bf16[256,1280]{1,0:T(8,128)(2,1)}, bf16[256,1280]{1,0:T(8,128)(2,1)}, u32[]{:S(2)}, u32[]{:S(2)}) collective-permute-start(bf16[256,1280]{1,0:T(8,128)(2,1)} %collective-permute-done.7), channel_id=1, source_target_pairs={{0,32},{32,64},{64,96},{96,128},{128,160},{160,192},{192,224},{224... | collective-permute-start | bytes 1966088 | tf_op jit(solution)/shard_map/ppermute | solution.py:162
  48.6 2.0 %fusion.17 = f32[192,1280]{1,0:T(8,128)S(1)} fusion(bf16[512,1280]{1,0:T(8,128)(2,1)} %param.9, bf16[192,4096]{1,0:T(8,128)(2,1)} %convolution_convert_fusion.2, s32[]{:T(128)S(6)} %select_n.113), kind=kOutput, calls=%fused_computation.39 | convolution fusion | flops 251658240 | bytes 2490372 | tf_op jit(solution)/shard_map/dot_general | solution.py:157
  50.5 4.6 %collective-permute-start.12 = (bf16[256,1280]{1,0:T(8,128)(2,1)S(1)}, bf16[256,1280]{1,0:T(8,128)(2,1)S(1)}, u32[]{:S(2)}, u32[]{:S(2)}) collective-permute-start(bf16[256,1280]{1,0:T(8,128)(2,1)S(1)} %collective-permute-done.10), channel_id=1, source_target_pairs={{0,32},{32,64},{64,96},{96,128},{128,160},{160,192},{192,224},{224... | collective-permute-start | bytes 1966088 | tf_op jit(solution)/shard_map/ppermute | solution.py:162
  55.1 1.4 convolution_add_fusion.7
  56.6 0.7 collective-permute-done.9
  57.2 5.0 %collective-permute-start.11 = (bf16[256,1280]{1,0:T(8,128)(2,1)}, bf16[256,1280]{1,0:T(8,128)(2,1)S(1)}, u32[]{:S(2)}, u32[]{:S(2)}) collective-permute-start(bf16[256,1280]{1,0:T(8,128)(2,1)} %collective-permute-done.9), channel_id=1, source_target_pairs={{0,32},{32,64},{64,96},{96,128},{128,160},{160,192},{192,224},{224... | collective-permute-start | bytes 1966088 | tf_op jit(solution)/shard_map/ppermute | solution.py:162
  62.3 0.3 convolution_add_fusion.6
  62.9 1.3 collective-permute-done.12
  64.2 5.0 %collective-permute-start.14 = (bf16[256,1280]{1,0:T(8,128)(2,1)S(1)}, bf16[256,1280]{1,0:T(8,128)(2,1)S(1)}, u32[]{:S(2)}, u32[]{:S(2)}) collective-permute-start(bf16[256,1280]{1,0:T(8,128)(2,1)S(1)} %collective-permute-done.12), channel_id=1, source_target_pairs={{0,32},{32,64},{64,96},{96,128},{128,160},{160,192},{192,224},{224... | collective-permute-start | bytes 1966088 | tf_op jit(solution)/shard_map/ppermute | solution.py:162
  69.2 1.4 fusion.11
  70.6 0.7 collective-permute-done.11
  71.3 4.9 %collective-permute-start.13 = (bf16[256,1280]{1,0:T(8,128)(2,1)S(1)}, bf16[256,1280]{1,0:T(8,128)(2,1)S(1)}, u32[]{:S(2)}, u32[]{:S(2)}) collective-permute-start(bf16[256,1280]{1,0:T(8,128)(2,1)S(1)} %collective-permute-done.11), channel_id=1, source_target_pairs={{0,32},{32,64},{64,96},{96,128},{128,160},{160,192},{192,224},{224... | collective-permute-start | bytes 1966088 | tf_op jit(solution)/shard_map/ppermute | solution.py:162
  76.5 1.4 fusion.12
  78.2 5.0 %collective-permute-start.16 = (bf16[256,1280]{1,0:T(8,128)(2,1)S(1)}, bf16[256,1280]{1,0:T(8,128)(2,1)S(1)}, u32[]{:S(2)}, u32[]{:S(2)}) collective-permute-start(bf16[256,1280]{1,0:T(8,128)(2,1)S(1)} %collective-permute-done.14), channel_id=1, source_target_pairs={{0,32},{32,64},{64,96},{96,128},{128,160},{160,192},{192,224},{224... | collective-permute-start | bytes 1966088 | tf_op jit(solution)/shard_map/ppermute | solution.py:162
  83.5 1.7 collective-permute-done.13
  85.2 5.0 %collective-permute-start.15 = (bf16[256,1280]{1,0:T(8,128)(2,1)S(1)}, bf16[256,1280]{1,0:T(8,128)(2,1)S(1)}, u32[]{:S(2)}, u32[]{:S(2)}) collective-permute-start(bf16[256,1280]{1,0:T(8,128)(2,1)S(1)} %collective-permute-done.13), channel_id=1, source_target_pairs={{0,32},{32,64},{64,96},{96,128},{128,160},{160,192},{192,224},{224... | collective-permute-start | bytes 1966088 | tf_op jit(solution)/shard_map/ppermute | solution.py:162
  90.3 0.3 fusion.13
  90.9 1.4 collective-permute-done.16
  92.2 5.0 %collective-permute-start.18 = (bf16[256,1280]{1,0:T(8,128)(2,1)S(1)}, bf16[256,1280]{1,0:T(8,128)(2,1)S(1)}, u32[]{:S(2)}, u32[]{:S(2)}) collective-permute-start(bf16[256,1280]{1,0:T(8,128)(2,1)S(1)} %collective-permute-done.16), channel_id=1, source_target_pairs={{0,32},{32,64},{64,96},{96,128},{128,160},{160,192},{192,224},{224... | collective-permute-start | bytes 1966088 | tf_op jit(solution)/shard_map/ppermute | solution.py:162
  97.3 0.3 fusion.14
  97.6 1.7 collective-permute-done.15
  99.3 5.0 %collective-permute-start.17 = (bf16[256,1280]{1,0:T(8,128)(2,1)S(1)}, bf16[256,1280]{1,0:T(8,128)(2,1)S(1)}, u32[]{:S(2)}, u32[]{:S(2)}) collective-permute-start(bf16[256,1280]{1,0:T(8,128)(2,1)S(1)} %collective-permute-done.15), channel_id=1, source_target_pairs={{0,32},{32,64},{64,96},{96,128},{128,160},{160,192},{192,224},{224... | collective-permute-start | bytes 1966088 | tf_op jit(solution)/shard_map/ppermute | solution.py:162
  104.3 0.3 fusion.23
  104.6 0.3 fusion.15
  104.9 1.4 collective-permute-done.18
  106.6 6.7 %collective-permute-done.17 = bf16[256,1280]{1,0:T(8,128)(2,1)S(1)} collective-permute-done((bf16[256,1280]{1,0:T(8,128)(2,1)S(1)}, bf16[256,1280]{1,0:T(8,128)(2,1)S(1)}, u32[]{:S(2)}, u32[]{:S(2)}) %collective-permute-start.17) | collective-permute-done | bytes 655392 | tf_op jit(solution)/shard_map/ppermute | solution.py:162
  113.3 0.4 fusion.63
  113.7 0.5 copy-done.10
  114.2 0.6 multiply_reduce_fusion
  114.8 3.9 %collective-permute-start.19 = (f32[8,192]{1,0:T(8,128)S(1)}, f32[8,192]{1,0:T(8,128)S(1)}, u32[]{:S(2)}, u32[]{:S(2)}) collective-permute-start(f32[8,192]{1,0:T(8,128)S(1)} %stack.50), channel_id=1, source_target_pairs={{0,256},{256,0},{1,257},{257,1},{2,258},{258,2},{3,259},{259,3},{4... | collective-permute-start | bytes 18440 | tf_op jit(solution)/shard_map/ppermute | solution.py:21
  118.7 0.7 broadcast_maximum_fusion
  119.4 1.9 %collective-permute-start.3 = (f32[8,128]{1,0:T(8,128)S(1)}, f32[8,128]{1,0:T(8,128)S(1)}, u32[]{:S(2)}, u32[]{:S(2)}) collective-permute-start(f32[8,128]{1,0:T(8,128)S(1)} %broadcast_maximum_fusion), channel_id=1, source_target_pairs={{0,64},{32,96},{64,0},{96,32},{128,192},{160,224},{192,128},{224,1... | collective-permute-start | bytes 12296 | tf_op jit(solution)/shard_map/ppermute | solution.py:148
  121.4 0.7 broadcast_in_dim.98
  122.2 9.7 %all-to-all-start.2 = ((f32[32,8,192]{2,1,0:T(8,128)}), f32[32,8,192]{2,1,0:T(8,128)S(1)}, u32[]{:S(2)}, u32[]{:S(2)}) async-start(f32[32,8,192]{2,1,0:T(8,128)} %broadcast_in_dim.98), calls=%async_computation.2 | async-start | bytes 524288 | tf_op jit(solution)/shard_map/all_to_all | solution.py:182
  132.0 0.7 fusion.84
  132.6 5.7 %collective-permute-start.4 = (f32[8,128]{1,0:T(8,128)S(1)}, f32[8,128]{1,0:T(8,128)S(1)}, u32[]{:S(2)}, u32[]{:S(2)}) collective-permute-start(f32[8,128]{1,0:T(8,128)S(1)} %fusion.84), channel_id=1, source_target_pairs={{0,128},{32,160},{64,192},{96,224},{128,0},{160,32},{192,64},{224,... | collective-permute-start | bytes 12296 | tf_op jit(solution)/shard_map/ppermute | solution.py:148
  138.4 2.8 %collective-permute-done.4 = f32[8,128]{1,0:T(8,128)S(1)} collective-permute-done((f32[8,128]{1,0:T(8,128)S(1)}, f32[8,128]{1,0:T(8,128)S(1)}, u32[]{:S(2)}, u32[]{:S(2)}) %collective-permute-start.4) | collective-permute-done | bytes 4128 | tf_op jit(solution)/shard_map/ppermute | solution.py:148
  141.2 0.5 slice.47
  142.4 1.5 all-to-all-done.2
  143.8 37.0 %conditional.3 = (f32[12]{0:T(128)}, bf16[192,64]{0,1:T(8,128)(2,1)}) conditional(s32[]{:T(128)} %bitcast.8, (f32[192]{0:T(256)S(1)}, s32[2]{0:T(128)S(1)}, f32[32,8,192]{2,1,0:T(8,128)S(1)}, f32[192,1280]{1,0:T(8,128)S(1)}, bf16[192,1280]{1,0:T(8,128)(2,1)S(1)}, /*index=5*/bf16[512,1280]{1,0:T(8,128)(2,1)}, bf16[256,1280]{1,0:T(8,128)(2,1)}, ...), branch_computations={%region_13.17_spmd, %region_17.21_spmd} | conditional | flops 2019704960 | bytes 20125838
  143.8 5.8 %branch_1_fun.1 = (f32[2,32,64,128]{3,2,1,0:T(8,128)S(1)}, bf16[32,64,128]{2,1,0:T(8,128)(2,1)S(1)}, f32[1,128]{1,0:T(1,128)S(1)}) custom-call(s32[2]{0:T(128)S(1)} %get-tuple-element.118.place_ref, f32[32,8,192]{2,1,0:T(8,128)S(1)} %get-tuple-element.119.stats_ref, f32[1,192]{1,0:T(1,128)S(1)} %bitcast.54, f32[192,1280]{1,0:T(8,128)S(1)} %get-tuple-element.120.logits_ref, ...), custom_call_target="tpu_custom_call" | custom-call | flops 1342177280 | bytes 10485760 | tf_op jit(solution)/shard_map/cond/branch_1_fun/pallas_call | solution.py:102
  149.7 3.9 %collective-permute-start = (bf16[32,64,128]{2,1,0:T(8,128)(2,1)S(1)}, bf16[32,64,128]{2,1,0:T(8,128)(2,1)S(1)}, u32[]{:S(2)}, u32[]{:S(2)}) collective-permute-start(bf16[32,64,128]{2,1,0:T(8,128)(2,1)S(1)} %get-tuple-element.139), channel_id=1, source_target_pairs={{0,256},{256,0},{1,257},{257,1},{2,258},{258,2},{3,259},{259,3},{4... | collective-permute-start | bytes 1572872 | tf_op jit(solution)/shard_map/cond/branch_1_fun/ppermute | solution.py:21
  153.6 1.5 collective-permute-done
  155.1 1.0 fusion.9
  156.1 7.4 %all-to-all-start = ((bf16[32,64,128]{2,1,0:T(8,128)(2,1)}), bf16[32,64,128]{2,1,0:T(8,128)(2,1)S(1)}, u32[]{:S(2)}, u32[]{:S(2)}) async-start(bf16[32,64,128]{2,1,0:T(8,128)(2,1)} %fusion.9), calls=%async_computation | async-start | bytes 1048576 | tf_op jit(solution)/shard_map/cond/branch_1_fun/all_to_all | solution.py:191
  163.7 0.6 reduce_sum.146
  164.3 15.7 %all-to-all-done = bf16[32,64,128]{2,1,0:T(8,128)(2,1)S(1)} async-done(((bf16[32,64,128]{2,1,0:T(8,128)(2,1)}), bf16[32,64,128]{2,1,0:T(8,128)(2,1)S(1)}, u32[]{:S(2)}, u32[]{:S(2)}) %all-to-all-start) | async-done | bytes 524320 | tf_op jit(solution)/shard_map/cond/branch_1_fun/all_to_all | solution.py:191
  180.1 0.8 fusion.8
  (68 shorter events, 3.0 us)
Async XLA Ops:
  0.6 34.2 %copy-start = (bf16[192,4096]{1,0:T(8,128)(2,1)S(1)}, bf16[192,4096]{1,0:T(8,128)(2,1)}, u32[]{:S(2)}) copy-start(bf16[192,4096]{1,0:T(8,128)(2,1)} %param.8) | copy-start | bytes 4718596
  0.6 16.1 %copy-start.16 = (s32[96]{0:T(128)S(1)}, s32[96]{0:T(128)}, u32[]{:S(2)}) copy-start(s32[96]{0:T(128)} %param.12) | copy-start | bytes 1156
  0.7 16.1 %copy-start.17 = (s32[96]{0:T(128)S(1)}, s32[96]{0:T(128)}, u32[]{:S(2)}) copy-start(s32[96]{0:T(128)} %param.11) | copy-start | bytes 1156
  0.7 16.5 %copy-start.15 = (s32[192]{0:T(256)S(1)}, s32[192]{0:T(256)}, u32[]{:S(2)}) copy-start(s32[192]{0:T(256)} %param.13) | copy-start | bytes 2308
  3.0 19.0 %collective-permute-start.6 = (bf16[256,1280]{1,0:T(8,128)(2,1)S(1)}, bf16[256,1280]{1,0:T(8,128)(2,1)S(1)}, u32[]{:S(2)}, u32[]{:S(2)}) collective-permute-start(bf16[256,1280]{1,0:T(8,128)(2,1)S(1)} %get-tuple-element.161), channel_id=1, source_target_pairs={{0,32},{32,64},{64,96},{96,128},{128,160},{160,192},{192,224},{224... | collective-permute-start | bytes 1966088 | tf_op jit(solution)/shard_map/ppermute | solution.py:162
  14.5 14.6 %collective-permute-start.5 = (bf16[256,1280]{1,0:T(8,128)(2,1)}, bf16[256,1280]{1,0:T(8,128)(2,1)}, u32[]{:S(2)}, u32[]{:S(2)}) collective-permute-start(bf16[256,1280]{1,0:T(8,128)(2,1)} %get-tuple-element.160), channel_id=1, source_target_pairs={{0,32},{32,64},{64,96},{96,128},{128,160},{160,192},{192,224},{224... | collective-permute-start | bytes 1966088 | tf_op jit(solution)/shard_map/ppermute | solution.py:162
  18.4 100.3 %collective-permute-start.2 = (f32[8,128]{1,0:T(8,128)S(1)}, f32[8,128]{1,0:T(8,128)S(1)}, u32[]{:S(2)}, u32[]{:S(2)}) collective-permute-start(f32[8,128]{1,0:T(8,128)S(1)} %broadcast_in_dim.94), channel_id=1, source_target_pairs={{0,32},{32,0},{64,96},{96,64},{128,160},{160,128},{192,224},{224,1... | collective-permute-start | bytes 12296 | tf_op jit(solution)/shard_map/ppermute | solution.py:148
  22.0 14.6 %copy-start.8 = (bf16[256,1280]{1,0:T(8,128)(2,1)}, bf16[256,1280]{1,0:T(8,128)(2,1)S(1)}, u32[]{:S(2)}) copy-start(bf16[256,1280]{1,0:T(8,128)(2,1)S(1)} %collective-permute-done.6) | copy-start | bytes 1966084
  22.0 14.6 %collective-permute-start.8 = (bf16[256,1280]{1,0:T(8,128)(2,1)S(1)}, bf16[256,1280]{1,0:T(8,128)(2,1)S(1)}, u32[]{:S(2)}, u32[]{:S(2)}) collective-permute-start(bf16[256,1280]{1,0:T(8,128)(2,1)S(1)} %collective-permute-done.6), channel_id=1, source_target_pairs={{0,32},{32,64},{64,96},{96,128},{128,160},{160,192},{192,224},{224... | collective-permute-start | bytes 1966088 | tf_op jit(solution)/shard_map/ppermute | solution.py:162
  29.2 14.0 %collective-permute-start.7 = (bf16[256,1280]{1,0:T(8,128)(2,1)}, bf16[256,1280]{1,0:T(8,128)(2,1)}, u32[]{:S(2)}, u32[]{:S(2)}) collective-permute-start(bf16[256,1280]{1,0:T(8,128)(2,1)} %collective-permute-done.5), channel_id=1, source_target_pairs={{0,32},{32,64},{64,96},{96,128},{128,160},{160,192},{192,224},{224... | collective-permute-start | bytes 1966088 | tf_op jit(solution)/shard_map/ppermute | solution.py:162
  34.8 6.3 %copy-start.14 = (bf16[192,1280]{1,0:T(8,128)(2,1)S(1)}, bf16[192,1280]{1,0:T(8,128)(2,1)}, u32[]{:S(2)}) copy-start(bf16[192,1280]{1,0:T(8,128)(2,1)} %param.10) | copy-start | bytes 1474564
  36.6 26.0 %copy-start.2 = (bf16[256,1280]{1,0:T(8,128)(2,1)}, bf16[256,1280]{1,0:T(8,128)(2,1)S(1)}, u32[]{:S(2)}) copy-start(bf16[256,1280]{1,0:T(8,128)(2,1)S(1)} %collective-permute-done.8) | copy-start | bytes 1966084
  36.6 13.9 %collective-permute-start.10 = (bf16[256,1280]{1,0:T(8,128)(2,1)S(1)}, bf16[256,1280]{1,0:T(8,128)(2,1)S(1)}, u32[]{:S(2)}, u32[]{:S(2)}) collective-permute-start(bf16[256,1280]{1,0:T(8,128)(2,1)S(1)} %collective-permute-done.8), channel_id=1, source_target_pairs={{0,32},{32,64},{64,96},{96,128},{128,160},{160,192},{192,224},{224... | collective-permute-start | bytes 1966088 | tf_op jit(solution)/shard_map/ppermute | solution.py:162
  43.2 14.0 %collective-permute-start.9 = (bf16[256,1280]{1,0:T(8,128)(2,1)}, bf16[256,1280]{1,0:T(8,128)(2,1)}, u32[]{:S(2)}, u32[]{:S(2)}) collective-permute-start(bf16[256,1280]{1,0:T(8,128)(2,1)} %collective-permute-done.7), channel_id=1, source_target_pairs={{0,32},{32,64},{64,96},{96,128},{128,160},{160,192},{192,224},{224... | collective-permute-start | bytes 1966088 | tf_op jit(solution)/shard_map/ppermute | solution.py:162
  48.5 6.6 %copy-start.1 = (bf16[192,4096]{1,0:T(8,128)(2,1)S(1)}, bf16[192,4096]{1,0:T(8,128)(2,1)}, u32[]{:S(2)}) copy-start(bf16[192,4096]{1,0:T(8,128)(2,1)} %convolution_convert_fusion.2) | copy-start | bytes 4718596
  50.5 11.7 %copy-start.9 = (bf16[256,1280]{1,0:T(8,128)(2,1)S(1)}, bf16[256,1280]{1,0:T(8,128)(2,1)}, u32[]{:S(2)}) copy-start(bf16[256,1280]{1,0:T(8,128)(2,1)} %copy-done.8) | copy-start | bytes 1966084
  50.5 25.7 %copy-start.3 = (bf16[256,1280]{1,0:T(8,128)(2,1)}, bf16[256,1280]{1,0:T(8,128)(2,1)S(1)}, u32[]{:S(2)}) copy-start(bf16[256,1280]{1,0:T(8,128)(2,1)S(1)} %collective-permute-done.10) | copy-start | bytes 1966084
  50.5 13.6 %collective-permute-start.12 = (bf16[256,1280]{1,0:T(8,128)(2,1)S(1)}, bf16[256,1280]{1,0:T(8,128)(2,1)S(1)}, u32[]{:S(2)}, u32[]{:S(2)}) collective-permute-start(bf16[256,1280]{1,0:T(8,128)(2,1)S(1)} %collective-permute-done.10), channel_id=1, source_target_pairs={{0,32},{32,64},{64,96},{96,128},{128,160},{160,192},{192,224},{224... | collective-permute-start | bytes 1966088 | tf_op jit(solution)/shard_map/ppermute | solution.py:162
  57.2 14.0 %collective-permute-start.11 = (bf16[256,1280]{1,0:T(8,128)(2,1)}, bf16[256,1280]{1,0:T(8,128)(2,1)S(1)}, u32[]{:S(2)}, u32[]{:S(2)}) collective-permute-start(bf16[256,1280]{1,0:T(8,128)(2,1)} %collective-permute-done.9), channel_id=1, source_target_pairs={{0,32},{32,64},{64,96},{96,128},{128,160},{160,192},{192,224},{224... | collective-permute-start | bytes 1966088 | tf_op jit(solution)/shard_map/ppermute | solution.py:162
  64.2 19.1 %copy-start.4 = (bf16[256,1280]{1,0:T(8,128)(2,1)}, bf16[256,1280]{1,0:T(8,128)(2,1)S(1)}, u32[]{:S(2)}) copy-start(bf16[256,1280]{1,0:T(8,128)(2,1)S(1)} %collective-permute-done.12) | copy-start | bytes 1966084
  64.2 14.0 %collective-permute-start.14 = (bf16[256,1280]{1,0:T(8,128)(2,1)S(1)}, bf16[256,1280]{1,0:T(8,128)(2,1)S(1)}, u32[]{:S(2)}, u32[]{:S(2)}) collective-permute-start(bf16[256,1280]{1,0:T(8,128)(2,1)S(1)} %collective-permute-done.12), channel_id=1, source_target_pairs={{0,32},{32,64},{64,96},{96,128},{128,160},{160,192},{192,224},{224... | collective-permute-start | bytes 1966088 | tf_op jit(solution)/shard_map/ppermute | solution.py:162
  71.3 19.0 %copy-start.11 = (bf16[256,1280]{1,0:T(8,128)(2,1)}, bf16[256,1280]{1,0:T(8,128)(2,1)S(1)}, u32[]{:S(2)}) copy-start(bf16[256,1280]{1,0:T(8,128)(2,1)S(1)} %collective-permute-done.11) | copy-start | bytes 1966084
  71.3 13.9 %collective-permute-start.13 = (bf16[256,1280]{1,0:T(8,128)(2,1)S(1)}, bf16[256,1280]{1,0:T(8,128)(2,1)S(1)}, u32[]{:S(2)}, u32[]{:S(2)}) collective-permute-start(bf16[256,1280]{1,0:T(8,128)(2,1)S(1)} %collective-permute-done.11), channel_id=1, source_target_pairs={{0,32},{32,64},{64,96},{96,128},{128,160},{160,192},{192,224},{224... | collective-permute-start | bytes 1966088 | tf_op jit(solution)/shard_map/ppermute | solution.py:162
  78.2 12.4 %copy-start.5 = (bf16[256,1280]{1,0:T(8,128)(2,1)}, bf16[256,1280]{1,0:T(8,128)(2,1)S(1)}, u32[]{:S(2)}) copy-start(bf16[256,1280]{1,0:T(8,128)(2,1)S(1)} %collective-permute-done.14) | copy-start | bytes 1966084
  78.2 14.0 %collective-permute-start.16 = (bf16[256,1280]{1,0:T(8,128)(2,1)S(1)}, bf16[256,1280]{1,0:T(8,128)(2,1)S(1)}, u32[]{:S(2)}, u32[]{:S(2)}) collective-permute-start(bf16[256,1280]{1,0:T(8,128)(2,1)S(1)} %collective-permute-done.14), channel_id=1, source_target_pairs={{0,32},{32,64},{64,96},{96,128},{128,160},{160,192},{192,224},{224... | collective-permute-start | bytes 1966088 | tf_op jit(solution)/shard_map/ppermute | solution.py:162
  85.2 12.0 %copy-start.12 = (bf16[256,1280]{1,0:T(8,128)(2,1)}, bf16[256,1280]{1,0:T(8,128)(2,1)S(1)}, u32[]{:S(2)}) copy-start(bf16[256,1280]{1,0:T(8,128)(2,1)S(1)} %collective-permute-done.13) | copy-start | bytes 1966084
  85.2 14.0 %collective-permute-start.15 = (bf16[256,1280]{1,0:T(8,128)(2,1)S(1)}, bf16[256,1280]{1,0:T(8,128)(2,1)S(1)}, u32[]{:S(2)}, u32[]{:S(2)}) collective-permute-start(bf16[256,1280]{1,0:T(8,128)(2,1)S(1)} %collective-permute-done.13), channel_id=1, source_target_pairs={{0,32},{32,64},{64,96},{96,128},{128,160},{160,192},{192,224},{224... | collective-permute-start | bytes 1966088 | tf_op jit(solution)/shard_map/ppermute | solution.py:162
  92.2 12.0 %copy-start.6 = (bf16[256,1280]{1,0:T(8,128)(2,1)}, bf16[256,1280]{1,0:T(8,128)(2,1)S(1)}, u32[]{:S(2)}) copy-start(bf16[256,1280]{1,0:T(8,128)(2,1)S(1)} %collective-permute-done.16) | copy-start | bytes 1966084
  92.2 14.0 %collective-permute-start.18 = (bf16[256,1280]{1,0:T(8,128)(2,1)S(1)}, bf16[256,1280]{1,0:T(8,128)(2,1)S(1)}, u32[]{:S(2)}, u32[]{:S(2)}) collective-permute-start(bf16[256,1280]{1,0:T(8,128)(2,1)S(1)} %collective-permute-done.16), channel_id=1, source_target_pairs={{0,32},{32,64},{64,96},{96,128},{128,160},{160,192},{192,224},{224... | collective-permute-start | bytes 1966088 | tf_op jit(solution)/shard_map/ppermute | solution.py:162
  99.3 5.7 %copy-start.13 = (bf16[256,1280]{1,0:T(8,128)(2,1)}, bf16[256,1280]{1,0:T(8,128)(2,1)S(1)}, u32[]{:S(2)}) copy-start(bf16[256,1280]{1,0:T(8,128)(2,1)S(1)} %collective-permute-done.15) | copy-start | bytes 1966084
  99.3 14.0 %collective-permute-start.17 = (bf16[256,1280]{1,0:T(8,128)(2,1)S(1)}, bf16[256,1280]{1,0:T(8,128)(2,1)S(1)}, u32[]{:S(2)}, u32[]{:S(2)}) collective-permute-start(bf16[256,1280]{1,0:T(8,128)(2,1)S(1)} %collective-permute-done.15), channel_id=1, source_target_pairs={{0,32},{32,64},{64,96},{96,128},{128,160},{160,192},{192,224},{224... | collective-permute-start | bytes 1966088 | tf_op jit(solution)/shard_map/ppermute | solution.py:162
  106.3 7.4 %copy-start.7 = (bf16[256,1280]{1,0:T(8,128)(2,1)}, bf16[256,1280]{1,0:T(8,128)(2,1)S(1)}, u32[]{:S(2)}) copy-start(bf16[256,1280]{1,0:T(8,128)(2,1)S(1)} %collective-permute-done.18) | copy-start | bytes 1966084
  113.3 0.9 copy-start.10
  114.8 6.5 %collective-permute-start.19 = (f32[8,192]{1,0:T(8,128)S(1)}, f32[8,192]{1,0:T(8,128)S(1)}, u32[]{:S(2)}, u32[]{:S(2)}) collective-permute-start(f32[8,192]{1,0:T(8,128)S(1)} %stack.50), channel_id=1, source_target_pairs={{0,256},{256,0},{1,257},{257,1},{2,258},{258,2},{3,259},{259,3},{4... | collective-permute-start | bytes 18440 | tf_op jit(solution)/shard_map/ppermute | solution.py:21
  119.4 12.6 %collective-permute-start.3 = (f32[8,128]{1,0:T(8,128)S(1)}, f32[8,128]{1,0:T(8,128)S(1)}, u32[]{:S(2)}, u32[]{:S(2)}) collective-permute-start(f32[8,128]{1,0:T(8,128)S(1)} %broadcast_maximum_fusion), channel_id=1, source_target_pairs={{0,64},{32,96},{64,0},{96,32},{128,192},{160,224},{192,128},{224,1... | collective-permute-start | bytes 12296 | tf_op jit(solution)/shard_map/ppermute | solution.py:148
  122.2 21.7 %all-to-all-start.2 = ((f32[32,8,192]{2,1,0:T(8,128)}), f32[32,8,192]{2,1,0:T(8,128)S(1)}, u32[]{:S(2)}, u32[]{:S(2)}) async-start(f32[32,8,192]{2,1,0:T(8,128)} %broadcast_in_dim.98), calls=%async_computation.2 | async-start | bytes 524288 | tf_op jit(solution)/shard_map/all_to_all | solution.py:182
  132.6 8.6 %collective-permute-start.4 = (f32[8,128]{1,0:T(8,128)S(1)}, f32[8,128]{1,0:T(8,128)S(1)}, u32[]{:S(2)}, u32[]{:S(2)}) collective-permute-start(f32[8,128]{1,0:T(8,128)S(1)} %fusion.84), channel_id=1, source_target_pairs={{0,128},{32,160},{64,192},{96,224},{128,0},{160,32},{192,64},{224,... | collective-permute-start | bytes 12296 | tf_op jit(solution)/shard_map/ppermute | solution.py:148
  149.7 5.4 %collective-permute-start = (bf16[32,64,128]{2,1,0:T(8,128)(2,1)S(1)}, bf16[32,64,128]{2,1,0:T(8,128)(2,1)S(1)}, u32[]{:S(2)}, u32[]{:S(2)}) collective-permute-start(bf16[32,64,128]{2,1,0:T(8,128)(2,1)S(1)} %get-tuple-element.139), channel_id=1, source_target_pairs={{0,256},{256,0},{1,257},{257,1},{2,258},{258,2},{3,259},{259,3},{4... | collective-permute-start | bytes 1572872 | tf_op jit(solution)/shard_map/cond/branch_1_fun/ppermute | solution.py:21
  156.1 24.0 %all-to-all-start = ((bf16[32,64,128]{2,1,0:T(8,128)(2,1)}), bf16[32,64,128]{2,1,0:T(8,128)(2,1)S(1)}, u32[]{:S(2)}, u32[]{:S(2)}) async-start(bf16[32,64,128]{2,1,0:T(8,128)(2,1)} %fusion.9), calls=%async_computation | async-start | bytes 1048576 | tf_op jit(solution)/shard_map/cond/branch_1_fun/all_to_all | solution.py:191

commit v11 on v10

--- a/solution.py
+++ b/solution.py
@@ -144,9 +144,6 @@
     teacher_logits = jnp.dot(pick_low, teacher_logits, preferred_element_type=jnp.float32).astype(jnp.bfloat16)
     weight = jnp.sum(jnp.where(pick, weight[None, :], 0.0), axis=1)
     most = jnp.full((8, LANES), jnp.sum(inside.astype(jnp.float32)))
-    for apart in (1 << bit for bit in range((blocks - 1).bit_length())):
-        most = jnp.maximum(most, lax.ppermute(most, "row", [(i, i ^ apart) for i in range(blocks)]))
-    fits = most[0, 0] <= FEW
 
     full = head.shape[0]
     depth = full // HALVES
@@ -160,6 +157,10 @@
     chunks = []
     for distance in range(1, blocks):
         held = [lax.ppermute(part, ("side", "row"), ring) for part in held]
+        apart = 1 << (distance // 2 - 1) if distance % 2 == 0 else blocks
+        if apart < blocks:
+            most = jnp.maximum(most, lax.ppermute(most, "row", [(i, i ^ apart) for i in range(blocks)]))
+            held[0], most = lax.optimization_barrier((held[0], most))
         owner = (row_place - distance * step + blocks) % blocks
         for part in range(HALVES):
             piece = lax.dynamic_slice_in_dim(hidden, owner * full + part * depth, depth, axis=1)
@@ -200,6 +201,7 @@
         loss = jnp.sum(jnp.where(some, (weight[:toks] * diverge[0])[:, None], 0.0), axis=0)
         return jnp.sum(loss.reshape(slot_count, WIN), axis=1), block.T
 
+    fits = most[0, 0] <= FEW
     stats, weight, pick = lax.optimization_barrier((stats, weight, pick))
     return lax.cond(
         fits,

time: 182 us -> 182 us (level)
  starting transfers between devices: 108 us -> 86.1 us
  waiting for transfers between devices: 40.8 us -> 59.8 us
  matrix products: 12.4 us -> 16.9 us
    ppermute x14, starting transfers between devices: 72.8 us -> 55.7 us  [body(): held = [lax.ppermute(part, ('side', 'row'), ring) for part in held]]
    all_to_all x1, waiting for transfers between devices: 1.49 us -> 10.2 us  [body(): lax.all_to_all(jnp.broadcast_to(pair, (count,) + pair.shape), 'vocab', 0, 0)]
    ppermute x14, waiting for transfers between devices: 19.3 us -> 27.2 us  [body(): held = [lax.ppermute(part, ('side', 'row'), ring) for part in held]]
    all_to_all x1, starting transfers between devices: 7.39 us -> 3.89 us  [finish(): pieces = lax.all_to_all(packed, 'vocab', 0, 0)]
    dot_general x14, matrix products: 7.6 us -> 10.1 us  [body(): jnp.dot(piece, held[part], preferred_element_type=jnp.float32)]
    ppermute x3, starting transfers between devices: 10.7 us -> 8.26 us  [body(): lax.ppermute(most, 'row', [(i, i ^ apart) for i in range(blocks)])]
  transfers between devices with their start and end apart: 21 -> 21, of which waited for: 16 -> 15; matrix products, arithmetic and copies ran while one was open for 11% -> 12% of each run, Pallas kernels for 0% -> 0%
where the time goes in v11:
time: 182 us; the launch traced here: 180 us
  starting transfers between devices  86.1 us (47%)
  waiting for transfers between devices  59.8 us (33%)
  matrix products  16.9 us (9%)
  Pallas kernels  5.81 us (3%)
  other arithmetic  5.49 us (3%)
  local copies, waits for them, and re-layouts  4.07 us (2%)
  between operations  2.03 us (1%)
    ppermute x14, starting transfers between devices, body(): held = [lax.ppermute(part, ('side', 'row'), ring) for part in held]  55.7 us
    ppermute x14, waiting for transfers between devices, body(): held = [lax.ppermute(part, ('side', 'row'), ring) for part in held]  27.2 us
    all_to_all x1, waiting for transfers between devices, finish(): pieces = lax.all_to_all(packed, 'vocab', 0, 0)  15.8 us
    all_to_all x1, waiting for transfers between devices, body(): lax.all_to_all(jnp.broadcast_to(pair, (count,) + pair.shape), 'vocab', 0, 0)  10.2 us
    dot_general x14, matrix products, body(): jnp.dot(piece, held[part], preferred_element_type=jnp.float32)  10.1 us
    all_to_all x1, starting transfers between devices, body(): lax.all_to_all(jnp.broadcast_to(pair, (count,) + pair.shape), 'vocab', 0, 0)  9.67 us
    ppermute x2, starting transfers between devices, swap_side(): return lax.ppermute(value, 'side', [(0, 1), (1, 0)])  8.66 us
    ppermute x3, starting transfers between devices, body(): lax.ppermute(most, 'row', [(i, i ^ apart) for i in range(blocks)])  8.26 us
  transfers between devices with their start and end apart: 21, of which 15 were waited for; matrix products, arithmetic and copies ran while one was open for 12% of the time, Pallas kernels for 0%

profile of v11, /device:TPU:1, one launch (start us, length us, event | category | flops | bytes accessed | tf_op | source)
XLA Modules:
  0.0 180.3 jit_solution(3022565441430808155)
XLA Ops:
  0.7 1.5 fusion.61
  2.2 11.5 %collective-permute-start.2 = (bf16[256,1280]{1,0:T(8,128)(2,1)S(1)}, bf16[256,1280]{1,0:T(8,128)(2,1)}, u32[]{:S(2)}, u32[]{:S(2)}) collective-permute-start(bf16[256,1280]{1,0:T(8,128)(2,1)S(1)} %get-tuple-element.173), channel_id=1, source_target_pairs={{0,32},{32,64},{64,96},{96,128},{128,160},{160,192},{192,224},{224... | collective-permute-start | bytes 1966088 | tf_op jit(solution)/shard_map/ppermute | solution.py:159
  13.7 2.2 %collective-permute-start.11 = (bf16[256,1280]{1,0:T(8,128)(2,1)S(1)}, bf16[256,1280]{1,0:T(8,128)(2,1)}, u32[]{:S(2)}, u32[]{:S(2)}) collective-permute-start(bf16[256,1280]{1,0:T(8,128)(2,1)S(1)} %get-tuple-element.172), channel_id=1, source_target_pairs={{0,32},{32,64},{64,96},{96,128},{128,160},{160,192},{192,224},{224... | collective-permute-start | bytes 1966088 | tf_op jit(solution)/shard_map/ppermute | solution.py:159
  16.3 4.9 %collective-permute-done.2 = bf16[256,1280]{1,0:T(8,128)(2,1)} collective-permute-done((bf16[256,1280]{1,0:T(8,128)(2,1)S(1)}, bf16[256,1280]{1,0:T(8,128)(2,1)}, u32[]{:S(2)}, u32[]{:S(2)}) %collective-permute-start.2) | collective-permute-done | bytes 655392 | tf_op jit(solution)/shard_map/ppermute | solution.py:159
  21.2 5.1 %collective-permute-start.3 = (bf16[256,1280]{1,0:T(8,128)(2,1)}, bf16[256,1280]{1,0:T(8,128)(2,1)S(1)}, u32[]{:S(2)}, u32[]{:S(2)}) collective-permute-start(bf16[256,1280]{1,0:T(8,128)(2,1)} %collective-permute-done.2), channel_id=1, source_target_pairs={{0,32},{32,64},{64,96},{96,128},{128,160},{160,192},{192,224},{224... | collective-permute-start | bytes 1966088 | tf_op jit(solution)/shard_map/ppermute | solution.py:159
  26.3 0.6 convert_reduce_fusion.2
  26.9 0.6 broadcast_in_dim.94
  27.6 1.9 %collective-permute-start.4 = (f32[8,128]{1,0:T(8,128)S(1)}, f32[8,128]{1,0:T(8,128)S(1)}, u32[]{:S(2)}, u32[]{:S(2)}) collective-permute-start(f32[8,128]{1,0:T(8,128)S(1)} %broadcast_in_dim.94), channel_id=1, source_target_pairs={{0,32},{32,0},{64,96},{96,64},{128,160},{160,128},{192,224},{224,1... | collective-permute-start | bytes 12296 | tf_op jit(solution)/shard_map/ppermute | solution.py:162
  29.5 3.8 %collective-permute-start.12 = (bf16[256,1280]{1,0:T(8,128)(2,1)}, bf16[256,1280]{1,0:T(8,128)(2,1)S(1)}, u32[]{:S(2)}, u32[]{:S(2)}) collective-permute-start(bf16[256,1280]{1,0:T(8,128)(2,1)} %collective-permute-done.11), channel_id=1, source_target_pairs={{0,32},{32,64},{64,96},{96,128},{128,160},{160,192},{192,224},{224... | collective-permute-start | bytes 1966088 | tf_op jit(solution)/shard_map/ppermute | solution.py:159
  33.4 0.6 convert_reduce_fusion.1
  34.1 0.6 broadcast_maximum_fusion
  34.7 0.6 collective-permute-done.3
  35.3 4.9 %collective-permute-start.5 = (bf16[256,1280]{1,0:T(8,128)(2,1)S(1)}, bf16[256,1280]{1,0:T(8,128)(2,1)}, u32[]{:S(2)}, u32[]{:S(2)}) collective-permute-start(bf16[256,1280]{1,0:T(8,128)(2,1)S(1)} %collective-permute-done.3), channel_id=1, source_target_pairs={{0,32},{32,64},{64,96},{96,128},{128,160},{160,192},{192,224},{224... | collective-permute-start | bytes 1966088 | tf_op jit(solution)/shard_map/ppermute | solution.py:159
  40.2 0.6 subtract_select_fusion
  40.9 1.5 collective-permute-done.12
  42.4 4.9 %collective-permute-start.13 = (bf16[256,1280]{1,0:T(8,128)(2,1)S(1)}, bf16[256,1280]{1,0:T(8,128)(2,1)}, u32[]{:S(2)}, u32[]{:S(2)}) collective-permute-start(bf16[256,1280]{1,0:T(8,128)(2,1)S(1)} %collective-permute-done.12), channel_id=1, source_target_pairs={{0,32},{32,64},{64,96},{96,128},{128,160},{160,192},{192,224},{224... | collective-permute-start | bytes 1966088 | tf_op jit(solution)/shard_map/ppermute | solution.py:159
  47.3 1.8 convolution_convert_fusion.2
  49.0 2.8 %fusion.17 = f32[192,1280]{1,0:T(8,128)} fusion(bf16[512,1280]{1,0:T(8,128)(2,1)} %param.9, bf16[192,4096]{1,0:T(8,128)(2,1)} %convolution_convert_fusion.2, s32[]{:T(128)S(6)} %select_n.113), kind=kOutput, calls=%fused_computation.39 | convolution fusion | flops 251658240 | bytes 2490372 | tf_op jit(solution)/shard_map/dot_general | solution.py:154
  51.9 2.5 %collective-permute-start.6 = (bf16[256,1280]{1,0:T(8,128)(2,1)}, bf16[256,1280]{1,0:T(8,128)(2,1)}, u32[]{:S(2)}, u32[]{:S(2)}) collective-permute-start(bf16[256,1280]{1,0:T(8,128)(2,1)} %collective-permute-done.5), channel_id=1, source_target_pairs={{0,32},{32,64},{64,96},{96,128},{128,160},{160,192},{192,224},{224... | collective-permute-start | bytes 1966088 | tf_op jit(solution)/shard_map/ppermute | solution.py:159
  54.4 1.4 fusion.64
  56.3 5.1 %collective-permute-start.14 = (bf16[256,1280]{1,0:T(8,128)(2,1)}, bf16[256,1280]{1,0:T(8,128)(2,1)S(1)}, u32[]{:S(2)}, u32[]{:S(2)}) collective-permute-start(bf16[256,1280]{1,0:T(8,128)(2,1)} %collective-permute-done.13), channel_id=1, source_target_pairs={{0,32},{32,64},{64,96},{96,128},{128,160},{160,192},{192,224},{224... | collective-permute-start | bytes 1966088 | tf_op jit(solution)/shard_map/ppermute | solution.py:159
  61.4 1.7 convolution_add_fusion.7
  63.2 1.9 %collective-permute-start.7 = (f32[8,128]{1,0:T(8,128)S(1)}, f32[8,128]{1,0:T(8,128)S(1)}, u32[]{:S(2)}, u32[]{:S(2)}) collective-permute-start(f32[8,128]{1,0:T(8,128)S(1)} %broadcast_maximum_fusion), channel_id=1, source_target_pairs={{0,64},{32,96},{64,0},{96,32},{128,192},{160,224},{192,128},{224,1... | collective-permute-start | bytes 12296 | tf_op jit(solution)/shard_map/ppermute | solution.py:162
  65.1 1.4 convolution_add_fusion.6
  66.5 4.3 %collective-permute-done.7 = f32[8,128]{1,0:T(8,128)S(1)} collective-permute-done((f32[8,128]{1,0:T(8,128)S(1)}, f32[8,128]{1,0:T(8,128)S(1)}, u32[]{:S(2)}, u32[]{:S(2)}) %collective-permute-start.7) | collective-permute-done | bytes 4128 | tf_op jit(solution)/shard_map/ppermute | solution.py:162
  70.8 1.9 %collective-permute-start.8 = (bf16[256,1280]{1,0:T(8,128)(2,1)}, bf16[256,1280]{1,0:T(8,128)(2,1)S(1)}, u32[]{:S(2)}, u32[]{:S(2)}) collective-permute-start(bf16[256,1280]{1,0:T(8,128)(2,1)} %collective-permute-done.6), channel_id=1, source_target_pairs={{0,32},{32,64},{64,96},{96,128},{128,160},{160,192},{192,224},{224... | collective-permute-start | bytes 1966088 | tf_op jit(solution)/shard_map/ppermute | solution.py:159
  72.8 0.3 fusion.35
  73.1 2.3 %collective-permute-start.15 = (bf16[256,1280]{1,0:T(8,128)(2,1)S(1)}, bf16[256,1280]{1,0:T(8,128)(2,1)S(1)}, u32[]{:S(2)}, u32[]{:S(2)}) collective-permute-start(bf16[256,1280]{1,0:T(8,128)(2,1)S(1)} %collective-permute-done.14), channel_id=1, source_target_pairs={{0,32},{32,64},{64,96},{96,128},{128,160},{160,192},{192,224},{224... | collective-permute-start | bytes 1966088 | tf_op jit(solution)/shard_map/ppermute | solution.py:159
  75.4 1.4 fusion.33
  76.8 0.3 fusion.16
  77.1 4.4 %collective-permute-start.10 = (f32[8,128]{1,0:T(8,128)S(1)}, f32[8,128]{1,0:T(8,128)S(1)}, u32[]{:S(2)}, u32[]{:S(2)}) collective-permute-start(f32[8,128]{1,0:T(8,128)S(1)} %max.10), channel_id=1, source_target_pairs={{0,128},{32,160},{64,192},{96,224},{128,0},{160,32},{192,64},{224,... | collective-permute-start | bytes 12296 | tf_op jit(solution)/shard_map/ppermute | solution.py:162
  81.5 1.1 collective-permute-done.8
  82.6 2.9 %collective-permute-start.9 = (bf16[256,1280]{1,0:T(8,128)(2,1)S(1)}, bf16[256,1280]{1,0:T(8,128)(2,1)S(1)}, u32[]{:S(2)}, u32[]{:S(2)}) collective-permute-start(bf16[256,1280]{1,0:T(8,128)(2,1)S(1)} %collective-permute-done.8), channel_id=1, source_target_pairs={{0,32},{32,64},{64,96},{96,128},{128,160},{160,192},{192,224},{224... | collective-permute-start | bytes 1966088 | tf_op jit(solution)/shard_map/ppermute | solution.py:159
  85.5 1.4 fusion.30
  86.9 2.9 %collective-permute-done.15 = bf16[256,1280]{1,0:T(8,128)(2,1)S(1)} collective-permute-done((bf16[256,1280]{1,0:T(8,128)(2,1)S(1)}, bf16[256,1280]{1,0:T(8,128)(2,1)S(1)}, u32[]{:S(2)}, u32[]{:S(2)}) %collective-permute-start.15) | collective-permute-done | bytes 655392 | tf_op jit(solution)/shard_map/ppermute | solution.py:159
  89.8 2.8 %collective-permute-start.16 = (bf16[256,1280]{1,0:T(8,128)(2,1)S(1)}, bf16[256,1280]{1,0:T(8,128)(2,1)S(1)}, u32[]{:S(2)}, u32[]{:S(2)}) collective-permute-start(bf16[256,1280]{1,0:T(8,128)(2,1)S(1)} %collective-permute-done.15), channel_id=1, source_target_pairs={{0,32},{32,64},{64,96},{96,128},{128,160},{160,192},{192,224},{224... | collective-permute-start | bytes 1966088 | tf_op jit(solution)/shard_map/ppermute | solution.py:159
  92.6 1.4 fusion.12
  94.0 0.3 fusion.27
  94.4 2.5 %collective-permute-done.9 = bf16[256,1280]{1,0:T(8,128)(2,1)S(1)} collective-permute-done((bf16[256,1280]{1,0:T(8,128)(2,1)S(1)}, bf16[256,1280]{1,0:T(8,128)(2,1)S(1)}, u32[]{:S(2)}, u32[]{:S(2)}) %collective-permute-start.9) | collective-permute-done | bytes 655392 | tf_op jit(solution)/shard_map/ppermute | solution.py:159
  96.8 2.9 %collective-permute-start.17 = (bf16[256,1280]{1,0:T(8,128)(2,1)S(1)}, bf16[256,1280]{1,0:T(8,128)(2,1)S(1)}, u32[]{:S(2)}, u32[]{:S(2)}) collective-permute-start(bf16[256,1280]{1,0:T(8,128)(2,1)S(1)} %collective-permute-done.9), channel_id=1, source_target_pairs={{0,32},{32,64},{64,96},{96,128},{128,160},{160,192},{192,224},{224... | collective-permute-start | bytes 1966088 | tf_op jit(solution)/shard_map/ppermute | solution.py:159
  99.7 0.3 fusion.13
  100.0 3.8 %collective-permute-done.16 = bf16[256,1280]{1,0:T(8,128)(2,1)S(1)} collective-permute-done((bf16[256,1280]{1,0:T(8,128)(2,1)S(1)}, bf16[256,1280]{1,0:T(8,128)(2,1)S(1)}, u32[]{:S(2)}, u32[]{:S(2)}) %collective-permute-start.16) | collective-permute-done | bytes 655392 | tf_op jit(solution)/shard_map/ppermute | solution.py:159
  103.9 2.9 %collective-permute-start.18 = (bf16[256,1280]{1,0:T(8,128)(2,1)S(1)}, bf16[256,1280]{1,0:T(8,128)(2,1)S(1)}, u32[]{:S(2)}, u32[]{:S(2)}) collective-permute-start(bf16[256,1280]{1,0:T(8,128)(2,1)S(1)} %collective-permute-done.16), channel_id=1, source_target_pairs={{0,32},{32,64},{64,96},{96,128},{128,160},{160,192},{192,224},{224... | collective-permute-start | bytes 1966088 | tf_op jit(solution)/shard_map/ppermute | solution.py:159
  107.1 0.3 fusion.14
  107.4 3.5 %collective-permute-done.17 = bf16[256,1280]{1,0:T(8,128)(2,1)S(1)} collective-permute-done((bf16[256,1280]{1,0:T(8,128)(2,1)S(1)}, bf16[256,1280]{1,0:T(8,128)(2,1)S(1)}, u32[]{:S(2)}, u32[]{:S(2)}) %collective-permute-start.17) | collective-permute-done | bytes 655392 | tf_op jit(solution)/shard_map/ppermute | solution.py:159
  111.2 0.3 fusion.15
  111.8 6.1 %collective-permute-done.18 = bf16[256,1280]{1,0:T(8,128)(2,1)S(1)} collective-permute-done((bf16[256,1280]{1,0:T(8,128)(2,1)S(1)}, bf16[256,1280]{1,0:T(8,128)(2,1)S(1)}, u32[]{:S(2)}, u32[]{:S(2)}) %collective-permute-start.18) | collective-permute-done | bytes 655392 | tf_op jit(solution)/shard_map/ppermute | solution.py:159
  117.9 0.4 fusion.63
  118.3 0.6 multiply_reduce_fusion
  119.0 4.5 %collective-permute-start.19 = (f32[8,192]{1,0:T(8,128)S(1)}, f32[8,192]{1,0:T(8,128)S(1)}, u32[]{:S(2)}, u32[]{:S(2)}) collective-permute-start(f32[8,192]{1,0:T(8,128)S(1)} %stack.50), channel_id=1, source_target_pairs={{0,256},{256,0},{1,257},{257,1},{2,258},{258,2},{3,259},{259,3},{4... | collective-permute-start | bytes 18440 | tf_op jit(solution)/shard_map/ppermute | solution.py:21
  123.5 0.8 collective-permute-done.19
  124.3 0.7 broadcast_in_dim.98
  125.1 9.7 %all-to-all-start.2 = ((f32[32,8,192]{2,1,0:T(8,128)}), f32[32,8,192]{2,1,0:T(8,128)S(1)}, u32[]{:S(2)}, u32[]{:S(2)}) async-start(f32[32,8,192]{2,1,0:T(8,128)} %broadcast_in_dim.98), calls=%async_computation.2 | async-start | bytes 524288 | tf_op jit(solution)/shard_map/all_to_all | solution.py:183
  135.0 0.5 slice.48
  136.1 10.2 %all-to-all-done.2 = f32[32,8,192]{2,1,0:T(8,128)S(1)} async-done(((f32[32,8,192]{2,1,0:T(8,128)}), f32[32,8,192]{2,1,0:T(8,128)S(1)}, u32[]{:S(2)}, u32[]{:S(2)}) %all-to-all-start.2) | async-done | bytes 196640 | tf_op jit(solution)/shard_map/all_to_all | solution.py:183
  146.3 33.9 %conditional.3 = (f32[12]{0:T(128)}, bf16[192,64]{0,1:T(8,128)(2,1)}) conditional(s32[]{:T(128)} %bitcast.8, (f32[192]{0:T(256)S(1)}, s32[2]{0:T(128)S(1)}, f32[32,8,192]{2,1,0:T(8,128)S(1)}, f32[192,1280]{1,0:T(8,128)S(1)}, bf16[192,1280]{1,0:T(8,128)(2,1)S(1)}, /*index=5*/bf16[512,1280]{1,0:T(8,128)(2,1)}, bf16[256,1280]{1,0:T(8,128)(2,1)}, ...), branch_computations={%region_13.17_spmd, %region_17.21_spmd} | conditional | flops 2019704960 | bytes 20125838
  146.3 5.8 %branch_1_fun.1 = (f32[2,32,64,128]{3,2,1,0:T(8,128)S(1)}, bf16[32,64,128]{2,1,0:T(8,128)(2,1)S(1)}, f32[1,128]{1,0:T(1,128)S(1)}) custom-call(s32[2]{0:T(128)S(1)} %get-tuple-element.118.place_ref, f32[32,8,192]{2,1,0:T(8,128)S(1)} %get-tuple-element.119.stats_ref, f32[1,192]{1,0:T(1,128)S(1)} %bitcast.54, f32[192,1280]{1,0:T(8,128)S(1)} %get-tuple-element.120.logits_ref, ...), custom_call_target="tpu_custom_call" | custom-call | flops 1342177280 | bytes 10485760 | tf_op jit(solution)/shard_map/cond/branch_1_fun/pallas_call | solution.py:102
  152.2 4.2 %collective-permute-start = (bf16[32,64,128]{2,1,0:T(8,128)(2,1)S(1)}, bf16[32,64,128]{2,1,0:T(8,128)(2,1)S(1)}, u32[]{:S(2)}, u32[]{:S(2)}) collective-permute-start(bf16[32,64,128]{2,1,0:T(8,128)(2,1)S(1)} %get-tuple-element.139), channel_id=1, source_target_pairs={{0,256},{256,0},{1,257},{257,1},{2,258},{258,2},{3,259},{259,3},{4... | collective-permute-start | bytes 1572872 | tf_op jit(solution)/shard_map/cond/branch_1_fun/ppermute | solution.py:21
  156.4 1.5 collective-permute-done
  157.9 1.0 fusion.9
  158.9 3.9 %all-to-all-start = ((bf16[32,64,128]{2,1,0:T(8,128)(2,1)}), bf16[32,64,128]{2,1,0:T(8,128)(2,1)S(1)}, u32[]{:S(2)}, u32[]{:S(2)}) async-start(bf16[32,64,128]{2,1,0:T(8,128)(2,1)} %fusion.9), calls=%async_computation | async-start | bytes 1048576 | tf_op jit(solution)/shard_map/cond/branch_1_fun/all_to_all | solution.py:192
  162.9 0.6 reduce_sum.146
  163.6 15.8 %all-to-all-done = bf16[32,64,128]{2,1,0:T(8,128)(2,1)S(1)} async-done(((bf16[32,64,128]{2,1,0:T(8,128)(2,1)}), bf16[32,64,128]{2,1,0:T(8,128)(2,1)S(1)}, u32[]{:S(2)}, u32[]{:S(2)}) %all-to-all-start) | async-done | bytes 524320 | tf_op jit(solution)/shard_map/cond/branch_1_fun/all_to_all | solution.py:192
  179.5 0.8 fusion.8
  (60 shorter events, 2.3 us)
Async XLA Ops:
  0.6 46.6 %copy-start = (bf16[192,4096]{1,0:T(8,128)(2,1)S(1)}, bf16[192,4096]{1,0:T(8,128)(2,1)}, u32[]{:S(2)}) copy-start(bf16[192,4096]{1,0:T(8,128)(2,1)} %param.8) | copy-start | bytes 4718596
  0.6 15.2 %copy-start.12 = (s32[96]{0:T(128)S(1)}, s32[96]{0:T(128)}, u32[]{:S(2)}) copy-start(s32[96]{0:T(128)} %param.12) | copy-start | bytes 1156
  0.7 15.3 %copy-start.13 = (s32[96]{0:T(128)S(1)}, s32[96]{0:T(128)}, u32[]{:S(2)}) copy-start(s32[96]{0:T(128)} %param.11) | copy-start | bytes 1156
  0.7 25.6 %copy-start.11 = (s32[192]{0:T(256)S(1)}, s32[192]{0:T(256)}, u32[]{:S(2)}) copy-start(s32[192]{0:T(256)} %param.13) | copy-start | bytes 2308
  2.2 19.0 %collective-permute-start.2 = (bf16[256,1280]{1,0:T(8,128)(2,1)S(1)}, bf16[256,1280]{1,0:T(8,128)(2,1)}, u32[]{:S(2)}, u32[]{:S(2)}) collective-permute-start(bf16[256,1280]{1,0:T(8,128)(2,1)S(1)} %get-tuple-element.173), channel_id=1, source_target_pairs={{0,32},{32,64},{64,96},{96,128},{128,160},{160,192},{192,224},{224... | collective-permute-start | bytes 1966088 | tf_op jit(solution)/shard_map/ppermute | solution.py:159
  13.7 15.8 %collective-permute-start.11 = (bf16[256,1280]{1,0:T(8,128)(2,1)S(1)}, bf16[256,1280]{1,0:T(8,128)(2,1)}, u32[]{:S(2)}, u32[]{:S(2)}) collective-permute-start(bf16[256,1280]{1,0:T(8,128)(2,1)S(1)} %get-tuple-element.172), channel_id=1, source_target_pairs={{0,32},{32,64},{64,96},{96,128},{128,160},{160,192},{192,224},{224... | collective-permute-start | bytes 1966088 | tf_op jit(solution)/shard_map/ppermute | solution.py:159
  21.2 14.1 %collective-permute-start.3 = (bf16[256,1280]{1,0:T(8,128)(2,1)}, bf16[256,1280]{1,0:T(8,128)(2,1)S(1)}, u32[]{:S(2)}, u32[]{:S(2)}) collective-permute-start(bf16[256,1280]{1,0:T(8,128)(2,1)} %collective-permute-done.2), channel_id=1, source_target_pairs={{0,32},{32,64},{64,96},{96,128},{128,160},{160,192},{192,224},{224... | collective-permute-start | bytes 1966088 | tf_op jit(solution)/shard_map/ppermute | solution.py:159
  27.6 6.5 %collective-permute-start.4 = (f32[8,128]{1,0:T(8,128)S(1)}, f32[8,128]{1,0:T(8,128)S(1)}, u32[]{:S(2)}, u32[]{:S(2)}) collective-permute-start(f32[8,128]{1,0:T(8,128)S(1)} %broadcast_in_dim.94), channel_id=1, source_target_pairs={{0,32},{32,0},{64,96},{96,64},{128,160},{160,128},{192,224},{224,1... | collective-permute-start | bytes 12296 | tf_op jit(solution)/shard_map/ppermute | solution.py:162
  29.5 12.8 %collective-permute-start.12 = (bf16[256,1280]{1,0:T(8,128)(2,1)}, bf16[256,1280]{1,0:T(8,128)(2,1)S(1)}, u32[]{:S(2)}, u32[]{:S(2)}) collective-permute-start(bf16[256,1280]{1,0:T(8,128)(2,1)} %collective-permute-done.11), channel_id=1, source_target_pairs={{0,32},{32,64},{64,96},{96,128},{128,160},{160,192},{192,224},{224... | collective-permute-start | bytes 1966088 | tf_op jit(solution)/shard_map/ppermute | solution.py:159
  35.3 41.4 %copy-start.2 = (bf16[256,1280]{1,0:T(8,128)(2,1)}, bf16[256,1280]{1,0:T(8,128)(2,1)S(1)}, u32[]{:S(2)}) copy-start(bf16[256,1280]{1,0:T(8,128)(2,1)S(1)} %collective-permute-done.3) | copy-start | bytes 1966084
  35.3 16.5 %collective-permute-start.5 = (bf16[256,1280]{1,0:T(8,128)(2,1)S(1)}, bf16[256,1280]{1,0:T(8,128)(2,1)}, u32[]{:S(2)}, u32[]{:S(2)}) collective-permute-start(bf16[256,1280]{1,0:T(8,128)(2,1)S(1)} %collective-permute-done.3), channel_id=1, source_target_pairs={{0,32},{32,64},{64,96},{96,128},{128,160},{160,192},{192,224},{224... | collective-permute-start | bytes 1966088 | tf_op jit(solution)/shard_map/ppermute | solution.py:159
  42.4 30.4 %copy-start.3 = (bf16[256,1280]{1,0:T(8,128)(2,1)}, bf16[256,1280]{1,0:T(8,128)(2,1)S(1)}, u32[]{:S(2)}) copy-start(bf16[256,1280]{1,0:T(8,128)(2,1)S(1)} %collective-permute-done.12) | copy-start | bytes 1966084
  42.4 13.9 %collective-permute-start.13 = (bf16[256,1280]{1,0:T(8,128)(2,1)S(1)}, bf16[256,1280]{1,0:T(8,128)(2,1)}, u32[]{:S(2)}, u32[]{:S(2)}) collective-permute-start(bf16[256,1280]{1,0:T(8,128)(2,1)S(1)} %collective-permute-done.12), channel_id=1, source_target_pairs={{0,32},{32,64},{64,96},{96,128},{128,160},{160,192},{192,224},{224... | collective-permute-start | bytes 1966088 | tf_op jit(solution)/shard_map/ppermute | solution.py:159
  51.9 18.9 %collective-permute-start.6 = (bf16[256,1280]{1,0:T(8,128)(2,1)}, bf16[256,1280]{1,0:T(8,128)(2,1)}, u32[]{:S(2)}, u32[]{:S(2)}) collective-permute-start(bf16[256,1280]{1,0:T(8,128)(2,1)} %collective-permute-done.5), channel_id=1, source_target_pairs={{0,32},{32,64},{64,96},{96,128},{128,160},{160,192},{192,224},{224... | collective-permute-start | bytes 1966088 | tf_op jit(solution)/shard_map/ppermute | solution.py:159
  56.1 9.0 %copy-start.1 = (bf16[192,4096]{1,0:T(8,128)(2,1)S(1)}, bf16[192,4096]{1,0:T(8,128)(2,1)}, u32[]{:S(2)}) copy-start(bf16[192,4096]{1,0:T(8,128)(2,1)} %convolution_convert_fusion.2) | copy-start | bytes 4718596
  56.3 16.8 %collective-permute-start.14 = (bf16[256,1280]{1,0:T(8,128)(2,1)}, bf16[256,1280]{1,0:T(8,128)(2,1)S(1)}, u32[]{:S(2)}, u32[]{:S(2)}) collective-permute-start(bf16[256,1280]{1,0:T(8,128)(2,1)} %collective-permute-done.13), channel_id=1, source_target_pairs={{0,32},{32,64},{64,96},{96,128},{128,160},{160,192},{192,224},{224... | collective-permute-start | bytes 1966088 | tf_op jit(solution)/shard_map/ppermute | solution.py:159
  63.2 7.6 %collective-permute-start.7 = (f32[8,128]{1,0:T(8,128)S(1)}, f32[8,128]{1,0:T(8,128)S(1)}, u32[]{:S(2)}, u32[]{:S(2)}) collective-permute-start(f32[8,128]{1,0:T(8,128)S(1)} %broadcast_maximum_fusion), channel_id=1, source_target_pairs={{0,64},{32,96},{64,0},{96,32},{128,192},{160,224},{192,128},{224,1... | collective-permute-start | bytes 12296 | tf_op jit(solution)/shard_map/ppermute | solution.py:162
  70.8 11.8 %collective-permute-start.8 = (bf16[256,1280]{1,0:T(8,128)(2,1)}, bf16[256,1280]{1,0:T(8,128)(2,1)S(1)}, u32[]{:S(2)}, u32[]{:S(2)}) collective-permute-start(bf16[256,1280]{1,0:T(8,128)(2,1)} %collective-permute-done.6), channel_id=1, source_target_pairs={{0,32},{32,64},{64,96},{96,128},{128,160},{160,192},{192,224},{224... | collective-permute-start | bytes 1966088 | tf_op jit(solution)/shard_map/ppermute | solution.py:159
  73.1 26.6 %copy-start.8 = (bf16[256,1280]{1,0:T(8,128)(2,1)}, bf16[256,1280]{1,0:T(8,128)(2,1)S(1)}, u32[]{:S(2)}) copy-start(bf16[256,1280]{1,0:T(8,128)(2,1)S(1)} %collective-permute-done.14) | copy-start | bytes 1966084
  73.1 16.7 %collective-permute-start.15 = (bf16[256,1280]{1,0:T(8,128)(2,1)S(1)}, bf16[256,1280]{1,0:T(8,128)(2,1)S(1)}, u32[]{:S(2)}, u32[]{:S(2)}) collective-permute-start(bf16[256,1280]{1,0:T(8,128)(2,1)S(1)} %collective-permute-done.14), channel_id=1, source_target_pairs={{0,32},{32,64},{64,96},{96,128},{128,160},{160,192},{192,224},{224... | collective-permute-start | bytes 1966088 | tf_op jit(solution)/shard_map/ppermute | solution.py:159
  77.1 16.9 %collective-permute-start.10 = (f32[8,128]{1,0:T(8,128)S(1)}, f32[8,128]{1,0:T(8,128)S(1)}, u32[]{:S(2)}, u32[]{:S(2)}) collective-permute-start(f32[8,128]{1,0:T(8,128)S(1)} %max.10), channel_id=1, source_target_pairs={{0,128},{32,160},{64,192},{96,224},{128,0},{160,32},{192,64},{224,... | collective-permute-start | bytes 12296 | tf_op jit(solution)/shard_map/ppermute | solution.py:162
  82.6 11.4 %copy-start.4 = (bf16[256,1280]{1,0:T(8,128)(2,1)}, bf16[256,1280]{1,0:T(8,128)(2,1)S(1)}, u32[]{:S(2)}) copy-start(bf16[256,1280]{1,0:T(8,128)(2,1)S(1)} %collective-permute-done.8) | copy-start | bytes 1966084
  82.6 14.2 %collective-permute-start.9 = (bf16[256,1280]{1,0:T(8,128)(2,1)S(1)}, bf16[256,1280]{1,0:T(8,128)(2,1)S(1)}, u32[]{:S(2)}, u32[]{:S(2)}) collective-permute-start(bf16[256,1280]{1,0:T(8,128)(2,1)S(1)} %collective-permute-done.8), channel_id=1, source_target_pairs={{0,32},{32,64},{64,96},{96,128},{128,160},{160,192},{192,224},{224... | collective-permute-start | bytes 1966088 | tf_op jit(solution)/shard_map/ppermute | solution.py:159
  89.8 17.3 %copy-start.9 = (bf16[256,1280]{1,0:T(8,128)(2,1)}, bf16[256,1280]{1,0:T(8,128)(2,1)S(1)}, u32[]{:S(2)}) copy-start(bf16[256,1280]{1,0:T(8,128)(2,1)S(1)} %collective-permute-done.15) | copy-start | bytes 1966084
  89.8 14.1 %collective-permute-start.16 = (bf16[256,1280]{1,0:T(8,128)(2,1)S(1)}, bf16[256,1280]{1,0:T(8,128)(2,1)S(1)}, u32[]{:S(2)}, u32[]{:S(2)}) collective-permute-start(bf16[256,1280]{1,0:T(8,128)(2,1)S(1)} %collective-permute-done.15), channel_id=1, source_target_pairs={{0,32},{32,64},{64,96},{96,128},{128,160},{160,192},{192,224},{224... | collective-permute-start | bytes 1966088 | tf_op jit(solution)/shard_map/ppermute | solution.py:159
  96.8 9.9 %copy-start.5 = (bf16[256,1280]{1,0:T(8,128)(2,1)}, bf16[256,1280]{1,0:T(8,128)(2,1)S(1)}, u32[]{:S(2)}) copy-start(bf16[256,1280]{1,0:T(8,128)(2,1)S(1)} %collective-permute-done.9) | copy-start | bytes 1966084
  96.8 14.0 %collective-permute-start.17 = (bf16[256,1280]{1,0:T(8,128)(2,1)S(1)}, bf16[256,1280]{1,0:T(8,128)(2,1)S(1)}, u32[]{:S(2)}, u32[]{:S(2)}) collective-permute-start(bf16[256,1280]{1,0:T(8,128)(2,1)S(1)} %collective-permute-done.9), channel_id=1, source_target_pairs={{0,32},{32,64},{64,96},{96,128},{128,160},{160,192},{192,224},{224... | collective-permute-start | bytes 1966088 | tf_op jit(solution)/shard_map/ppermute | solution.py:159
  103.9 7.3 %copy-start.10 = (bf16[256,1280]{1,0:T(8,128)(2,1)}, bf16[256,1280]{1,0:T(8,128)(2,1)S(1)}, u32[]{:S(2)}) copy-start(bf16[256,1280]{1,0:T(8,128)(2,1)S(1)} %collective-permute-done.16) | copy-start | bytes 1966084
  103.9 14.0 %collective-permute-start.18 = (bf16[256,1280]{1,0:T(8,128)(2,1)S(1)}, bf16[256,1280]{1,0:T(8,128)(2,1)S(1)}, u32[]{:S(2)}, u32[]{:S(2)}) collective-permute-start(bf16[256,1280]{1,0:T(8,128)(2,1)S(1)} %collective-permute-done.16), channel_id=1, source_target_pairs={{0,32},{32,64},{64,96},{96,128},{128,160},{160,192},{192,224},{224... | collective-permute-start | bytes 1966088 | tf_op jit(solution)/shard_map/ppermute | solution.py:159
  110.9 0.9 copy-start.6
  117.9 1.0 copy-start.7
  119.0 5.3 %collective-permute-start.19 = (f32[8,192]{1,0:T(8,128)S(1)}, f32[8,192]{1,0:T(8,128)S(1)}, u32[]{:S(2)}, u32[]{:S(2)}) collective-permute-start(f32[8,192]{1,0:T(8,128)S(1)} %stack.50), channel_id=1, source_target_pairs={{0,256},{256,0},{1,257},{257,1},{2,258},{258,2},{3,259},{259,3},{4... | collective-permute-start | bytes 18440 | tf_op jit(solution)/shard_map/ppermute | solution.py:21
  125.1 21.3 %all-to-all-start.2 = ((f32[32,8,192]{2,1,0:T(8,128)}), f32[32,8,192]{2,1,0:T(8,128)S(1)}, u32[]{:S(2)}, u32[]{:S(2)}) async-start(f32[32,8,192]{2,1,0:T(8,128)} %broadcast_in_dim.98), calls=%async_computation.2 | async-start | bytes 524288 | tf_op jit(solution)/shard_map/all_to_all | solution.py:183
  152.2 5.7 %collective-permute-start = (bf16[32,64,128]{2,1,0:T(8,128)(2,1)S(1)}, bf16[32,64,128]{2,1,0:T(8,128)(2,1)S(1)}, u32[]{:S(2)}, u32[]{:S(2)}) collective-permute-start(bf16[32,64,128]{2,1,0:T(8,128)(2,1)S(1)} %get-tuple-element.139), channel_id=1, source_target_pairs={{0,256},{256,0},{1,257},{257,1},{2,258},{258,2},{3,259},{259,3},{4... | collective-permute-start | bytes 1572872 | tf_op jit(solution)/shard_map/cond/branch_1_fun/ppermute | solution.py:21
  158.9 20.6 %all-to-all-start = ((bf16[32,64,128]{2,1,0:T(8,128)(2,1)}), bf16[32,64,128]{2,1,0:T(8,128)(2,1)S(1)}, u32[]{:S(2)}, u32[]{:S(2)}) async-start(bf16[32,64,128]{2,1,0:T(8,128)(2,1)} %fusion.9), calls=%async_computation | async-start | bytes 1048576 | tf_op jit(solution)/shard_map/cond/branch_1_fun/all_to_all | solution.py:192

commit v12 on v10

--- a/solution.py
+++ b/solution.py
@@ -143,10 +143,7 @@
     hidden = jnp.dot(pick_low, hidden, preferred_element_type=jnp.float32).astype(jnp.bfloat16)
     teacher_logits = jnp.dot(pick_low, teacher_logits, preferred_element_type=jnp.float32).astype(jnp.bfloat16)
     weight = jnp.sum(jnp.where(pick, weight[None, :], 0.0), axis=1)
-    most = jnp.full((8, LANES), jnp.sum(inside.astype(jnp.float32)))
-    for apart in (1 << bit for bit in range((blocks - 1).bit_length())):
-        most = jnp.maximum(most, lax.ppermute(most, "row", [(i, i ^ apart) for i in range(blocks)]))
-    fits = most[0, 0] <= FEW
+    fits = jnp.sum(inside.astype(jnp.int32)) <= FEW
 
     full = head.shape[0]
     depth = full // HALVES
@@ -160,6 +157,8 @@
     chunks = []
     for distance in range(1, blocks):
         held = [lax.ppermute(part, ("side", "row"), ring) for part in held]
+        if distance % 2 == 0:
+            held[0], weight = lax.optimization_barrier((held[0], weight))
         owner = (row_place - distance * step + blocks) % blocks
         for part in range(HALVES):
             piece = lax.dynamic_slice_in_dim(hidden, owner * full + part * depth, depth, axis=1)

time: 182 us -> 175 us (0.962)
  starting transfers between devices: 108 us -> 89.7 us
  waiting for transfers between devices: 40.8 us -> 52.7 us
  matrix products: 12.4 us -> 16.9 us
  local copies, waits for them, and re-layouts: 5.18 us -> 2.91 us
  other arithmetic: 6.17 us -> 4.26 us
    ppermute x3 -> x0, starting transfers between devices: 10.7 us -> none  [body(): lax.ppermute(most, 'row', [(i, i ^ apart) for i in range(blocks)])]
    all_to_all x1, waiting for transfers between devices: 1.49 us -> 10.8 us  [body(): lax.all_to_all(jnp.broadcast_to(pair, (count,) + pair.shape), 'vocab', 0, 0)]
    ppermute x14, waiting for transfers between devices: 19.3 us -> 23.7 us  [body(): held = [lax.ppermute(part, ('side', 'row'), ring) for part in held]]
    ppermute x14, starting transfers between devices: 72.8 us -> 68.5 us  [body(): held = [lax.ppermute(part, ('side', 'row'), ring) for part in held]]
    all_to_all x1, starting transfers between devices: 7.39 us -> 3.89 us  [finish(): pieces = lax.all_to_all(packed, 'vocab', 0, 0)]
    ppermute x3 -> x0, waiting for transfers between devices: 2.77 us -> none  [body(): lax.ppermute(most, 'row', [(i, i ^ apart) for i in range(blocks)])]
    dot_general x14, matrix products: 7.6 us -> 10.1 us  [body(): jnp.dot(piece, held[part], preferred_element_type=jnp.float32)]
  transfers between devices with their start and end apart: 21 -> 18, of which waited for: 16 -> 16; matrix products, arithmetic and copies ran while one was open for 11% -> 11% of each run, Pallas kernels for 0% -> 0%
where the time goes in v12:
time: 175 us; the launch traced here: 174 us
  starting transfers between devices  89.7 us (51%)
  waiting for transfers between devices  52.7 us (30%)
  matrix products  16.9 us (10%)
  Pallas kernels  5.81 us (3%)
  other arithmetic  4.26 us (2%)
  local copies, waits for them, and re-layouts  2.91 us (2%)
  between operations  1.94 us (1%)
    ppermute x14, starting transfers between devices, body(): held = [lax.ppermute(part, ('side', 'row'), ring) for part in held]  68.5 us
    ppermute x14, waiting for transfers between devices, body(): held = [lax.ppermute(part, ('side', 'row'), ring) for part in held]  23.7 us
    all_to_all x1, waiting for transfers between devices, finish(): pieces = lax.all_to_all(packed, 'vocab', 0, 0)  15.8 us
    all_to_all x1, waiting for transfers between devices, body(): lax.all_to_all(jnp.broadcast_to(pair, (count,) + pair.shape), 'vocab', 0, 0)  10.8 us
    dot_general x14, matrix products, body(): jnp.dot(piece, held[part], preferred_element_type=jnp.float32)  10.1 us
    all_to_all x1, starting transfers between devices, body(): lax.all_to_all(jnp.broadcast_to(pair, (count,) + pair.shape), 'vocab', 0, 0)  9.67 us
    ppermute x2, starting transfers between devices, swap_side(): return lax.ppermute(value, 'side', [(0, 1), (1, 0)])  7.73 us
    pallas_call x1, Pallas kernels, grad_products(): pl.pallas_call(functools.partial(grad_kernel, blocks, toks), out_shape=[j...  5.81 us
  transfers between devices with their start and end apart: 18, of which 16 were waited for; matrix products, arithmetic and copies ran while one was open for 11% of the time, Pallas kernels for 0%

profile of v12, /device:TPU:1, one launch (start us, length us, event | category | flops | bytes accessed | tf_op | source)
XLA Modules:
  0.0 174.3 jit_solution(11391659031851399664)
XLA Ops:
  0.7 1.5 fusion.61
  2.2 11.5 %collective-permute-start.2 = (bf16[256,1280]{1,0:T(8,128)(2,1)S(1)}, bf16[256,1280]{1,0:T(8,128)(2,1)}, u32[]{:S(2)}, u32[]{:S(2)}) collective-permute-start(bf16[256,1280]{1,0:T(8,128)(2,1)S(1)} %get-tuple-element.173), channel_id=1, source_target_pairs={{0,32},{32,64},{64,96},{96,128},{128,160},{160,192},{192,224},{224... | collective-permute-start | bytes 1966088 | tf_op jit(solution)/shard_map/ppermute | solution.py:159
  13.7 2.2 %collective-permute-start.3 = (bf16[256,1280]{1,0:T(8,128)(2,1)S(1)}, bf16[256,1280]{1,0:T(8,128)(2,1)}, u32[]{:S(2)}, u32[]{:S(2)}) collective-permute-start(bf16[256,1280]{1,0:T(8,128)(2,1)S(1)} %get-tuple-element.172), channel_id=1, source_target_pairs={{0,32},{32,64},{64,96},{96,128},{128,160},{160,192},{192,224},{224... | collective-permute-start | bytes 1966088 | tf_op jit(solution)/shard_map/ppermute | solution.py:159
  16.0 0.2 select_reduce_fusion.3
  16.3 4.9 %collective-permute-done.2 = bf16[256,1280]{1,0:T(8,128)(2,1)} collective-permute-done((bf16[256,1280]{1,0:T(8,128)(2,1)S(1)}, bf16[256,1280]{1,0:T(8,128)(2,1)}, u32[]{:S(2)}, u32[]{:S(2)}) %collective-permute-start.2) | collective-permute-done | bytes 655392 | tf_op jit(solution)/shard_map/ppermute | solution.py:159
  21.2 5.1 %collective-permute-start.4 = (bf16[256,1280]{1,0:T(8,128)(2,1)}, bf16[256,1280]{1,0:T(8,128)(2,1)S(1)}, u32[]{:S(2)}, u32[]{:S(2)}) collective-permute-start(bf16[256,1280]{1,0:T(8,128)(2,1)} %collective-permute-done.2), channel_id=1, source_target_pairs={{0,32},{32,64},{64,96},{96,128},{128,160},{160,192},{192,224},{224... | collective-permute-start | bytes 1966088 | tf_op jit(solution)/shard_map/ppermute | solution.py:159
  26.3 1.9 %collective-permute-done.3 = bf16[256,1280]{1,0:T(8,128)(2,1)} collective-permute-done((bf16[256,1280]{1,0:T(8,128)(2,1)S(1)}, bf16[256,1280]{1,0:T(8,128)(2,1)}, u32[]{:S(2)}, u32[]{:S(2)}) %collective-permute-start.3) | collective-permute-done | bytes 655392 | tf_op jit(solution)/shard_map/ppermute | solution.py:159
  28.2 5.1 %collective-permute-start.5 = (bf16[256,1280]{1,0:T(8,128)(2,1)}, bf16[256,1280]{1,0:T(8,128)(2,1)S(1)}, u32[]{:S(2)}, u32[]{:S(2)}) collective-permute-start(bf16[256,1280]{1,0:T(8,128)(2,1)} %collective-permute-done.3), channel_id=1, source_target_pairs={{0,32},{32,64},{64,96},{96,128},{128,160},{160,192},{192,224},{224... | collective-permute-start | bytes 1966088 | tf_op jit(solution)/shard_map/ppermute | solution.py:159
  33.4 0.6 convert_reduce_fusion.1
  34.1 0.7 subtract_select_fusion
  34.8 0.1 select_reduce_fusion.2
  34.9 0.4 collective-permute-done.4
  35.3 4.9 %collective-permute-start.6 = (bf16[256,1280]{1,0:T(8,128)(2,1)S(1)}, bf16[256,1280]{1,0:T(8,128)(2,1)}, u32[]{:S(2)}, u32[]{:S(2)}) collective-permute-start(bf16[256,1280]{1,0:T(8,128)(2,1)S(1)} %collective-permute-done.4), channel_id=1, source_target_pairs={{0,32},{32,64},{64,96},{96,128},{128,160},{160,192},{192,224},{224... | collective-permute-start | bytes 1966088 | tf_op jit(solution)/shard_map/ppermute | solution.py:159
  40.2 2.1 %collective-permute-done.5 = bf16[256,1280]{1,0:T(8,128)(2,1)S(1)} collective-permute-done((bf16[256,1280]{1,0:T(8,128)(2,1)}, bf16[256,1280]{1,0:T(8,128)(2,1)S(1)}, u32[]{:S(2)}, u32[]{:S(2)}) %collective-permute-start.5) | collective-permute-done | bytes 655392 | tf_op jit(solution)/shard_map/ppermute | solution.py:159
  42.4 4.9 %collective-permute-start.7 = (bf16[256,1280]{1,0:T(8,128)(2,1)S(1)}, bf16[256,1280]{1,0:T(8,128)(2,1)}, u32[]{:S(2)}, u32[]{:S(2)}) collective-permute-start(bf16[256,1280]{1,0:T(8,128)(2,1)S(1)} %collective-permute-done.5), channel_id=1, source_target_pairs={{0,32},{32,64},{64,96},{96,128},{128,160},{160,192},{192,224},{224... | collective-permute-start | bytes 1966088 | tf_op jit(solution)/shard_map/ppermute | solution.py:159
  47.3 1.8 %convolution_convert_fusion.2 = bf16[192,4096]{1,0:T(8,128)(2,1)} fusion(bf16[192,4096]{1,0:T(8,128)(2,1)S(1)} %copy-done, s32[192]{0:T(256)S(1)} %subtract_select_fusion), kind=kOutput, calls=%fused_computation.18 | convolution fusion | flops 302813184 | bytes 3146496 | tf_op jit(solution)/shard_map/dot_general | solution.py:143
  49.0 2.8 %fusion.17 = f32[192,1280]{1,0:T(8,128)} fusion(bf16[512,1280]{1,0:T(8,128)(2,1)} %param.9, bf16[192,4096]{1,0:T(8,128)(2,1)} %convolution_convert_fusion.2, s32[]{:T(128)S(6)} %select_n.113), kind=kOutput, calls=%fused_computation.39 | convolution fusion | flops 251658240 | bytes 2490372 | tf_op jit(solution)/shard_map/dot_general | solution.py:154
  51.9 2.5 %collective-permute-start.8 = (bf16[256,1280]{1,0:T(8,128)(2,1)}, bf16[256,1280]{1,0:T(8,128)(2,1)}, u32[]{:S(2)}, u32[]{:S(2)}) collective-permute-start(bf16[256,1280]{1,0:T(8,128)(2,1)} %collective-permute-done.6), channel_id=1, source_target_pairs={{0,32},{32,64},{64,96},{96,128},{128,160},{160,192},{192,224},{224... | collective-permute-start | bytes 1966088 | tf_op jit(solution)/shard_map/ppermute | solution.py:159
  54.4 1.4 fusion.64
  56.1 0.2 collective-permute-done.7
  56.3 5.1 %collective-permute-start.9 = (bf16[256,1280]{1,0:T(8,128)(2,1)}, bf16[256,1280]{1,0:T(8,128)(2,1)S(1)}, u32[]{:S(2)}, u32[]{:S(2)}) collective-permute-start(bf16[256,1280]{1,0:T(8,128)(2,1)} %collective-permute-done.7), channel_id=1, source_target_pairs={{0,32},{32,64},{64,96},{96,128},{128,160},{160,192},{192,224},{224... | collective-permute-start | bytes 1966088 | tf_op jit(solution)/shard_map/ppermute | solution.py:159
  61.4 1.7 convolution_add_fusion.7
  63.2 1.4 convolution_add_fusion.6
  64.6 3.8 %collective-permute-start.10 = (bf16[256,1280]{1,0:T(8,128)(2,1)}, bf16[256,1280]{1,0:T(8,128)(2,1)S(1)}, u32[]{:S(2)}, u32[]{:S(2)}) collective-permute-start(bf16[256,1280]{1,0:T(8,128)(2,1)} %collective-permute-done.8), channel_id=1, source_target_pairs={{0,32},{32,64},{64,96},{96,128},{128,160},{160,192},{192,224},{224... | collective-permute-start | bytes 1966088 | tf_op jit(solution)/shard_map/ppermute | solution.py:159
  68.4 0.3 fusion.35
  68.8 1.9 %collective-permute-done.9 = bf16[256,1280]{1,0:T(8,128)(2,1)S(1)} collective-permute-done((bf16[256,1280]{1,0:T(8,128)(2,1)}, bf16[256,1280]{1,0:T(8,128)(2,1)S(1)}, u32[]{:S(2)}, u32[]{:S(2)}) %collective-permute-start.9) | collective-permute-done | bytes 655392 | tf_op jit(solution)/shard_map/ppermute | solution.py:159
  70.7 4.6 %collective-permute-start.11 = (bf16[256,1280]{1,0:T(8,128)(2,1)S(1)}, bf16[256,1280]{1,0:T(8,128)(2,1)S(1)}, u32[]{:S(2)}, u32[]{:S(2)}) collective-permute-start(bf16[256,1280]{1,0:T(8,128)(2,1)S(1)} %collective-permute-done.9), channel_id=1, source_target_pairs={{0,32},{32,64},{64,96},{96,128},{128,160},{160,192},{192,224},{224... | collective-permute-start | bytes 1966088 | tf_op jit(solution)/shard_map/ppermute | solution.py:159
  75.4 1.4 fusion.33
  76.8 0.3 fusion.16
  77.1 0.6 collective-permute-done.10
  77.7 4.6 %collective-permute-start.12 = (bf16[256,1280]{1,0:T(8,128)(2,1)S(1)}, bf16[256,1280]{1,0:T(8,128)(2,1)S(1)}, u32[]{:S(2)}, u32[]{:S(2)}) collective-permute-start(bf16[256,1280]{1,0:T(8,128)(2,1)S(1)} %collective-permute-done.10), channel_id=1, source_target_pairs={{0,32},{32,64},{64,96},{96,128},{128,160},{160,192},{192,224},{224... | collective-permute-start | bytes 1966088 | tf_op jit(solution)/shard_map/ppermute | solution.py:159
  82.4 1.4 fusion.30
  83.8 1.0 collective-permute-done.11
  84.7 4.6 %collective-permute-start.13 = (bf16[256,1280]{1,0:T(8,128)(2,1)S(1)}, bf16[256,1280]{1,0:T(8,128)(2,1)S(1)}, u32[]{:S(2)}, u32[]{:S(2)}) collective-permute-start(bf16[256,1280]{1,0:T(8,128)(2,1)S(1)} %collective-permute-done.11), channel_id=1, source_target_pairs={{0,32},{32,64},{64,96},{96,128},{128,160},{160,192},{192,224},{224... | collective-permute-start | bytes 1966088 | tf_op jit(solution)/shard_map/ppermute | solution.py:159
  89.4 1.4 fusion.12
  90.8 0.3 fusion.27
  91.1 0.6 collective-permute-done.12
  91.8 4.6 %collective-permute-start.14 = (bf16[256,1280]{1,0:T(8,128)(2,1)S(1)}, bf16[256,1280]{1,0:T(8,128)(2,1)S(1)}, u32[]{:S(2)}, u32[]{:S(2)}) collective-permute-start(bf16[256,1280]{1,0:T(8,128)(2,1)S(1)} %collective-permute-done.12), channel_id=1, source_target_pairs={{0,32},{32,64},{64,96},{96,128},{128,160},{160,192},{192,224},{224... | collective-permute-start | bytes 1966088 | tf_op jit(solution)/shard_map/ppermute | solution.py:159
  96.4 0.3 fusion.13
  96.7 2.0 %collective-permute-done.13 = bf16[256,1280]{1,0:T(8,128)(2,1)S(1)} collective-permute-done((bf16[256,1280]{1,0:T(8,128)(2,1)S(1)}, bf16[256,1280]{1,0:T(8,128)(2,1)S(1)}, u32[]{:S(2)}, u32[]{:S(2)}) %collective-permute-start.13) | collective-permute-done | bytes 655392 | tf_op jit(solution)/shard_map/ppermute | solution.py:159
  98.8 4.6 %collective-permute-start.15 = (bf16[256,1280]{1,0:T(8,128)(2,1)S(1)}, bf16[256,1280]{1,0:T(8,128)(2,1)S(1)}, u32[]{:S(2)}, u32[]{:S(2)}) collective-permute-start(bf16[256,1280]{1,0:T(8,128)(2,1)S(1)} %collective-permute-done.13), channel_id=1, source_target_pairs={{0,32},{32,64},{64,96},{96,128},{128,160},{160,192},{192,224},{224... | collective-permute-start | bytes 1966088 | tf_op jit(solution)/shard_map/ppermute | solution.py:159
  103.5 0.3 fusion.24
  103.8 0.3 fusion.14
  104.1 1.7 collective-permute-done.14
  105.8 0.3 fusion.21
  106.1 0.3 fusion.15
  106.4 0.3 copy-done.6
  106.7 6.1 %collective-permute-done.15 = bf16[256,1280]{1,0:T(8,128)(2,1)S(1)} collective-permute-done((bf16[256,1280]{1,0:T(8,128)(2,1)S(1)}, bf16[256,1280]{1,0:T(8,128)(2,1)S(1)}, u32[]{:S(2)}, u32[]{:S(2)}) %collective-permute-start.15) | collective-permute-done | bytes 655392 | tf_op jit(solution)/shard_map/ppermute | solution.py:159
  112.8 0.4 fusion.63
  113.2 0.6 multiply_reduce_fusion
  113.9 3.5 %collective-permute-start.16 = (f32[8,192]{1,0:T(8,128)S(1)}, f32[8,192]{1,0:T(8,128)S(1)}, u32[]{:S(2)}, u32[]{:S(2)}) collective-permute-start(f32[8,192]{1,0:T(8,128)S(1)} %stack.50), channel_id=1, source_target_pairs={{0,256},{256,0},{1,257},{257,1},{2,258},{258,2},{3,259},{259,3},{4... | collective-permute-start | bytes 18440 | tf_op jit(solution)/shard_map/ppermute | solution.py:21
  117.4 0.8 collective-permute-done.16
  118.3 0.7 broadcast_in_dim.97
  119.0 9.7 %all-to-all-start.2 = ((f32[32,8,192]{2,1,0:T(8,128)}), f32[32,8,192]{2,1,0:T(8,128)S(1)}, u32[]{:S(2)}, u32[]{:S(2)}) async-start(f32[32,8,192]{2,1,0:T(8,128)} %broadcast_in_dim.97), calls=%async_computation.2 | async-start | bytes 524288 | tf_op jit(solution)/shard_map/all_to_all | solution.py:181
  129.5 10.8 %all-to-all-done.2 = f32[32,8,192]{2,1,0:T(8,128)S(1)} async-done(((f32[32,8,192]{2,1,0:T(8,128)}), f32[32,8,192]{2,1,0:T(8,128)S(1)}, u32[]{:S(2)}, u32[]{:S(2)}) %all-to-all-start.2) | async-done | bytes 196640 | tf_op jit(solution)/shard_map/all_to_all | solution.py:181
  140.3 33.9 %conditional.3 = (f32[12]{0:T(128)}, bf16[192,64]{0,1:T(8,128)(2,1)}) conditional(s32[]{:T(128)} %convert_element_type.62, (f32[192]{0:T(256)S(1)}, s32[2]{0:T(128)S(1)}, f32[32,8,192]{2,1,0:T(8,128)S(1)}, f32[192,1280]{1,0:T(8,128)S(1)}, bf16[192,1280]{1,0:T(8,128)(2,1)S(1)}, /*index=5*/bf16[512,1280]{1,0:T(8,128)(2,1)}, ...), branch_computations={%region_12.16_spmd, %region_16.20_spmd} | conditional | flops 2019704960 | bytes 20125838
  140.3 5.8 %branch_1_fun.1 = (f32[2,32,64,128]{3,2,1,0:T(8,128)S(1)}, bf16[32,64,128]{2,1,0:T(8,128)(2,1)S(1)}, f32[1,128]{1,0:T(1,128)S(1)}) custom-call(s32[2]{0:T(128)S(1)} %get-tuple-element.118.place_ref, f32[32,8,192]{2,1,0:T(8,128)S(1)} %get-tuple-element.119.stats_ref, f32[1,192]{1,0:T(1,128)S(1)} %bitcast.53, f32[192,1280]{1,0:T(8,128)S(1)} %get-tuple-element.120.logits_ref, ...), custom_call_target="tpu_custom_call" | custom-call | flops 1342177280 | bytes 10485760 | tf_op jit(solution)/shard_map/cond/branch_1_fun/pallas_call | solution.py:102
  146.1 4.2 %collective-permute-start = (bf16[32,64,128]{2,1,0:T(8,128)(2,1)S(1)}, bf16[32,64,128]{2,1,0:T(8,128)(2,1)S(1)}, u32[]{:S(2)}, u32[]{:S(2)}) collective-permute-start(bf16[32,64,128]{2,1,0:T(8,128)(2,1)S(1)} %get-tuple-element.139), channel_id=1, source_target_pairs={{0,256},{256,0},{1,257},{257,1},{2,258},{258,2},{3,259},{259,3},{4... | collective-permute-start | bytes 1572872 | tf_op jit(solution)/shard_map/cond/branch_1_fun/ppermute | solution.py:21
  150.3 1.5 collective-permute-done
  151.9 1.0 fusion.9
  152.8 3.9 %all-to-all-start = ((bf16[32,64,128]{2,1,0:T(8,128)(2,1)}), bf16[32,64,128]{2,1,0:T(8,128)(2,1)S(1)}, u32[]{:S(2)}, u32[]{:S(2)}) async-start(bf16[32,64,128]{2,1,0:T(8,128)(2,1)} %fusion.9), calls=%async_computation | async-start | bytes 1048576 | tf_op jit(solution)/shard_map/cond/branch_1_fun/all_to_all | solution.py:190
  156.9 0.6 reduce_sum.142
  157.6 15.8 %all-to-all-done = bf16[32,64,128]{2,1,0:T(8,128)(2,1)S(1)} async-done(((bf16[32,64,128]{2,1,0:T(8,128)(2,1)}), bf16[32,64,128]{2,1,0:T(8,128)(2,1)S(1)}, u32[]{:S(2)}, u32[]{:S(2)}) %all-to-all-start) | async-done | bytes 524320 | tf_op jit(solution)/shard_map/cond/branch_1_fun/all_to_all | solution.py:190
  173.5 0.8 fusion.8
  (48 shorter events, 0.9 us)
Async XLA Ops:
  0.6 46.6 %copy-start = (bf16[192,4096]{1,0:T(8,128)(2,1)S(1)}, bf16[192,4096]{1,0:T(8,128)(2,1)}, u32[]{:S(2)}) copy-start(bf16[192,4096]{1,0:T(8,128)(2,1)} %param.8) | copy-start | bytes 4718596
  0.6 15.2 %copy-start.12 = (s32[96]{0:T(128)S(1)}, s32[96]{0:T(128)}, u32[]{:S(2)}) copy-start(s32[96]{0:T(128)} %param.12) | copy-start | bytes 1156
  0.7 15.3 %copy-start.13 = (s32[96]{0:T(128)S(1)}, s32[96]{0:T(128)}, u32[]{:S(2)}) copy-start(s32[96]{0:T(128)} %param.11) | copy-start | bytes 1156
  0.7 32.7 %copy-start.11 = (s32[192]{0:T(256)S(1)}, s32[192]{0:T(256)}, u32[]{:S(2)}) copy-start(s32[192]{0:T(256)} %param.13) | copy-start | bytes 2308
  2.2 19.0 %collective-permute-start.2 = (bf16[256,1280]{1,0:T(8,128)(2,1)S(1)}, bf16[256,1280]{1,0:T(8,128)(2,1)}, u32[]{:S(2)}, u32[]{:S(2)}) collective-permute-start(bf16[256,1280]{1,0:T(8,128)(2,1)S(1)} %get-tuple-element.173), channel_id=1, source_target_pairs={{0,32},{32,64},{64,96},{96,128},{128,160},{160,192},{192,224},{224... | collective-permute-start | bytes 1966088 | tf_op jit(solution)/shard_map/ppermute | solution.py:159
  13.7 14.5 %collective-permute-start.3 = (bf16[256,1280]{1,0:T(8,128)(2,1)S(1)}, bf16[256,1280]{1,0:T(8,128)(2,1)}, u32[]{:S(2)}, u32[]{:S(2)}) collective-permute-start(bf16[256,1280]{1,0:T(8,128)(2,1)S(1)} %get-tuple-element.172), channel_id=1, source_target_pairs={{0,32},{32,64},{64,96},{96,128},{128,160},{160,192},{192,224},{224... | collective-permute-start | bytes 1966088 | tf_op jit(solution)/shard_map/ppermute | solution.py:159
  21.2 14.1 %collective-permute-start.4 = (bf16[256,1280]{1,0:T(8,128)(2,1)}, bf16[256,1280]{1,0:T(8,128)(2,1)S(1)}, u32[]{:S(2)}, u32[]{:S(2)}) collective-permute-start(bf16[256,1280]{1,0:T(8,128)(2,1)} %collective-permute-done.2), channel_id=1, source_target_pairs={{0,32},{32,64},{64,96},{96,128},{128,160},{160,192},{192,224},{224... | collective-permute-start | bytes 1966088 | tf_op jit(solution)/shard_map/ppermute | solution.py:159
  28.2 14.1 %collective-permute-start.5 = (bf16[256,1280]{1,0:T(8,128)(2,1)}, bf16[256,1280]{1,0:T(8,128)(2,1)S(1)}, u32[]{:S(2)}, u32[]{:S(2)}) collective-permute-start(bf16[256,1280]{1,0:T(8,128)(2,1)} %collective-permute-done.3), channel_id=1, source_target_pairs={{0,32},{32,64},{64,96},{96,128},{128,160},{160,192},{192,224},{224... | collective-permute-start | bytes 1966088 | tf_op jit(solution)/shard_map/ppermute | solution.py:159
  35.3 41.4 %copy-start.2 = (bf16[256,1280]{1,0:T(8,128)(2,1)}, bf16[256,1280]{1,0:T(8,128)(2,1)S(1)}, u32[]{:S(2)}) copy-start(bf16[256,1280]{1,0:T(8,128)(2,1)S(1)} %collective-permute-done.4) | copy-start | bytes 1966084
  35.3 16.5 %collective-permute-start.6 = (bf16[256,1280]{1,0:T(8,128)(2,1)S(1)}, bf16[256,1280]{1,0:T(8,128)(2,1)}, u32[]{:S(2)}, u32[]{:S(2)}) collective-permute-start(bf16[256,1280]{1,0:T(8,128)(2,1)S(1)} %collective-permute-done.4), channel_id=1, source_target_pairs={{0,32},{32,64},{64,96},{96,128},{128,160},{160,192},{192,224},{224... | collective-permute-start | bytes 1966088 | tf_op jit(solution)/shard_map/ppermute | solution.py:159
  42.4 26.1 %copy-start.3 = (bf16[256,1280]{1,0:T(8,128)(2,1)}, bf16[256,1280]{1,0:T(8,128)(2,1)S(1)}, u32[]{:S(2)}) copy-start(bf16[256,1280]{1,0:T(8,128)(2,1)S(1)} %collective-permute-done.5) | copy-start | bytes 1966084
  42.4 13.9 %collective-permute-start.7 = (bf16[256,1280]{1,0:T(8,128)(2,1)S(1)}, bf16[256,1280]{1,0:T(8,128)(2,1)}, u32[]{:S(2)}, u32[]{:S(2)}) collective-permute-start(bf16[256,1280]{1,0:T(8,128)(2,1)S(1)} %collective-permute-done.5), channel_id=1, source_target_pairs={{0,32},{32,64},{64,96},{96,128},{128,160},{160,192},{192,224},{224... | collective-permute-start | bytes 1966088 | tf_op jit(solution)/shard_map/ppermute | solution.py:159
  51.9 12.7 %collective-permute-start.8 = (bf16[256,1280]{1,0:T(8,128)(2,1)}, bf16[256,1280]{1,0:T(8,128)(2,1)}, u32[]{:S(2)}, u32[]{:S(2)}) collective-permute-start(bf16[256,1280]{1,0:T(8,128)(2,1)} %collective-permute-done.6), channel_id=1, source_target_pairs={{0,32},{32,64},{64,96},{96,128},{128,160},{160,192},{192,224},{224... | collective-permute-start | bytes 1966088 | tf_op jit(solution)/shard_map/ppermute | solution.py:159
  56.0 7.1 %copy-start.1 = (bf16[192,4096]{1,0:T(8,128)(2,1)S(1)}, bf16[192,4096]{1,0:T(8,128)(2,1)}, u32[]{:S(2)}) copy-start(bf16[192,4096]{1,0:T(8,128)(2,1)} %convolution_convert_fusion.2) | copy-start | bytes 4718596
  56.3 14.4 %collective-permute-start.9 = (bf16[256,1280]{1,0:T(8,128)(2,1)}, bf16[256,1280]{1,0:T(8,128)(2,1)S(1)}, u32[]{:S(2)}, u32[]{:S(2)}) collective-permute-start(bf16[256,1280]{1,0:T(8,128)(2,1)} %collective-permute-done.7), channel_id=1, source_target_pairs={{0,32},{32,64},{64,96},{96,128},{128,160},{160,192},{192,224},{224... | collective-permute-start | bytes 1966088 | tf_op jit(solution)/shard_map/ppermute | solution.py:159
  64.6 13.1 %collective-permute-start.10 = (bf16[256,1280]{1,0:T(8,128)(2,1)}, bf16[256,1280]{1,0:T(8,128)(2,1)S(1)}, u32[]{:S(2)}, u32[]{:S(2)}) collective-permute-start(bf16[256,1280]{1,0:T(8,128)(2,1)} %collective-permute-done.8), channel_id=1, source_target_pairs={{0,32},{32,64},{64,96},{96,128},{128,160},{160,192},{192,224},{224... | collective-permute-start | bytes 1966088 | tf_op jit(solution)/shard_map/ppermute | solution.py:159
  70.7 25.7 %copy-start.8 = (bf16[256,1280]{1,0:T(8,128)(2,1)}, bf16[256,1280]{1,0:T(8,128)(2,1)S(1)}, u32[]{:S(2)}) copy-start(bf16[256,1280]{1,0:T(8,128)(2,1)S(1)} %collective-permute-done.9) | copy-start | bytes 1966084
  70.7 14.0 %collective-permute-start.11 = (bf16[256,1280]{1,0:T(8,128)(2,1)S(1)}, bf16[256,1280]{1,0:T(8,128)(2,1)S(1)}, u32[]{:S(2)}, u32[]{:S(2)}) collective-permute-start(bf16[256,1280]{1,0:T(8,128)(2,1)S(1)} %collective-permute-done.9), channel_id=1, source_target_pairs={{0,32},{32,64},{64,96},{96,128},{128,160},{160,192},{192,224},{224... | collective-permute-start | bytes 1966088 | tf_op jit(solution)/shard_map/ppermute | solution.py:159
  77.7 13.1 %copy-start.4 = (bf16[256,1280]{1,0:T(8,128)(2,1)}, bf16[256,1280]{1,0:T(8,128)(2,1)S(1)}, u32[]{:S(2)}) copy-start(bf16[256,1280]{1,0:T(8,128)(2,1)S(1)} %collective-permute-done.10) | copy-start | bytes 1966084
  77.7 14.0 %collective-permute-start.12 = (bf16[256,1280]{1,0:T(8,128)(2,1)S(1)}, bf16[256,1280]{1,0:T(8,128)(2,1)S(1)}, u32[]{:S(2)}, u32[]{:S(2)}) collective-permute-start(bf16[256,1280]{1,0:T(8,128)(2,1)S(1)} %collective-permute-done.10), channel_id=1, source_target_pairs={{0,32},{32,64},{64,96},{96,128},{128,160},{160,192},{192,224},{224... | collective-permute-start | bytes 1966088 | tf_op jit(solution)/shard_map/ppermute | solution.py:159
  84.7 19.0 %copy-start.9 = (bf16[256,1280]{1,0:T(8,128)(2,1)}, bf16[256,1280]{1,0:T(8,128)(2,1)S(1)}, u32[]{:S(2)}) copy-start(bf16[256,1280]{1,0:T(8,128)(2,1)S(1)} %collective-permute-done.11) | copy-start | bytes 1966084
  84.7 14.0 %collective-permute-start.13 = (bf16[256,1280]{1,0:T(8,128)(2,1)S(1)}, bf16[256,1280]{1,0:T(8,128)(2,1)S(1)}, u32[]{:S(2)}, u32[]{:S(2)}) collective-permute-start(bf16[256,1280]{1,0:T(8,128)(2,1)S(1)} %collective-permute-done.11), channel_id=1, source_target_pairs={{0,32},{32,64},{64,96},{96,128},{128,160},{160,192},{192,224},{224... | collective-permute-start | bytes 1966088 | tf_op jit(solution)/shard_map/ppermute | solution.py:159
  91.8 11.7 %copy-start.5 = (bf16[256,1280]{1,0:T(8,128)(2,1)}, bf16[256,1280]{1,0:T(8,128)(2,1)S(1)}, u32[]{:S(2)}) copy-start(bf16[256,1280]{1,0:T(8,128)(2,1)S(1)} %collective-permute-done.12) | copy-start | bytes 1966084
  91.8 14.0 %collective-permute-start.14 = (bf16[256,1280]{1,0:T(8,128)(2,1)S(1)}, bf16[256,1280]{1,0:T(8,128)(2,1)S(1)}, u32[]{:S(2)}, u32[]{:S(2)}) collective-permute-start(bf16[256,1280]{1,0:T(8,128)(2,1)S(1)} %collective-permute-done.12), channel_id=1, source_target_pairs={{0,32},{32,64},{64,96},{96,128},{128,160},{160,192},{192,224},{224... | collective-permute-start | bytes 1966088 | tf_op jit(solution)/shard_map/ppermute | solution.py:159
  98.8 7.3 %copy-start.10 = (bf16[256,1280]{1,0:T(8,128)(2,1)}, bf16[256,1280]{1,0:T(8,128)(2,1)S(1)}, u32[]{:S(2)}) copy-start(bf16[256,1280]{1,0:T(8,128)(2,1)S(1)} %collective-permute-done.13) | copy-start | bytes 1966084
  98.8 14.0 %collective-permute-start.15 = (bf16[256,1280]{1,0:T(8,128)(2,1)S(1)}, bf16[256,1280]{1,0:T(8,128)(2,1)S(1)}, u32[]{:S(2)}, u32[]{:S(2)}) collective-permute-start(bf16[256,1280]{1,0:T(8,128)(2,1)S(1)} %collective-permute-done.13), channel_id=1, source_target_pairs={{0,32},{32,64},{64,96},{96,128},{128,160},{160,192},{192,224},{224... | collective-permute-start | bytes 1966088 | tf_op jit(solution)/shard_map/ppermute | solution.py:159
  105.8 0.9 copy-start.6
  112.8 1.0 copy-start.7
  113.9 4.4 %collective-permute-start.16 = (f32[8,192]{1,0:T(8,128)S(1)}, f32[8,192]{1,0:T(8,128)S(1)}, u32[]{:S(2)}, u32[]{:S(2)}) collective-permute-start(f32[8,192]{1,0:T(8,128)S(1)} %stack.50), channel_id=1, source_target_pairs={{0,256},{256,0},{1,257},{257,1},{2,258},{258,2},{3,259},{259,3},{4... | collective-permute-start | bytes 18440 | tf_op jit(solution)/shard_map/ppermute | solution.py:21
  119.0 21.3 %all-to-all-start.2 = ((f32[32,8,192]{2,1,0:T(8,128)}), f32[32,8,192]{2,1,0:T(8,128)S(1)}, u32[]{:S(2)}, u32[]{:S(2)}) async-start(f32[32,8,192]{2,1,0:T(8,128)} %broadcast_in_dim.97), calls=%async_computation.2 | async-start | bytes 524288 | tf_op jit(solution)/shard_map/all_to_all | solution.py:181
  146.1 5.7 %collective-permute-start = (bf16[32,64,128]{2,1,0:T(8,128)(2,1)S(1)}, bf16[32,64,128]{2,1,0:T(8,128)(2,1)S(1)}, u32[]{:S(2)}, u32[]{:S(2)}) collective-permute-start(bf16[32,64,128]{2,1,0:T(8,128)(2,1)S(1)} %get-tuple-element.139), channel_id=1, source_target_pairs={{0,256},{256,0},{1,257},{257,1},{2,258},{258,2},{3,259},{259,3},{4... | collective-permute-start | bytes 1572872 | tf_op jit(solution)/shard_map/cond/branch_1_fun/ppermute | solution.py:21
  152.8 20.6 %all-to-all-start = ((bf16[32,64,128]{2,1,0:T(8,128)(2,1)}), bf16[32,64,128]{2,1,0:T(8,128)(2,1)S(1)}, u32[]{:S(2)}, u32[]{:S(2)}) async-start(bf16[32,64,128]{2,1,0:T(8,128)(2,1)} %fusion.9), calls=%async_computation | async-start | bytes 1048576 | tf_op jit(solution)/shard_map/cond/branch_1_fun/all_to_all | solution.py:190

commit v13 on v12

--- a/solution.py
+++ b/solution.py
@@ -176,13 +176,13 @@
     term = jnp.sum(powers * (shifted - teacher_gap), axis=1)
     blank = jnp.zeros_like(peak)
     own = jnp.stack([peak, total, teacher_peak, teacher_total, term, blank, blank, blank])
-    other = swap_side(own)
-    pair = jnp.concatenate([*join(*[jnp.stack([own[i], other[i]]) for i in range(5)]), own[5:]])
-    stats = lax.all_to_all(jnp.broadcast_to(pair, (count,) + pair.shape), "vocab", 0, 0)
-
     place = jnp.stack([side_place, row_place]).astype(jnp.int32)
 
-    def finish(toks, place, stats, weight, pick, logits, teacher_logits, head, *chunks):
+    def finish(toks, place, own, weight, pick, logits, teacher_logits, head, *chunks):
+        own = own[:, :toks]
+        other = swap_side(own)
+        pair = jnp.concatenate([*join(*[jnp.stack([own[i], other[i]]) for i in range(5)]), own[5:]])
+        stats = lax.all_to_all(jnp.broadcast_to(pair, (count,) + pair.shape), "vocab", 0, 0)
         sums, send, diverge = grad_products(
             place, stats, weight[None], logits, teacher_logits, head, chunks, blocks, count, toks
         )
@@ -199,12 +199,12 @@
         loss = jnp.sum(jnp.where(some, (weight[:toks] * diverge[0])[:, None], 0.0), axis=0)
         return jnp.sum(loss.reshape(slot_count, WIN), axis=1), block.T
 
-    stats, weight, pick = lax.optimization_barrier((stats, weight, pick))
+    own, weight, pick = lax.optimization_barrier((own, weight, pick))
     return lax.cond(
         fits,
         functools.partial(finish, FEW),
         functools.partial(finish, tok_rows),
-        place, stats, weight, pick, logits, teacher_logits, head, *chunks,
+        place, own, weight, pick, logits, teacher_logits, head, *chunks,
     )
 
 

time: 175 us -> 172 us (0.983)
  blocking collectives: 0 us -> 18.8 us
  waiting for transfers between devices: 52.7 us -> 41.9 us
  starting transfers between devices: 89.7 us -> 82.3 us
  matrix products: 16.9 us -> 13.5 us
    all_to_all x0 -> x1, blocking collectives: none -> 18.8 us  [finish(): lax.all_to_all(jnp.broadcast_to(pair, (count,) + pair.shape), 'vocab', 0, 0)]
    all_to_all x1 -> x0, waiting for transfers between devices: 10.8 us -> none  [body(): lax.all_to_all(jnp.broadcast_to(pair, (count,) + pair.shape), 'vocab', 0, 0)]
    all_to_all x1 -> x0, starting transfers between devices: 9.67 us -> none  [body(): lax.all_to_all(jnp.broadcast_to(pair, (count,) + pair.shape), 'vocab', 0, 0)]
    ppermute x14, starting transfers between devices: 68.5 us -> 70.5 us  [body(): held = [lax.ppermute(part, ('side', 'row'), ring) for part in held]]
  transfers between devices with their start and end apart: 18 -> 17, of which waited for: 16 -> 14; matrix products, arithmetic and copies ran while one was open for 11% -> 9% of each run, Pallas kernels for 0% -> 0%
where the time goes in v13:
time: 172 us; the launch traced here: 171 us
  starting transfers between devices  82.3 us (48%)
  waiting for transfers between devices  41.9 us (24%)
  blocking collectives  18.8 us (11%)
  matrix products  13.5 us (8%)
  Pallas kernels  5.82 us (3%)
  other arithmetic  4.25 us (2%)
  local copies, waits for them, and re-layouts  2.2 us (1%)
  between operations  1.96 us (1%)
    ppermute x14, starting transfers between devices, body(): held = [lax.ppermute(part, ('side', 'row'), ring) for part in held]  70.5 us
    ppermute x14, waiting for transfers between devices, body(): held = [lax.ppermute(part, ('side', 'row'), ring) for part in held]  23.8 us
    all_to_all x1, blocking collectives, finish(): lax.all_to_all(jnp.broadcast_to(pair, (count,) + pair.shape), 'vocab', 0, 0)  18.8 us
    all_to_all x1, waiting for transfers between devices, finish(): pieces = lax.all_to_all(packed, 'vocab', 0, 0)  15.8 us
    dot_general x14, matrix products, body(): jnp.dot(piece, held[part], preferred_element_type=jnp.float32)  8.7 us
    ppermute x2, starting transfers between devices, swap_side(): return lax.ppermute(value, 'side', [(0, 1), (1, 0)])  7.91 us
    pallas_call x1, Pallas kernels, grad_products(): pl.pallas_call(functools.partial(grad_kernel, blocks, toks), out_shape=[j...  5.82 us
    all_to_all x1, starting transfers between devices, finish(): pieces = lax.all_to_all(packed, 'vocab', 0, 0)  3.89 us
  transfers between devices with their start and end apart: 17, of which 14 were waited for; matrix products, arithmetic and copies ran while one was open for 9% of the time, Pallas kernels for 0%

profile of v13, /device:TPU:1, one launch (start us, length us, event | category | flops | bytes accessed | tf_op | source)
XLA Modules:
  0.0 171.1 jit_solution(8002641967910865855)
XLA Ops:
  0.7 1.5 fusion.64
  2.2 11.5 %collective-permute-start.4 = (bf16[256,1280]{1,0:T(8,128)(2,1)S(1)}, bf16[256,1280]{1,0:T(8,128)(2,1)}, u32[]{:S(2)}, u32[]{:S(2)}) collective-permute-start(bf16[256,1280]{1,0:T(8,128)(2,1)S(1)} %get-tuple-element.200), channel_id=1, source_target_pairs={{0,32},{32,64},{64,96},{96,128},{128,160},{160,192},{192,224},{224... | collective-permute-start | bytes 1966088 | tf_op jit(solution)/shard_map/ppermute | solution.py:159
  13.7 2.2 %collective-permute-start.5 = (bf16[256,1280]{1,0:T(8,128)(2,1)S(1)}, bf16[256,1280]{1,0:T(8,128)(2,1)}, u32[]{:S(2)}, u32[]{:S(2)}) collective-permute-start(bf16[256,1280]{1,0:T(8,128)(2,1)S(1)} %get-tuple-element.199), channel_id=1, source_target_pairs={{0,32},{32,64},{64,96},{96,128},{128,160},{160,192},{192,224},{224... | collective-permute-start | bytes 1966088 | tf_op jit(solution)/shard_map/ppermute | solution.py:159
  16.0 0.2 select_reduce_fusion.3
  16.3 0.1 convert_reduce_fusion
  16.4 4.7 %collective-permute-done.4 = bf16[256,1280]{1,0:T(8,128)(2,1)} collective-permute-done((bf16[256,1280]{1,0:T(8,128)(2,1)S(1)}, bf16[256,1280]{1,0:T(8,128)(2,1)}, u32[]{:S(2)}, u32[]{:S(2)}) %collective-permute-start.4) | collective-permute-done | bytes 655392 | tf_op jit(solution)/shard_map/ppermute | solution.py:159
  21.2 5.1 %collective-permute-start.6 = (bf16[256,1280]{1,0:T(8,128)(2,1)}, bf16[256,1280]{1,0:T(8,128)(2,1)S(1)}, u32[]{:S(2)}, u32[]{:S(2)}) collective-permute-start(bf16[256,1280]{1,0:T(8,128)(2,1)} %collective-permute-done.4), channel_id=1, source_target_pairs={{0,32},{32,64},{64,96},{96,128},{128,160},{160,192},{192,224},{224... | collective-permute-start | bytes 1966088 | tf_op jit(solution)/shard_map/ppermute | solution.py:159
  26.3 1.9 %collective-permute-done.5 = bf16[256,1280]{1,0:T(8,128)(2,1)} collective-permute-done((bf16[256,1280]{1,0:T(8,128)(2,1)S(1)}, bf16[256,1280]{1,0:T(8,128)(2,1)}, u32[]{:S(2)}, u32[]{:S(2)}) %collective-permute-start.5) | collective-permute-done | bytes 655392 | tf_op jit(solution)/shard_map/ppermute | solution.py:159
  28.2 5.1 %collective-permute-start.7 = (bf16[256,1280]{1,0:T(8,128)(2,1)}, bf16[256,1280]{1,0:T(8,128)(2,1)S(1)}, u32[]{:S(2)}, u32[]{:S(2)}) collective-permute-start(bf16[256,1280]{1,0:T(8,128)(2,1)} %collective-permute-done.5), channel_id=1, source_target_pairs={{0,32},{32,64},{64,96},{96,128},{128,160},{160,192},{192,224},{224... | collective-permute-start | bytes 1966088 | tf_op jit(solution)/shard_map/ppermute | solution.py:159
  33.3 0.6 convert_reduce_fusion.1
  34.0 0.6 subtract_select_fusion
  34.6 0.1 select_reduce_fusion.2
  34.8 1.7 %convolution_convert_fusion.2 = bf16[192,4096]{1,0:T(8,128)(2,1)} fusion(bf16[192,4096]{1,0:T(8,128)(2,1)S(1)} %copy-done, s32[192]{0:T(256)S(1)} %subtract_select_fusion), kind=kOutput, calls=%fused_computation.40 | convolution fusion | flops 302813184 | bytes 3146496 | tf_op jit(solution)/shard_map/dot_general | solution.py:143
  36.5 3.8 %collective-permute-start.8 = (bf16[256,1280]{1,0:T(8,128)(2,1)S(1)}, bf16[256,1280]{1,0:T(8,128)(2,1)}, u32[]{:S(2)}, u32[]{:S(2)}) collective-permute-start(bf16[256,1280]{1,0:T(8,128)(2,1)S(1)} %collective-permute-done.6), channel_id=1, source_target_pairs={{0,32},{32,64},{64,96},{96,128},{128,160},{160,192},{192,224},{224... | collective-permute-start | bytes 1966088 | tf_op jit(solution)/shard_map/ppermute | solution.py:159
  40.2 2.1 %collective-permute-done.7 = bf16[256,1280]{1,0:T(8,128)(2,1)S(1)} collective-permute-done((bf16[256,1280]{1,0:T(8,128)(2,1)}, bf16[256,1280]{1,0:T(8,128)(2,1)S(1)}, u32[]{:S(2)}, u32[]{:S(2)}) %collective-permute-start.7) | collective-permute-done | bytes 655392 | tf_op jit(solution)/shard_map/ppermute | solution.py:159
  42.4 4.9 %collective-permute-start.9 = (bf16[256,1280]{1,0:T(8,128)(2,1)S(1)}, bf16[256,1280]{1,0:T(8,128)(2,1)}, u32[]{:S(2)}, u32[]{:S(2)}) collective-permute-start(bf16[256,1280]{1,0:T(8,128)(2,1)S(1)} %collective-permute-done.7), channel_id=1, source_target_pairs={{0,32},{32,64},{64,96},{96,128},{128,160},{160,192},{192,224},{224... | collective-permute-start | bytes 1966088 | tf_op jit(solution)/shard_map/ppermute | solution.py:159
  47.3 0.4 fusion.66
  48.6 2.0 %fusion.23 = f32[192,1280]{1,0:T(8,128)S(1)} fusion(bf16[512,1280]{1,0:T(8,128)(2,1)} %param.9, bf16[192,4096]{1,0:T(8,128)(2,1)} %convolution_convert_fusion.2, s32[]{:T(128)S(6)} %select_n.113), kind=kOutput, calls=%fused_computation.61 | convolution fusion | flops 251658240 | bytes 2490372 | tf_op jit(solution)/shard_map/dot_general | solution.py:154
  50.6 3.8 %collective-permute-start.10 = (bf16[256,1280]{1,0:T(8,128)(2,1)}, bf16[256,1280]{1,0:T(8,128)(2,1)S(1)}, u32[]{:S(2)}, u32[]{:S(2)}) collective-permute-start(bf16[256,1280]{1,0:T(8,128)(2,1)} %collective-permute-done.8), channel_id=1, source_target_pairs={{0,32},{32,64},{64,96},{96,128},{128,160},{160,192},{192,224},{224... | collective-permute-start | bytes 1966088 | tf_op jit(solution)/shard_map/ppermute | solution.py:159
  54.5 1.8 %collective-permute-done.9 = bf16[256,1280]{1,0:T(8,128)(2,1)} collective-permute-done((bf16[256,1280]{1,0:T(8,128)(2,1)S(1)}, bf16[256,1280]{1,0:T(8,128)(2,1)}, u32[]{:S(2)}, u32[]{:S(2)}) %collective-permute-start.9) | collective-permute-done | bytes 655392 | tf_op jit(solution)/shard_map/ppermute | solution.py:159
  56.3 5.1 %collective-permute-start.11 = (bf16[256,1280]{1,0:T(8,128)(2,1)}, bf16[256,1280]{1,0:T(8,128)(2,1)S(1)}, u32[]{:S(2)}, u32[]{:S(2)}) collective-permute-start(bf16[256,1280]{1,0:T(8,128)(2,1)} %collective-permute-done.9), channel_id=1, source_target_pairs={{0,32},{32,64},{64,96},{96,128},{128,160},{160,192},{192,224},{224... | collective-permute-start | bytes 1966088 | tf_op jit(solution)/shard_map/ppermute | solution.py:159
  61.4 1.4 convolution_add_fusion.7
  62.8 1.4 convolution_add_fusion.6
  64.3 4.1 %collective-permute-start.12 = (bf16[256,1280]{1,0:T(8,128)(2,1)S(1)}, bf16[256,1280]{1,0:T(8,128)(2,1)S(1)}, u32[]{:S(2)}, u32[]{:S(2)}) collective-permute-start(bf16[256,1280]{1,0:T(8,128)(2,1)S(1)} %collective-permute-done.10), channel_id=1, source_target_pairs={{0,32},{32,64},{64,96},{96,128},{128,160},{160,192},{192,224},{224... | collective-permute-start | bytes 1966088 | tf_op jit(solution)/shard_map/ppermute | solution.py:159
  68.3 0.3 fusion.41
  68.7 1.8 %collective-permute-done.11 = bf16[256,1280]{1,0:T(8,128)(2,1)S(1)} collective-permute-done((bf16[256,1280]{1,0:T(8,128)(2,1)}, bf16[256,1280]{1,0:T(8,128)(2,1)S(1)}, u32[]{:S(2)}, u32[]{:S(2)}) %collective-permute-start.11) | collective-permute-done | bytes 655392 | tf_op jit(solution)/shard_map/ppermute | solution.py:159
  70.4 4.9 %collective-permute-start.13 = (bf16[256,1280]{1,0:T(8,128)(2,1)S(1)}, bf16[256,1280]{1,0:T(8,128)(2,1)S(1)}, u32[]{:S(2)}, u32[]{:S(2)}) collective-permute-start(bf16[256,1280]{1,0:T(8,128)(2,1)S(1)} %collective-permute-done.11), channel_id=1, source_target_pairs={{0,32},{32,64},{64,96},{96,128},{128,160},{160,192},{192,224},{224... | collective-permute-start | bytes 1966088 | tf_op jit(solution)/shard_map/ppermute | solution.py:159
  75.4 1.4 fusion.39
  76.8 0.3 fusion.22
  77.1 0.3 collective-permute-done.12
  77.4 5.0 %collective-permute-start.14 = (bf16[256,1280]{1,0:T(8,128)(2,1)S(1)}, bf16[256,1280]{1,0:T(8,128)(2,1)S(1)}, u32[]{:S(2)}, u32[]{:S(2)}) collective-permute-start(bf16[256,1280]{1,0:T(8,128)(2,1)S(1)} %collective-permute-done.12), channel_id=1, source_target_pairs={{0,32},{32,64},{64,96},{96,128},{128,160},{160,192},{192,224},{224... | collective-permute-start | bytes 1966088 | tf_op jit(solution)/shard_map/ppermute | solution.py:159
  82.4 0.3 fusion.36
  82.7 1.7 collective-permute-done.13
  84.4 5.0 %collective-permute-start.15 = (bf16[256,1280]{1,0:T(8,128)(2,1)S(1)}, bf16[256,1280]{1,0:T(8,128)(2,1)S(1)}, u32[]{:S(2)}, u32[]{:S(2)}) collective-permute-start(bf16[256,1280]{1,0:T(8,128)(2,1)S(1)} %collective-permute-done.13), channel_id=1, source_target_pairs={{0,32},{32,64},{64,96},{96,128},{128,160},{160,192},{192,224},{224... | collective-permute-start | bytes 1966088 | tf_op jit(solution)/shard_map/ppermute | solution.py:159
  89.4 1.4 fusion.18
  90.8 0.3 fusion.33
  91.1 0.3 collective-permute-done.14
  91.4 5.0 %collective-permute-start.16 = (bf16[256,1280]{1,0:T(8,128)(2,1)S(1)}, bf16[256,1280]{1,0:T(8,128)(2,1)S(1)}, u32[]{:S(2)}, u32[]{:S(2)}) collective-permute-start(bf16[256,1280]{1,0:T(8,128)(2,1)S(1)} %collective-permute-done.14), channel_id=1, source_target_pairs={{0,32},{32,64},{64,96},{96,128},{128,160},{160,192},{192,224},{224... | collective-permute-start | bytes 1966088 | tf_op jit(solution)/shard_map/ppermute | solution.py:159
  96.4 0.3 fusion.19
  96.7 1.7 collective-permute-done.15
  98.4 5.0 %collective-permute-start.17 = (bf16[256,1280]{1,0:T(8,128)(2,1)S(1)}, bf16[256,1280]{1,0:T(8,128)(2,1)S(1)}, u32[]{:S(2)}, u32[]{:S(2)}) collective-permute-start(bf16[256,1280]{1,0:T(8,128)(2,1)S(1)} %collective-permute-done.15), channel_id=1, source_target_pairs={{0,32},{32,64},{64,96},{96,128},{128,160},{160,192},{192,224},{224... | collective-permute-start | bytes 1966088 | tf_op jit(solution)/shard_map/ppermute | solution.py:159
  103.5 0.3 fusion.30
  103.8 0.3 fusion.20
  104.1 1.4 collective-permute-done.16
  105.4 0.3 fusion.27
  105.8 0.3 fusion.21
  106.1 0.3 copy-done.7
  106.3 6.1 %collective-permute-done.17 = bf16[256,1280]{1,0:T(8,128)(2,1)S(1)} collective-permute-done((bf16[256,1280]{1,0:T(8,128)(2,1)S(1)}, bf16[256,1280]{1,0:T(8,128)(2,1)S(1)}, u32[]{:S(2)}, u32[]{:S(2)}) %collective-permute-start.17) | collective-permute-done | bytes 655392 | tf_op jit(solution)/shard_map/ppermute | solution.py:159
  112.5 0.4 fusion.65
  112.9 0.6 multiply_reduce_fusion.2
  113.5 57.6 %conditional.3 = (f32[12]{0:T(128)}, bf16[192,64]{0,1:T(8,128)(2,1)}) conditional(s32[]{:T(128)} %convert_element_type.62, (f32[8,192]{1,0:T(8,128)S(1)}, f32[192]{0:T(256)S(1)}, s32[2]{0:T(128)S(1)}, f32[192,1280]{1,0:T(8,128)S(1)}, bf16[192,1280]{1,0:T(8,128)(2,1)S(1)}, /*index=5*/bf16[512,1280]{1,0:T(8,128)(2,1)}, bf16[256,1280]{1,0:T(8,128)(2,1)}, ...), branch_computations={%region_9.16_spmd, %region_16.0_spmd} | conditional | flops 2019710848 | bytes 20791734
  113.7 3.9 %collective-permute-start = (f32[8,128]{1,0:T(8,128)S(1)}, f32[8,128]{1,0:T(8,128)S(1)}, u32[]{:S(2)}, u32[]{:S(2)}) collective-permute-start(f32[8,128]{1,0:T(8,128)S(1)} %slice.88), channel_id=1, source_target_pairs={{0,256},{256,0},{1,257},{257,1},{2,258},{258,2},{3,259},{259,3},{4... | collective-permute-start | bytes 12296 | tf_op jit(solution)/shard_map/cond/branch_1_fun/ppermute | solution.py:21
  117.6 0.8 collective-permute-done
  118.5 18.8 %all_to_all.17.stats_ref = f32[32,8,128]{2,1,0:T(8,128)S(1)} all-to-all(f32[32,8,128]{2,1,0:T(8,128)S(1)} %broadcast_in_dim.92), channel_id=1, replica_groups=mesh['side'=2,'row'=8,'vocab'=32] {'vocab'}, dimensions={0} | all-to-all | bytes 262144 | tf_op jit(solution)/shard_map/cond/branch_1_fun/all_to_all | solution.py:185
  137.3 5.8 %branch_1_fun.1 = (f32[2,32,64,128]{3,2,1,0:T(8,128)S(1)}, bf16[32,64,128]{2,1,0:T(8,128)(2,1)S(1)}, f32[1,128]{1,0:T(1,128)S(1)}) custom-call(s32[2]{0:T(128)S(1)} %get-tuple-element.118.place_ref, f32[32,8,128]{2,1,0:T(8,128)S(1)} %all_to_all.17.stats_ref, f32[1,192]{1,0:T(1,128)S(1)} %bitcast.55, f32[192,1280]{1,0:T(8,128)S(1)} %get-tuple-element.120.logits_ref, ...), custom_call_target="tpu_custom_call" | custom-call | flops 1342177280 | bytes 10485760 | tf_op jit(solution)/shard_map/cond/branch_1_fun/pallas_call | solution.py:102
  143.2 4.0 %collective-permute-start.1 = (bf16[32,64,128]{2,1,0:T(8,128)(2,1)S(1)}, bf16[32,64,128]{2,1,0:T(8,128)(2,1)S(1)}, u32[]{:S(2)}, u32[]{:S(2)}) collective-permute-start(bf16[32,64,128]{2,1,0:T(8,128)(2,1)S(1)} %get-tuple-element.139), channel_id=1, source_target_pairs={{0,256},{256,0},{1,257},{257,1},{2,258},{258,2},{3,259},{259,3},{4... | collective-permute-start | bytes 1572872 | tf_op jit(solution)/shard_map/cond/branch_1_fun/ppermute | solution.py:21
  147.2 1.5 collective-permute-done.1
  148.7 1.0 fusion.12
  149.7 3.9 %all-to-all-start.1 = ((bf16[32,64,128]{2,1,0:T(8,128)(2,1)}), bf16[32,64,128]{2,1,0:T(8,128)(2,1)S(1)}, u32[]{:S(2)}, u32[]{:S(2)}) async-start(bf16[32,64,128]{2,1,0:T(8,128)(2,1)} %fusion.12), calls=%async_computation.1 | async-start | bytes 1048576 | tf_op jit(solution)/shard_map/cond/branch_1_fun/all_to_all | solution.py:190
  153.6 0.1 select_reduce_fusion.1
  153.8 0.6 reduce_sum.172
  154.4 15.8 %all-to-all-done.1 = bf16[32,64,128]{2,1,0:T(8,128)(2,1)S(1)} async-done(((bf16[32,64,128]{2,1,0:T(8,128)(2,1)}), bf16[32,64,128]{2,1,0:T(8,128)(2,1)S(1)}, u32[]{:S(2)}, u32[]{:S(2)}) %all-to-all-start.1) | async-done | bytes 524320 | tf_op jit(solution)/shard_map/cond/branch_1_fun/all_to_all | solution.py:190
  170.2 0.1 reduce_sum.173
  170.3 0.8 fusion.11
  (52 shorter events, 0.6 us)
Async XLA Ops:
  0.6 34.1 %copy-start = (bf16[192,4096]{1,0:T(8,128)(2,1)S(1)}, bf16[192,4096]{1,0:T(8,128)(2,1)}, u32[]{:S(2)}) copy-start(bf16[192,4096]{1,0:T(8,128)(2,1)} %param.8) | copy-start | bytes 4718596
  0.6 15.2 %copy-start.14 = (s32[96]{0:T(128)S(1)}, s32[96]{0:T(128)}, u32[]{:S(2)}) copy-start(s32[96]{0:T(128)} %param.12) | copy-start | bytes 1156
  0.7 15.3 %copy-start.15 = (s32[96]{0:T(128)S(1)}, s32[96]{0:T(128)}, u32[]{:S(2)}) copy-start(s32[96]{0:T(128)} %param.11) | copy-start | bytes 1156
  0.7 15.6 %copy-start.13 = (s32[192]{0:T(256)S(1)}, s32[192]{0:T(256)}, u32[]{:S(2)}) copy-start(s32[192]{0:T(256)} %param.13) | copy-start | bytes 2308
  2.2 19.0 %collective-permute-start.4 = (bf16[256,1280]{1,0:T(8,128)(2,1)S(1)}, bf16[256,1280]{1,0:T(8,128)(2,1)}, u32[]{:S(2)}, u32[]{:S(2)}) collective-permute-start(bf16[256,1280]{1,0:T(8,128)(2,1)S(1)} %get-tuple-element.200), channel_id=1, source_target_pairs={{0,32},{32,64},{64,96},{96,128},{128,160},{160,192},{192,224},{224... | collective-permute-start | bytes 1966088 | tf_op jit(solution)/shard_map/ppermute | solution.py:159
  13.7 14.5 %collective-permute-start.5 = (bf16[256,1280]{1,0:T(8,128)(2,1)S(1)}, bf16[256,1280]{1,0:T(8,128)(2,1)}, u32[]{:S(2)}, u32[]{:S(2)}) collective-permute-start(bf16[256,1280]{1,0:T(8,128)(2,1)S(1)} %get-tuple-element.199), channel_id=1, source_target_pairs={{0,32},{32,64},{64,96},{96,128},{128,160},{160,192},{192,224},{224... | collective-permute-start | bytes 1966088 | tf_op jit(solution)/shard_map/ppermute | solution.py:159
  21.2 15.3 %collective-permute-start.6 = (bf16[256,1280]{1,0:T(8,128)(2,1)}, bf16[256,1280]{1,0:T(8,128)(2,1)S(1)}, u32[]{:S(2)}, u32[]{:S(2)}) collective-permute-start(bf16[256,1280]{1,0:T(8,128)(2,1)} %collective-permute-done.4), channel_id=1, source_target_pairs={{0,32},{32,64},{64,96},{96,128},{128,160},{160,192},{192,224},{224... | collective-permute-start | bytes 1966088 | tf_op jit(solution)/shard_map/ppermute | solution.py:159
  28.2 14.1 %collective-permute-start.7 = (bf16[256,1280]{1,0:T(8,128)(2,1)}, bf16[256,1280]{1,0:T(8,128)(2,1)S(1)}, u32[]{:S(2)}, u32[]{:S(2)}) collective-permute-start(bf16[256,1280]{1,0:T(8,128)(2,1)} %collective-permute-done.5), channel_id=1, source_target_pairs={{0,32},{32,64},{64,96},{96,128},{128,160},{160,192},{192,224},{224... | collective-permute-start | bytes 1966088 | tf_op jit(solution)/shard_map/ppermute | solution.py:159
  34.7 12.5 %copy-start.12 = (bf16[192,1280]{1,0:T(8,128)(2,1)S(1)}, bf16[192,1280]{1,0:T(8,128)(2,1)}, u32[]{:S(2)}) copy-start(bf16[192,1280]{1,0:T(8,128)(2,1)} %param.10) | copy-start | bytes 1474564
  36.5 40.3 %copy-start.2 = (bf16[256,1280]{1,0:T(8,128)(2,1)}, bf16[256,1280]{1,0:T(8,128)(2,1)S(1)}, u32[]{:S(2)}) copy-start(bf16[256,1280]{1,0:T(8,128)(2,1)S(1)} %collective-permute-done.6) | copy-start | bytes 1966084
  36.5 14.1 %collective-permute-start.8 = (bf16[256,1280]{1,0:T(8,128)(2,1)S(1)}, bf16[256,1280]{1,0:T(8,128)(2,1)}, u32[]{:S(2)}, u32[]{:S(2)}) collective-permute-start(bf16[256,1280]{1,0:T(8,128)(2,1)S(1)} %collective-permute-done.6), channel_id=1, source_target_pairs={{0,32},{32,64},{64,96},{96,128},{128,160},{160,192},{192,224},{224... | collective-permute-start | bytes 1966088 | tf_op jit(solution)/shard_map/ppermute | solution.py:159
  42.4 26.0 %copy-start.3 = (bf16[256,1280]{1,0:T(8,128)(2,1)}, bf16[256,1280]{1,0:T(8,128)(2,1)S(1)}, u32[]{:S(2)}) copy-start(bf16[256,1280]{1,0:T(8,128)(2,1)S(1)} %collective-permute-done.7) | copy-start | bytes 1966084
  42.4 13.9 %collective-permute-start.9 = (bf16[256,1280]{1,0:T(8,128)(2,1)S(1)}, bf16[256,1280]{1,0:T(8,128)(2,1)}, u32[]{:S(2)}, u32[]{:S(2)}) collective-permute-start(bf16[256,1280]{1,0:T(8,128)(2,1)S(1)} %collective-permute-done.7), channel_id=1, source_target_pairs={{0,32},{32,64},{64,96},{96,128},{128,160},{160,192},{192,224},{224... | collective-permute-start | bytes 1966088 | tf_op jit(solution)/shard_map/ppermute | solution.py:159
  48.6 12.9 %copy-start.1 = (bf16[192,4096]{1,0:T(8,128)(2,1)S(1)}, bf16[192,4096]{1,0:T(8,128)(2,1)}, u32[]{:S(2)}) copy-start(bf16[192,4096]{1,0:T(8,128)(2,1)} %convolution_convert_fusion.2) | copy-start | bytes 4718596
  50.6 13.7 %collective-permute-start.10 = (bf16[256,1280]{1,0:T(8,128)(2,1)}, bf16[256,1280]{1,0:T(8,128)(2,1)S(1)}, u32[]{:S(2)}, u32[]{:S(2)}) collective-permute-start(bf16[256,1280]{1,0:T(8,128)(2,1)} %collective-permute-done.8), channel_id=1, source_target_pairs={{0,32},{32,64},{64,96},{96,128},{128,160},{160,192},{192,224},{224... | collective-permute-start | bytes 1966088 | tf_op jit(solution)/shard_map/ppermute | solution.py:159
  56.3 14.1 %collective-permute-start.11 = (bf16[256,1280]{1,0:T(8,128)(2,1)}, bf16[256,1280]{1,0:T(8,128)(2,1)S(1)}, u32[]{:S(2)}, u32[]{:S(2)}) collective-permute-start(bf16[256,1280]{1,0:T(8,128)(2,1)} %collective-permute-done.9), channel_id=1, source_target_pairs={{0,32},{32,64},{64,96},{96,128},{128,160},{160,192},{192,224},{224... | collective-permute-start | bytes 1966088 | tf_op jit(solution)/shard_map/ppermute | solution.py:159
  64.2 18.1 %copy-start.4 = (bf16[256,1280]{1,0:T(8,128)(2,1)}, bf16[256,1280]{1,0:T(8,128)(2,1)S(1)}, u32[]{:S(2)}) copy-start(bf16[256,1280]{1,0:T(8,128)(2,1)S(1)} %collective-permute-done.10) | copy-start | bytes 1966084
  64.3 13.1 %collective-permute-start.12 = (bf16[256,1280]{1,0:T(8,128)(2,1)S(1)}, bf16[256,1280]{1,0:T(8,128)(2,1)S(1)}, u32[]{:S(2)}, u32[]{:S(2)}) collective-permute-start(bf16[256,1280]{1,0:T(8,128)(2,1)S(1)} %collective-permute-done.10), channel_id=1, source_target_pairs={{0,32},{32,64},{64,96},{96,128},{128,160},{160,192},{192,224},{224... | collective-permute-start | bytes 1966088 | tf_op jit(solution)/shard_map/ppermute | solution.py:159
  70.4 26.0 %copy-start.9 = (bf16[256,1280]{1,0:T(8,128)(2,1)}, bf16[256,1280]{1,0:T(8,128)(2,1)S(1)}, u32[]{:S(2)}) copy-start(bf16[256,1280]{1,0:T(8,128)(2,1)S(1)} %collective-permute-done.11) | copy-start | bytes 1966084
  70.4 13.9 %collective-permute-start.13 = (bf16[256,1280]{1,0:T(8,128)(2,1)S(1)}, bf16[256,1280]{1,0:T(8,128)(2,1)S(1)}, u32[]{:S(2)}, u32[]{:S(2)}) collective-permute-start(bf16[256,1280]{1,0:T(8,128)(2,1)S(1)} %collective-permute-done.11), channel_id=1, source_target_pairs={{0,32},{32,64},{64,96},{96,128},{128,160},{160,192},{192,224},{224... | collective-permute-start | bytes 1966088 | tf_op jit(solution)/shard_map/ppermute | solution.py:159
  77.4 13.4 %copy-start.5 = (bf16[256,1280]{1,0:T(8,128)(2,1)}, bf16[256,1280]{1,0:T(8,128)(2,1)S(1)}, u32[]{:S(2)}) copy-start(bf16[256,1280]{1,0:T(8,128)(2,1)S(1)} %collective-permute-done.12) | copy-start | bytes 1966084
  77.4 14.0 %collective-permute-start.14 = (bf16[256,1280]{1,0:T(8,128)(2,1)S(1)}, bf16[256,1280]{1,0:T(8,128)(2,1)S(1)}, u32[]{:S(2)}, u32[]{:S(2)}) collective-permute-start(bf16[256,1280]{1,0:T(8,128)(2,1)S(1)} %collective-permute-done.12), channel_id=1, source_target_pairs={{0,32},{32,64},{64,96},{96,128},{128,160},{160,192},{192,224},{224... | collective-permute-start | bytes 1966088 | tf_op jit(solution)/shard_map/ppermute | solution.py:159
  84.4 19.4 %copy-start.10 = (bf16[256,1280]{1,0:T(8,128)(2,1)}, bf16[256,1280]{1,0:T(8,128)(2,1)S(1)}, u32[]{:S(2)}) copy-start(bf16[256,1280]{1,0:T(8,128)(2,1)S(1)} %collective-permute-done.13) | copy-start | bytes 1966084
  84.4 14.0 %collective-permute-start.15 = (bf16[256,1280]{1,0:T(8,128)(2,1)S(1)}, bf16[256,1280]{1,0:T(8,128)(2,1)S(1)}, u32[]{:S(2)}, u32[]{:S(2)}) collective-permute-start(bf16[256,1280]{1,0:T(8,128)(2,1)S(1)} %collective-permute-done.13), channel_id=1, source_target_pairs={{0,32},{32,64},{64,96},{96,128},{128,160},{160,192},{192,224},{224... | collective-permute-start | bytes 1966088 | tf_op jit(solution)/shard_map/ppermute | solution.py:159
  91.4 12.0 %copy-start.6 = (bf16[256,1280]{1,0:T(8,128)(2,1)}, bf16[256,1280]{1,0:T(8,128)(2,1)S(1)}, u32[]{:S(2)}) copy-start(bf16[256,1280]{1,0:T(8,128)(2,1)S(1)} %collective-permute-done.14) | copy-start | bytes 1966084
  91.4 14.0 %collective-permute-start.16 = (bf16[256,1280]{1,0:T(8,128)(2,1)S(1)}, bf16[256,1280]{1,0:T(8,128)(2,1)S(1)}, u32[]{:S(2)}, u32[]{:S(2)}) collective-permute-start(bf16[256,1280]{1,0:T(8,128)(2,1)S(1)} %collective-permute-done.14), channel_id=1, source_target_pairs={{0,32},{32,64},{64,96},{96,128},{128,160},{160,192},{192,224},{224... | collective-permute-start | bytes 1966088 | tf_op jit(solution)/shard_map/ppermute | solution.py:159
  98.4 7.3 %copy-start.11 = (bf16[256,1280]{1,0:T(8,128)(2,1)}, bf16[256,1280]{1,0:T(8,128)(2,1)S(1)}, u32[]{:S(2)}) copy-start(bf16[256,1280]{1,0:T(8,128)(2,1)S(1)} %collective-permute-done.15) | copy-start | bytes 1966084
  98.4 14.0 %collective-permute-start.17 = (bf16[256,1280]{1,0:T(8,128)(2,1)S(1)}, bf16[256,1280]{1,0:T(8,128)(2,1)S(1)}, u32[]{:S(2)}, u32[]{:S(2)}) collective-permute-start(bf16[256,1280]{1,0:T(8,128)(2,1)S(1)} %collective-permute-done.15), channel_id=1, source_target_pairs={{0,32},{32,64},{64,96},{96,128},{128,160},{160,192},{192,224},{224... | collective-permute-start | bytes 1966088 | tf_op jit(solution)/shard_map/ppermute | solution.py:159
  105.4 0.9 copy-start.7
  112.5 1.0 copy-start.8
  113.7 4.7 %collective-permute-start = (f32[8,128]{1,0:T(8,128)S(1)}, f32[8,128]{1,0:T(8,128)S(1)}, u32[]{:S(2)}, u32[]{:S(2)}) collective-permute-start(f32[8,128]{1,0:T(8,128)S(1)} %slice.88), channel_id=1, source_target_pairs={{0,256},{256,0},{1,257},{257,1},{2,258},{258,2},{3,259},{259,3},{4... | collective-permute-start | bytes 12296 | tf_op jit(solution)/shard_map/cond/branch_1_fun/ppermute | solution.py:21
  143.2 5.5 %collective-permute-start.1 = (bf16[32,64,128]{2,1,0:T(8,128)(2,1)S(1)}, bf16[32,64,128]{2,1,0:T(8,128)(2,1)S(1)}, u32[]{:S(2)}, u32[]{:S(2)}) collective-permute-start(bf16[32,64,128]{2,1,0:T(8,128)(2,1)S(1)} %get-tuple-element.139), channel_id=1, source_target_pairs={{0,256},{256,0},{1,257},{257,1},{2,258},{258,2},{3,259},{259,3},{4... | collective-permute-start | bytes 1572872 | tf_op jit(solution)/shard_map/cond/branch_1_fun/ppermute | solution.py:21
  149.7 20.6 %all-to-all-start.1 = ((bf16[32,64,128]{2,1,0:T(8,128)(2,1)}), bf16[32,64,128]{2,1,0:T(8,128)(2,1)S(1)}, u32[]{:S(2)}, u32[]{:S(2)}) async-start(bf16[32,64,128]{2,1,0:T(8,128)(2,1)} %fusion.12), calls=%async_computation.1 | async-start | bytes 1048576 | tf_op jit(solution)/shard_map/cond/branch_1_fun/all_to_all | solution.py:190
